TPU v7x, 128 devices: a whole 4x4x4 slice. The times are simulated.
128 devices in a mesh: feat: 8 (over y, core), dom: 16 (over x, z).
Axes of the slice: x: 4, y: 4, z: 4, core: 2. Of those that a mesh axis runs over, the one named last changes fastest.
Arguments:
- features: bfloat16 [768, 16, 2048], P('feat', 'dom'), may hold values from -6 to 6
- first_weight: bfloat16 [768, 1024], P('feat'), may hold values from -4 to 4
- second_weight: bfloat16 [1024, 153], replicated, may hold values from -6 to 6
- degree: int32 [16, 2048], P('dom', 'feat'), may hold values from 1 to 801, as said below
- neighbour_block: int32 [16, 16, 6], P('dom', 'feat'), may hold values from -1 to 31, as said below
- neighbour_mask: int32 [16, 16, 6, 128, 128], P('dom', 'feat'), may hold values from 0 to 1, as said below
- upstream: bfloat16 [16, 2048, 153], P('dom', 'feat'), may hold values from -0.078125 to 0.078125
Outputs:
- hidden: bfloat16 [16, 2048, 1024], P('dom', 'feat')
- grad_first: float32 [768, 1024], P('feat')
- grad_second: float32 [1024, 153], replicated
Inputs may be any that keep to these rules, and one draw needn't show every extreme that they name: `neighbour_block`: within each group the block pattern is symmetric: the block row of block t names block c in some slot exactly when the block row of c names t. A block row names distinct blocks other than its own, live ones in its first slots and -1 in the others; in every group some block row has all 6 slots live. `neighbour_mask`: all zeros in slots that hold -1. The mask in the slot where block t names c is the transpose of the mask in the slot where c names t. `degree`: at least one plus the number of ones in the node's rows of its block row's masks.
All inputs are finite; a program needn't handle non-finite values.
Results may differ from a plain program's by a relative error of at most 0.018.
Values may be sent and summed in bfloat16 or wider, within the bound.
No kernel may reach another device: no remote copies, remote signals or barrier semaphores. Data moves between devices by JAX's collectives and lax.ppermute only.
A program may use at most 128 MiB of HBM per device.

v0:
```python
import jax
import jax.numpy as jnp
from jax import lax
from jax.sharding import PartitionSpec as P


def body(features, first_weight, second_weight, degree, neighbour_block, neighbour_mask, upstream):
    own_columns = features[:, 0, :]
    row_count = degree.shape[1]
    block_rows = neighbour_block.shape[1]
    slot_count = neighbour_block.shape[2]
    block_width = neighbour_mask.shape[-1]
    hidden_width = first_weight.shape[1]
    inverse_root = lax.rsqrt(degree[0].astype(jnp.float32))[:, None]
    block_masks = neighbour_mask[0].astype(jnp.bfloat16)
    neighbours = jnp.maximum(neighbour_block[0], 0)
    pick_rows = (
        neighbours[:, :, None] * block_width + jnp.arange(block_width)[None, None, :]
    ).reshape(-1)

    def apply_masks(whole):
        picked = jnp.take(whole, pick_rows, axis=0)
        blocks = picked.reshape(block_rows, slot_count, block_width, hidden_width)
        summed = jnp.einsum(
            "bkij,bkjh->bih", block_masks, blocks, preferred_element_type=jnp.float32
        )
        return summed.reshape(row_count, hidden_width)

    def forward_mix(vector):
        whole = lax.all_gather(vector, "dom", axis=0, tiled=True)
        return apply_masks(whole)

    def pull_back(vector):
        group_blocks = lax.axis_size("dom") * block_rows
        own_blocks = vector.reshape(block_rows, block_width, hidden_width)
        spread = jnp.einsum(
            "bkij,bih->bkjh", block_masks, own_blocks, preferred_element_type=jnp.float32
        )
        pooled = jax.ops.segment_sum(
            spread.reshape(block_rows * slot_count, block_width, hidden_width),
            neighbours.reshape(-1),
            num_segments=group_blocks,
        )
        pooled = pooled.reshape(group_blocks * block_width, hidden_width)
        return lax.psum_scatter(
            pooled.astype(jnp.bfloat16), "dom", scatter_dimension=0, tiled=True
        ).astype(jnp.float32)

    columns = own_columns
    product = lax.dot_general(
        columns, first_weight, (((0,), (0,)), ((), ())), preferred_element_type=jnp.float32
    )
    projected = lax.psum_scatter(
        lax.optimization_barrier(product.astype(jnp.bfloat16))
        .astype(jnp.float32)
        .astype(jnp.bfloat16),
        "feat",
        scatter_dimension=0,
        tiled=True,
    ).astype(jnp.float32)
    scaled_zero = (inverse_root * projected).astype(jnp.bfloat16)
    mixed_zero = inverse_root * (scaled_zero.astype(jnp.float32) + forward_mix(scaled_zero))
    sigma = jax.nn.sigmoid(mixed_zero)
    hidden = (mixed_zero * sigma).astype(jnp.bfloat16)
    scaled_one = (inverse_root * hidden.astype(jnp.float32)).astype(jnp.bfloat16)
    mixed_one = (inverse_root * (scaled_one.astype(jnp.float32) + forward_mix(scaled_one))).astype(
        jnp.bfloat16
    )
    upstream_rows = upstream[0]
    second_term = lax.dot_general(
        mixed_one, upstream_rows, (((0,), (0,)), ((), ())), preferred_element_type=jnp.float32
    )
    grad_second = lax.psum(second_term, ("feat", "dom"))
    back_product = lax.dot_general(
        upstream_rows, second_weight, (((1,), (1,)), ((), ())), preferred_element_type=jnp.float32
    )
    back_one = (inverse_root * back_product).astype(jnp.bfloat16)
    pulled_one = back_one.astype(jnp.float32) + pull_back(back_one)
    slope = sigma * (1.0 + mixed_zero * (1.0 - sigma))
    back_zero = (inverse_root * inverse_root * pulled_one * slope).astype(jnp.bfloat16)
    grad_rows = (inverse_root * (back_zero.astype(jnp.float32) + pull_back(back_zero))).astype(
        jnp.bfloat16
    )
    columns = own_columns
    first_term_sum = jnp.dot(
        columns,
        lax.all_gather(grad_rows, "feat", axis=0, tiled=True),
        preferred_element_type=jnp.float32,
    )
    grad_first = lax.psum(first_term_sum.astype(jnp.bfloat16), "dom").astype(jnp.float32)
    return (hidden[None], grad_first, grad_second)


def solution(mesh):
    placed = (
        P("feat", "dom", None),
        P("feat", None),
        P(),
        P("dom", "feat"),
        P("dom", "feat", None),
        P("dom", "feat", None, None, None),
        P("dom", "feat", None),
    )
    return jax.shard_map(
        body,
        mesh=mesh,
        in_specs=placed,
        out_specs=(P("dom", "feat", None), P("feat", None), P()),
        check_vma=False,
    )
```

profile of v0, /device:TPU:0, one launch (start us, length us, event | category | flops | bytes accessed | tf_op | source)
XLA Modules:
  0.0 654.1 jit_solution(2552267453419995001)
XLA Ops:
  7.2 0.9 copy-done
  8.2 4.1 convolution_convert_fusion
  12.4 0.6 copy-done.19
  13.0 39.8 %reduce-scatter.4.cloned.1.call-done = bf16[256,1024]{1,0:T(8,128)(2,1)} async-done(((bf16[2048,1024]{1,0:T(8,128)(2,1)}), bf16[256,1024]{1,0:T(8,128)(2,1)}) %reduce-scatter.4.cloned.1.call-update) | async-done | bytes 524304 | tf_op jit(solution)/shard_map/reduce_scatter | solution.py:53
  52.8 2.0 multiply_convert_fusion.4
  55.7 3.7 fusion.9
  59.4 6.6 %copy.15 = f32[12,128,1024]{2,1,0:T(8,128)} copy(f32[12,128,1024]{1,2,0:T(8,128)} %bitcast.80) | data formatting | bytes 12582912 | tf_op jit(solution)/shard_map/reshape | solution.py:40
  66.1 7.9 %broadcast.42.clone = f32[32,128,1024]{2,1,0:T(8,128)} broadcast(f32[]{:T(128)} %constant.3.clone.1), dimensions={} | broadcast | bytes 16777220 | tf_op jit(solution)/shard_map/broadcast.4
  74.0 13.6 %scatter_fusion = f32[32,128,1024]{2,1,0:T(8,128)} fusion(f32[32,128,1024]{2,1,0:T(8,128)} %broadcast.42.clone, s32[12]{0:T(128)S(1)} %reshape.106, f32[12,128,1024]{2,1,0:T(8,128)} %copy.15), kind=kCustom, calls=%fused_computation.2 | custom fusion | flops 1572864 | bytes 18874416 | tf_op jit(solution)/shard_map/scatter-add | solution.py:39
  87.6 9.5 %convert_element_type.98 = bf16[32,128,1024]{2,1,0:T(8,128)(2,1)} convert(f32[32,128,1024]{2,1,0:T(8,128)} %scatter_fusion) | non-fusion elementwise | flops 4194304 | bytes 25165824 | tf_op jit(solution)/shard_map/convert_element_type | solution.py:46
  97.8 27.4 %all-gather.4.cloned.1.call-done = bf16[4096,1024]{1,0:T(8,128)(2,1)} async-done(((bf16[256,1024]{1,0:T(8,128)(2,1)}), bf16[4096,1024]{1,0:T(8,128)(2,1)}) %all-gather.4.cloned.1.call-update) | async-done | bytes 8388624 | tf_op jit(solution)/shard_map/all_gather | solution.py:30
  125.3 11.6 %gather_fusion = bf16[1536,1024]{1,0:T(8,128)(2,1)S(1)} fusion(bf16[4096,1024]{1,0:T(8,128)(2,1)} %all-gather.4.cloned.1.call-done, s32[2048]{0:T(1024)S(1)} %pad_clamp_fusion), kind=kCustom, calls=%fused_computation.clone | custom fusion | bytes 6297600 | tf_op jit(solution)/shard_map/jit(_take)/gather | solution.py:22
  136.9 0.9 broadcast_select_fusion.1
  138.5 74.7 %reduce-scatter.6.cloned.1.call-done = bf16[256,1024]{1,0:T(8,128)(2,1)} async-done(((bf16[4096,1024]{1,0:T(8,128)(2,1)}), bf16[256,1024]{1,0:T(8,128)(2,1)}) %reduce-scatter.6.cloned.1.call-update) | async-done | bytes 524304 | tf_op jit(solution)/shard_map/reduce_scatter | solution.py:45
  213.3 2.9 multiply_convert_fusion
  216.4 3.7 fusion.7
  220.1 6.6 %copy.17 = f32[12,128,1024]{2,1,0:T(8,128)} copy(f32[12,128,1024]{1,2,0:T(8,128)} %bitcast.81) | data formatting | bytes 12582912 | tf_op jit(solution)/shard_map/reshape | solution.py:40
  226.7 7.9 %broadcast.42 = f32[32,128,1024]{2,1,0:T(8,128)} broadcast(f32[]{:T(128)} %constant.3.clone.1), dimensions={} | broadcast | bytes 16777220 | tf_op jit(solution)/shard_map/broadcast.4
  234.6 13.6 %scatter_fusion.1 = f32[32,128,1024]{2,1,0:T(8,128)} fusion(f32[32,128,1024]{2,1,0:T(8,128)} %broadcast.42, s32[12]{0:T(128)S(1)} %copy-done.17, f32[12,128,1024]{2,1,0:T(8,128)} %copy.17), kind=kCustom, calls=%fused_computation.3 | custom fusion | flops 1572864 | bytes 18874416 | tf_op jit(solution)/shard_map/scatter-add | solution.py:39
  248.2 9.8 %convert_element_type.103 = bf16[32,128,1024]{2,1,0:T(8,128)(2,1)} convert(f32[32,128,1024]{2,1,0:T(8,128)} %scatter_fusion.1) | non-fusion elementwise | flops 4194304 | bytes 25165824 | tf_op jit(solution)/shard_map/convert_element_type | solution.py:46
  258.1 28.4 %all-gather.8.cloned.1.call-done = bf16[4096,1024]{1,0:T(8,128)(2,1)} async-done(((bf16[256,1024]{1,0:T(8,128)(2,1)}), bf16[4096,1024]{1,0:T(8,128)(2,1)}) %all-gather.8.cloned.1.call-update) | async-done | bytes 8388624 | tf_op jit(solution)/shard_map/all_gather | solution.py:30
  286.5 11.6 %gather_fusion.1 = bf16[1536,1024]{1,0:T(8,128)(2,1)S(1)} fusion(bf16[4096,1024]{1,0:T(8,128)(2,1)} %all-gather.8.cloned.1.call-done, s32[2048]{0:T(1024)S(1)} %pad_clamp_fusion), kind=kCustom, calls=%fused_computation.1.clone | custom fusion | bytes 6297600 | tf_op jit(solution)/shard_map/jit(_take)/gather | solution.py:22
  298.0 0.9 broadcast_select_fusion
  299.7 74.9 %reduce-scatter.8.cloned.1.call-done = bf16[256,1024]{1,0:T(8,128)(2,1)} async-done(((bf16[4096,1024]{1,0:T(8,128)(2,1)}), bf16[256,1024]{1,0:T(8,128)(2,1)}) %reduce-scatter.8.cloned.1.call-update) | async-done | bytes 524304 | tf_op jit(solution)/shard_map/reduce_scatter | solution.py:45
  374.6 2.3 fusion.3
  377.1 31.6 %all-gather.6.cloned.1.call-done = bf16[2048,1024]{1,0:T(8,128)(2,1)} async-done(((bf16[256,1024]{1,0:T(8,128)(2,1)}), bf16[2048,1024]{1,0:T(8,128)(2,1)}) %all-gather.6.cloned.1.call-update) | async-done | bytes 4194320 | tf_op jit(solution)/shard_map/all_gather | solution.py:87
  408.6 3.7 fusion.1
  412.4 1.1 fusion.15
  413.5 82.5 %all-reduce.3.cloned.1.call-done = bf16[96,1024]{1,0:T(8,128)(2,1)} async-done(((bf16[96,1024]{1,0:T(8,128)(2,1)}), bf16[96,1024]{1,0:T(8,128)(2,1)}) %all-reduce.3.cloned.1.call-update) | async-done | bytes 196624 | tf_op jit(solution)/shard_map/psum | solution.py:90
  496.0 1.7 convert_element_type.109
  497.7 147.6 %all-reduce.5.cloned.1.call-done = f32[1024,153]{0,1:T(8,128)} async-done(((f32[1024,153]{0,1:T(8,128)}), f32[1024,153]{0,1:T(8,128)}) %all-reduce.5.cloned.1.call-update) | async-done | bytes 626704 | tf_op jit(solution)/shard_map/psum | solution.py:73
  645.3 2.0 copy.30
  (67 shorter events, 3.7 us)
Async XLA Ops:
  7.2 1.0 copy-start
  7.2 45.6 %reduce-scatter.4.cloned.1.call-start = ((), (), s32[]{:S(2)}) async-start(), calls=%async_computation.3 | async-start | bytes 4718592 | tf_op jit(solution)/shard_map/reduce_scatter | solution.py:53
  12.3 0.7 copy-start.19
  12.3 42.5 %copy-start.11 = (s32[1,2,6,128,128]{4,3,2,1,0:T(8,128)S(1)}, s32[1,2,6,128,128]{4,3,2,1,0:T(8,128)}, u32[]{:S(2)}) copy-start(s32[1,2,6,128,128]{4,3,2,1,0:T(8,128)} %param.14) | copy-start | bytes 2359300
  12.3 42.6 %copy-start.12 = (bf16[1,256,153]{1,2,0:T(8,128)(2,1)S(1)}, bf16[1,256,153]{1,2,0:T(8,128)(2,1)}, u32[]{:S(2)}) copy-start(bf16[1,256,153]{1,2,0:T(8,128)(2,1)} %param.15) | copy-start | bytes 235012
  12.3 42.6 %copy-start.14 = (bf16[1024,153]{0,1:T(8,128)(2,1)S(1)}, bf16[1024,153]{0,1:T(8,128)(2,1)}, u32[]{:S(2)}) copy-start(bf16[1024,153]{0,1:T(8,128)(2,1)} %param.11) | copy-start | bytes 940036
  12.3 112.9 %all-gather.4.cloned.1.call-start = ((), (), s32[]{:S(2)}) async-start(), calls=%async_computation.4 | async-start | bytes 8912896 | tf_op jit(solution)/shard_map/all_gather | solution.py:30
  54.8 158.5 %reduce-scatter.6.cloned.1.call-start = ((), (), s32[]{:S(2)}) async-start(), calls=%async_computation.5 | async-start | bytes 8912896 | tf_op jit(solution)/shard_map/reduce_scatter | solution.py:45
  54.9 0.7 copy-start.1
  55.3 4.1 copy-start.5
  59.4 6.6 %copy-start.18 = (s32[1,2,6]{2,1,0:T(2,128)S(1)}, s32[1,2,6]{2,1,0:T(2,128)}, u32[]{:S(2)}) copy-start(s32[1,2,6]{2,1,0:T(2,128)} %param.13) | copy-start | bytes 148
  66.1 7.9 %copy-start.16 = (s32[12]{0:T(128)}, s32[12]{0:T(128)S(1)}, u32[]{:S(2)}) copy-start(s32[12]{0:T(128)S(1)} %reshape.106) | copy-start | bytes 148
  97.1 189.3 %all-gather.8.cloned.1.call-start = ((), (), s32[]{:S(2)}) async-start(), calls=%async_computation.9 | async-start | bytes 8912896 | tf_op jit(solution)/shard_map/all_gather | solution.py:30
  136.9 1.1 copy-start.2
  137.8 75.5 %copy-start.6 = (bf16[256,1024]{1,0:T(8,128)(2,1)S(1)}, bf16[256,1024]{1,0:T(8,128)(2,1)}, u32[]{:S(2)}) copy-start(bf16[256,1024]{1,0:T(8,128)(2,1)} %copy-done.5) | copy-start | bytes 1572868
  137.8 75.5 %copy-start.9 = (bf16[256,1024]{1,0:T(8,128)(2,1)S(1)}, bf16[256,1024]{1,0:T(8,128)(2,1)}, u32[]{:S(2)}) copy-start(bf16[256,1024]{1,0:T(8,128)(2,1)} %reduce-scatter.4.cloned.1.call-done) | copy-start | bytes 1572868
  137.8 75.5 %copy-start.15 = (f32[256]{0:T(256)S(1)}, f32[256]{0:T(256)}, u32[]{:S(2)}) copy-start(f32[256]{0:T(256)} %mul.83) | copy-start | bytes 3076
  138.0 78.5 %copy-start.3 = (bf16[1,2,6,128,128]{4,3,2,1,0:T(8,128)(2,1)S(1)}, bf16[1,2,6,128,128]{4,3,2,1,0:T(8,128)(2,1)}, u32[]{:S(2)}) copy-start(bf16[1,2,6,128,128]{4,3,2,1,0:T(8,128)(2,1)} %copy-done.1) | copy-start | bytes 1179652
  216.2 10.6 %copy-start.7 = (bf16[256,1024]{1,0:T(8,128)(2,1)}, bf16[256,1024]{1,0:T(8,128)(2,1)S(1)}, u32[]{:S(2)}) copy-start(bf16[256,1024]{1,0:T(8,128)(2,1)S(1)} %get-tuple-element.6) | copy-start | bytes 1572868
  216.2 158.4 %reduce-scatter.8.cloned.1.call-start = ((), (), s32[]{:S(2)}) async-start(), calls=%async_computation.6 | async-start | bytes 8912896 | tf_op jit(solution)/shard_map/reduce_scatter | solution.py:45
  226.7 7.9 %copy-start.17 = (s32[12]{0:T(128)S(1)}, s32[12]{0:T(128)}, u32[]{:S(2)}) copy-start(s32[12]{0:T(128)} %copy-done.16) | copy-start | bytes 148
  258.0 150.6 %all-gather.6.cloned.1.call-start = ((), (), s32[]{:S(2)}) async-start(), calls=%async_computation.7 | async-start | bytes 4718592 | tf_op jit(solution)/shard_map/all_gather | solution.py:87
  298.0 1.1 copy-start.4
  299.0 75.6 %copy-start.8 = (bf16[256,1024]{1,0:T(8,128)(2,1)S(1)}, bf16[256,1024]{1,0:T(8,128)(2,1)}, u32[]{:S(2)}) copy-start(bf16[256,1024]{1,0:T(8,128)(2,1)} %copy-done.7) | copy-start | bytes 1572868
  299.0 75.6 %copy-start.10 = (bf16[256,1024]{1,0:T(8,128)(2,1)S(1)}, bf16[256,1024]{1,0:T(8,128)(2,1)}, u32[]{:S(2)}) copy-start(bf16[256,1024]{1,0:T(8,128)(2,1)} %get-tuple-element.5) | copy-start | bytes 1572868
  374.6 37.7 %copy-start.13 = (bf16[1,256,153]{1,2,0:T(8,128)(2,1)S(1)}, bf16[1,256,153]{1,2,0:T(8,128)(2,1)}, u32[]{:S(2)}) copy-start(bf16[1,256,153]{1,2,0:T(8,128)(2,1)} %param.15) | copy-start | bytes 235012
  377.0 119.0 %all-reduce.3.cloned.1.call-start = ((), (), s32[]{:S(2)}) async-start(), calls=%async_computation.8 | async-start | bytes 393216 | tf_op jit(solution)/shard_map/psum | solution.py:90
  412.3 233.0 %all-reduce.5.cloned.1.call-start = ((), (), s32[]{:S(2)}) async-start(), calls=%async_computation.10 | async-start | bytes 1310720 | tf_op jit(solution)/shard_map/psum | solution.py:73
Sparse Core Ops, SparseCore 0:
  12.5 40.2 reduce-scatter.3
  55.5 69.7 all-gather.3
  128.7 84.5 reduce-scatter.5
  216.3 70.1 all-gather.7
  289.7 84.8 reduce-scatter.7
  377.1 31.4 all-gather.5
  412.4 83.4 all-reduce.2
  501.3 143.9 all-reduce.4
where the time goes:
time: 657 us; the launch traced here: 654 us
  waiting for transfers between devices  507 us (77%)
  other arithmetic  58 us (9%)
  local copies, waits for them, and re-layouts  56.5 us (9%)
  matrix products  17.7 us (3%)
  between operations  14.3 us (2%)
    reduce_scatter x2, waiting for transfers between devices, pull_back(): lax.psum_scatter(pooled.astype(jnp.bfloat16), 'dom', scatter_dimension=0,...  150 us
    psum x1, waiting for transfers between devices, body(): grad_second = lax.psum(second_term, ('feat', 'dom'))  148 us
    psum x1, waiting for transfers between devices, body(): lax.psum(first_term_sum.astype(jnp.bfloat16), 'dom').astype(jnp.float32)  82.5 us
    all_gather x2, waiting for transfers between devices, forward_mix(): whole = lax.all_gather(vector, 'dom', axis=0, tiled=True)  55.9 us
    reduce_scatter x1, waiting for transfers between devices, body(): lax.psum_scatter(lax.optimization_barrier(product.astype(jnp.bfloat16)).a...  39.8 us
    all_gather x1, waiting for transfers between devices, body(): lax.all_gather(grad_rows, 'feat', axis=0, tiled=True)  31.6 us
    scatter-add x2, other arithmetic, pull_back(): jax.ops.segment_sum(spread.reshape(block_rows * slot_count, block_width,...  27.2 us
    gather x2, local copies, waits for them, and re-layouts, apply_masks(): picked = jnp.take(whole, pick_rows, axis=0)  23.1 us
  transfers between devices with their start and end apart: 8, of which 8 were waited for; matrix products, arithmetic and copies ran while one was open for 17% of the time, Pallas kernels for 0%

commit v1 on v0

v1 whole, which is shorter than its diff:
```python
import jax
import jax.numpy as jnp
from jax import lax
from jax.experimental import pallas as pl
from jax.experimental.pallas import tpu as pltpu
from jax.sharding import Mesh
from jax.sharding import PartitionSpec as P

BF = jnp.bfloat16
F32 = jnp.float32
I32 = jnp.int32
VMEM = pl.BlockSpec(memory_space=pltpu.VMEM)
SMEM = pl.BlockSpec(memory_space=pltpu.SMEM)
LIMIT = 48 * 1024 * 1024
RING = (0, 1, -1, 2)
NT = (((1,), (1,)), ((), ()))


def dot(a, b, dims=(((1,), (0,)), ((), ()))):
    return lax.dot_general(a, b, dims, preferred_element_type=F32)


def columns_of(row):
    return jnp.broadcast_to(row, (128, 128)).T


def halves(a, b):
    low = lax.broadcasted_iota(I32, a.shape, 1) < 64
    return jnp.where(low, a, pltpu.roll(b, 64, 1)), jnp.where(low, pltpu.roll(a, 64, 1), b)


def owner(block):
    return (block % 4) * 4 + block // 4


def mask_kernel(mask_ref, out_ref):
    for b in range(2):
        for k in range(6):
            out_ref[b, :, k * 128 : k * 128 + 128] = mask_ref[b, k].astype(F32).astype(BF)


def project_kernel(*refs):
    x_ref, up_ref, sw_ref, deg_ref, at_ref = refs[:5]
    w_refs, out_ref = refs[5:13], refs[13]
    sources = []
    for flip in range(2):
        for shift in RING:
            y, core = (at_ref[3] + shift + 4) % 4, (at_ref[4] + flip) % 2
            sources.append(y * 2 + core)
    for b in range(2):
        row = lax.rsqrt(deg_ref[b : b + 1, :].astype(F32))
        inv = columns_of(row)
        rows = pl.ds(b * 128, 128)
        x = jnp.concatenate([x_ref[f, :, rows] for f in sources], axis=0)
        for j in range(4):
            cols = pl.ds(j * 256, 256)
            w = jnp.concatenate([w_ref[:, cols] for w_ref in w_refs], axis=0)
            sz = dot(x, w, (((0,), (0,)), ((), ())))
            bo = (row * dot(sw_ref[cols, :], up_ref[rows, :], NT)).astype(BF)
            for h in range(2):
                s = (inv * sz[:, h * 128 : h * 128 + 128]).T.astype(BF)
                for q in range(2):
                    d = owner(j * 4 + h * 2 + q)
                    out_ref[d, b, 0:64, :] = s[q * 64 : q * 64 + 64]
                    out_ref[d, b, 64:128, :] = bo[h * 128 + q * 64 : h * 128 + q * 64 + 64]


def mix_kernel(
    v_ref, m_ref, small_ref, links_ref, at_ref, hid_ref, mo_ref, g0_ref, g1_ref, g2_ref, g3_ref, v2_ref
):
    def inverse(d, h):
        return lax.rsqrt(small_ref[d, h : h + 1, :].astype(F32))

    def spread(d, h, source):
        t = d * 2 + h
        named = [source[links_ref[d, 2, h * 6 + k]] for k in range(6)]
        return source[t].astype(F32) + dot(jnp.concatenate(named, axis=1), m_ref[t], NT)

    for d in range(16):
        for h in range(2):
            inv = inverse(d, h)
            total = spread(d, h, v_ref)
            m = inv * total[0:64]
            s = jax.nn.sigmoid(m)
            hid = (m * s).astype(BF)
            hid_ref[d, :, h * 128 : h * 128 + 128] = hid
            slope = s * (1.0 + m * (1.0 - s))
            v2_ref[d * 2 + h, 0:64] = (inv * hid.astype(F32)).astype(BF)
            v2_ref[d * 2 + h, 64:128] = (inv * inv * total[64:128] * slope).astype(BF)
    for shift, g_ref in zip(RING, (g0_ref, g1_ref, g2_ref, g3_ref)):
        for z in range(4):
            d = ((at_ref[1] + shift + 4) % 4) * 4 + z
            for h in range(2):
                total = (inverse(d, h) * spread(d, h, v2_ref)).astype(BF)
                mo_ref[d, :, h * 128 : h * 128 + 128] = total[0:64]
                g_ref[z, :, h * 128 : h * 128 + 128] = total[64:128]


def second_kernel(u_ref, mo_ref, out_ref):
    total = jnp.zeros((160, 64), F32)
    for d in range(16):
        total = total + dot(u_ref[d], mo_ref[d], NT)
    out_ref[...] = jnp.concatenate([total[:80], total[80:]], axis=1).astype(BF)


def weigh_kernel(x0_ref, x1_ref, x2_ref, x3_ref, g0_ref, g1_ref, g2_ref, g3_ref, at_ref, out_ref):
    rights = []
    for shift in RING:
        z = (at_ref[2] + shift + 4) % 4
        rights.append(jnp.concatenate([g[z] for g in (g0_ref, g1_ref, g2_ref, g3_ref)], axis=0))
    for f in range(8):
        acc = jnp.zeros((96, 256), F32)
        for x_ref, right in zip((x0_ref, x1_ref, x2_ref, x3_ref), rights):
            acc = acc + dot(x_ref[f], right, NT)
        for p in range(2):
            g = acc[:, p * 128 : p * 128 + 128]
            for part, shift in zip(halves(g[:48], g[48:]), RING[2 * p : 2 * p + 2]):
                out_ref[f, (at_ref[1] - shift + 4) % 4] = part.astype(BF)


def add_kernel(part_ref, s0_ref, s1_ref, s2_ref, s3_ref, hid_ref, out_ref):
    first = part_ref[0].astype(F32)
    for i in range(1, 32):
        first = first + part_ref[i].astype(F32)
    second = s0_ref[...].astype(F32)
    for ref in (s1_ref, s2_ref, s3_ref):
        second = second + ref[...].astype(F32)
    both = jnp.concatenate([first, second], axis=0).astype(BF)
    for d in range(16):
        out_ref[d, 0:128] = both
        out_ref[d, 128:192] = hid_ref[d, :, 0:128]
        out_ref[d, 192:256] = hid_ref[d, :, 128:256]


def final_kernel(in_ref, hidden_ref, first_ref, second_ref):
    for j in range(8):
        cols = pl.ds(j * 128, 128)
        even, odd = owner(2 * j), owner(2 * j + 1)
        one, two = halves(in_ref[even, 0:128].astype(F32), in_ref[odd, 0:128].astype(F32))
        first_ref[0:48, cols] = one[:48]
        first_ref[48:96, cols] = two[:48]
        second_ref[0:80, cols] = one[48:]
        second_ref[80:153, cols] = two[48:121]
        for h in range(2):
            rows = pl.ds(128 + h * 64, 64)
            both = jnp.concatenate([in_ref[even, rows], in_ref[odd, rows]], axis=0)
            hidden_ref[h * 128 : h * 128 + 128, cols] = both.astype(F32).T.astype(BF)


def call(kernel, shape, specs, scratch=(), flops=0, moved=0):
    return pl.pallas_call(
        kernel,
        out_shape=shape,
        in_specs=specs,
        out_specs=jax.tree.map(lambda _: VMEM, shape),
        scratch_shapes=list(scratch),
        compiler_params=pltpu.CompilerParams(vmem_limit_bytes=LIMIT),
        cost_estimate=pl.CostEstimate(flops=flops, bytes_accessed=moved, transcendentals=0),
    )


def fetch(value, axis, shift):
    return lax.ppermute(value, axis, [((i + shift) % 4, i) for i in range(4)])


def ring(value, axis):
    return [value] + [fetch(value, axis, shift) for shift in RING[1:]]


def body(features, first_weight, second_weight, degree, neighbour_block, neighbour_mask, upstream):
    feat, dom = ("y", "c"), ("x", "z")
    shape = jax.ShapeDtypeStruct
    x, z = lax.axis_index("x"), lax.axis_index("z")
    at = jnp.stack([x * 4 + z, x, z, lax.axis_index("y"), lax.axis_index("c")])
    masks = call(mask_kernel, shape((2, 128, 768), BF), [VMEM], moved=1_200_000)(neighbour_mask[0])
    masks = lax.all_gather(masks, dom, axis=0, tiled=True)
    weights = ring(first_weight, "y")
    weights = weights + [lax.ppermute(w, "c", [(0, 1), (1, 0)]) for w in weights]
    x_own = lax.all_to_all(
        features.reshape(96, 8, 256).transpose(1, 0, 2), feat, 0, 0, tiled=True
    )
    links = jnp.pad(jnp.maximum(neighbour_block.reshape(12), 0), (0, 244))
    small = jnp.concatenate([degree.reshape(2, 128), links.reshape(2, 128)], axis=0)
    up = jnp.pad(upstream[0].T, ((0, 7), (0, 0)))
    x_own, small, up = lax.optimization_barrier((x_own, small, up))
    small = lax.all_to_all(jnp.broadcast_to(small, (16, 4, 128)), dom, 0, 0, tiled=True)
    up = lax.all_to_all(jnp.broadcast_to(up, (16, 160, 256)), dom, 0, 0, tiled=True)

    v = call(
        project_kernel,
        shape((16, 2, 128, 128), BF),
        [VMEM] * 4 + [SMEM] + [VMEM] * 8,
        flops=500_000_000,
        moved=4_000_000,
    )(x_own, upstream[0], second_weight, degree.reshape(2, 128), at, *weights)
    v = lax.all_to_all(v, dom, 0, 0, tiled=True).reshape(32, 128, 128)
    v, x_own = lax.optimization_barrier((v, x_own))
    x_wide = ring(x_own, "z")
    hid, mo, *g = call(
        mix_kernel,
        (shape((16, 64, 256), BF), shape((16, 64, 256), BF)) + (shape((4, 64, 256), BF),) * 4,
        [VMEM, VMEM, VMEM, SMEM, SMEM],
        [pltpu.VMEM((32, 128, 128), BF)],
        flops=1_600_000_000,
        moved=9_000_000,
    )(v, masks, small, small, at)
    g = [g[0]] + [fetch(value, "x", -shift) for value, shift in zip(g[1:], RING[1:])]
    second = call(second_kernel, shape((80, 128), BF), [VMEM] * 2, flops=100_000_000, moved=2_000_000)(
        up, mo
    )
    other = lax.ppermute(second, "c", [(0, 1), (1, 0)])
    second = ring((second.astype(F32) + other.astype(F32)).astype(BF), "y")
    part = call(
        weigh_kernel,
        shape((8, 4, 48, 128), BF),
        [VMEM] * 8 + [SMEM],
        flops=400_000_000,
        moved=3_000_000,
    )(*x_wide, *g, at)
    part = lax.all_to_all(part.reshape(32, 48, 128), ("y", "c", "x"), 0, 0, tiled=True)
    done = call(add_kernel, shape((16, 256, 128), BF), [VMEM] * 6, moved=3_000_000)(part, *second, hid)
    done = lax.all_to_all(done, dom, 0, 0, tiled=True)
    hidden, grad_first, grad_second = call(
        final_kernel,
        (shape((256, 1024), BF), shape((96, 1024), F32), shape((153, 1024), F32)),
        [VMEM],
        moved=2_500_000,
    )(done)
    return (hidden[None], grad_first, grad_second.T)


def solution(mesh):
    wide = Mesh(mesh.devices.reshape(4, 2, 4, 4), ("y", "c", "x", "z"))
    feat, dom = ("y", "c"), ("x", "z")
    placed = (
        P(feat, dom, None),
        P(feat, None),
        P(),
        P(dom, feat),
        P(dom, feat, None),
        P(dom, feat, None, None, None),
        P(dom, feat, None),
    )
    return jax.shard_map(
        body,
        mesh=wide,
        in_specs=placed,
        out_specs=(P(dom, feat, None), P(feat, None), P()),
        check_vma=False,
    )
```

time: 657 us -> 170 us (0.26)
  waiting for transfers between devices: 507 us -> 56 us
  other arithmetic: 58 us -> 0.02 us
  starting transfers between devices: 0.51 us -> 58 us
  local copies, waits for them, and re-layouts: 56.5 us -> 5.38 us
  blocking collectives: 0 us -> 20.3 us
  matrix products: 17.7 us -> 0 us
  Pallas kernels: 0 us -> 15.3 us
    psum x2 -> x0, waiting for transfers between devices: 230 us -> none  [the longest x1 148 us: body(): grad_second = lax.psum(second_term, ('feat', 'dom'))]
    reduce_scatter x3 -> x0, waiting for transfers between devices: 189 us -> none  [the longest x2 150 us: pull_back(): lax.psum_scatter(pooled.astype(jnp.bfloat16), 'dom', scatter_dimension=0,...]
    all_gather x3 -> x1, waiting for transfers between devices: 87.4 us -> 8.32 us  [body(): masks = lax.all_gather(masks, dom, axis=0, tiled=True)]
    all_to_all x0 -> x5, waiting for transfers between devices: none -> 32.6 us  [the longest x1 25.1 us: body(): v = lax.all_to_all(v, dom, 0, 0, tiled=True).reshape(32, 128, 128)]
    all_to_all x0 -> x5, starting transfers between devices: none -> 30 us  [the longest x1 8.27 us: body(): lax.all_to_all(part.reshape(32, 48, 128), ('y', 'c', 'x'), 0, 0, tiled=True)]
    convert_element_type x7 -> x1, other arithmetic: 28.3 us -> 0.01 us  [body(): second = ring((second.astype(F32) + other.astype(F32)).astype(BF), 'y')]
    ppermute x0 -> x17, starting transfers between devices: none -> 28 us  [the longest x12 27.3 us: fetch(): return lax.ppermute(value, axis, [((i + shift) % 4, i) for i in range(4)])]
    scatter-add x2 -> x0, other arithmetic: 27.2 us -> none  [pull_back(): jax.ops.segment_sum(spread.reshape(block_rows * slot_count, block_width,...]
  transfers between devices with their start and end apart: 8 -> 23, of which waited for: 8 -> 11; matrix products, arithmetic and copies ran while one was open for 17% -> 2% of each run, Pallas kernels for 0% -> 8%
where the time goes in v1:
time: 170 us; the launch traced here: 169 us
  starting transfers between devices  58 us (34%)
  waiting for transfers between devices  56 us (33%)
  blocking collectives  20.3 us (12%)
  Pallas kernels  15.3 us (9%)
  between operations  14.2 us (8%)
  local copies, waits for them, and re-layouts  5.38 us (3%)
    ppermute x12, starting transfers between devices, fetch(): return lax.ppermute(value, axis, [((i + shift) % 4, i) for i in range(4)])  27.3 us
    all_to_all x1, waiting for transfers between devices, body(): v = lax.all_to_all(v, dom, 0, 0, tiled=True).reshape(32, 128, 128)  25.1 us
    all_to_all x1, blocking collectives, body(): done = lax.all_to_all(done, dom, 0, 0, tiled=True)  20.3 us
    ppermute x12, waiting for transfers between devices, fetch(): return lax.ppermute(value, axis, [((i + shift) % 4, i) for i in range(4)])  13.9 us
    all_gather x1, waiting for transfers between devices, body(): masks = lax.all_gather(masks, dom, axis=0, tiled=True)  8.32 us
    all_to_all x1, starting transfers between devices, body(): lax.all_to_all(part.reshape(32, 48, 128), ('y', 'c', 'x'), 0, 0, tiled=True)  8.27 us
    all_to_all x1, starting transfers between devices, body(): lax.all_to_all(jnp.broadcast_to(small, (16, 4, 128)), dom, 0, 0, tiled=True)  7.88 us
    all_to_all x1, starting transfers between devices, body(): lax.all_to_all(jnp.broadcast_to(up, (16, 160, 256)), dom, 0, 0, tiled=True)  6.79 us
  transfers between devices with their start and end apart: 23, of which 11 were waited for; matrix products, arithmetic and copies ran while one was open for 2% of the time, Pallas kernels for 8%

profile of v1, /device:TPU:0, one launch (start us, length us, event | category | flops | bytes accessed | tf_op | source)
XLA Modules:
  0.0 169.2 jit_solution(3234537904430403759)
XLA Ops:
  7.2 1.1 copy-done
  9.3 3.1 %collective-permute-start = (bf16[96,1024]{1,0:T(8,128)(2,1)S(1)}, bf16[96,1024]{1,0:T(8,128)(2,1)S(1)}, u32[]{:S(2)}, u32[]{:S(2)}) collective-permute-start(bf16[96,1024]{1,0:T(8,128)(2,1)S(1)} %copy-done.3), channel_id=1, source_target_pairs={{32,0},{64,32},{96,64},{0,96},{33,1},{65,33},{97,65},{1,97},{34,2}... | collective-permute-start | bytes 589832 | tf_op jit(solution)/shard_map/ppermute | solution.py:163
  12.4 2.2 %collective-permute-start.2 = (bf16[96,1024]{1,0:T(8,128)(2,1)S(1)}, bf16[96,1024]{1,0:T(8,128)(2,1)S(1)}, u32[]{:S(2)}, u32[]{:S(2)}) collective-permute-start(bf16[96,1024]{1,0:T(8,128)(2,1)S(1)} %copy-done.3), channel_id=1, source_target_pairs={{64,0},{96,32},{0,64},{32,96},{65,1},{97,33},{1,65},{33,97},{66,2}... | collective-permute-start | bytes 589832 | tf_op jit(solution)/shard_map/ppermute | solution.py:163
  14.7 0.8 copy.23
  15.5 3.5 %all-to-all-start = ((bf16[8,96,256]{2,1,0:T(8,128)(2,1)}), bf16[8,96,256]{2,1,0:T(8,128)(2,1)S(1)}, u32[]{:S(2)}, u32[]{:S(2)}) async-start(bf16[8,96,256]{2,1,0:T(8,128)(2,1)} %bitcast.22), calls=%async_computation | async-start | bytes 786432 | tf_op jit(solution)/shard_map/all_to_all | solution.py:179
  19.6 2.0 %collective-permute-done.refs_6_ = bf16[96,1024]{1,0:T(8,128)(2,1)S(1)} collective-permute-done((bf16[96,1024]{1,0:T(8,128)(2,1)S(1)}, bf16[96,1024]{1,0:T(8,128)(2,1)S(1)}, u32[]{:S(2)}, u32[]{:S(2)}) %collective-permute-start) | collective-permute-done | bytes 196640 | tf_op jit(solution)/shard_map/ppermute | solution.py:163
  21.6 3.9 %collective-permute-done.1.refs_7_ = bf16[96,1024]{1,0:T(8,128)(2,1)S(1)} collective-permute-done((bf16[96,1024]{1,0:T(8,128)(2,1)S(1)}, bf16[96,1024]{1,0:T(8,128)(2,1)S(1)}, u32[]{:S(2)}, u32[]{:S(2)}) %collective-permute-start.1) | collective-permute-done | bytes 196640 | tf_op jit(solution)/shard_map/ppermute | solution.py:163
  26.0 2.4 %all-to-all-done.refs_0_.x0_ref = bf16[8,96,256]{2,1,0:T(8,128)(2,1)S(1)} async-done(((bf16[8,96,256]{2,1,0:T(8,128)(2,1)}), bf16[8,96,256]{2,1,0:T(8,128)(2,1)S(1)}, u32[]{:S(2)}, u32[]{:S(2)}) %all-to-all-start) | async-done | bytes 393248 | tf_op jit(solution)/shard_map/all_to_all | solution.py:179
  29.0 7.9 %all-to-all-start.2 = ((s32[16,4,128]{2,1,0:T(4,128)}), s32[16,4,128]{2,1,0:T(4,128)S(1)}, u32[]{:S(2)}, u32[]{:S(2)}) async-start(s32[16,4,128]{2,1,0:T(4,128)} %broadcast_in_dim.9), calls=%async_computation.2 | async-start | bytes 65536 | tf_op jit(solution)/shard_map/all_to_all | solution.py:186
  37.0 2.4 %shard_map.94 = bf16[16,2,128,128]{3,2,1,0:T(8,128)(2,1)} custom-call(bf16[8,96,256]{2,1,0:T(8,128)(2,1)S(1)} %all-to-all-done.refs_0_.x0_ref, bf16[256,153]{1,0:T(8,128)(2,1)S(1)} %bitcast.25, bf16[1024,153]{1,0:T(8,128)(2,1)S(1)} %copy.19.refs_2_, s32[2,128]{1,0:T(2,128)S(1)} %bitcast.28, s32[5]{0:T(128)S(1)} %stack.23.refs_4_.at_ref, ...), custom_call_target="tpu_custom_call" | custom-call | flops 500000000 | bytes 4000000 | tf_op jit(solution)/shard_map/pallas_call | solution.py:189
  39.4 5.1 %all-to-all-done.2.small_ref.links_ref = s32[16,4,128]{2,1,0:T(4,128)S(1)} async-done(((s32[16,4,128]{2,1,0:T(4,128)}), s32[16,4,128]{2,1,0:T(4,128)S(1)}, u32[]{:S(2)}, u32[]{:S(2)}) %all-to-all-start.2) | async-done | bytes 32800 | tf_op jit(solution)/shard_map/all_to_all | solution.py:186
  44.5 3.7 %all-to-all-start.1 = ((bf16[16,2,128,128]{3,2,1,0:T(8,128)(2,1)}), bf16[16,2,128,128]{3,2,1,0:T(8,128)(2,1)S(1)}, u32[]{:S(2)}, u32[]{:S(2)}) async-start(bf16[16,2,128,128]{3,2,1,0:T(8,128)(2,1)} %shard_map.94), calls=%async_computation.1 | async-start | bytes 2097152 | tf_op jit(solution)/shard_map/all_to_all | solution.py:196
  48.3 25.1 %all-to-all-done.1 = bf16[16,2,128,128]{3,2,1,0:T(8,128)(2,1)S(1)} async-done(((bf16[16,2,128,128]{3,2,1,0:T(8,128)(2,1)}), bf16[16,2,128,128]{3,2,1,0:T(8,128)(2,1)S(1)}, u32[]{:S(2)}, u32[]{:S(2)}) %all-to-all-start.1) | async-done | bytes 1048608 | tf_op jit(solution)/shard_map/all_to_all | solution.py:196
  73.4 1.2 broadcast_in_dim.10
  74.5 6.8 %all-to-all-start.4 = ((bf16[16,160,256]{2,1,0:T(8,128)(2,1)}), bf16[16,160,256]{2,1,0:T(8,128)(2,1)S(1)}, u32[]{:S(2)}, u32[]{:S(2)}) async-start(bf16[16,160,256]{2,1,0:T(8,128)(2,1)} %broadcast_in_dim.10), calls=%async_computation.4 | async-start | bytes 2621440 | tf_op jit(solution)/shard_map/all_to_all | solution.py:187
  81.3 3.1 %collective-permute-start.7 = (bf16[8,96,256]{2,1,0:T(8,128)(2,1)S(1)}, bf16[8,96,256]{2,1,0:T(8,128)(2,1)}, u32[]{:S(2)}, u32[]{:S(2)}) collective-permute-start(bf16[8,96,256]{2,1,0:T(8,128)(2,1)S(1)} %all-to-all-done.refs_0_.x0_ref), channel_id=1, source_target_pairs={{1,0},{2,1},{3,2},{0,3},{5,4},{6,5},{7,6},{4,7},{9,8},{10,9},{11,1... | collective-permute-start | bytes 1179656 | tf_op jit(solution)/shard_map/ppermute | solution.py:163
  84.5 2.3 %collective-permute-start.9 = (bf16[8,96,256]{2,1,0:T(8,128)(2,1)S(1)}, bf16[8,96,256]{2,1,0:T(8,128)(2,1)}, u32[]{:S(2)}, u32[]{:S(2)}) collective-permute-start(bf16[8,96,256]{2,1,0:T(8,128)(2,1)S(1)} %all-to-all-done.refs_0_.x0_ref), channel_id=1, source_target_pairs={{2,0},{3,1},{0,2},{1,3},{6,4},{7,5},{4,6},{5,7},{10,8},{11,9},{8,1... | collective-permute-start | bytes 1179656 | tf_op jit(solution)/shard_map/ppermute | solution.py:163
  86.8 8.3 %all-gather.2.cloned.1.call-done.m_ref = bf16[32,128,768]{2,1,0:T(8,128)(2,1)} async-done(((bf16[2,128,768]{2,1,0:T(8,128)(2,1)}), bf16[32,128,768]{2,1,0:T(8,128)(2,1)}) %all-gather.2.cloned.1.call-update) | async-done | bytes 6291472 | tf_op jit(solution)/shard_map/all_gather | solution.py:176
  95.1 6.4 %shard_map.96 = (bf16[16,64,256]{2,1,0:T(8,128)(2,1)S(1)}, bf16[16,64,256]{2,1,0:T(8,128)(2,1)S(1)}, bf16[4,64,256]{2,1,0:T(8,128)(2,1)S(1)}, bf16[4,64,256]{2,1...) custom-call(bf16[32,128,128]{2,1,0:T(8,128)(2,1)S(1)} %bitcast.23, ...), custom_call_target="tpu_custom_call" | custom-call | flops 1600000000 | bytes 9000000 | tf_op jit(solution)/shard_map/pallas_call | solution.py:199
  102.3 8.0 %collective-permute-start.10 = (bf16[4,64,256]{2,1,0:T(8,128)(2,1)S(1)}, bf16[4,64,256]{2,1,0:T(8,128)(2,1)S(1)}, u32[]{:S(2)}, u32[]{:S(2)}) collective-permute-start(bf16[4,64,256]{2,1,0:T(8,128)(2,1)S(1)} %get-tuple-element.22), channel_id=1, source_target_pairs={{12,0},{0,4},{4,8},{8,12},{13,1},{1,5},{5,9},{9,13},{14,2},{2,6},{... | collective-permute-start | bytes 393224 | tf_op jit(solution)/shard_map/ppermute | solution.py:163
  110.3 1.2 collective-permute-start.11
  111.5 2.1 %collective-permute-start.12 = (bf16[4,64,256]{2,1,0:T(8,128)(2,1)S(1)}, bf16[4,64,256]{2,1,0:T(8,128)(2,1)S(1)}, u32[]{:S(2)}, u32[]{:S(2)}) collective-permute-start(bf16[4,64,256]{2,1,0:T(8,128)(2,1)S(1)} %get-tuple-element.24), channel_id=1, source_target_pairs={{8,0},{12,4},{0,8},{4,12},{9,1},{13,5},{1,9},{5,13},{10,2},{14,6},... | collective-permute-start | bytes 393224 | tf_op jit(solution)/shard_map/ppermute | solution.py:163
  113.6 3.0 %collective-permute-done.9.x3_ref = bf16[8,96,256]{2,1,0:T(8,128)(2,1)} collective-permute-done((bf16[8,96,256]{2,1,0:T(8,128)(2,1)S(1)}, bf16[8,96,256]{2,1,0:T(8,128)(2,1)}, u32[]{:S(2)}, u32[]{:S(2)}) %collective-permute-start.9) | collective-permute-done | bytes 393248 | tf_op jit(solution)/shard_map/ppermute | solution.py:163
  116.6 1.9 %collective-permute-done.12.g3_ref = bf16[4,64,256]{2,1,0:T(8,128)(2,1)S(1)} collective-permute-done((bf16[4,64,256]{2,1,0:T(8,128)(2,1)S(1)}, bf16[4,64,256]{2,1,0:T(8,128)(2,1)S(1)}, u32[]{:S(2)}, u32[]{:S(2)}) %collective-permute-start.12) | collective-permute-done | bytes 131104 | tf_op jit(solution)/shard_map/ppermute | solution.py:163
  118.5 3.5 %shard_map.97 = bf16[8,4,48,128]{3,2,1,0:T(8,128)(2,1)} custom-call(bf16[8,96,256]{2,1,0:T(8,128)(2,1)S(1)} %all-to-all-done.refs_0_.x0_ref, bf16[8,96,256]{2,1,0:T(8,128)(2,1)} %collective-permute-done.7.x1_ref, bf16[8,96,256]{2,1,0:T(8,128)(2,1)} %collective-permute-done.8.x2_ref, bf16[8,96,256]{2,1,0:T(8,128)(2,1)} %collective-permute-done.9.x3_ref, ...), custom_call_target="tpu_custom_call" | custom-call | flops 400000000 | bytes 3000000 | tf_op jit(solution)/shard_map/pallas_call | solution.py:213
  121.9 8.3 %all-to-all-start.3 = ((bf16[32,48,128]{2,1,0:T(8,128)(2,1)}), bf16[32,48,128]{2,1,0:T(8,128)(2,1)S(1)}, u32[]{:S(2)}, u32[]{:S(2)}) async-start(bf16[32,48,128]{2,1,0:T(8,128)(2,1)} %bitcast.12), calls=%async_computation.3 | async-start | bytes 786432 | tf_op jit(solution)/shard_map/all_to_all | solution.py:220
  131.0 1.1 collective-permute-done.13
  132.1 2.9 %collective-permute-start.14 = (bf16[80,128]{1,0:T(8,128)(2,1)S(1)}, bf16[80,128]{1,0:T(8,128)(2,1)S(1)}, u32[]{:S(2)}, u32[]{:S(2)}) collective-permute-start(bf16[80,128]{1,0:T(8,128)(2,1)S(1)} %add_convert_fusion.s0_ref), channel_id=1, source_target_pairs={{32,0},{64,32},{96,64},{0,96},{33,1},{65,33},{97,65},{1,97},{34,2}... | collective-permute-start | bytes 61448 | tf_op jit(solution)/shard_map/ppermute | solution.py:163
  135.0 2.3 %collective-permute-start.16 = (bf16[80,128]{1,0:T(8,128)(2,1)S(1)}, bf16[80,128]{1,0:T(8,128)(2,1)S(1)}, u32[]{:S(2)}, u32[]{:S(2)}) collective-permute-start(bf16[80,128]{1,0:T(8,128)(2,1)S(1)} %add_convert_fusion.s0_ref), channel_id=1, source_target_pairs={{64,0},{96,32},{0,64},{32,96},{65,1},{97,33},{1,65},{33,97},{66,2}... | collective-permute-start | bytes 61448 | tf_op jit(solution)/shard_map/ppermute | solution.py:163
  137.3 3.0 %collective-permute-done.15.s2_ref = bf16[80,128]{1,0:T(8,128)(2,1)S(1)} collective-permute-done((bf16[80,128]{1,0:T(8,128)(2,1)S(1)}, bf16[80,128]{1,0:T(8,128)(2,1)S(1)}, u32[]{:S(2)}, u32[]{:S(2)}) %collective-permute-start.15) | collective-permute-done | bytes 20512 | tf_op jit(solution)/shard_map/ppermute | solution.py:163
  140.6 20.3 %all_to_all.30.in_ref = bf16[16,256,128]{2,1,0:T(8,128)(2,1)S(1)} all-to-all(bf16[16,256,128]{2,1,0:T(8,128)(2,1)S(1)} %shard_map.99), channel_id=1, replica_groups=mesh['y'=4,'c'=2,'x'=4,'z'=4] {'x','z'}, dimensions={0} | all-to-all | bytes 2097152 | tf_op jit(solution)/shard_map/all_to_all | solution.py:222
  160.9 1.4 shard_map.100
  (55 shorter events, 4.8 us)
Async XLA Ops:
  7.2 88.0 %all-gather.2.cloned.1.call-start = ((), (), s32[]{:S(2)}) async-start(), calls=%async_computation.6 | async-start | bytes 6684672 | tf_op jit(solution)/shard_map/all_gather | solution.py:176
  7.2 1.1 copy-start
  8.3 1.0 copy-start.3
  8.3 6.3 %copy-start.5 = (bf16[96,1,2048]{2,0,1:T(8,128)(2,1)S(1)}, bf16[96,1,2048]{2,0,1:T(8,128)(2,1)}, u32[]{:S(2)}) copy-start(bf16[96,1,2048]{2,0,1:T(8,128)(2,1)} %param.7) | copy-start | bytes 1179652
  9.1 9.9 %copy-start.7 = (bf16[1,256,153]{1,2,0:T(8,128)(2,1)S(1)}, bf16[1,256,153]{1,2,0:T(8,128)(2,1)}, u32[]{:S(2)}) copy-start(bf16[1,256,153]{1,2,0:T(8,128)(2,1)} %param.13) | copy-start | bytes 235012
  9.3 9.8 %copy-start.8 = (s32[1,2,6]{2,1,0:T(2,128)S(1)}, s32[1,2,6]{2,1,0:T(2,128)}, u32[]{:S(2)}) copy-start(s32[1,2,6]{2,1,0:T(2,128)} %param.11) | copy-start | bytes 148
  9.3 9.9 %copy-start.6 = (bf16[1024,153]{0,1:T(8,128)(2,1)S(1)}, bf16[1024,153]{0,1:T(8,128)(2,1)}, u32[]{:S(2)}) copy-start(bf16[1024,153]{0,1:T(8,128)(2,1)} %param.9) | copy-start | bytes 940036
  9.3 12.2 %collective-permute-start = (bf16[96,1024]{1,0:T(8,128)(2,1)S(1)}, bf16[96,1024]{1,0:T(8,128)(2,1)S(1)}, u32[]{:S(2)}, u32[]{:S(2)}) collective-permute-start(bf16[96,1024]{1,0:T(8,128)(2,1)S(1)} %copy-done.3), channel_id=1, source_target_pairs={{32,0},{64,32},{96,64},{0,96},{33,1},{65,33},{97,65},{1,97},{34,2}... | collective-permute-start | bytes 589832 | tf_op jit(solution)/shard_map/ppermute | solution.py:163
  12.4 13.1 %collective-permute-start.1 = (bf16[96,1024]{1,0:T(8,128)(2,1)S(1)}, bf16[96,1024]{1,0:T(8,128)(2,1)S(1)}, u32[]{:S(2)}, u32[]{:S(2)}) collective-permute-start(bf16[96,1024]{1,0:T(8,128)(2,1)S(1)} %copy-done.3), channel_id=1, source_target_pairs={{96,0},{0,32},{32,64},{64,96},{97,1},{1,33},{33,65},{65,97},{98,2}... | collective-permute-start | bytes 589832 | tf_op jit(solution)/shard_map/ppermute | solution.py:163
  12.4 13.1 %collective-permute-start.2 = (bf16[96,1024]{1,0:T(8,128)(2,1)S(1)}, bf16[96,1024]{1,0:T(8,128)(2,1)S(1)}, u32[]{:S(2)}, u32[]{:S(2)}) collective-permute-start(bf16[96,1024]{1,0:T(8,128)(2,1)S(1)} %copy-done.3), channel_id=1, source_target_pairs={{64,0},{96,32},{0,64},{32,96},{65,1},{97,33},{1,65},{33,97},{66,2}... | collective-permute-start | bytes 589832 | tf_op jit(solution)/shard_map/ppermute | solution.py:163
  14.6 22.3 %collective-permute-start.3 = (bf16[96,1024]{1,0:T(8,128)(2,1)S(1)}, bf16[96,1024]{1,0:T(8,128)(2,1)S(1)}, u32[]{:S(2)}, u32[]{:S(2)}) collective-permute-start(bf16[96,1024]{1,0:T(8,128)(2,1)S(1)} %copy-done.3), channel_id=1, source_target_pairs={{0,16},{16,0},{1,17},{17,1},{2,18},{18,2},{3,19},{19,3},{4,20},{20... | collective-permute-start | bytes 589832 | tf_op jit(solution)/shard_map/ppermute | solution.py:178
  14.7 11.3 %copy-start.4 = (s32[1,256]{1,0:T(1,128)S(1)}, s32[1,256]{1,0:T(1,128)}, u32[]{:S(2)}) copy-start(s32[1,256]{1,0:T(1,128)} %param.10) | copy-start | bytes 3076
  15.5 12.9 %all-to-all-start = ((bf16[8,96,256]{2,1,0:T(8,128)(2,1)}), bf16[8,96,256]{2,1,0:T(8,128)(2,1)S(1)}, u32[]{:S(2)}, u32[]{:S(2)}) async-start(bf16[8,96,256]{2,1,0:T(8,128)(2,1)} %bitcast.22), calls=%async_computation | async-start | bytes 786432 | tf_op jit(solution)/shard_map/all_to_all | solution.py:179
  21.6 15.4 %collective-permute-start.4 = (bf16[96,1024]{1,0:T(8,128)(2,1)S(1)}, bf16[96,1024]{1,0:T(8,128)(2,1)S(1)}, u32[]{:S(2)}, u32[]{:S(2)}) collective-permute-start(bf16[96,1024]{1,0:T(8,128)(2,1)S(1)} %collective-permute-done.refs_6_), channel_id=1, source_target_pairs={{0,16},{16,0},{1,17},{17,1},{2,18},{18,2},{3,19},{19,3},{4,20},{20... | collective-permute-start | bytes 589832 | tf_op jit(solution)/shard_map/ppermute | solution.py:178
  25.5 11.5 %collective-permute-start.5 = (bf16[96,1024]{1,0:T(8,128)(2,1)S(1)}, bf16[96,1024]{1,0:T(8,128)(2,1)S(1)}, u32[]{:S(2)}, u32[]{:S(2)}) collective-permute-start(bf16[96,1024]{1,0:T(8,128)(2,1)S(1)} %collective-permute-done.1.refs_7_), channel_id=1, source_target_pairs={{0,16},{16,0},{1,17},{17,1},{2,18},{18,2},{3,19},{19,3},{4,20},{20... | collective-permute-start | bytes 589832 | tf_op jit(solution)/shard_map/ppermute | solution.py:178
  25.5 11.5 %collective-permute-start.6 = (bf16[96,1024]{1,0:T(8,128)(2,1)S(1)}, bf16[96,1024]{1,0:T(8,128)(2,1)S(1)}, u32[]{:S(2)}, u32[]{:S(2)}) collective-permute-start(bf16[96,1024]{1,0:T(8,128)(2,1)S(1)} %collective-permute-done.2.refs_8_), channel_id=1, source_target_pairs={{0,16},{16,0},{1,17},{17,1},{2,18},{18,2},{3,19},{19,3},{4,20},{20... | collective-permute-start | bytes 589832 | tf_op jit(solution)/shard_map/ppermute | solution.py:178
  29.0 15.5 %all-to-all-start.2 = ((s32[16,4,128]{2,1,0:T(4,128)}), s32[16,4,128]{2,1,0:T(4,128)S(1)}, u32[]{:S(2)}, u32[]{:S(2)}) async-start(s32[16,4,128]{2,1,0:T(4,128)} %broadcast_in_dim.9), calls=%async_computation.2 | async-start | bytes 65536 | tf_op jit(solution)/shard_map/all_to_all | solution.py:186
  44.5 28.8 %all-to-all-start.1 = ((bf16[16,2,128,128]{3,2,1,0:T(8,128)(2,1)}), bf16[16,2,128,128]{3,2,1,0:T(8,128)(2,1)S(1)}, u32[]{:S(2)}, u32[]{:S(2)}) async-start(bf16[16,2,128,128]{3,2,1,0:T(8,128)(2,1)} %shard_map.94), calls=%async_computation.1 | async-start | bytes 2097152 | tf_op jit(solution)/shard_map/all_to_all | solution.py:196
  74.5 47.4 %all-to-all-start.4 = ((bf16[16,160,256]{2,1,0:T(8,128)(2,1)}), bf16[16,160,256]{2,1,0:T(8,128)(2,1)S(1)}, u32[]{:S(2)}, u32[]{:S(2)}) async-start(bf16[16,160,256]{2,1,0:T(8,128)(2,1)} %broadcast_in_dim.10), calls=%async_computation.4 | async-start | bytes 2621440 | tf_op jit(solution)/shard_map/all_to_all | solution.py:187
  81.3 30.2 %collective-permute-start.7 = (bf16[8,96,256]{2,1,0:T(8,128)(2,1)S(1)}, bf16[8,96,256]{2,1,0:T(8,128)(2,1)}, u32[]{:S(2)}, u32[]{:S(2)}) collective-permute-start(bf16[8,96,256]{2,1,0:T(8,128)(2,1)S(1)} %all-to-all-done.refs_0_.x0_ref), channel_id=1, source_target_pairs={{1,0},{2,1},{3,2},{0,3},{5,4},{6,5},{7,6},{4,7},{9,8},{10,9},{11,1... | collective-permute-start | bytes 1179656 | tf_op jit(solution)/shard_map/ppermute | solution.py:163
  84.5 29.1 %collective-permute-start.8 = (bf16[8,96,256]{2,1,0:T(8,128)(2,1)S(1)}, bf16[8,96,256]{2,1,0:T(8,128)(2,1)}, u32[]{:S(2)}, u32[]{:S(2)}) collective-permute-start(bf16[8,96,256]{2,1,0:T(8,128)(2,1)S(1)} %all-to-all-done.refs_0_.x0_ref), channel_id=1, source_target_pairs={{3,0},{0,1},{1,2},{2,3},{7,4},{4,5},{5,6},{6,7},{11,8},{8,9},{9,10... | collective-permute-start | bytes 1179656 | tf_op jit(solution)/shard_map/ppermute | solution.py:163
  84.5 32.1 %collective-permute-start.9 = (bf16[8,96,256]{2,1,0:T(8,128)(2,1)S(1)}, bf16[8,96,256]{2,1,0:T(8,128)(2,1)}, u32[]{:S(2)}, u32[]{:S(2)}) collective-permute-start(bf16[8,96,256]{2,1,0:T(8,128)(2,1)S(1)} %all-to-all-done.refs_0_.x0_ref), channel_id=1, source_target_pairs={{2,0},{3,1},{0,2},{1,3},{6,4},{7,5},{4,6},{5,7},{10,8},{11,9},{8,1... | collective-permute-start | bytes 1179656 | tf_op jit(solution)/shard_map/ppermute | solution.py:163
  101.5 0.8 copy-start.1
  102.3 14.3 %collective-permute-start.10 = (bf16[4,64,256]{2,1,0:T(8,128)(2,1)S(1)}, bf16[4,64,256]{2,1,0:T(8,128)(2,1)S(1)}, u32[]{:S(2)}, u32[]{:S(2)}) collective-permute-start(bf16[4,64,256]{2,1,0:T(8,128)(2,1)S(1)} %get-tuple-element.22), channel_id=1, source_target_pairs={{12,0},{0,4},{4,8},{8,12},{13,1},{1,5},{5,9},{9,13},{14,2},{2,6},{... | collective-permute-start | bytes 393224 | tf_op jit(solution)/shard_map/ppermute | solution.py:163
  110.3 6.3 %collective-permute-start.11 = (bf16[4,64,256]{2,1,0:T(8,128)(2,1)S(1)}, bf16[4,64,256]{2,1,0:T(8,128)(2,1)S(1)}, u32[]{:S(2)}, u32[]{:S(2)}) collective-permute-start(bf16[4,64,256]{2,1,0:T(8,128)(2,1)S(1)} %get-tuple-element.23), channel_id=1, source_target_pairs={{4,0},{8,4},{12,8},{0,12},{5,1},{9,5},{13,9},{1,13},{6,2},{10,6},{... | collective-permute-start | bytes 393224 | tf_op jit(solution)/shard_map/ppermute | solution.py:163
  111.5 6.9 %collective-permute-start.12 = (bf16[4,64,256]{2,1,0:T(8,128)(2,1)S(1)}, bf16[4,64,256]{2,1,0:T(8,128)(2,1)S(1)}, u32[]{:S(2)}, u32[]{:S(2)}) collective-permute-start(bf16[4,64,256]{2,1,0:T(8,128)(2,1)S(1)} %get-tuple-element.24), channel_id=1, source_target_pairs={{8,0},{12,4},{0,8},{4,12},{9,1},{13,5},{1,9},{5,13},{10,2},{14,6},... | collective-permute-start | bytes 393224 | tf_op jit(solution)/shard_map/ppermute | solution.py:163
  121.9 18.5 %copy-start.2 = (bf16[16,64,256]{2,1,0:T(8,128)(2,1)S(1)}, bf16[16,64,256]{2,1,0:T(8,128)(2,1)}, u32[]{:S(2)}) copy-start(bf16[16,64,256]{2,1,0:T(8,128)(2,1)} %copy-done.1) | copy-start | bytes 1572868
  121.9 18.5 %all-to-all-start.3 = ((bf16[32,48,128]{2,1,0:T(8,128)(2,1)}), bf16[32,48,128]{2,1,0:T(8,128)(2,1)S(1)}, u32[]{:S(2)}, u32[]{:S(2)}) async-start(bf16[32,48,128]{2,1,0:T(8,128)(2,1)} %bitcast.12), calls=%async_computation.3 | async-start | bytes 786432 | tf_op jit(solution)/shard_map/all_to_all | solution.py:220
  130.8 1.3 collective-permute-start.13
  132.1 5.2 %collective-permute-start.14 = (bf16[80,128]{1,0:T(8,128)(2,1)S(1)}, bf16[80,128]{1,0:T(8,128)(2,1)S(1)}, u32[]{:S(2)}, u32[]{:S(2)}) collective-permute-start(bf16[80,128]{1,0:T(8,128)(2,1)S(1)} %add_convert_fusion.s0_ref), channel_id=1, source_target_pairs={{32,0},{64,32},{96,64},{0,96},{33,1},{65,33},{97,65},{1,97},{34,2}... | collective-permute-start | bytes 61448 | tf_op jit(solution)/shard_map/ppermute | solution.py:163
  135.0 5.3 %collective-permute-start.15 = (bf16[80,128]{1,0:T(8,128)(2,1)S(1)}, bf16[80,128]{1,0:T(8,128)(2,1)S(1)}, u32[]{:S(2)}, u32[]{:S(2)}) collective-permute-start(bf16[80,128]{1,0:T(8,128)(2,1)S(1)} %add_convert_fusion.s0_ref), channel_id=1, source_target_pairs={{96,0},{0,32},{32,64},{64,96},{97,1},{1,33},{33,65},{65,97},{98,2}... | collective-permute-start | bytes 61448 | tf_op jit(solution)/shard_map/ppermute | solution.py:163
  135.0 5.5 %collective-permute-start.16 = (bf16[80,128]{1,0:T(8,128)(2,1)S(1)}, bf16[80,128]{1,0:T(8,128)(2,1)S(1)}, u32[]{:S(2)}, u32[]{:S(2)}) collective-permute-start(bf16[80,128]{1,0:T(8,128)(2,1)S(1)} %add_convert_fusion.s0_ref), channel_id=1, source_target_pairs={{64,0},{96,32},{0,64},{32,96},{65,1},{97,33},{1,65},{33,97},{66,2}... | collective-permute-start | bytes 61448 | tf_op jit(solution)/shard_map/ppermute | solution.py:163
Sparse Core Ops, SparseCore 0:
  10.8 84.3 all-gather.1

commit v2 on v1

--- a/solution.py
+++ b/solution.py
@@ -33,74 +33,99 @@
     return (block % 4) * 4 + block // 4
 
 
-def mask_kernel(mask_ref, out_ref):
+def mask_kernel(mask_ref, up_ref, out_ref):
     for b in range(2):
         for k in range(6):
-            out_ref[b, :, k * 128 : k * 128 + 128] = mask_ref[b, k].astype(F32).astype(BF)
+            out_ref[b * 128 : b * 128 + 128, k * 128 : k * 128 + 128] = (
+                mask_ref[b, k].astype(F32).astype(BF)
+            )
+    out_ref[256:320, 0:256] = up_ref[0:64, :]
+    out_ref[256:320, 256:512] = up_ref[64:128, :]
+    rest = jnp.concatenate([up_ref[128:153, :].astype(F32), jnp.zeros((39, 256), F32)], axis=0)
+    out_ref[256:320, 512:768] = rest.astype(BF)
 
 
 def project_kernel(*refs):
-    x_ref, up_ref, sw_ref, deg_ref, at_ref = refs[:5]
-    w_refs, out_ref = refs[5:13], refs[13]
+    x_ref, deg_ref, links_ref, at_ref = refs[:4]
+    w_refs, out_ref = refs[4:12], refs[12]
     sources = []
     for flip in range(2):
         for shift in RING:
             y, core = (at_ref[3] + shift + 4) % 4, (at_ref[4] + flip) % 2
             sources.append(y * 2 + core)
+    info = []
     for b in range(2):
-        row = lax.rsqrt(deg_ref[b : b + 1, :].astype(F32))
-        inv = columns_of(row)
+        degree = deg_ref[b : b + 1, :]
+        info += [degree >> 5, degree & 31]
+        inv = columns_of(lax.rsqrt(degree.astype(F32)))
         rows = pl.ds(b * 128, 128)
         x = jnp.concatenate([x_ref[f, :, rows] for f in sources], axis=0)
         for j in range(4):
             cols = pl.ds(j * 256, 256)
             w = jnp.concatenate([w_ref[:, cols] for w_ref in w_refs], axis=0)
             sz = dot(x, w, (((0,), (0,)), ((), ())))
-            bo = (row * dot(sw_ref[cols, :], up_ref[rows, :], NT)).astype(BF)
             for h in range(2):
                 s = (inv * sz[:, h * 128 : h * 128 + 128]).T.astype(BF)
                 for q in range(2):
                     d = owner(j * 4 + h * 2 + q)
-                    out_ref[d, b, 0:64, :] = s[q * 64 : q * 64 + 64]
-                    out_ref[d, b, 64:128, :] = bo[h * 128 + q * 64 : h * 128 + q * 64 + 64]
+                    out_ref[d, b * 64 : b * 64 + 64, :] = s[q * 64 : q * 64 + 64]
+    info = jnp.concatenate(info + [links_ref[...]] + [jnp.zeros((11, 128), I32)], axis=0)
+    info = info.astype(F32).astype(BF)
+    for d in range(16):
+        out_ref[d, 128:144, :] = info
 
 
 def mix_kernel(
-    v_ref, m_ref, small_ref, links_ref, at_ref, hid_ref, mo_ref, g0_ref, g1_ref, g2_ref, g3_ref, v2_ref
+    v_ref, m_ref, sw_ref, at_ref, hid_ref, second_ref, g0_ref, g1_ref, g2_ref, g3_ref,
+    src_ref, v2_ref, inv_ref, stage_ref, links_ref, link_sem,
 ):
-    def inverse(d, h):
-        return lax.rsqrt(small_ref[d, h : h + 1, :].astype(F32))
+    links = []
+    for d in range(16):
+        info = v_ref[d, 128:144, :].astype(F32)
+        links.append(info[4:5])
+        for h in range(2):
+            t = d * 2 + h
+            inv = lax.rsqrt(info[2 * h : 2 * h + 1] * 32.0 + info[2 * h + 1 : 2 * h + 2])
+            inv_ref[t] = inv
+            src_ref[t, 0:64] = v_ref[d, h * 64 : h * 64 + 64, :]
+            for c in range(3):
+                rows = min(64, 160 - 64 * c)
+                up = m_ref[d, 256 : 256 + rows, c * 256 + h * 128 : c * 256 + h * 128 + 128]
+                src_ref[t, 64 + 64 * c : 64 + 64 * c + rows] = (inv * up.astype(F32)).astype(BF)
+    stage_ref[...] = jnp.concatenate(links, axis=0).astype(I32)
+    to_scalars = pltpu.make_async_copy(stage_ref, links_ref, link_sem)
+    to_scalars.start()
+    to_scalars.wait()
 
     def spread(d, h, source):
-        t = d * 2 + h
-        named = [source[links_ref[d, 2, h * 6 + k]] for k in range(6)]
-        return source[t].astype(F32) + dot(jnp.concatenate(named, axis=1), m_ref[t], NT)
-
-    for d in range(16):
+        named = [source[links_ref[d, h * 6 + k]] for k in range(6)]
+        weights = m_ref[d, h * 128 : h * 128 + 128, :]
+        return source[d * 2 + h].astype(F32) + dot(jnp.concatenate(named, axis=1), weights, NT)
+
+    second = jnp.zeros((160, 64), F32)
+    for d in range(16):
+        ones, pulls = [], []
         for h in range(2):
-            inv = inverse(d, h)
-            total = spread(d, h, v_ref)
+            t = d * 2 + h
+            inv = inv_ref[t]
+            total = spread(d, h, src_ref)
             m = inv * total[0:64]
             s = jax.nn.sigmoid(m)
             hid = (m * s).astype(BF)
             hid_ref[d, :, h * 128 : h * 128 + 128] = hid
+            ones.append((inv * hid.astype(F32)).astype(BF))
+            pull = total[64:224].astype(BF)
+            pulls.append(pull)
             slope = s * (1.0 + m * (1.0 - s))
-            v2_ref[d * 2 + h, 0:64] = (inv * hid.astype(F32)).astype(BF)
-            v2_ref[d * 2 + h, 64:128] = (inv * inv * total[64:128] * slope).astype(BF)
+            v2_ref[t] = (inv * inv * dot(sw_ref[...], pull) * slope).astype(BF)
+        second = second + dot(jnp.concatenate(pulls, axis=1), jnp.concatenate(ones, axis=1), NT)
+    second_ref[...] = jnp.concatenate([second[:80], second[80:]], axis=1).astype(BF)
     for shift, g_ref in zip(RING, (g0_ref, g1_ref, g2_ref, g3_ref)):
         for z in range(4):
             d = ((at_ref[1] + shift + 4) % 4) * 4 + z
             for h in range(2):
-                total = (inverse(d, h) * spread(d, h, v2_ref)).astype(BF)
-                mo_ref[d, :, h * 128 : h * 128 + 128] = total[0:64]
-                g_ref[z, :, h * 128 : h * 128 + 128] = total[64:128]
-
-
-def second_kernel(u_ref, mo_ref, out_ref):
-    total = jnp.zeros((160, 64), F32)
-    for d in range(16):
-        total = total + dot(u_ref[d], mo_ref[d], NT)
-    out_ref[...] = jnp.concatenate([total[:80], total[80:]], axis=1).astype(BF)
+                g = inv_ref[d * 2 + h] * spread(d, h, v2_ref)
+                g_ref[z, :, h * 128 : h * 128 + 128] = g.astype(BF)
 
 
 def weigh_kernel(x0_ref, x1_ref, x2_ref, x3_ref, g0_ref, g1_ref, g2_ref, g3_ref, at_ref, out_ref):
@@ -172,44 +197,47 @@
     shape = jax.ShapeDtypeStruct
     x, z = lax.axis_index("x"), lax.axis_index("z")
     at = jnp.stack([x * 4 + z, x, z, lax.axis_index("y"), lax.axis_index("c")])
-    masks = call(mask_kernel, shape((2, 128, 768), BF), [VMEM], moved=1_200_000)(neighbour_mask[0])
-    masks = lax.all_gather(masks, dom, axis=0, tiled=True)
+    masks = call(mask_kernel, shape((320, 768), BF), [VMEM] * 2, moved=1_200_000)(
+        neighbour_mask[0], upstream[0].T
+    )
+    masks = lax.all_gather(masks, dom, axis=0)
+    x_own = lax.all_to_all(
+        features.reshape(96, 8, 256).transpose(1, 0, 2), feat, 0, 0, tiled=True
+    )
     weights = ring(first_weight, "y")
     weights = weights + [lax.ppermute(w, "c", [(0, 1), (1, 0)]) for w in weights]
-    x_own = lax.all_to_all(
-        features.reshape(96, 8, 256).transpose(1, 0, 2), feat, 0, 0, tiled=True
-    )
-    links = jnp.pad(jnp.maximum(neighbour_block.reshape(12), 0), (0, 244))
-    small = jnp.concatenate([degree.reshape(2, 128), links.reshape(2, 128)], axis=0)
-    up = jnp.pad(upstream[0].T, ((0, 7), (0, 0)))
-    x_own, small, up = lax.optimization_barrier((x_own, small, up))
-    small = lax.all_to_all(jnp.broadcast_to(small, (16, 4, 128)), dom, 0, 0, tiled=True)
-    up = lax.all_to_all(jnp.broadcast_to(up, (16, 160, 256)), dom, 0, 0, tiled=True)
-
+    links = jnp.pad(jnp.maximum(neighbour_block.reshape(1, 12), 0), ((0, 0), (0, 116)))
+    own_second = lax.dynamic_slice(second_weight, ((z * 4 + x) * 64, 0), (64, 153))
+    own_second = jnp.pad(own_second, ((0, 0), (0, 7)))
     v = call(
         project_kernel,
-        shape((16, 2, 128, 128), BF),
-        [VMEM] * 4 + [SMEM] + [VMEM] * 8,
-        flops=500_000_000,
-        moved=4_000_000,
-    )(x_own, upstream[0], second_weight, degree.reshape(2, 128), at, *weights)
-    v = lax.all_to_all(v, dom, 0, 0, tiled=True).reshape(32, 128, 128)
+        shape((16, 144, 128), BF),
+        [VMEM] * 3 + [SMEM] + [VMEM] * 8,
+        flops=400_000_000,
+        moved=3_000_000,
+    )(x_own, degree.reshape(2, 128), links, at, *weights)
+    v = lax.all_to_all(v, dom, 0, 0, tiled=True)
     v, x_own = lax.optimization_barrier((v, x_own))
-    x_wide = ring(x_own, "z")
-    hid, mo, *g = call(
+    v, *x_wide = lax.optimization_barrier((v, *ring(x_own, "z")))
+    hid, second, *g = call(
         mix_kernel,
-        (shape((16, 64, 256), BF), shape((16, 64, 256), BF)) + (shape((4, 64, 256), BF),) * 4,
-        [VMEM, VMEM, VMEM, SMEM, SMEM],
-        [pltpu.VMEM((32, 128, 128), BF)],
+        (shape((16, 64, 256), BF), shape((80, 128), BF)) + (shape((4, 64, 256), BF),) * 4,
+        [VMEM, VMEM, VMEM, SMEM],
+        [
+            pltpu.VMEM((32, 224, 128), BF),
+            pltpu.VMEM((32, 64, 128), BF),
+            pltpu.VMEM((32, 1, 128), F32),
+            pltpu.VMEM((16, 128), I32),
+            pltpu.SMEM((16, 128), I32),
+            pltpu.SemaphoreType.DMA,
+        ],
         flops=1_600_000_000,
-        moved=9_000_000,
-    )(v, masks, small, small, at)
+        moved=10_000_000,
+    )(v, masks, own_second, at)
     g = [g[0]] + [fetch(value, "x", -shift) for value, shift in zip(g[1:], RING[1:])]
-    second = call(second_kernel, shape((80, 128), BF), [VMEM] * 2, flops=100_000_000, moved=2_000_000)(
-        up, mo
-    )
     other = lax.ppermute(second, "c", [(0, 1), (1, 0)])
     second = ring((second.astype(F32) + other.astype(F32)).astype(BF), "y")
+    *g, second[1], second[2], second[3] = lax.optimization_barrier((*g, *second[1:]))
     part = call(
         weigh_kernel,
         shape((8, 4, 48, 128), BF),

time: 170 us -> 178 us (1.047)
  blocking collectives: 20.3 us -> 59.4 us
  starting transfers between devices: 58 us -> 23.7 us
  Pallas kernels: 15.3 us -> 20.5 us
  waiting for transfers between devices: 56 us -> 53.1 us
    all_to_all x0 -> x2, blocking collectives: none -> 38.6 us  [the longest x1 22 us: body(): v = lax.all_to_all(v, dom, 0, 0, tiled=True)]
    all_to_all x4 -> x0, waiting for transfers between devices: 30.2 us -> none  [the longest x1 25.1 us: body(): v = lax.all_to_all(v, dom, 0, 0, tiled=True).reshape(32, 128, 128)]
    all_to_all x4 -> x0, starting transfers between devices: 26.6 us -> none  [the longest x1 8.27 us: body(): lax.all_to_all(part.reshape(32, 48, 128), ('y', 'c', 'x'), 0, 0, tiled=True)]
    ppermute x12, waiting for transfers between devices: 13.9 us -> 36.6 us  [fetch(): return lax.ppermute(value, axis, [((i + shift) % 4, i) for i in range(4)])]
    ppermute x12, starting transfers between devices: 27.3 us -> 19.2 us  [fetch(): return lax.ppermute(value, axis, [((i + shift) % 4, i) for i in range(4)])]
    pallas_call x4 -> x3, Pallas kernels: 10.2 us -> 16.9 us  [the longest x1 14.8 us: body(): call(mix_kernel, (shape((16, 64, 256), BF), shape((80, 128), BF)) + (shap...]
    all_to_all x1, waiting for transfers between devices: 2.4 us -> 6.75 us  [body(): lax.all_to_all(features.reshape(96, 8, 256).transpose(1, 0, 2), feat, 0,...]
    unnamed x21 -> x12, local copies, waits for them, and re-layouts: 2.47 us -> 4.83 us
  transfers between devices with their start and end apart: 23 -> 19, of which waited for: 11 -> 9; matrix products, arithmetic and copies ran while one was open for 2% -> 2% of each run, Pallas kernels for 8% -> 1%
where the time goes in v2:
time: 178 us; the launch traced here: 177 us
  blocking collectives  59.4 us (33%)
  waiting for transfers between devices  53.1 us (30%)
  starting transfers between devices  23.7 us (13%)
  Pallas kernels  20.5 us (12%)
  between operations  14.1 us (8%)
  local copies, waits for them, and re-layouts  5.92 us (3%)
    ppermute x12, waiting for transfers between devices, fetch(): return lax.ppermute(value, axis, [((i + shift) % 4, i) for i in range(4)])  36.6 us
    all_to_all x1, blocking collectives, body(): v = lax.all_to_all(v, dom, 0, 0, tiled=True)  22 us
    all_to_all x1, blocking collectives, body(): done = lax.all_to_all(done, dom, 0, 0, tiled=True)  20.8 us
    ppermute x12, starting transfers between devices, fetch(): return lax.ppermute(value, axis, [((i + shift) % 4, i) for i in range(4)])  19.2 us
    all_to_all x1, blocking collectives, body(): lax.all_to_all(part.reshape(32, 48, 128), ('y', 'c', 'x'), 0, 0, tiled=True)  16.6 us
    pallas_call x1, Pallas kernels, body(): call(mix_kernel, (shape((16, 64, 256), BF), shape((80, 128), BF)) + (shap...  14.8 us
    all_gather x1, waiting for transfers between devices, body(): masks = lax.all_gather(masks, dom, axis=0)  9.7 us
    all_to_all x1, waiting for transfers between devices, body(): lax.all_to_all(features.reshape(96, 8, 256).transpose(1, 0, 2), feat, 0,...  6.75 us
  transfers between devices with their start and end apart: 19, of which 9 were waited for; matrix products, arithmetic and copies ran while one was open for 2% of the time, Pallas kernels for 1%

profile of v2, /device:TPU:0, one launch (start us, length us, event | category | flops | bytes accessed | tf_op | source)
XLA Modules:
  0.0 177.5 jit_solution(15115503136111652283)
XLA Ops:
  7.2 1.2 copy-done.1
  8.4 0.9 copy-done.3
  9.3 0.8 shard_map.95
  10.1 3.4 %collective-permute-start.2 = (bf16[96,1024]{1,0:T(8,128)(2,1)}, bf16[96,1024]{1,0:T(8,128)(2,1)S(1)}, u32[]{:S(2)}, u32[]{:S(2)}) collective-permute-start(bf16[96,1024]{1,0:T(8,128)(2,1)} %refs_4_.1), channel_id=1, source_target_pairs={{64,0},{96,32},{0,64},{32,96},{65,1},{97,33},{1,65},{33,97},{66,2}... | collective-permute-start | bytes 589832 | tf_op jit(solution)/shard_map/ppermute | solution.py:188
  13.5 0.7 collective-permute-start.1
  14.2 2.6 %collective-permute-start = (bf16[96,1024]{1,0:T(8,128)(2,1)}, bf16[96,1024]{1,0:T(8,128)(2,1)S(1)}, u32[]{:S(2)}, u32[]{:S(2)}) collective-permute-start(bf16[96,1024]{1,0:T(8,128)(2,1)} %refs_4_.1), channel_id=1, source_target_pairs={{32,0},{64,32},{96,64},{0,96},{33,1},{65,33},{97,65},{1,97},{34,2}... | collective-permute-start | bytes 589832 | tf_op jit(solution)/shard_map/ppermute | solution.py:188
  16.7 1.1 copy.14
  17.8 0.8 copy.16
  18.6 3.5 %all-to-all-start = ((bf16[8,96,256]{2,1,0:T(8,128)(2,1)}), bf16[8,96,256]{2,1,0:T(8,128)(2,1)S(1)}, u32[]{:S(2)}, u32[]{:S(2)}) async-start(bf16[8,96,256]{2,1,0:T(8,128)(2,1)} %bitcast.20), calls=%async_computation | async-start | bytes 786432 | tf_op jit(solution)/shard_map/all_to_all | solution.py:204
  23.3 0.7 broadcast_maximum_fusion
  24.2 6.8 %all-to-all-done.refs_0_.x0_ref = bf16[8,96,256]{2,1,0:T(8,128)(2,1)S(1)} async-done(((bf16[8,96,256]{2,1,0:T(8,128)(2,1)}), bf16[8,96,256]{2,1,0:T(8,128)(2,1)S(1)}, u32[]{:S(2)}, u32[]{:S(2)}) %all-to-all-start) | async-done | bytes 393248 | tf_op jit(solution)/shard_map/all_to_all | solution.py:204
  31.0 0.9 copy-done.2
  32.6 1.2 shard_map.94
  33.8 22.0 %all_to_all.20.v_ref = bf16[16,144,128]{2,1,0:T(8,128)(2,1)S(1)} all-to-all(bf16[16,144,128]{2,1,0:T(8,128)(2,1)S(1)} %shard_map.94), channel_id=1, replica_groups=mesh['y'=4,'c'=2,'x'=4,'z'=4] {'x','z'}, dimensions={0} | all-to-all | bytes 1179648 | tf_op jit(solution)/shard_map/all_to_all | solution.py:219
  55.8 1.5 collective-permute-start.9
  57.3 0.8 collective-permute-start.8
  58.1 2.4 %collective-permute-start.7 = (bf16[8,96,256]{2,1,0:T(8,128)(2,1)S(1)}, bf16[8,96,256]{2,1,0:T(8,128)(2,1)S(1)}, u32[]{:S(2)}, u32[]{:S(2)}) collective-permute-start(bf16[8,96,256]{2,1,0:T(8,128)(2,1)S(1)} %all-to-all-done.refs_0_.x0_ref), channel_id=1, source_target_pairs={{1,0},{2,1},{3,2},{0,3},{5,4},{6,5},{7,6},{4,7},{9,8},{10,9},{11,1... | collective-permute-start | bytes 1179656 | tf_op jit(solution)/shard_map/ppermute | solution.py:188
  60.8 16.9 %collective-permute-done.9.x3_ref = bf16[8,96,256]{2,1,0:T(8,128)(2,1)S(1)} collective-permute-done((bf16[8,96,256]{2,1,0:T(8,128)(2,1)S(1)}, bf16[8,96,256]{2,1,0:T(8,128)(2,1)S(1)}, u32[]{:S(2)}, u32[]{:S(2)}) %collective-permute-start.9) | collective-permute-done | bytes 393248 | tf_op jit(solution)/shard_map/ppermute | solution.py:188
  77.7 12.6 %collective-permute-done.8.x2_ref = bf16[8,96,256]{2,1,0:T(8,128)(2,1)S(1)} collective-permute-done((bf16[8,96,256]{2,1,0:T(8,128)(2,1)S(1)}, bf16[8,96,256]{2,1,0:T(8,128)(2,1)S(1)}, u32[]{:S(2)}, u32[]{:S(2)}) %collective-permute-start.8) | collective-permute-done | bytes 393248 | tf_op jit(solution)/shard_map/ppermute | solution.py:188
  90.3 1.3 collective-permute-done.7.x1_ref
  91.6 9.7 %all-gather.3.cloned.1.call-done = bf16[5120,768]{1,0:T(8,128)(2,1)} async-done(((bf16[320,768]{1,0:T(8,128)(2,1)}), bf16[5120,768]{1,0:T(8,128)(2,1)}) %all-gather.3.cloned.1.call-update) | async-done | bytes 7864336 | tf_op jit(solution)/shard_map/all_gather | solution.py:203
  101.3 14.8 %shard_map.96 = (bf16[16,64,256]{2,1,0:T(8,128)(2,1)S(1)}, bf16[80,128]{1,0:T(8,128)(2,1)S(1)}, bf16[4,64,256]{2,1,0:T(8,128)(2,1)S(1)}, bf16[4,64,256]{2,1,0:T(...) custom-call(bf16[16,144,128]{2,1,0:T(8,128)(2,1)S(1)} %all_to_all.20.v_ref, ...), custom_call_target="tpu_custom_call" | custom-call | flops 1600000000 | bytes 10000000 | tf_op jit(solution)/shard_map/pallas_call | solution.py:222
  116.8 2.8 %collective-permute-start.11 = (bf16[4,64,256]{2,1,0:T(8,128)(2,1)S(1)}, bf16[4,64,256]{2,1,0:T(8,128)(2,1)S(1)}, u32[]{:S(2)}, u32[]{:S(2)}) collective-permute-start(bf16[4,64,256]{2,1,0:T(8,128)(2,1)S(1)} %get-tuple-element.35), channel_id=1, source_target_pairs={{4,0},{8,4},{12,8},{0,12},{5,1},{9,5},{13,9},{1,13},{6,2},{10,6},{... | collective-permute-start | bytes 393224 | tf_op jit(solution)/shard_map/ppermute | solution.py:188
  120.2 1.7 collective-permute-start.16
  121.8 0.9 collective-permute-start.15
  122.7 3.0 %collective-permute-done.16.s3_ref = bf16[80,128]{1,0:T(8,128)(2,1)S(1)} collective-permute-done((bf16[80,128]{1,0:T(8,128)(2,1)S(1)}, bf16[80,128]{1,0:T(8,128)(2,1)S(1)}, u32[]{:S(2)}, u32[]{:S(2)}) %collective-permute-start.16) | collective-permute-done | bytes 20512 | tf_op jit(solution)/shard_map/ppermute | solution.py:188
  125.8 1.4 collective-permute-start.14
  127.2 2.4 %collective-permute-done.14.s1_ref = bf16[80,128]{1,0:T(8,128)(2,1)S(1)} collective-permute-done((bf16[80,128]{1,0:T(8,128)(2,1)S(1)}, bf16[80,128]{1,0:T(8,128)(2,1)S(1)}, u32[]{:S(2)}, u32[]{:S(2)}) %collective-permute-start.14) | collective-permute-done | bytes 20512 | tf_op jit(solution)/shard_map/ppermute | solution.py:188
  129.6 2.0 %shard_map.97 = bf16[8,4,48,128]{3,2,1,0:T(8,128)(2,1)S(1)} custom-call(bf16[8,96,256]{2,1,0:T(8,128)(2,1)S(1)} %all-to-all-done.refs_0_.x0_ref, bf16[8,96,256]{2,1,0:T(8,128)(2,1)S(1)} %collective-permute-done.7.x1_ref, bf16[8,96,256]{2,1,0:T(8,128)(2,1)S(1)} %collective-permute-done.8.x2_ref, bf16[8,96,256]{2,1,0:T(8,128)(2,1)S(1)} %collective-permute-done.9.x3_ref, ...), custom_call_target="tpu_custom_call" | custom-call | flops 400000000 | bytes 3000000 | tf_op jit(solution)/shard_map/pallas_call | solution.py:241
  131.6 16.6 %all_to_all.21.part_ref = bf16[32,48,128]{2,1,0:T(8,128)(2,1)S(1)} all-to-all(bf16[32,48,128]{2,1,0:T(8,128)(2,1)S(1)} %bitcast.21), channel_id=1, replica_groups=mesh['y'=4,'c'=2,'x'=4,'z'=4] {'y','c','x'}, dimensions={0} | all-to-all | bytes 786432 | tf_op jit(solution)/shard_map/all_to_all | solution.py:248
  148.4 20.8 %all_to_all.22.in_ref = bf16[16,256,128]{2,1,0:T(8,128)(2,1)S(1)} all-to-all(bf16[16,256,128]{2,1,0:T(8,128)(2,1)S(1)} %shard_map.98), channel_id=1, replica_groups=mesh['y'=4,'c'=2,'x'=4,'z'=4] {'x','z'}, dimensions={0} | all-to-all | bytes 2097152 | tf_op jit(solution)/shard_map/all_to_all | solution.py:250
  169.2 1.4 shard_map.99
  (36 shorter events, 3.8 us)
Async XLA Ops:
  7.2 53.4 %copy-start = (bf16[1024,153]{0,1:T(8,128)(2,1)S(1)}, bf16[1024,153]{0,1:T(8,128)(2,1)}, u32[]{:S(2)}) copy-start(bf16[1024,153]{0,1:T(8,128)(2,1)} %param.9) | copy-start | bytes 940036
  7.2 94.2 %all-gather.3.cloned.1.call-start = ((), (), s32[]{:S(2)}) async-start(), calls=%async_computation.4 | async-start | bytes 8355840 | tf_op jit(solution)/shard_map/all_gather | solution.py:203
  7.2 1.2 copy-start.1
  8.4 0.9 copy-start.3
  10.1 12.4 %collective-permute-start.2 = (bf16[96,1024]{1,0:T(8,128)(2,1)}, bf16[96,1024]{1,0:T(8,128)(2,1)S(1)}, u32[]{:S(2)}, u32[]{:S(2)}) collective-permute-start(bf16[96,1024]{1,0:T(8,128)(2,1)} %refs_4_.1), channel_id=1, source_target_pairs={{64,0},{96,32},{0,64},{32,96},{65,1},{97,33},{1,65},{33,97},{66,2}... | collective-permute-start | bytes 589832 | tf_op jit(solution)/shard_map/ppermute | solution.py:188
  13.5 9.3 %collective-permute-start.1 = (bf16[96,1024]{1,0:T(8,128)(2,1)}, bf16[96,1024]{1,0:T(8,128)(2,1)S(1)}, u32[]{:S(2)}, u32[]{:S(2)}) collective-permute-start(bf16[96,1024]{1,0:T(8,128)(2,1)} %refs_4_.1), channel_id=1, source_target_pairs={{96,0},{0,32},{32,64},{64,96},{97,1},{1,33},{33,65},{65,97},{98,2}... | collective-permute-start | bytes 589832 | tf_op jit(solution)/shard_map/ppermute | solution.py:188
  14.2 9.0 %collective-permute-start = (bf16[96,1024]{1,0:T(8,128)(2,1)}, bf16[96,1024]{1,0:T(8,128)(2,1)S(1)}, u32[]{:S(2)}, u32[]{:S(2)}) collective-permute-start(bf16[96,1024]{1,0:T(8,128)(2,1)} %refs_4_.1), channel_id=1, source_target_pairs={{32,0},{64,32},{96,64},{0,96},{33,1},{65,33},{97,65},{1,97},{34,2}... | collective-permute-start | bytes 589832 | tf_op jit(solution)/shard_map/ppermute | solution.py:188
  18.6 12.3 %all-to-all-start = ((bf16[8,96,256]{2,1,0:T(8,128)(2,1)}), bf16[8,96,256]{2,1,0:T(8,128)(2,1)S(1)}, u32[]{:S(2)}, u32[]{:S(2)}) async-start(bf16[8,96,256]{2,1,0:T(8,128)(2,1)} %bitcast.20), calls=%async_computation | async-start | bytes 786432 | tf_op jit(solution)/shard_map/all_to_all | solution.py:204
  22.1 2.1 %collective-permute-start.3 = (bf16[96,1024]{1,0:T(8,128)(2,1)}, bf16[96,1024]{1,0:T(8,128)(2,1)S(1)}, u32[]{:S(2)}, u32[]{:S(2)}) collective-permute-start(bf16[96,1024]{1,0:T(8,128)(2,1)} %refs_4_.1), channel_id=1, source_target_pairs={{0,16},{16,0},{1,17},{17,1},{2,18},{18,2},{3,19},{19,3},{4,20},{20... | collective-permute-start | bytes 589832 | tf_op jit(solution)/shard_map/ppermute | solution.py:208
  22.5 8.5 %collective-permute-start.6 = (bf16[96,1024]{1,0:T(8,128)(2,1)S(1)}, bf16[96,1024]{1,0:T(8,128)(2,1)S(1)}, u32[]{:S(2)}, u32[]{:S(2)}) collective-permute-start(bf16[96,1024]{1,0:T(8,128)(2,1)S(1)} %collective-permute-done.2.refs_7_), channel_id=1, source_target_pairs={{0,16},{16,0},{1,17},{17,1},{2,18},{18,2},{3,19},{19,3},{4,20},{20... | collective-permute-start | bytes 589832 | tf_op jit(solution)/shard_map/ppermute | solution.py:208
  22.8 8.1 %collective-permute-start.5 = (bf16[96,1024]{1,0:T(8,128)(2,1)S(1)}, bf16[96,1024]{1,0:T(8,128)(2,1)S(1)}, u32[]{:S(2)}, u32[]{:S(2)}) collective-permute-start(bf16[96,1024]{1,0:T(8,128)(2,1)S(1)} %collective-permute-done.1.refs_6_), channel_id=1, source_target_pairs={{0,16},{16,0},{1,17},{17,1},{2,18},{18,2},{3,19},{19,3},{4,20},{20... | collective-permute-start | bytes 589832 | tf_op jit(solution)/shard_map/ppermute | solution.py:208
  23.2 7.8 %collective-permute-start.4 = (bf16[96,1024]{1,0:T(8,128)(2,1)S(1)}, bf16[96,1024]{1,0:T(8,128)(2,1)S(1)}, u32[]{:S(2)}, u32[]{:S(2)}) collective-permute-start(bf16[96,1024]{1,0:T(8,128)(2,1)S(1)} %collective-permute-done.refs_5_), channel_id=1, source_target_pairs={{0,16},{16,0},{1,17},{17,1},{2,18},{18,2},{3,19},{19,3},{4,20},{20... | collective-permute-start | bytes 589832 | tf_op jit(solution)/shard_map/ppermute | solution.py:208
  31.0 0.9 copy-start.2
  31.9 0.7 copy-start.4
  55.8 21.9 %collective-permute-start.9 = (bf16[8,96,256]{2,1,0:T(8,128)(2,1)S(1)}, bf16[8,96,256]{2,1,0:T(8,128)(2,1)S(1)}, u32[]{:S(2)}, u32[]{:S(2)}) collective-permute-start(bf16[8,96,256]{2,1,0:T(8,128)(2,1)S(1)} %all-to-all-done.refs_0_.x0_ref), channel_id=1, source_target_pairs={{2,0},{3,1},{0,2},{1,3},{6,4},{7,5},{4,6},{5,7},{10,8},{11,9},{8,1... | collective-permute-start | bytes 1179656 | tf_op jit(solution)/shard_map/ppermute | solution.py:188
  57.3 33.0 %collective-permute-start.8 = (bf16[8,96,256]{2,1,0:T(8,128)(2,1)S(1)}, bf16[8,96,256]{2,1,0:T(8,128)(2,1)S(1)}, u32[]{:S(2)}, u32[]{:S(2)}) collective-permute-start(bf16[8,96,256]{2,1,0:T(8,128)(2,1)S(1)} %all-to-all-done.refs_0_.x0_ref), channel_id=1, source_target_pairs={{3,0},{0,1},{1,2},{2,3},{7,4},{4,5},{5,6},{6,7},{11,8},{8,9},{9,10... | collective-permute-start | bytes 1179656 | tf_op jit(solution)/shard_map/ppermute | solution.py:188
  58.1 33.5 %collective-permute-start.7 = (bf16[8,96,256]{2,1,0:T(8,128)(2,1)S(1)}, bf16[8,96,256]{2,1,0:T(8,128)(2,1)S(1)}, u32[]{:S(2)}, u32[]{:S(2)}) collective-permute-start(bf16[8,96,256]{2,1,0:T(8,128)(2,1)S(1)} %all-to-all-done.refs_0_.x0_ref), channel_id=1, source_target_pairs={{1,0},{2,1},{3,2},{0,3},{5,4},{6,5},{7,6},{4,7},{9,8},{10,9},{11,1... | collective-permute-start | bytes 1179656 | tf_op jit(solution)/shard_map/ppermute | solution.py:188
  116.2 4.0 %collective-permute-start.13 = (bf16[80,128]{1,0:T(8,128)(2,1)S(1)}, bf16[80,128]{1,0:T(8,128)(2,1)S(1)}, u32[]{:S(2)}, u32[]{:S(2)}) collective-permute-start(bf16[80,128]{1,0:T(8,128)(2,1)S(1)} %get-tuple-element.37), channel_id=1, source_target_pairs={{0,16},{16,0},{1,17},{17,1},{2,18},{18,2},{3,19},{19,3},{4,20},{20... | collective-permute-start | bytes 61448 | tf_op jit(solution)/shard_map/ppermute | solution.py:238
  116.3 13.2 %collective-permute-start.10 = (bf16[4,64,256]{2,1,0:T(8,128)(2,1)S(1)}, bf16[4,64,256]{2,1,0:T(8,128)(2,1)S(1)}, u32[]{:S(2)}, u32[]{:S(2)}) collective-permute-start(bf16[4,64,256]{2,1,0:T(8,128)(2,1)S(1)} %get-tuple-element.34), channel_id=1, source_target_pairs={{12,0},{0,4},{4,8},{8,12},{13,1},{1,5},{5,9},{9,13},{14,2},{2,6},{... | collective-permute-start | bytes 393224 | tf_op jit(solution)/shard_map/ppermute | solution.py:188
  116.8 12.8 %collective-permute-start.11 = (bf16[4,64,256]{2,1,0:T(8,128)(2,1)S(1)}, bf16[4,64,256]{2,1,0:T(8,128)(2,1)S(1)}, u32[]{:S(2)}, u32[]{:S(2)}) collective-permute-start(bf16[4,64,256]{2,1,0:T(8,128)(2,1)S(1)} %get-tuple-element.35), channel_id=1, source_target_pairs={{4,0},{8,4},{12,8},{0,12},{5,1},{9,5},{13,9},{1,13},{6,2},{10,6},{... | collective-permute-start | bytes 393224 | tf_op jit(solution)/shard_map/ppermute | solution.py:188
  119.6 10.0 %collective-permute-start.12 = (bf16[4,64,256]{2,1,0:T(8,128)(2,1)S(1)}, bf16[4,64,256]{2,1,0:T(8,128)(2,1)S(1)}, u32[]{:S(2)}, u32[]{:S(2)}) collective-permute-start(bf16[4,64,256]{2,1,0:T(8,128)(2,1)S(1)} %get-tuple-element.36), channel_id=1, source_target_pairs={{8,0},{12,4},{0,8},{4,12},{9,1},{13,5},{1,9},{5,13},{10,2},{14,6},... | collective-permute-start | bytes 393224 | tf_op jit(solution)/shard_map/ppermute | solution.py:188
  120.2 5.6 %collective-permute-start.16 = (bf16[80,128]{1,0:T(8,128)(2,1)S(1)}, bf16[80,128]{1,0:T(8,128)(2,1)S(1)}, u32[]{:S(2)}, u32[]{:S(2)}) collective-permute-start(bf16[80,128]{1,0:T(8,128)(2,1)S(1)} %add_convert_fusion.s0_ref), channel_id=1, source_target_pairs={{64,0},{96,32},{0,64},{32,96},{65,1},{97,33},{1,65},{33,97},{66,2}... | collective-permute-start | bytes 61448 | tf_op jit(solution)/shard_map/ppermute | solution.py:188
  121.8 5.3 %collective-permute-start.15 = (bf16[80,128]{1,0:T(8,128)(2,1)S(1)}, bf16[80,128]{1,0:T(8,128)(2,1)S(1)}, u32[]{:S(2)}, u32[]{:S(2)}) collective-permute-start(bf16[80,128]{1,0:T(8,128)(2,1)S(1)} %add_convert_fusion.s0_ref), channel_id=1, source_target_pairs={{96,0},{0,32},{32,64},{64,96},{97,1},{1,33},{33,65},{65,97},{98,2}... | collective-permute-start | bytes 61448 | tf_op jit(solution)/shard_map/ppermute | solution.py:188
  125.8 3.8 %collective-permute-start.14 = (bf16[80,128]{1,0:T(8,128)(2,1)S(1)}, bf16[80,128]{1,0:T(8,128)(2,1)S(1)}, u32[]{:S(2)}, u32[]{:S(2)}) collective-permute-start(bf16[80,128]{1,0:T(8,128)(2,1)S(1)} %add_convert_fusion.s0_ref), channel_id=1, source_target_pairs={{32,0},{64,32},{96,64},{0,96},{33,1},{65,33},{97,65},{1,97},{34,2}... | collective-permute-start | bytes 61448 | tf_op jit(solution)/shard_map/ppermute | solution.py:188
Sparse Core Ops, SparseCore 0:
  10.8 90.5 all-gather.2

commit v3 on v2

v3 whole, which is shorter than its diff:
```python
import functools

import jax
import jax.numpy as jnp
from jax import lax
from jax.experimental import pallas as pl
from jax.experimental.pallas import tpu as pltpu
from jax.sharding import Mesh
from jax.sharding import PartitionSpec as P

BF = jnp.bfloat16
F32 = jnp.float32
I32 = jnp.int32
VMEM = pl.BlockSpec(memory_space=pltpu.VMEM)
SMEM = pl.BlockSpec(memory_space=pltpu.SMEM)
ANY = pl.BlockSpec(memory_space=pl.ANY)
LIMIT = 48 * 1024 * 1024
RING = (0, 1, -1, 2)
NT = (((1,), (1,)), ((), ()))


def dot(a, b, dims=(((1,), (0,)), ((), ()))):
    return lax.dot_general(a, b, dims, preferred_element_type=F32)


def columns_of(row):
    return jnp.broadcast_to(row, (128, 128)).T


def halves(a, b):
    low = lax.broadcasted_iota(I32, a.shape, 1) < 64
    return jnp.where(low, a, pltpu.roll(b, 64, 1)), jnp.where(low, pltpu.roll(a, 64, 1), b)


def owner(block):
    return (block % 4) * 4 + block // 4


def orient_kernel(small_ref, table_ref):
    links = small_ref[0, 2:4, :]
    for d in range(1, 16):
        links = links + small_ref[d, 2:4, :]
    links = links.astype(F32)
    row = jnp.concatenate([links[0:1], links[1:2]], axis=1)
    side = jnp.concatenate([columns_of(links[0:1]), columns_of(links[1:2])], axis=0)
    link_r = jnp.broadcast_to(row, (256, 256)) - 2.0
    link_c = jnp.concatenate([side, side], axis=1) - 2.0
    index_c = lax.broadcasted_iota(I32, (256, 256), 0)
    index_r = lax.broadcasted_iota(I32, (256, 256), 1)
    block_c = ((index_c * 10923) >> 16).astype(F32)
    block_r = ((index_r * 10923) >> 16).astype(F32)
    opposite = (link_c == block_r) & (link_r == block_c)
    paired = ((index_c ^ 1) == index_r) & (link_c >= 0.0) & (link_r >= 0.0)
    opposite = jnp.where(opposite, 1.0, 0.0)
    paired = jnp.where(paired, 1.0, 0.0)
    near = dot(paired.astype(BF), opposite.astype(BF)) + dot(opposite.astype(BF), paired.astype(BF))
    reach = jnp.where((near > 0.0) | (index_c == index_r), 1.0, 0.0).astype(BF)
    for _ in range(7):
        reach = jnp.where(dot(reach, reach) > 0.0, 1.0, 0.0).astype(BF)
    reach = reach.astype(F32)
    label_c = jnp.min(jnp.where(reach > 0.0, index_r.astype(F32), 999.0), axis=1, keepdims=True)
    label_r = jnp.min(jnp.where(reach > 0.0, index_c.astype(F32), 999.0), axis=0, keepdims=True)
    other_r = jnp.sum(opposite * label_c, axis=0, keepdims=True)
    sends_r = (label_r < other_r) & (row >= 2.0)
    table_ref[...] = jnp.where(sends_r, row - 1.0, 0.0).astype(I32)


def mask_kernel(mask_ref, up_ref, a_ref, b_ref):
    for b, out_ref in enumerate((a_ref, b_ref)):
        for k in range(6):
            out_ref[0:128, k * 128 : k * 128 + 128] = mask_ref[b, k].astype(F32).astype(BF)
    a_ref[128:192, 0:256] = up_ref[0:64, :]
    a_ref[128:192, 256:512] = up_ref[64:128, :]
    rest = jnp.concatenate([up_ref[128:153, :].astype(F32), jnp.zeros((39, 256), F32)], axis=0)
    a_ref[128:192, 512:768] = rest.astype(BF)


def select_kernel(which, *refs):
    blocks, table_ref, at_ref, outs = refs[:4], refs[4], refs[5], refs[6:8]
    height = outs[0].shape[0] // 2
    for k, ref in enumerate(blocks):
        if which == 0:
            d = at_ref[1] * 4 + (at_ref[2] + RING[k] + 4) % 4
        else:
            d = ((at_ref[1] + RING[k] + 4) % 4) * 4 + at_ref[2]
        out_ref, base = outs[k // 2], (k % 2) * height
        for m in range(3):
            at = d * 12 + which * 6 + m * 2
            first = jnp.where(table_ref[0, at] > 0, 1.0, 0.0)
            second = jnp.where(table_ref[0, at + 1] > 0, 1.0, 0.0)
            one = ref[0:128, m * 256 : m * 256 + 128].astype(F32)
            two = ref[0:128, m * 256 + 128 : m * 256 + 256].astype(F32)
            out_ref[base : base + 128, m * 128 : m * 128 + 128] = (first * one + second * two).astype(BF)
        if which == 0:
            out_ref[base + 128 : base + 192, :] = ref[128:192, 0:384]
            out_ref[base + 192 : base + 256, :] = ref[128:192, 384:768]


def project_kernel(*refs):
    x_refs, w_refs, small_ref, at_ref = refs[:8], refs[8:12], refs[12], refs[13]
    v_refs, w_ref, t_ref = refs[14:18], refs[18], refs[19]
    for k, shift in enumerate(RING):
        for flip in range(2):
            f = ((at_ref[3] + shift + 4) % 4) * 2 + (at_ref[4] + flip) % 2
            w_ref[f] = w_refs[k][flip]
    w = w_ref[...].reshape(768, 256).astype(F32).T.astype(BF)
    for k, shift in enumerate(RING):
        z = (at_ref[2] + shift + 4) % 4
        degree = small_ref[at_ref[1] * 4 + z].astype(F32)
        inv = lax.rsqrt(jnp.concatenate([degree[0:1], degree[1:2]], axis=1))
        low, high = x_refs[2 * k][...].reshape(384, 256), x_refs[2 * k + 1][...].reshape(384, 256)
        t_ref[k] = (inv * (dot(w[:, 0:384], low) + dot(w[:, 384:768], high))).astype(BF)
        for v_ref, to in zip(v_refs, RING):
            at = pl.multiple_of(((at_ref[1] + to + 4) % 4) * 64, 64)
            v_ref[z] = t_ref[k, pl.ds(at, 64), :]


def places(at_ref):
    found = []
    for i, dx in enumerate(RING):
        for j, dz in enumerate(RING):
            found.append((i, j, ((at_ref[1] + dx + 4) % 4) * 4 + (at_ref[2] + dz + 4) % 4))
    return found


def mix_kernel(*refs):
    v_refs, small_ref, tab_ref, sw_ref, at_ref = refs[:4], refs[4], refs[5], refs[6], refs[7]
    mask_refs = refs[8:24]
    hid_ref, second_ref, g_refs = refs[24], refs[25], refs[26:30]
    ma_ref, mb_ref, src_ref, acc_ref, v2_ref, acc2_ref, inv_ref, sems = refs[30:]
    copies = []
    for i, ref in enumerate(mask_refs):
        to = ma_ref.at[i] if i < 8 else mb_ref.at[i - 8]
        copies.append(pltpu.make_async_copy(ref, to, sems.at[i]))
    for copy in copies:
        copy.start()
    for d in range(16):
        degree = small_ref[d].astype(F32)
        for h in range(2):
            inv_ref[2 * d + h] = lax.rsqrt(degree[h : h + 1])
    for copy in copies:
        copy.wait()
    for i, j, d in places(at_ref):
        at, base = i * 2 + j // 2, (j % 2) * 256 + 128
        v_ref = v_refs[(0, 2, 1, 3)[i]]
        z = (at_ref[2] + RING[j] + 4) % 4
        for h in range(2):
            t = d * 2 + h
            inv = inv_ref[t]
            v = v_ref[z, :, h * 128 : h * 128 + 128]
            src_ref[t, 0:64] = v
            acc_ref[t, 0:64] = v.astype(F32)
            second = (base, 256) if h == 0 else (base + 64, 0)
            for c, rows, (row, lane) in (
                (0, 64, (base, h * 128)), (1, 64, second), (2, 32, (base + 64, 128 + h * 128))
            ):
                up = (inv * ma_ref[at, row : row + rows, lane : lane + 128].astype(F32)).astype(BF)
                src_ref[t, 64 + 64 * c : 64 + 64 * c + rows] = up
                acc_ref[t, 64 + 64 * c : 64 + 64 * c + rows] = up.astype(F32)

    def spread(source, total_ref):
        for i, j, d in places(at_ref):
            for h in range(2):
                t = d * 2 + h
                if h == 0:
                    weights = ma_ref[i * 2 + j // 2, (j % 2) * 256 : (j % 2) * 256 + 128, :]
                else:
                    weights = mb_ref[j * 2 + i // 2, (i % 2) * 128 : (i % 2) * 128 + 128, :]
                named = []
                for m in range(3):
                    c = tab_ref[0, 6 * t + 2 * m] + tab_ref[0, 6 * t + 2 * m + 1]
                    named.append(jnp.maximum(c - 1, 0))
                own = source[t]
                others = jnp.concatenate([source[c] for c in named], axis=1)
                back = dot(own, weights)
                total_ref[t] = total_ref[t] + dot(others, weights, NT)
                for m in range(3):
                    total_ref[named[m]] = total_ref[named[m]] + back[:, m * 128 : m * 128 + 128]

    spread(src_ref, acc_ref)
    second = jnp.zeros((160, 64), F32)
    for d in range(16):
        ones, pulls = [], []
        for h in range(2):
            t = d * 2 + h
            inv = inv_ref[t]
            m = inv * acc_ref[t, 0:64]
            s = jax.nn.sigmoid(m)
            hid = (m * s).astype(BF)
            hid_ref[d, :, h * 128 : h * 128 + 128] = hid
            ones.append((inv * hid.astype(F32)).astype(BF))
            pull = acc_ref[t, 64:224].astype(BF)
            pulls.append(pull)
            slope = s * (1.0 + m * (1.0 - s))
            back = (inv * inv * dot(sw_ref[...], pull) * slope).astype(BF)
            v2_ref[t] = back
            acc2_ref[t] = back.astype(F32)
        second = second + dot(jnp.concatenate(pulls, axis=1), jnp.concatenate(ones, axis=1), NT)
    second_ref[...] = jnp.concatenate([second[:80], second[80:]], axis=1).astype(BF)
    spread(v2_ref, acc2_ref)
    for shift, g_ref in zip(RING, g_refs):
        for z in range(4):
            d = ((at_ref[1] + shift + 4) % 4) * 4 + z
            for h in range(2):
                g_ref[z, :, h * 128 : h * 128 + 128] = (
                    inv_ref[d * 2 + h] * acc2_ref[d * 2 + h]
                ).astype(BF)


def weigh_kernel(*refs):
    x_refs, g_refs, at_ref, out_ref = refs[:8], refs[8:12], refs[12], refs[13]
    rights = []
    for shift in RING:
        z = (at_ref[2] + shift + 4) % 4
        rights.append(jnp.concatenate([g[z] for g in g_refs], axis=0))
    for f in range(8):
        acc = jnp.zeros((96, 256), F32)
        for k, right in enumerate(rights):
            acc = acc + dot(x_refs[2 * k + f // 4][f % 4], right, NT)
        for p in range(2):
            g = acc[:, p * 128 : p * 128 + 128]
            for part, shift in zip(halves(g[:48], g[48:]), RING[2 * p : 2 * p + 2]):
                out_ref[f, (at_ref[1] - shift + 4) % 4] = part.astype(BF)


def add_kernel(part_ref, s0_ref, s1_ref, s2_ref, s3_ref, hid_ref, out_ref):
    first = part_ref[0].astype(F32)
    for i in range(1, 32):
        first = first + part_ref[i].astype(F32)
    second = s0_ref[...].astype(F32)
    for ref in (s1_ref, s2_ref, s3_ref):
        second = second + ref[...].astype(F32)
    both = jnp.concatenate([first, second], axis=0).astype(BF)
    for d in range(16):
        out_ref[d, 0:128] = both
        out_ref[d, 128:192] = hid_ref[d, :, 0:128]
        out_ref[d, 192:256] = hid_ref[d, :, 128:256]


def final_kernel(in_ref, hidden_ref, first_ref, second_ref):
    for j in range(8):
        cols = pl.ds(j * 128, 128)
        even, odd = owner(2 * j), owner(2 * j + 1)
        one, two = halves(in_ref[even, 0:128].astype(F32), in_ref[odd, 0:128].astype(F32))
        first_ref[0:48, cols] = one[:48]
        first_ref[48:96, cols] = two[:48]
        second_ref[0:80, cols] = one[48:]
        second_ref[80:153, cols] = two[48:121]
        for h in range(2):
            rows = pl.ds(128 + h * 64, 64)
            both = jnp.concatenate([in_ref[even, rows], in_ref[odd, rows]], axis=0)
            hidden_ref[h * 128 : h * 128 + 128, cols] = both.astype(F32).T.astype(BF)


def call(kernel, shape, specs, scratch=(), flops=0, moved=0):
    return pl.pallas_call(
        kernel,
        out_shape=shape,
        in_specs=specs,
        out_specs=jax.tree.map(lambda _: VMEM, shape),
        scratch_shapes=list(scratch),
        compiler_params=pltpu.CompilerParams(vmem_limit_bytes=LIMIT),
        cost_estimate=pl.CostEstimate(flops=flops, bytes_accessed=moved, transcendentals=0),
    )


def fetch(value, axis, shift):
    return lax.ppermute(value, axis, [((i + shift) % 4, i) for i in range(4)])


def ring(value, axis):
    return [value] + [fetch(value, axis, shift) for shift in RING[1:]]


def rounds(low, high, axis):
    after = [fetch(low, axis, 1), fetch(high, axis, 1)]
    before = [fetch(low, axis, -1), fetch(high, axis, -1)]
    low2, high2, *rest = lax.optimization_barrier((after[0], before[1], low, high))
    far = [fetch(low2, axis, 1), fetch(high2, axis, -1)]
    return [*rest, low2, after[1], before[0], high2, *far]


def body(features, first_weight, second_weight, degree, neighbour_block, neighbour_mask, upstream):
    feat, dom = ("y", "c"), ("x", "z")
    shape = jax.ShapeDtypeStruct
    x, z = lax.axis_index("x"), lax.axis_index("z")
    at = jnp.stack([x * 4 + z, x, z, lax.axis_index("y"), lax.axis_index("c")])
    links = lax.dynamic_update_slice(
        jnp.zeros((256,), I32), neighbour_block.reshape(12) + 2, ((x * 4 + z) * 12,)
    )
    small = jnp.concatenate([degree.reshape(2, 128), links.reshape(2, 128)], axis=0)
    small = lax.all_to_all(jnp.broadcast_to(small, (16, 4, 128)), dom, 0, 0, tiled=True)
    mask_a, mask_b = call(
        mask_kernel, (shape((192, 768), BF), shape((128, 768), BF)), [VMEM] * 2, moved=1_200_000
    )(neighbour_mask[0], upstream[0].T)
    features, small, mask_a, mask_b = lax.optimization_barrier((features, small, mask_a, mask_b))
    x_own = lax.all_to_all(
        features.reshape(96, 8, 256).transpose(1, 0, 2), feat, 0, 0, tiled=True
    )
    blocks_a, blocks_b = ring(mask_a, "z"), ring(mask_b, "x")
    table = call(orient_kernel, shape((1, 256), I32), [VMEM], flops=300_000_000)(small)

    weight = lax.dynamic_slice(first_weight, (0, z * 256), (96, 256))
    weight = jnp.stack([weight, lax.ppermute(weight, "c", [(0, 1), (1, 0)])])
    weights = ring(weight, "y")
    table, *blocks = lax.optimization_barrier((table, *blocks_a, *blocks_b))
    pair_a, pair_b = shape((512, 384), BF), shape((256, 384), BF)
    sent_a = call(functools.partial(select_kernel, 0), (pair_a, pair_a), [VMEM] * 4 + [SMEM] * 2, moved=2_000_000)(
        *blocks[:4], table, at
    )
    sent_b = call(functools.partial(select_kernel, 1), (pair_b, pair_b), [VMEM] * 4 + [SMEM] * 2, moved=2_000_000)(
        *blocks[4:], table, at
    )
    masks = rounds(*sent_a, "x") + rounds(*sent_b, "z")
    x_wide = rounds(x_own[:4], x_own[4:], "z")
    own_second = lax.dynamic_slice(second_weight, ((z * 4 + x) * 64, 0), (64, 153))
    own_second = jnp.pad(own_second, ((0, 0), (0, 7)))
    part = shape((4, 64, 256), BF)
    v = call(
        project_kernel,
        (part,) * 4,
        [VMEM] * 13 + [SMEM],
        [pltpu.VMEM((8, 96, 256), BF), pltpu.VMEM((4, 256, 256), BF)],
        flops=400_000_000,
        moved=3_000_000,
    )(*x_wide, *weights, small, at)
    v = [v[0]] + [fetch(value, "x", -shift) for value, shift in zip(v[1:], RING[1:])]
    hid, second, *g = call(
        mix_kernel,
        (shape((16, 64, 256), BF), shape((80, 128), BF)) + (part,) * 4,
        [VMEM] * 5 + [SMEM, VMEM, SMEM] + [ANY] * 16,
        [
            pltpu.VMEM((8, 512, 384), BF),
            pltpu.VMEM((8, 256, 384), BF),
            pltpu.VMEM((32, 224, 128), BF),
            pltpu.VMEM((32, 224, 128), F32),
            pltpu.VMEM((32, 64, 128), BF),
            pltpu.VMEM((32, 64, 128), F32),
            pltpu.VMEM((32, 1, 128), F32),
            pltpu.SemaphoreType.DMA((16,)),
        ],
        flops=1_600_000_000,
        moved=10_000_000,
    )(*v, small, table, own_second, at, *masks)
    g = [g[0]] + [fetch(value, "x", -shift) for value, shift in zip(g[1:], RING[1:])]
    other = lax.ppermute(second, "c", [(0, 1), (1, 0)])
    second = ring((second.astype(F32) + other.astype(F32)).astype(BF), "y")
    *g, second[1], second[2], second[3] = lax.optimization_barrier((*g, *second[1:]))
    part = call(
        weigh_kernel,
        shape((8, 4, 48, 128), BF),
        [VMEM] * 12 + [SMEM],
        flops=400_000_000,
        moved=3_000_000,
    )(*x_wide, *g, at)
    part = lax.all_to_all(part.reshape(32, 48, 128), ("y", "c", "x"), 0, 0, tiled=True)
    done = call(add_kernel, shape((16, 256, 128), BF), [VMEM] * 6, moved=3_000_000)(part, *second, hid)
    done = lax.all_to_all(done, dom, 0, 0, tiled=True)
    hidden, grad_first, grad_second = call(
        final_kernel,
        (shape((256, 1024), BF), shape((96, 1024), F32), shape((153, 1024), F32)),
        [VMEM],
        moved=2_500_000,
    )(done)
    return (hidden[None], grad_first, grad_second.T)


def solution(mesh):
    wide = Mesh(mesh.devices.reshape(4, 2, 4, 4), ("y", "c", "x", "z"))
    feat, dom = ("y", "c"), ("x", "z")
    placed = (
        P(feat, dom, None),
        P(feat, None),
        P(),
        P(dom, feat),
        P(dom, feat, None),
        P(dom, feat, None, None, None),
        P(dom, feat, None),
    )
    return jax.shard_map(
        body,
        mesh=wide,
        in_specs=placed,
        out_specs=(P(dom, feat, None), P(feat, None), P()),
        check_vma=False,
    )
```

time: 178 us -> 175 us (0.983)
  starting transfers between devices: 23.7 us -> 59.1 us
  blocking collectives: 59.4 us -> 37.4 us
  waiting for transfers between devices: 53.1 us -> 34 us
  local copies, waits for them, and re-layouts: 5.92 us -> 19.8 us
  between operations: 14.1 us -> 0.95 us
    ppermute x12 -> x36, starting transfers between devices: 19.2 us -> 45.9 us  [fetch(): return lax.ppermute(value, axis, [((i + shift) % 4, i) for i in range(4)])]
    all_to_all x1 -> x0, blocking collectives: 22 us -> none  [body(): v = lax.all_to_all(v, dom, 0, 0, tiled=True)]
    unnamed x12 -> x62, local copies, waits for them, and re-layouts: 4.83 us -> 17.9 us
    all_gather x1 -> x0, waiting for transfers between devices: 9.7 us -> none  [body(): masks = lax.all_gather(masks, dom, axis=0)]
    ppermute x12 -> x36, waiting for transfers between devices: 36.6 us -> 27.6 us  [fetch(): return lax.ppermute(value, axis, [((i + shift) % 4, i) for i in range(4)])]
    all_to_all x0 -> x1, starting transfers between devices: none -> 7.96 us  [body(): lax.all_to_all(jnp.broadcast_to(small, (16, 4, 128)), dom, 0, 0, tiled=True)]
    all_to_all x1, waiting for transfers between devices: 6.75 us -> 0.01 us  [body(): lax.all_to_all(features.reshape(96, 8, 256).transpose(1, 0, 2), feat, 0,...]
    all_to_all x0 -> x1, waiting for transfers between devices: none -> 6.41 us  [body(): lax.all_to_all(jnp.broadcast_to(small, (16, 4, 128)), dom, 0, 0, tiled=True)]
  transfers between devices with their start and end apart: 19 -> 40, of which waited for: 9 -> 13; matrix products, arithmetic and copies ran while one was open for 2% -> 1% of each run, Pallas kernels for 1% -> 3%
where the time goes in v3:
time: 175 us; the launch traced here: 174 us
  starting transfers between devices  59.1 us (34%)
  blocking collectives  37.4 us (21%)
  waiting for transfers between devices  34 us (19%)
  Pallas kernels  21.1 us (12%)
  local copies, waits for them, and re-layouts  19.8 us (11%)
    ppermute x36, starting transfers between devices, fetch(): return lax.ppermute(value, axis, [((i + shift) % 4, i) for i in range(4)])  45.9 us
    ppermute x36, waiting for transfers between devices, fetch(): return lax.ppermute(value, axis, [((i + shift) % 4, i) for i in range(4)])  27.6 us
    all_to_all x1, blocking collectives, body(): done = lax.all_to_all(done, dom, 0, 0, tiled=True)  20.8 us
    unnamed x62, local copies, waits for them, and re-layouts  17.9 us
    all_to_all x1, blocking collectives, body(): lax.all_to_all(part.reshape(32, 48, 128), ('y', 'c', 'x'), 0, 0, tiled=True)  16.6 us
    pallas_call x1, Pallas kernels, body(): call(mix_kernel, (shape((16, 64, 256), BF), shape((80, 128), BF)) + (part...  11.4 us
    all_to_all x1, starting transfers between devices, body(): lax.all_to_all(jnp.broadcast_to(small, (16, 4, 128)), dom, 0, 0, tiled=True)  7.96 us
    all_to_all x1, waiting for transfers between devices, body(): lax.all_to_all(jnp.broadcast_to(small, (16, 4, 128)), dom, 0, 0, tiled=True)  6.41 us
  transfers between devices with their start and end apart: 40, of which 13 were waited for; matrix products, arithmetic and copies ran while one was open for 1% of the time, Pallas kernels for 3%

profile of v3, /device:TPU:0, one launch (start us, length us, event | category | flops | bytes accessed | tf_op | source)
XLA Modules:
  0.0 173.8 jit_solution(10634717211540489547)
XLA Ops:
  3.0 8.0 %all-to-all-start = ((s32[16,4,128]{2,1,0:T(4,128)}), s32[16,4,128]{2,1,0:T(4,128)S(1)}, u32[]{:S(2)}, u32[]{:S(2)}) async-start(s32[16,4,128]{2,1,0:T(4,128)} %broadcast_in_dim.10), calls=%async_computation | async-start | bytes 65536 | tf_op jit(solution)/shard_map/all_to_all | solution.py:292
  12.2 6.4 %all-to-all-done.refs_12_.small_ref.refs_4_ = s32[16,4,128]{2,1,0:T(4,128)S(1)} async-done(((s32[16,4,128]{2,1,0:T(4,128)}), s32[16,4,128]{2,1,0:T(4,128)S(1)}, u32[]{:S(2)}, u32[]{:S(2)}) %all-to-all-start) | async-done | bytes 32800 | tf_op jit(solution)/shard_map/all_to_all | solution.py:292
  20.7 4.6 %all-to-all-start.1 = ((bf16[8,96,256]{2,1,0:T(8,128)(2,1)}), bf16[8,96,256]{2,1,0:T(8,128)(2,1)S(1)}, u32[]{:S(2)}, u32[]{:S(2)}) async-start(bf16[8,96,256]{2,1,0:T(8,128)(2,1)} %bitcast.23), calls=%async_computation.1 | async-start | bytes 786432 | tf_op jit(solution)/shard_map/all_to_all | solution.py:297
  27.9 2.5 %collective-permute-start.13 = (bf16[192,768]{1,0:T(8,128)(2,1)S(1)}, bf16[192,768]{1,0:T(8,128)(2,1)S(1)}, u32[]{:S(2)}, u32[]{:S(2)}) collective-permute-start(bf16[192,768]{1,0:T(8,128)(2,1)S(1)} %get-tuple-element.69.refs_0_), channel_id=1, source_target_pairs={{1,0},{2,1},{3,2},{0,3},{5,4},{6,5},{7,6},{4,7},{9,8},{10,9},{11,1... | collective-permute-start | bytes 884744 | tf_op jit(solution)/shard_map/ppermute | solution.py:268
  31.2 2.4 %collective-permute-start.16 = (bf16[128,768]{1,0:T(8,128)(2,1)S(1)}, bf16[128,768]{1,0:T(8,128)(2,1)S(1)}, u32[]{:S(2)}, u32[]{:S(2)}) collective-permute-start(bf16[128,768]{1,0:T(8,128)(2,1)S(1)} %get-tuple-element.79.refs_0_), channel_id=1, source_target_pairs={{4,0},{8,4},{12,8},{0,12},{5,1},{9,5},{13,9},{1,13},{6,2},{10,6},{... | collective-permute-start | bytes 589832 | tf_op jit(solution)/shard_map/ppermute | solution.py:268
  33.7 1.8 %shard_map.96.refs_4_.refs_5_ = s32[1,256]{1,0:T(1,128)S(1)} custom-call(s32[16,4,128]{2,1,0:T(4,128)S(1)} %all-to-all-done.refs_12_.small_ref.refs_4_), custom_call_target="tpu_custom_call" | custom-call | flops 300000000 | tf_op jit(solution)/shard_map/pallas_call | solution.py:301
  35.5 2.1 %collective-permute-done.17.refs_2_ = bf16[128,768]{1,0:T(8,128)(2,1)S(1)} collective-permute-done((bf16[128,768]{1,0:T(8,128)(2,1)S(1)}, bf16[128,768]{1,0:T(8,128)(2,1)S(1)}, u32[]{:S(2)}, u32[]{:S(2)}) %collective-permute-start.17) | collective-permute-done | bytes 196640 | tf_op jit(solution)/shard_map/ppermute | solution.py:268
  37.7 3.4 %collective-permute-start.9 = (bf16[2,96,256]{2,1,0:T(8,128)(2,1)S(1)}, bf16[2,96,256]{2,1,0:T(8,128)(2,1)S(1)}, u32[]{:S(2)}, u32[]{:S(2)}) collective-permute-start(bf16[2,96,256]{2,1,0:T(8,128)(2,1)S(1)} %pad_maximum_fusion.refs_8_), channel_id=1, source_target_pairs={{64,0},{96,32},{0,64},{32,96},{65,1},{97,33},{1,65},{33,97},{66,2}... | collective-permute-start | bytes 294920 | tf_op jit(solution)/shard_map/ppermute | solution.py:268
  41.7 2.7 %collective-permute-start.7 = (bf16[2,96,256]{2,1,0:T(8,128)(2,1)S(1)}, bf16[2,96,256]{2,1,0:T(8,128)(2,1)S(1)}, u32[]{:S(2)}, u32[]{:S(2)}) collective-permute-start(bf16[2,96,256]{2,1,0:T(8,128)(2,1)S(1)} %pad_maximum_fusion.refs_8_), channel_id=1, source_target_pairs={{32,0},{64,32},{96,64},{0,96},{33,1},{65,33},{97,65},{1,97},{34,2}... | collective-permute-start | bytes 294920 | tf_op jit(solution)/shard_map/ppermute | solution.py:268
  44.4 1.3 shard_map.98
  45.7 3.2 %collective-permute-start.25 = (bf16[256,384]{1,0:T(8,128)(2,1)S(1)}, bf16[256,384]{1,0:T(8,128)(2,1)}, u32[]{:S(2)}, u32[]{:S(2)}) collective-permute-start(bf16[256,384]{1,0:T(8,128)(2,1)S(1)} %get-tuple-element.85.refs_16_), channel_id=1, source_target_pairs={{1,0},{2,1},{3,2},{0,3},{5,4},{6,5},{7,6},{4,7},{9,8},{10,9},{11,1... | collective-permute-start | bytes 589832 | tf_op jit(solution)/shard_map/ppermute | solution.py:268
  49.2 3.2 %collective-permute-start = (bf16[4,96,256]{2,1,0:T(8,128)(2,1)S(1)}, bf16[4,96,256]{2,1,0:T(8,128)(2,1)S(1)}, u32[]{:S(2)}, u32[]{:S(2)}) collective-permute-start(bf16[4,96,256]{2,1,0:T(8,128)(2,1)S(1)} %get-tuple-element.57.refs_0_), channel_id=1, source_target_pairs={{1,0},{2,1},{3,2},{0,3},{5,4},{6,5},{7,6},{4,7},{9,8},{10,9},{11,1... | collective-permute-start | bytes 589832 | tf_op jit(solution)/shard_map/ppermute | solution.py:268
  57.1 1.5 collective-permute-done.26.refs_21_
  58.6 2.4 %collective-permute-done.1.refs_5_ = bf16[4,96,256]{2,1,0:T(8,128)(2,1)S(1)} collective-permute-done((bf16[4,96,256]{2,1,0:T(8,128)(2,1)S(1)}, bf16[4,96,256]{2,1,0:T(8,128)(2,1)S(1)}, u32[]{:S(2)}, u32[]{:S(2)}) %collective-permute-start.1) | collective-permute-done | bytes 196640 | tf_op jit(solution)/shard_map/ppermute | solution.py:268
  61.0 2.0 %collective-permute-start.3 = (bf16[4,96,256]{2,1,0:T(8,128)(2,1)S(1)}, bf16[4,96,256]{2,1,0:T(8,128)(2,1)S(1)}, u32[]{:S(2)}, u32[]{:S(2)}) collective-permute-start(bf16[4,96,256]{2,1,0:T(8,128)(2,1)S(1)} %get-tuple-element.57.refs_0_), channel_id=1, source_target_pairs={{3,0},{0,1},{1,2},{2,3},{7,4},{4,5},{5,6},{6,7},{11,8},{8,9},{9,10... | collective-permute-start | bytes 589832 | tf_op jit(solution)/shard_map/ppermute | solution.py:268
  63.0 3.5 %collective-permute-done.27.refs_19_ = bf16[256,384]{1,0:T(8,128)(2,1)S(1)} collective-permute-done((bf16[256,384]{1,0:T(8,128)(2,1)}, bf16[256,384]{1,0:T(8,128)(2,1)S(1)}, u32[]{:S(2)}, u32[]{:S(2)}) %collective-permute-start.27) | collective-permute-done | bytes 196640 | tf_op jit(solution)/shard_map/ppermute | solution.py:268
  68.5 2.2 %collective-permute-done.2.refs_3_ = bf16[4,96,256]{2,1,0:T(8,128)(2,1)S(1)} collective-permute-done((bf16[4,96,256]{2,1,0:T(8,128)(2,1)S(1)}, bf16[4,96,256]{2,1,0:T(8,128)(2,1)S(1)}, u32[]{:S(2)}, u32[]{:S(2)}) %collective-permute-start.2) | collective-permute-done | bytes 196640 | tf_op jit(solution)/shard_map/ppermute | solution.py:268
  72.8 3.2 %collective-permute-start.21 = (bf16[512,384]{1,0:T(8,128)(2,1)S(1)}, bf16[512,384]{1,0:T(8,128)(2,1)S(1)}, u32[]{:S(2)}, u32[]{:S(2)}) collective-permute-start(bf16[512,384]{1,0:T(8,128)(2,1)S(1)} %get-tuple-element.76.refs_9_), channel_id=1, source_target_pairs={{4,0},{8,4},{12,8},{0,12},{5,1},{9,5},{13,9},{1,13},{6,2},{10,6},{... | collective-permute-start | bytes 1179656 | tf_op jit(solution)/shard_map/ppermute | solution.py:268
  78.9 2.1 %shard_map.95 = (bf16[4,64,256]{2,1,0:T(8,128)(2,1)S(1)}, bf16[4,64,256]{2,1,0:T(8,128)(2,1)}, bf16[4,64,256]{2,1,0:T(8,128)(2,1)}, bf16[4,64,256]{2,1,0:T(8,128)(2,1)}) custom-call(bf16[4,96,256]{2,1,0:T(8,128)(2,1)S(1)} %get-tuple-element.57.refs_0_, bf16[4,96,256]{2,1,0:T(8,128)(2,1)S(1)} %get-tuple-element.58.refs_1_, ...), custom_call_target="tpu_custom_call" | custom-call | flops 400000000 | bytes 3000000 | tf_op jit(solution)/shard_map/pallas_call | solution.py:319
  81.7 4.1 %collective-permute-done.30.refs_23_ = bf16[256,384]{1,0:T(8,128)(2,1)S(1)} collective-permute-done((bf16[256,384]{1,0:T(8,128)(2,1)S(1)}, bf16[256,384]{1,0:T(8,128)(2,1)S(1)}, u32[]{:S(2)}, u32[]{:S(2)}) %collective-permute-start.30) | collective-permute-done | bytes 196640 | tf_op jit(solution)/shard_map/ppermute | solution.py:268
  87.2 3.3 %collective-permute-start.11 = (bf16[4,64,256]{2,1,0:T(8,128)(2,1)}, bf16[4,64,256]{2,1,0:T(8,128)(2,1)S(1)}, u32[]{:S(2)}, u32[]{:S(2)}) collective-permute-start(bf16[4,64,256]{2,1,0:T(8,128)(2,1)} %get-tuple-element.64), channel_id=1, source_target_pairs={{4,0},{8,4},{12,8},{0,12},{5,1},{9,5},{13,9},{1,13},{6,2},{10,6},{... | collective-permute-start | bytes 393224 | tf_op jit(solution)/shard_map/ppermute | solution.py:268
  91.3 1.5 collective-permute-start.12
  92.9 1.4 collective-permute-done.10.refs_1_
  95.7 2.4 %collective-permute-done.12.refs_3_ = bf16[4,64,256]{2,1,0:T(8,128)(2,1)} collective-permute-done((bf16[4,64,256]{2,1,0:T(8,128)(2,1)}, bf16[4,64,256]{2,1,0:T(8,128)(2,1)}, u32[]{:S(2)}, u32[]{:S(2)}) %collective-permute-start.12) | collective-permute-done | bytes 131104 | tf_op jit(solution)/shard_map/ppermute | solution.py:268
  108.5 11.4 %shard_map.99 = (bf16[16,64,256]{2,1,0:T(8,128)(2,1)}, bf16[80,128]{1,0:T(8,128)(2,1)S(1)}, bf16[4,64,256]{2,1,0:T(8,128)(2,1)S(1)}, bf16[4,64,256]{2,1,0:T(8,12...) custom-call(bf16[4,64,256]{2,1,0:T(8,128)(2,1)S(1)} %copy-done.23, ...), custom_call_target="tpu_custom_call" | custom-call | flops 1600000000 | bytes 10000000 | tf_op jit(solution)/shard_map/pallas_call | solution.py:328
  120.1 3.2 %collective-permute-start.32 = (bf16[4,64,256]{2,1,0:T(8,128)(2,1)S(1)}, bf16[4,64,256]{2,1,0:T(8,128)(2,1)S(1)}, u32[]{:S(2)}, u32[]{:S(2)}) collective-permute-start(bf16[4,64,256]{2,1,0:T(8,128)(2,1)S(1)} %get-tuple-element.91), channel_id=1, source_target_pairs={{4,0},{8,4},{12,8},{0,12},{5,1},{9,5},{13,9},{1,13},{6,2},{10,6},{... | collective-permute-start | bytes 393224 | tf_op jit(solution)/shard_map/ppermute | solution.py:268
  125.4 3.5 %collective-permute-done.37.s3_ref = bf16[80,128]{1,0:T(8,128)(2,1)S(1)} collective-permute-done((bf16[80,128]{1,0:T(8,128)(2,1)S(1)}, bf16[80,128]{1,0:T(8,128)(2,1)S(1)}, u32[]{:S(2)}, u32[]{:S(2)}) %collective-permute-start.37) | collective-permute-done | bytes 20512 | tf_op jit(solution)/shard_map/ppermute | solution.py:268
  129.9 2.9 %collective-permute-done.35.s1_ref = bf16[80,128]{1,0:T(8,128)(2,1)S(1)} collective-permute-done((bf16[80,128]{1,0:T(8,128)(2,1)S(1)}, bf16[80,128]{1,0:T(8,128)(2,1)S(1)}, u32[]{:S(2)}, u32[]{:S(2)}) %collective-permute-start.35) | collective-permute-done | bytes 20512 | tf_op jit(solution)/shard_map/ppermute | solution.py:268
  132.7 2.0 %shard_map.100 = bf16[8,4,48,128]{3,2,1,0:T(8,128)(2,1)S(1)} custom-call(bf16[4,96,256]{2,1,0:T(8,128)(2,1)S(1)} %get-tuple-element.57.refs_0_, bf16[4,96,256]{2,1,0:T(8,128)(2,1)S(1)} %get-tuple-element.58.refs_1_, bf16[4,96,256]{2,1,0:T(8,128)(2,1)S(1)} %collective-permute-done.refs_2_, bf16[4,96,256]{2,1,0:T(8,128)(2,1)S(1)} %collective-permute-done.2.refs_3_, ...), custom_call_target="tpu_custom_call" | custom-call | flops 400000000 | bytes 3000000 | tf_op jit(solution)/shard_map/pallas_call | solution.py:349
  134.8 16.6 %all_to_all.20.part_ref = bf16[32,48,128]{2,1,0:T(8,128)(2,1)S(1)} all-to-all(bf16[32,48,128]{2,1,0:T(8,128)(2,1)S(1)} %bitcast.24), channel_id=1, replica_groups=mesh['y'=4,'c'=2,'x'=4,'z'=4] {'y','c','x'}, dimensions={0} | all-to-all | bytes 786432 | tf_op jit(solution)/shard_map/all_to_all | solution.py:356
  151.6 20.8 %all_to_all.21.in_ref = bf16[16,256,128]{2,1,0:T(8,128)(2,1)S(1)} all-to-all(bf16[16,256,128]{2,1,0:T(8,128)(2,1)S(1)} %shard_map.101), channel_id=1, replica_groups=mesh['y'=4,'c'=2,'x'=4,'z'=4] {'x','z'}, dimensions={0} | all-to-all | bytes 2097152 | tf_op jit(solution)/shard_map/all_to_all | solution.py:358
  172.4 1.4 shard_map.102
  (136 shorter events, 39.6 us)
Async XLA Ops:
  3.0 15.6 %all-to-all-start = ((s32[16,4,128]{2,1,0:T(4,128)}), s32[16,4,128]{2,1,0:T(4,128)S(1)}, u32[]{:S(2)}, u32[]{:S(2)}) async-start(s32[16,4,128]{2,1,0:T(4,128)} %broadcast_in_dim.10), calls=%async_computation | async-start | bytes 65536 | tf_op jit(solution)/shard_map/all_to_all | solution.py:292
  18.6 12.6 %collective-permute-start.18 = (bf16[128,768]{1,0:T(8,128)(2,1)S(1)}, bf16[128,768]{1,0:T(8,128)(2,1)S(1)}, u32[]{:S(2)}, u32[]{:S(2)}) collective-permute-start(bf16[128,768]{1,0:T(8,128)(2,1)S(1)} %get-tuple-element.79.refs_0_), channel_id=1, source_target_pairs={{8,0},{12,4},{0,8},{4,12},{9,1},{13,5},{1,9},{5,13},{10,2},{14,6},... | collective-permute-start | bytes 589832 | tf_op jit(solution)/shard_map/ppermute | solution.py:268
  20.7 28.2 %all-to-all-start.1 = ((bf16[8,96,256]{2,1,0:T(8,128)(2,1)}), bf16[8,96,256]{2,1,0:T(8,128)(2,1)S(1)}, u32[]{:S(2)}, u32[]{:S(2)}) async-start(bf16[8,96,256]{2,1,0:T(8,128)(2,1)} %bitcast.23), calls=%async_computation.1 | async-start | bytes 786432 | tf_op jit(solution)/shard_map/all_to_all | solution.py:297
  25.9 15.8 %collective-permute-start.15 = (bf16[192,768]{1,0:T(8,128)(2,1)S(1)}, bf16[192,768]{1,0:T(8,128)(2,1)S(1)}, u32[]{:S(2)}, u32[]{:S(2)}) collective-permute-start(bf16[192,768]{1,0:T(8,128)(2,1)S(1)} %get-tuple-element.69.refs_0_), channel_id=1, source_target_pairs={{2,0},{3,1},{0,2},{1,3},{6,4},{7,5},{4,6},{5,7},{10,8},{11,9},{8,1... | collective-permute-start | bytes 884744 | tf_op jit(solution)/shard_map/ppermute | solution.py:268
  27.2 17.2 %collective-permute-start.14 = (bf16[192,768]{1,0:T(8,128)(2,1)S(1)}, bf16[192,768]{1,0:T(8,128)(2,1)S(1)}, u32[]{:S(2)}, u32[]{:S(2)}) collective-permute-start(bf16[192,768]{1,0:T(8,128)(2,1)S(1)} %get-tuple-element.69.refs_0_), channel_id=1, source_target_pairs={{3,0},{0,1},{1,2},{2,3},{7,4},{4,5},{5,6},{6,7},{11,8},{8,9},{9,10... | collective-permute-start | bytes 884744 | tf_op jit(solution)/shard_map/ppermute | solution.py:268
  27.9 16.4 %collective-permute-start.13 = (bf16[192,768]{1,0:T(8,128)(2,1)S(1)}, bf16[192,768]{1,0:T(8,128)(2,1)S(1)}, u32[]{:S(2)}, u32[]{:S(2)}) collective-permute-start(bf16[192,768]{1,0:T(8,128)(2,1)S(1)} %get-tuple-element.69.refs_0_), channel_id=1, source_target_pairs={{1,0},{2,1},{3,2},{0,3},{5,4},{6,5},{7,6},{4,7},{9,8},{10,9},{11,1... | collective-permute-start | bytes 884744 | tf_op jit(solution)/shard_map/ppermute | solution.py:268
  30.4 7.3 %collective-permute-start.17 = (bf16[128,768]{1,0:T(8,128)(2,1)S(1)}, bf16[128,768]{1,0:T(8,128)(2,1)S(1)}, u32[]{:S(2)}, u32[]{:S(2)}) collective-permute-start(bf16[128,768]{1,0:T(8,128)(2,1)S(1)} %get-tuple-element.79.refs_0_), channel_id=1, source_target_pairs={{12,0},{0,4},{4,8},{8,12},{13,1},{1,5},{5,9},{9,13},{14,2},{2,6},{... | collective-permute-start | bytes 589832 | tf_op jit(solution)/shard_map/ppermute | solution.py:268
  31.2 9.9 %collective-permute-start.16 = (bf16[128,768]{1,0:T(8,128)(2,1)S(1)}, bf16[128,768]{1,0:T(8,128)(2,1)S(1)}, u32[]{:S(2)}, u32[]{:S(2)}) collective-permute-start(bf16[128,768]{1,0:T(8,128)(2,1)S(1)} %get-tuple-element.79.refs_0_), channel_id=1, source_target_pairs={{4,0},{8,4},{12,8},{0,12},{5,1},{9,5},{13,9},{1,13},{6,2},{10,6},{... | collective-permute-start | bytes 589832 | tf_op jit(solution)/shard_map/ppermute | solution.py:268
  37.7 11.3 %collective-permute-start.9 = (bf16[2,96,256]{2,1,0:T(8,128)(2,1)S(1)}, bf16[2,96,256]{2,1,0:T(8,128)(2,1)S(1)}, u32[]{:S(2)}, u32[]{:S(2)}) collective-permute-start(bf16[2,96,256]{2,1,0:T(8,128)(2,1)S(1)} %pad_maximum_fusion.refs_8_), channel_id=1, source_target_pairs={{64,0},{96,32},{0,64},{32,96},{65,1},{97,33},{1,65},{33,97},{66,2}... | collective-permute-start | bytes 294920 | tf_op jit(solution)/shard_map/ppermute | solution.py:268
  41.1 7.9 %collective-permute-start.8 = (bf16[2,96,256]{2,1,0:T(8,128)(2,1)S(1)}, bf16[2,96,256]{2,1,0:T(8,128)(2,1)S(1)}, u32[]{:S(2)}, u32[]{:S(2)}) collective-permute-start(bf16[2,96,256]{2,1,0:T(8,128)(2,1)S(1)} %pad_maximum_fusion.refs_8_), channel_id=1, source_target_pairs={{96,0},{0,32},{32,64},{64,96},{97,1},{1,33},{33,65},{65,97},{98,2}... | collective-permute-start | bytes 294920 | tf_op jit(solution)/shard_map/ppermute | solution.py:268
  41.7 7.5 %collective-permute-start.7 = (bf16[2,96,256]{2,1,0:T(8,128)(2,1)S(1)}, bf16[2,96,256]{2,1,0:T(8,128)(2,1)S(1)}, u32[]{:S(2)}, u32[]{:S(2)}) collective-permute-start(bf16[2,96,256]{2,1,0:T(8,128)(2,1)S(1)} %pad_maximum_fusion.refs_8_), channel_id=1, source_target_pairs={{32,0},{64,32},{96,64},{0,96},{33,1},{65,33},{97,65},{1,97},{34,2}... | collective-permute-start | bytes 294920 | tf_op jit(solution)/shard_map/ppermute | solution.py:268
  45.7 8.7 %collective-permute-start.28 = (bf16[256,384]{1,0:T(8,128)(2,1)S(1)}, bf16[256,384]{1,0:T(8,128)(2,1)S(1)}, u32[]{:S(2)}, u32[]{:S(2)}) collective-permute-start(bf16[256,384]{1,0:T(8,128)(2,1)S(1)} %get-tuple-element.85.refs_16_), channel_id=1, source_target_pairs={{3,0},{0,1},{1,2},{2,3},{7,4},{4,5},{5,6},{6,7},{11,8},{8,9},{9,10... | collective-permute-start | bytes 589832 | tf_op jit(solution)/shard_map/ppermute | solution.py:268
  45.7 10.2 %collective-permute-start.25 = (bf16[256,384]{1,0:T(8,128)(2,1)S(1)}, bf16[256,384]{1,0:T(8,128)(2,1)}, u32[]{:S(2)}, u32[]{:S(2)}) collective-permute-start(bf16[256,384]{1,0:T(8,128)(2,1)S(1)} %get-tuple-element.85.refs_16_), channel_id=1, source_target_pairs={{1,0},{2,1},{3,2},{0,3},{5,4},{6,5},{7,6},{4,7},{9,8},{10,9},{11,1... | collective-permute-start | bytes 589832 | tf_op jit(solution)/shard_map/ppermute | solution.py:268
  49.0 9.6 %collective-permute-start.26 = (bf16[256,384]{1,0:T(8,128)(2,1)}, bf16[256,384]{1,0:T(8,128)(2,1)S(1)}, u32[]{:S(2)}, u32[]{:S(2)}) collective-permute-start(bf16[256,384]{1,0:T(8,128)(2,1)} %get-tuple-element.86.refs_17_), channel_id=1, source_target_pairs={{3,0},{0,1},{1,2},{2,3},{7,4},{4,5},{5,6},{6,7},{11,8},{8,9},{9,10... | collective-permute-start | bytes 589832 | tf_op jit(solution)/shard_map/ppermute | solution.py:268
  49.1 11.9 %collective-permute-start.1 = (bf16[4,96,256]{2,1,0:T(8,128)(2,1)S(1)}, bf16[4,96,256]{2,1,0:T(8,128)(2,1)S(1)}, u32[]{:S(2)}, u32[]{:S(2)}) collective-permute-start(bf16[4,96,256]{2,1,0:T(8,128)(2,1)S(1)} %get-tuple-element.58.refs_1_), channel_id=1, source_target_pairs={{3,0},{0,1},{1,2},{2,3},{7,4},{4,5},{5,6},{6,7},{11,8},{8,9},{9,10... | collective-permute-start | bytes 589832 | tf_op jit(solution)/shard_map/ppermute | solution.py:268
  49.2 11.8 %collective-permute-start = (bf16[4,96,256]{2,1,0:T(8,128)(2,1)S(1)}, bf16[4,96,256]{2,1,0:T(8,128)(2,1)S(1)}, u32[]{:S(2)}, u32[]{:S(2)}) collective-permute-start(bf16[4,96,256]{2,1,0:T(8,128)(2,1)S(1)} %get-tuple-element.57.refs_0_), channel_id=1, source_target_pairs={{1,0},{2,1},{3,2},{0,3},{5,4},{6,5},{7,6},{4,7},{9,8},{10,9},{11,1... | collective-permute-start | bytes 589832 | tf_op jit(solution)/shard_map/ppermute | solution.py:268
  55.1 17.7 %collective-permute-start.19 = (bf16[512,384]{1,0:T(8,128)(2,1)S(1)}, bf16[512,384]{1,0:T(8,128)(2,1)S(1)}, u32[]{:S(2)}, u32[]{:S(2)}) collective-permute-start(bf16[512,384]{1,0:T(8,128)(2,1)S(1)} %get-tuple-element.75.refs_8_), channel_id=1, source_target_pairs={{4,0},{8,4},{12,8},{0,12},{5,1},{9,5},{13,9},{1,13},{6,2},{10,6},{... | collective-permute-start | bytes 1179656 | tf_op jit(solution)/shard_map/ppermute | solution.py:268
  55.9 16.8 %collective-permute-start.20 = (bf16[512,384]{1,0:T(8,128)(2,1)S(1)}, bf16[512,384]{1,0:T(8,128)(2,1)}, u32[]{:S(2)}, u32[]{:S(2)}) collective-permute-start(bf16[512,384]{1,0:T(8,128)(2,1)S(1)} %get-tuple-element.76.refs_9_), channel_id=1, source_target_pairs={{12,0},{0,4},{4,8},{8,12},{13,1},{1,5},{5,9},{9,13},{14,2},{2,6},{... | collective-permute-start | bytes 1179656 | tf_op jit(solution)/shard_map/ppermute | solution.py:268
  58.6 7.9 %collective-permute-start.27 = (bf16[256,384]{1,0:T(8,128)(2,1)}, bf16[256,384]{1,0:T(8,128)(2,1)S(1)}, u32[]{:S(2)}, u32[]{:S(2)}) collective-permute-start(bf16[256,384]{1,0:T(8,128)(2,1)} %get-tuple-element.86.refs_17_), channel_id=1, source_target_pairs={{1,0},{2,1},{3,2},{0,3},{5,4},{6,5},{7,6},{4,7},{9,8},{10,9},{11,1... | collective-permute-start | bytes 589832 | tf_op jit(solution)/shard_map/ppermute | solution.py:268
  61.0 9.7 %collective-permute-start.2 = (bf16[4,96,256]{2,1,0:T(8,128)(2,1)S(1)}, bf16[4,96,256]{2,1,0:T(8,128)(2,1)S(1)}, u32[]{:S(2)}, u32[]{:S(2)}) collective-permute-start(bf16[4,96,256]{2,1,0:T(8,128)(2,1)S(1)} %get-tuple-element.58.refs_1_), channel_id=1, source_target_pairs={{1,0},{2,1},{3,2},{0,3},{5,4},{6,5},{7,6},{4,7},{9,8},{10,9},{11,1... | collective-permute-start | bytes 589832 | tf_op jit(solution)/shard_map/ppermute | solution.py:268
  61.0 11.0 %collective-permute-start.3 = (bf16[4,96,256]{2,1,0:T(8,128)(2,1)S(1)}, bf16[4,96,256]{2,1,0:T(8,128)(2,1)S(1)}, u32[]{:S(2)}, u32[]{:S(2)}) collective-permute-start(bf16[4,96,256]{2,1,0:T(8,128)(2,1)S(1)} %get-tuple-element.57.refs_0_), channel_id=1, source_target_pairs={{3,0},{0,1},{1,2},{2,3},{7,4},{4,5},{5,6},{6,7},{11,8},{8,9},{9,10... | collective-permute-start | bytes 589832 | tf_op jit(solution)/shard_map/ppermute | solution.py:268
  67.2 8.8 %collective-permute-start.29 = (bf16[256,384]{1,0:T(8,128)(2,1)}, bf16[256,384]{1,0:T(8,128)(2,1)S(1)}, u32[]{:S(2)}, u32[]{:S(2)}) collective-permute-start(bf16[256,384]{1,0:T(8,128)(2,1)} %collective-permute-done.25.refs_18_), channel_id=1, source_target_pairs={{1,0},{2,1},{3,2},{0,3},{5,4},{6,5},{7,6},{4,7},{9,8},{10,9},{11,1... | collective-permute-start | bytes 589832 | tf_op jit(solution)/shard_map/ppermute | solution.py:268
  72.0 6.9 %collective-permute-start.5 = (bf16[4,96,256]{2,1,0:T(8,128)(2,1)S(1)}, bf16[4,96,256]{2,1,0:T(8,128)(2,1)S(1)}, u32[]{:S(2)}, u32[]{:S(2)}) collective-permute-start(bf16[4,96,256]{2,1,0:T(8,128)(2,1)S(1)} %collective-permute-done.1.refs_5_), channel_id=1, source_target_pairs={{3,0},{0,1},{1,2},{2,3},{7,4},{4,5},{5,6},{6,7},{11,8},{8,9},{9,10... | collective-permute-start | bytes 589832 | tf_op jit(solution)/shard_map/ppermute | solution.py:268
  72.7 13.7 %collective-permute-start.22 = (bf16[512,384]{1,0:T(8,128)(2,1)S(1)}, bf16[512,384]{1,0:T(8,128)(2,1)S(1)}, u32[]{:S(2)}, u32[]{:S(2)}) collective-permute-start(bf16[512,384]{1,0:T(8,128)(2,1)S(1)} %get-tuple-element.75.refs_8_), channel_id=1, source_target_pairs={{12,0},{0,4},{4,8},{8,12},{13,1},{1,5},{5,9},{9,13},{14,2},{2,6},{... | collective-permute-start | bytes 1179656 | tf_op jit(solution)/shard_map/ppermute | solution.py:268
  72.8 17.7 %collective-permute-start.21 = (bf16[512,384]{1,0:T(8,128)(2,1)S(1)}, bf16[512,384]{1,0:T(8,128)(2,1)S(1)}, u32[]{:S(2)}, u32[]{:S(2)}) collective-permute-start(bf16[512,384]{1,0:T(8,128)(2,1)S(1)} %get-tuple-element.76.refs_9_), channel_id=1, source_target_pairs={{4,0},{8,4},{12,8},{0,12},{5,1},{9,5},{13,9},{1,13},{6,2},{10,6},{... | collective-permute-start | bytes 1179656 | tf_op jit(solution)/shard_map/ppermute | solution.py:268
  76.7 21.4 %collective-permute-start.23 = (bf16[512,384]{1,0:T(8,128)(2,1)S(1)}, bf16[512,384]{1,0:T(8,128)(2,1)}, u32[]{:S(2)}, u32[]{:S(2)}) collective-permute-start(bf16[512,384]{1,0:T(8,128)(2,1)S(1)} %collective-permute-done.19.refs_10_), channel_id=1, source_target_pairs={{4,0},{8,4},{12,8},{0,12},{5,1},{9,5},{13,9},{1,13},{6,2},{10,6},{... | collective-permute-start | bytes 1179656 | tf_op jit(solution)/shard_map/ppermute | solution.py:268
  77.4 20.6 %collective-permute-start.24 = (bf16[512,384]{1,0:T(8,128)(2,1)}, bf16[512,384]{1,0:T(8,128)(2,1)}, u32[]{:S(2)}, u32[]{:S(2)}) collective-permute-start(bf16[512,384]{1,0:T(8,128)(2,1)} %collective-permute-done.20.refs_13_), channel_id=1, source_target_pairs={{12,0},{0,4},{4,8},{8,12},{13,1},{1,5},{5,9},{9,13},{14,2},{2,6},{... | collective-permute-start | bytes 1179656 | tf_op jit(solution)/shard_map/ppermute | solution.py:268
  86.4 7.9 %collective-permute-start.10 = (bf16[4,64,256]{2,1,0:T(8,128)(2,1)}, bf16[4,64,256]{2,1,0:T(8,128)(2,1)S(1)}, u32[]{:S(2)}, u32[]{:S(2)}) collective-permute-start(bf16[4,64,256]{2,1,0:T(8,128)(2,1)} %get-tuple-element.63), channel_id=1, source_target_pairs={{12,0},{0,4},{4,8},{8,12},{13,1},{1,5},{5,9},{9,13},{14,2},{2,6},{... | collective-permute-start | bytes 393224 | tf_op jit(solution)/shard_map/ppermute | solution.py:268
  87.2 7.8 %collective-permute-start.11 = (bf16[4,64,256]{2,1,0:T(8,128)(2,1)}, bf16[4,64,256]{2,1,0:T(8,128)(2,1)S(1)}, u32[]{:S(2)}, u32[]{:S(2)}) collective-permute-start(bf16[4,64,256]{2,1,0:T(8,128)(2,1)} %get-tuple-element.64), channel_id=1, source_target_pairs={{4,0},{8,4},{12,8},{0,12},{5,1},{9,5},{13,9},{1,13},{6,2},{10,6},{... | collective-permute-start | bytes 393224 | tf_op jit(solution)/shard_map/ppermute | solution.py:268
  120.0 12.7 %collective-permute-start.31 = (bf16[4,64,256]{2,1,0:T(8,128)(2,1)S(1)}, bf16[4,64,256]{2,1,0:T(8,128)(2,1)S(1)}, u32[]{:S(2)}, u32[]{:S(2)}) collective-permute-start(bf16[4,64,256]{2,1,0:T(8,128)(2,1)S(1)} %get-tuple-element.90), channel_id=1, source_target_pairs={{12,0},{0,4},{4,8},{8,12},{13,1},{1,5},{5,9},{9,13},{14,2},{2,6},{... | collective-permute-start | bytes 393224 | tf_op jit(solution)/shard_map/ppermute | solution.py:268
  120.1 12.7 %collective-permute-start.32 = (bf16[4,64,256]{2,1,0:T(8,128)(2,1)S(1)}, bf16[4,64,256]{2,1,0:T(8,128)(2,1)S(1)}, u32[]{:S(2)}, u32[]{:S(2)}) collective-permute-start(bf16[4,64,256]{2,1,0:T(8,128)(2,1)S(1)} %get-tuple-element.91), channel_id=1, source_target_pairs={{4,0},{8,4},{12,8},{0,12},{5,1},{9,5},{13,9},{1,13},{6,2},{10,6},{... | collective-permute-start | bytes 393224 | tf_op jit(solution)/shard_map/ppermute | solution.py:268
  123.3 9.4 %collective-permute-start.33 = (bf16[4,64,256]{2,1,0:T(8,128)(2,1)S(1)}, bf16[4,64,256]{2,1,0:T(8,128)(2,1)S(1)}, u32[]{:S(2)}, u32[]{:S(2)}) collective-permute-start(bf16[4,64,256]{2,1,0:T(8,128)(2,1)S(1)} %get-tuple-element.92), channel_id=1, source_target_pairs={{8,0},{12,4},{0,8},{4,12},{9,1},{13,5},{1,9},{5,13},{10,2},{14,6},... | collective-permute-start | bytes 393224 | tf_op jit(solution)/shard_map/ppermute | solution.py:268
  (38 other events, 267.4 us)

commit v4 on v3

--- a/solution.py
+++ b/solution.py
@@ -13,8 +13,7 @@
 I32 = jnp.int32
 VMEM = pl.BlockSpec(memory_space=pltpu.VMEM)
 SMEM = pl.BlockSpec(memory_space=pltpu.SMEM)
-ANY = pl.BlockSpec(memory_space=pl.ANY)
-LIMIT = 48 * 1024 * 1024
+MIB = 1024 * 1024
 RING = (0, 1, -1, 2)
 NT = (((1,), (1,)), ((), ()))
 
@@ -76,29 +75,34 @@
 
 
 def select_kernel(which, *refs):
-    blocks, table_ref, at_ref, outs = refs[:4], refs[4], refs[5], refs[6:8]
-    height = outs[0].shape[0] // 2
-    for k, ref in enumerate(blocks):
+    far = jnp.concatenate([refs[3][...], refs[4][...]], axis=0)
+    blocks, table_ref, at_ref, out_ref = refs[:3] + (far,), refs[5], refs[6], refs[7]
+    height = out_ref.shape[0] // 4
+    for k, block in enumerate(blocks):
         if which == 0:
             d = at_ref[1] * 4 + (at_ref[2] + RING[k] + 4) % 4
         else:
             d = ((at_ref[1] + RING[k] + 4) % 4) * 4 + at_ref[2]
-        out_ref, base = outs[k // 2], (k % 2) * height
+        base = k * height
         for m in range(3):
             at = d * 12 + which * 6 + m * 2
             first = jnp.where(table_ref[0, at] > 0, 1.0, 0.0)
             second = jnp.where(table_ref[0, at + 1] > 0, 1.0, 0.0)
-            one = ref[0:128, m * 256 : m * 256 + 128].astype(F32)
-            two = ref[0:128, m * 256 + 128 : m * 256 + 256].astype(F32)
+            one = block[0:128, m * 256 : m * 256 + 128].astype(F32)
+            two = block[0:128, m * 256 + 128 : m * 256 + 256].astype(F32)
             out_ref[base : base + 128, m * 128 : m * 128 + 128] = (first * one + second * two).astype(BF)
         if which == 0:
-            out_ref[base + 128 : base + 192, :] = ref[128:192, 0:384]
-            out_ref[base + 192 : base + 256, :] = ref[128:192, 384:768]
+            out_ref[base + 128 : base + 192, :] = block[128:192, 0:384]
+            out_ref[base + 192 : base + 256, :] = block[128:192, 384:768]
+
+
+def features_at(refs, k, f):
+    return refs[k][f] if k < 3 else refs[3 + f // 4][f % 4]
 
 
 def project_kernel(*refs):
-    x_refs, w_refs, small_ref, at_ref = refs[:8], refs[8:12], refs[12], refs[13]
-    v_refs, w_ref, t_ref = refs[14:18], refs[18], refs[19]
+    x_refs, w_refs, small_ref, at_ref = refs[:5], refs[5:9], refs[9], refs[10]
+    v_refs, w_ref, t_ref = refs[11:15], refs[15], refs[16]
     for k, shift in enumerate(RING):
         for flip in range(2):
             f = ((at_ref[3] + shift + 4) % 4) * 2 + (at_ref[4] + flip) % 2
@@ -108,78 +112,78 @@
         z = (at_ref[2] + shift + 4) % 4
         degree = small_ref[at_ref[1] * 4 + z].astype(F32)
         inv = lax.rsqrt(jnp.concatenate([degree[0:1], degree[1:2]], axis=1))
-        low, high = x_refs[2 * k][...].reshape(384, 256), x_refs[2 * k + 1][...].reshape(384, 256)
-        t_ref[k] = (inv * (dot(w[:, 0:384], low) + dot(w[:, 384:768], high))).astype(BF)
+        whole = jnp.concatenate([features_at(x_refs, k, f) for f in range(8)], axis=0)
+        t_ref[k] = (inv * dot(w, whole)).astype(BF)
         for v_ref, to in zip(v_refs, RING):
             at = pl.multiple_of(((at_ref[1] + to + 4) % 4) * 64, 64)
             v_ref[z] = t_ref[k, pl.ds(at, 64), :]
 
 
-def places(at_ref):
-    found = []
-    for i, dx in enumerate(RING):
-        for j, dz in enumerate(RING):
-            found.append((i, j, ((at_ref[1] + dx + 4) % 4) * 4 + (at_ref[2] + dz + 4) % 4))
-    return found
-
-
 def mix_kernel(*refs):
     v_refs, small_ref, tab_ref, sw_ref, at_ref = refs[:4], refs[4], refs[5], refs[6], refs[7]
-    mask_refs = refs[8:24]
-    hid_ref, second_ref, g_refs = refs[24], refs[25], refs[26:30]
-    ma_ref, mb_ref, src_ref, acc_ref, v2_ref, acc2_ref, inv_ref, sems = refs[30:]
-    copies = []
-    for i, ref in enumerate(mask_refs):
-        to = ma_ref.at[i] if i < 8 else mb_ref.at[i - 8]
-        copies.append(pltpu.make_async_copy(ref, to, sems.at[i]))
-    for copy in copies:
-        copy.start()
+    a_refs, b_refs = refs[8:13], refs[13:18]
+    hid_ref, second_ref, g_refs = refs[18], refs[19], refs[20:24]
+    src_ref, acc_ref, v2_ref, acc2_ref, inv_ref = refs[24:]
+    x, z = at_ref[1], at_ref[2]
+
+    def along(step):
+        for buffer, first, count in ((0, 0, 4), (1, 0, 4), (2, 0, 4), (3, 0, 2), (4, 2, 2)):
+            def turn(k, carry, buffer=buffer, first=first):
+                q = k + first
+                step(a_refs[buffer], b_refs[buffer], k, min(buffer, 3), q ^ (q >> 1))
+                return carry
+            lax.fori_loop(0, count, turn, 0)
+
     for d in range(16):
         degree = small_ref[d].astype(F32)
         for h in range(2):
             inv_ref[2 * d + h] = lax.rsqrt(degree[h : h + 1])
-    for copy in copies:
-        copy.wait()
-    for i, j, d in places(at_ref):
-        at, base = i * 2 + j // 2, (j % 2) * 256 + 128
-        v_ref = v_refs[(0, 2, 1, 3)[i]]
-        z = (at_ref[2] + RING[j] + 4) % 4
+
+    def prepare(a_ref, b_ref, k, n, shift):
+        to = (z + shift) & 3
+        d = ((x + RING[n] + 4) & 3) * 4 + to
+        v_ref = v_refs[(0, 2, 1, 3)[n]]
+        low = a_ref[pl.ds(pl.multiple_of(k * 256 + 128, 64), 64), :]
+        high = a_ref[pl.ds(pl.multiple_of(k * 256 + 192, 64), 64), :]
         for h in range(2):
             t = d * 2 + h
             inv = inv_ref[t]
-            v = v_ref[z, :, h * 128 : h * 128 + 128]
-            src_ref[t, 0:64] = v
-            acc_ref[t, 0:64] = v.astype(F32)
-            second = (base, 256) if h == 0 else (base + 64, 0)
-            for c, rows, (row, lane) in (
-                (0, 64, (base, h * 128)), (1, 64, second), (2, 32, (base + 64, 128 + h * 128))
-            ):
-                up = (inv * ma_ref[at, row : row + rows, lane : lane + 128].astype(F32)).astype(BF)
-                src_ref[t, 64 + 64 * c : 64 + 64 * c + rows] = up
-                acc_ref[t, 64 + 64 * c : 64 + 64 * c + rows] = up.astype(F32)
+            middle = low[:, 256:384] if h == 0 else high[:, 0:128]
+            parts = [low[:, h * 128 : h * 128 + 128], middle, high[0:32, 128 + h * 128 : 256 + h * 128]]
+            up = (inv * jnp.concatenate(parts, axis=0).astype(F32)).astype(BF)
+            own = jnp.concatenate([v_ref[to, :, h * 128 : h * 128 + 128], up], axis=0)
+            src_ref[t] = own
+            acc_ref[t] = own.astype(F32)
+
+    along(prepare)
 
     def spread(source, total_ref):
-        for i, j, d in places(at_ref):
-            for h in range(2):
-                t = d * 2 + h
-                if h == 0:
-                    weights = ma_ref[i * 2 + j // 2, (j % 2) * 256 : (j % 2) * 256 + 128, :]
-                else:
-                    weights = mb_ref[j * 2 + i // 2, (i % 2) * 128 : (i % 2) * 128 + 128, :]
-                named = []
-                for m in range(3):
-                    c = tab_ref[0, 6 * t + 2 * m] + tab_ref[0, 6 * t + 2 * m + 1]
-                    named.append(jnp.maximum(c - 1, 0))
-                own = source[t]
-                others = jnp.concatenate([source[c] for c in named], axis=1)
-                back = dot(own, weights)
-                total_ref[t] = total_ref[t] + dot(others, weights, NT)
+        def send(t, weights):
+            named = []
+            for m in range(3):
+                c = tab_ref[0, 6 * t + 2 * m] + tab_ref[0, 6 * t + 2 * m + 1]
+                named.append(jnp.maximum(c - 1, 0))
+            own = source[t]
+            others = jnp.concatenate([source[c] for c in named], axis=1)
+            return named, dot(own, weights), dot(others, weights, NT)
+
+        def both(a_ref, b_ref, k, n, shift):
+            t_a = (((x + RING[n] + 4) & 3) * 4 + ((z + shift) & 3)) * 2
+            t_b = (((x + shift) & 3) * 4 + ((z + RING[n] + 4) & 3)) * 2 + 1
+            sent = [
+                (t_a, *send(t_a, a_ref[pl.ds(pl.multiple_of(k * 256, 128), 128), :])),
+                (t_b, *send(t_b, b_ref[pl.ds(pl.multiple_of(k * 128, 128), 128), :])),
+            ]
+            for t, named, back, forth in sent:
+                total_ref[t] = total_ref[t] + forth
                 for m in range(3):
                     total_ref[named[m]] = total_ref[named[m]] + back[:, m * 128 : m * 128 + 128]
 
+        along(both)
+
     spread(src_ref, acc_ref)
-    second = jnp.zeros((160, 64), F32)
-    for d in range(16):
+
+    def turn(d, second):
         ones, pulls = [], []
         for h in range(2):
             t = d * 2 + h
@@ -195,20 +199,22 @@
             back = (inv * inv * dot(sw_ref[...], pull) * slope).astype(BF)
             v2_ref[t] = back
             acc2_ref[t] = back.astype(F32)
-        second = second + dot(jnp.concatenate(pulls, axis=1), jnp.concatenate(ones, axis=1), NT)
+        return second + dot(jnp.concatenate(pulls, axis=1), jnp.concatenate(ones, axis=1), NT)
+
+    second = lax.fori_loop(0, 16, turn, jnp.zeros((160, 64), F32))
     second_ref[...] = jnp.concatenate([second[:80], second[80:]], axis=1).astype(BF)
     spread(v2_ref, acc2_ref)
     for shift, g_ref in zip(RING, g_refs):
-        for z in range(4):
-            d = ((at_ref[1] + shift + 4) % 4) * 4 + z
+        for k in range(4):
+            d = ((x + shift + 4) & 3) * 4 + k
             for h in range(2):
-                g_ref[z, :, h * 128 : h * 128 + 128] = (
+                g_ref[k, :, h * 128 : h * 128 + 128] = (
                     inv_ref[d * 2 + h] * acc2_ref[d * 2 + h]
                 ).astype(BF)
 
 
 def weigh_kernel(*refs):
-    x_refs, g_refs, at_ref, out_ref = refs[:8], refs[8:12], refs[12], refs[13]
+    x_refs, g_refs, at_ref, out_ref = refs[:5], refs[5:9], refs[9], refs[10]
     rights = []
     for shift in RING:
         z = (at_ref[2] + shift + 4) % 4
@@ -216,7 +222,7 @@
     for f in range(8):
         acc = jnp.zeros((96, 256), F32)
         for k, right in enumerate(rights):
-            acc = acc + dot(x_refs[2 * k + f // 4][f % 4], right, NT)
+            acc = acc + dot(features_at(x_refs, k, f), right, NT)
         for p in range(2):
             g = acc[:, p * 128 : p * 128 + 128]
             for part, shift in zip(halves(g[:48], g[48:]), RING[2 * p : 2 * p + 2]):
@@ -252,14 +258,14 @@
             hidden_ref[h * 128 : h * 128 + 128, cols] = both.astype(F32).T.astype(BF)
 
 
-def call(kernel, shape, specs, scratch=(), flops=0, moved=0):
+def call(kernel, shape, specs, scratch=(), flops=0, moved=0, limit=8):
     return pl.pallas_call(
         kernel,
         out_shape=shape,
         in_specs=specs,
         out_specs=jax.tree.map(lambda _: VMEM, shape),
         scratch_shapes=list(scratch),
-        compiler_params=pltpu.CompilerParams(vmem_limit_bytes=LIMIT),
+        compiler_params=pltpu.CompilerParams(vmem_limit_bytes=limit * MIB),
         cost_estimate=pl.CostEstimate(flops=flops, bytes_accessed=moved, transcendentals=0),
     )
 
@@ -272,12 +278,10 @@
     return [value] + [fetch(value, axis, shift) for shift in RING[1:]]
 
 
-def rounds(low, high, axis):
-    after = [fetch(low, axis, 1), fetch(high, axis, 1)]
-    before = [fetch(low, axis, -1), fetch(high, axis, -1)]
-    low2, high2, *rest = lax.optimization_barrier((after[0], before[1], low, high))
-    far = [fetch(low2, axis, 1), fetch(high2, axis, -1)]
-    return [*rest, low2, after[1], before[0], high2, *far]
+def rounds(value, axis):
+    half = value.shape[0] // 2
+    after, before = fetch(value, axis, 1), fetch(value, axis, -1)
+    return [value, after, before, fetch(after[:half], axis, 1), fetch(before[half:], axis, -1)]
 
 
 def body(features, first_weight, second_weight, degree, neighbour_block, neighbour_mask, upstream):
@@ -285,41 +289,42 @@
     shape = jax.ShapeDtypeStruct
     x, z = lax.axis_index("x"), lax.axis_index("z")
     at = jnp.stack([x * 4 + z, x, z, lax.axis_index("y"), lax.axis_index("c")])
-    links = lax.dynamic_update_slice(
-        jnp.zeros((256,), I32), neighbour_block.reshape(12) + 2, ((x * 4 + z) * 12,)
-    )
-    small = jnp.concatenate([degree.reshape(2, 128), links.reshape(2, 128)], axis=0)
-    small = lax.all_to_all(jnp.broadcast_to(small, (16, 4, 128)), dom, 0, 0, tiled=True)
+    x_own = lax.all_to_all(
+        features.reshape(96, 8, 256).transpose(1, 0, 2), feat, 0, 0, tiled=True
+    )
     mask_a, mask_b = call(
         mask_kernel, (shape((192, 768), BF), shape((128, 768), BF)), [VMEM] * 2, moved=1_200_000
     )(neighbour_mask[0], upstream[0].T)
-    features, small, mask_a, mask_b = lax.optimization_barrier((features, small, mask_a, mask_b))
-    x_own = lax.all_to_all(
-        features.reshape(96, 8, 256).transpose(1, 0, 2), feat, 0, 0, tiled=True
-    )
-    blocks_a, blocks_b = ring(mask_a, "z"), ring(mask_b, "x")
+    links = lax.dynamic_update_slice(
+        jnp.zeros((256,), I32), neighbour_block.reshape(12) + 2, ((x * 4 + z) * 12,)
+    )
+    small = jnp.concatenate([degree.reshape(2, 128), links.reshape(2, 128)], axis=0)
+    small = jnp.broadcast_to(small, (16, 4, 128))
+    small, x_own = lax.optimization_barrier((small, x_own))
+    small = lax.all_to_all(small, dom, 0, 0, tiled=True)
+    blocks_a, blocks_b = rounds(mask_a, "z"), rounds(mask_b, "x")
+    x_wide = rounds(x_own, "z")
     table = call(orient_kernel, shape((1, 256), I32), [VMEM], flops=300_000_000)(small)
 
     weight = lax.dynamic_slice(first_weight, (0, z * 256), (96, 256))
     weight = jnp.stack([weight, lax.ppermute(weight, "c", [(0, 1), (1, 0)])])
     weights = ring(weight, "y")
-    table, *blocks = lax.optimization_barrier((table, *blocks_a, *blocks_b))
-    pair_a, pair_b = shape((512, 384), BF), shape((256, 384), BF)
-    sent_a = call(functools.partial(select_kernel, 0), (pair_a, pair_a), [VMEM] * 4 + [SMEM] * 2, moved=2_000_000)(
-        *blocks[:4], table, at
-    )
-    sent_b = call(functools.partial(select_kernel, 1), (pair_b, pair_b), [VMEM] * 4 + [SMEM] * 2, moved=2_000_000)(
-        *blocks[4:], table, at
-    )
-    masks = rounds(*sent_a, "x") + rounds(*sent_b, "z")
-    x_wide = rounds(x_own[:4], x_own[4:], "z")
+    sent_a = call(
+        functools.partial(select_kernel, 0), shape((1024, 384), BF), [VMEM] * 5 + [SMEM] * 2,
+        moved=2_000_000,
+    )(*blocks_a, table, at)
+    sent_b = call(
+        functools.partial(select_kernel, 1), shape((512, 384), BF), [VMEM] * 5 + [SMEM] * 2,
+        moved=2_000_000,
+    )(*blocks_b, table, at)
+    masks = rounds(sent_a, "x") + rounds(sent_b, "z")
     own_second = lax.dynamic_slice(second_weight, ((z * 4 + x) * 64, 0), (64, 153))
     own_second = jnp.pad(own_second, ((0, 0), (0, 7)))
     part = shape((4, 64, 256), BF)
     v = call(
         project_kernel,
         (part,) * 4,
-        [VMEM] * 13 + [SMEM],
+        [VMEM] * 10 + [SMEM],
         [pltpu.VMEM((8, 96, 256), BF), pltpu.VMEM((4, 256, 256), BF)],
         flops=400_000_000,
         moved=3_000_000,
@@ -328,19 +333,17 @@
     hid, second, *g = call(
         mix_kernel,
         (shape((16, 64, 256), BF), shape((80, 128), BF)) + (part,) * 4,
-        [VMEM] * 5 + [SMEM, VMEM, SMEM] + [ANY] * 16,
+        [VMEM] * 5 + [SMEM, VMEM, SMEM] + [VMEM] * 10,
         [
-            pltpu.VMEM((8, 512, 384), BF),
-            pltpu.VMEM((8, 256, 384), BF),
             pltpu.VMEM((32, 224, 128), BF),
             pltpu.VMEM((32, 224, 128), F32),
             pltpu.VMEM((32, 64, 128), BF),
             pltpu.VMEM((32, 64, 128), F32),
             pltpu.VMEM((32, 1, 128), F32),
-            pltpu.SemaphoreType.DMA((16,)),
         ],
         flops=1_600_000_000,
         moved=10_000_000,
+        limit=24,
     )(*v, small, table, own_second, at, *masks)
     g = [g[0]] + [fetch(value, "x", -shift) for value, shift in zip(g[1:], RING[1:])]
     other = lax.ppermute(second, "c", [(0, 1), (1, 0)])
@@ -349,7 +352,7 @@
     part = call(
         weigh_kernel,
         shape((8, 4, 48, 128), BF),
-        [VMEM] * 12 + [SMEM],
+        [VMEM] * 9 + [SMEM],
         flops=400_000_000,
         moved=3_000_000,
     )(*x_wide, *g, at)

time: 175 us -> 184 us (1.051)
  waiting for transfers between devices: 34 us -> 52.7 us
  starting transfers between devices: 59.1 us -> 51.4 us
  local copies, waits for them, and re-layouts: 19.8 us -> 15 us
  Pallas kernels: 21.1 us -> 24.5 us
    ppermute x36 -> x32, waiting for transfers between devices: 27.6 us -> 41.8 us  [fetch(): return lax.ppermute(value, axis, [((i + shift) % 4, i) for i in range(4)])]
    unnamed x62 -> x40, local copies, waits for them, and re-layouts: 17.9 us -> 10.7 us
    ppermute x36 -> x32, starting transfers between devices: 45.9 us -> 41 us  [fetch(): return lax.ppermute(value, axis, [((i + shift) % 4, i) for i in range(4)])]
    pallas_call x1, Pallas kernels: 11.4 us -> 15.5 us  [body(): call(mix_kernel, (shape((16, 64, 256), BF), shape((80, 128), BF)) + (part...]
    all_to_all x1, waiting for transfers between devices: 0.01 us -> 3.3 us  [body(): lax.all_to_all(features.reshape(96, 8, 256).transpose(1, 0, 2), feat, 0,...]
    all_to_all x1, starting transfers between devices: 7.96 us -> 5.78 us  [body(): small = lax.all_to_all(small, dom, 0, 0, tiled=True)]
  transfers between devices with their start and end apart: 40 -> 36, of which waited for: 13 -> 16; matrix products, arithmetic and copies ran while one was open for 1% -> 3% of each run, Pallas kernels for 3% -> 2%
where the time goes in v4:
time: 184 us; the launch traced here: 183 us
  waiting for transfers between devices  52.7 us (29%)
  starting transfers between devices  51.4 us (28%)
  blocking collectives  38.3 us (21%)
  Pallas kernels  24.5 us (13%)
  local copies, waits for them, and re-layouts  15 us (8%)
    ppermute x32, waiting for transfers between devices, fetch(): return lax.ppermute(value, axis, [((i + shift) % 4, i) for i in range(4)])  41.8 us
    ppermute x32, starting transfers between devices, fetch(): return lax.ppermute(value, axis, [((i + shift) % 4, i) for i in range(4)])  41 us
    all_to_all x1, blocking collectives, body(): done = lax.all_to_all(done, dom, 0, 0, tiled=True)  21.2 us
    all_to_all x1, blocking collectives, body(): lax.all_to_all(part.reshape(32, 48, 128), ('y', 'c', 'x'), 0, 0, tiled=True)  17.1 us
    pallas_call x1, Pallas kernels, body(): call(mix_kernel, (shape((16, 64, 256), BF), shape((80, 128), BF)) + (part...  15.5 us
    unnamed x40, local copies, waits for them, and re-layouts  10.7 us
    all_to_all x1, waiting for transfers between devices, body(): small = lax.all_to_all(small, dom, 0, 0, tiled=True)  7.53 us
    all_to_all x1, starting transfers between devices, body(): small = lax.all_to_all(small, dom, 0, 0, tiled=True)  5.78 us
  transfers between devices with their start and end apart: 36, of which 16 were waited for; matrix products, arithmetic and copies ran while one was open for 3% of the time, Pallas kernels for 2%

profile of v4, /device:TPU:0, one launch (start us, length us, event | category | flops | bytes accessed | tf_op | source)
XLA Modules:
  0.0 183.0 jit_solution(7897822030845379917)
XLA Ops:
  2.8 2.1 %collective-permute-start.12 = (bf16[192,768]{1,0:T(8,128)(2,1)S(1)}, bf16[192,768]{1,0:T(8,128)(2,1)S(1)}, u32[]{:S(2)}, u32[]{:S(2)}) collective-permute-start(bf16[192,768]{1,0:T(8,128)(2,1)S(1)} %get-tuple-element.33.refs_0_), channel_id=1, source_target_pairs={{3,0},{0,1},{1,2},{2,3},{7,4},{4,5},{5,6},{6,7},{11,8},{8,9},{9,10... | collective-permute-start | bytes 884744 | tf_op jit(solution)/shard_map/ppermute | solution.py:274
  4.8 2.2 %collective-permute-start.11 = (bf16[192,768]{1,0:T(8,128)(2,1)S(1)}, bf16[192,768]{1,0:T(8,128)(2,1)S(1)}, u32[]{:S(2)}, u32[]{:S(2)}) collective-permute-start(bf16[192,768]{1,0:T(8,128)(2,1)S(1)} %get-tuple-element.33.refs_0_), channel_id=1, source_target_pairs={{1,0},{2,1},{3,2},{0,3},{5,4},{6,5},{7,6},{4,7},{9,8},{10,9},{11,1... | collective-permute-start | bytes 884744 | tf_op jit(solution)/shard_map/ppermute | solution.py:274
  8.0 4.5 %all-to-all-start = ((bf16[8,96,256]{2,1,0:T(8,128)(2,1)}), bf16[8,96,256]{2,1,0:T(8,128)(2,1)S(1)}, u32[]{:S(2)}, u32[]{:S(2)}) async-start(bf16[8,96,256]{2,1,0:T(8,128)(2,1)} %bitcast.23), calls=%async_computation | async-start | bytes 786432 | tf_op jit(solution)/shard_map/all_to_all | solution.py:292
  14.1 3.3 %collective-permute-start.13 = (bf16[96,768]{1,0:T(8,128)(2,1)S(1)}, bf16[96,768]{1,0:T(8,128)(2,1)S(1)}, u32[]{:S(2)}, u32[]{:S(2)}) collective-permute-start(bf16[96,768]{1,0:T(8,128)(2,1)S(1)} %slice.42), channel_id=1, source_target_pairs={{1,0},{2,1},{3,2},{0,3},{5,4},{6,5},{7,6},{4,7},{9,8},{10,9},{11,1... | collective-permute-start | bytes 442376 | tf_op jit(solution)/shard_map/ppermute | solution.py:274
  18.1 3.3 %all-to-all-done.refs_0_ = bf16[8,96,256]{2,1,0:T(8,128)(2,1)S(1)} async-done(((bf16[8,96,256]{2,1,0:T(8,128)(2,1)}), bf16[8,96,256]{2,1,0:T(8,128)(2,1)S(1)}, u32[]{:S(2)}, u32[]{:S(2)}) %all-to-all-start) | async-done | bytes 393248 | tf_op jit(solution)/shard_map/all_to_all | solution.py:292
  22.0 5.8 %all-to-all-start.1 = ((s32[16,4,128]{2,1,0:T(4,128)}), s32[16,4,128]{2,1,0:T(4,128)S(1)}, u32[]{:S(2)}, u32[]{:S(2)}) async-start(s32[16,4,128]{2,1,0:T(4,128)} %broadcast_in_dim.10), calls=%async_computation.1 | async-start | bytes 65536 | tf_op jit(solution)/shard_map/all_to_all | solution.py:304
  27.9 7.5 %all-to-all-done.1.refs_9_.small_ref.refs_4_ = s32[16,4,128]{2,1,0:T(4,128)S(1)} async-done(((s32[16,4,128]{2,1,0:T(4,128)}), s32[16,4,128]{2,1,0:T(4,128)S(1)}, u32[]{:S(2)}, u32[]{:S(2)}) %all-to-all-start.1) | async-done | bytes 32800 | tf_op jit(solution)/shard_map/all_to_all | solution.py:304
  35.4 1.8 shard_map.95.refs_5_
  38.6 2.7 %collective-permute-start.15 = (bf16[1024,384]{1,0:T(8,128)(2,1)S(1)}, bf16[1024,384]{1,0:T(8,128)(2,1)S(1)}, u32[]{:S(2)}, u32[]{:S(2)}) collective-permute-start(bf16[1024,384]{1,0:T(8,128)(2,1)S(1)} %shard_map.97.refs_8_), channel_id=1, source_target_pairs={{4,0},{8,4},{12,8},{0,12},{5,1},{9,5},{13,9},{1,13},{6,2},{10,6},{... | collective-permute-start | bytes 2359304 | tf_op jit(solution)/shard_map/ppermute | solution.py:274
  41.4 3.2 %collective-permute-start.19 = (bf16[128,768]{1,0:T(8,128)(2,1)S(1)}, bf16[128,768]{1,0:T(8,128)(2,1)S(1)}, u32[]{:S(2)}, u32[]{:S(2)}) collective-permute-start(bf16[128,768]{1,0:T(8,128)(2,1)S(1)} %get-tuple-element.34.refs_0_), channel_id=1, source_target_pairs={{4,0},{8,4},{12,8},{0,12},{5,1},{9,5},{13,9},{1,13},{6,2},{10,6},{... | collective-permute-start | bytes 589832 | tf_op jit(solution)/shard_map/ppermute | solution.py:274
  45.3 15.8 %collective-permute-done.20.refs_2_ = bf16[128,768]{1,0:T(8,128)(2,1)S(1)} collective-permute-done((bf16[128,768]{1,0:T(8,128)(2,1)S(1)}, bf16[128,768]{1,0:T(8,128)(2,1)S(1)}, u32[]{:S(2)}, u32[]{:S(2)}) %collective-permute-start.20) | collective-permute-done | bytes 196640 | tf_op jit(solution)/shard_map/ppermute | solution.py:274
  61.9 5.4 %collective-permute-done.7.refs_8_ = bf16[2,96,256]{2,1,0:T(8,128)(2,1)S(1)} collective-permute-done((bf16[2,96,256]{2,1,0:T(8,128)(2,1)S(1)}, bf16[2,96,256]{2,1,0:T(8,128)(2,1)S(1)}, u32[]{:S(2)}, u32[]{:S(2)}) %collective-permute-start.7) | collective-permute-done | bytes 98336 | tf_op jit(solution)/shard_map/ppermute | solution.py:274
  67.7 1.4 collective-permute-start.6
  69.0 2.8 %collective-permute-done.21.refs_3_ = bf16[64,768]{1,0:T(8,128)(2,1)S(1)} collective-permute-done((bf16[64,768]{1,0:T(8,128)(2,1)S(1)}, bf16[64,768]{1,0:T(8,128)(2,1)S(1)}, u32[]{:S(2)}, u32[]{:S(2)}) %collective-permute-start.21) | collective-permute-done | bytes 98336 | tf_op jit(solution)/shard_map/ppermute | solution.py:274
  74.7 2.4 %collective-permute-start.23 = (bf16[512,384]{1,0:T(8,128)(2,1)S(1)}, bf16[512,384]{1,0:T(8,128)(2,1)S(1)}, u32[]{:S(2)}, u32[]{:S(2)}) collective-permute-start(bf16[512,384]{1,0:T(8,128)(2,1)S(1)} %shard_map.98.refs_13_), channel_id=1, source_target_pairs={{1,0},{2,1},{3,2},{0,3},{5,4},{6,5},{7,6},{4,7},{9,8},{10,9},{11,1... | collective-permute-start | bytes 1179656 | tf_op jit(solution)/shard_map/ppermute | solution.py:274
  77.2 1.2 collective-permute-start.5
  80.1 1.9 %collective-permute-done.5.refs_6_ = bf16[2,96,256]{2,1,0:T(8,128)(2,1)S(1)} collective-permute-done((bf16[2,96,256]{2,1,0:T(8,128)(2,1)S(1)}, bf16[2,96,256]{2,1,0:T(8,128)(2,1)S(1)}, u32[]{:S(2)}, u32[]{:S(2)}) %collective-permute-start.5) | collective-permute-done | bytes 98336 | tf_op jit(solution)/shard_map/ppermute | solution.py:274
  83.9 1.3 collective-permute-start.17
  85.2 3.2 %collective-permute-start.2 = (bf16[4,96,256]{2,1,0:T(8,128)(2,1)S(1)}, bf16[4,96,256]{2,1,0:T(8,128)(2,1)S(1)}, u32[]{:S(2)}, u32[]{:S(2)}) collective-permute-start(bf16[4,96,256]{2,1,0:T(8,128)(2,1)S(1)} %slice.40), channel_id=1, source_target_pairs={{1,0},{2,1},{3,2},{0,3},{5,4},{6,5},{7,6},{4,7},{9,8},{10,9},{11,1... | collective-permute-start | bytes 589832 | tf_op jit(solution)/shard_map/ppermute | solution.py:274
  88.4 2.3 %collective-permute-done.23.refs_14_ = bf16[512,384]{1,0:T(8,128)(2,1)S(1)} collective-permute-done((bf16[512,384]{1,0:T(8,128)(2,1)S(1)}, bf16[512,384]{1,0:T(8,128)(2,1)S(1)}, u32[]{:S(2)}, u32[]{:S(2)}) %collective-permute-start.23) | collective-permute-done | bytes 393248 | tf_op jit(solution)/shard_map/ppermute | solution.py:274
  91.4 2.9 %collective-permute-start.25 = (bf16[256,384]{1,0:T(8,128)(2,1)S(1)}, bf16[256,384]{1,0:T(8,128)(2,1)S(1)}, u32[]{:S(2)}, u32[]{:S(2)}) collective-permute-start(bf16[256,384]{1,0:T(8,128)(2,1)S(1)} %slice.48), channel_id=1, source_target_pairs={{1,0},{2,1},{3,2},{0,3},{5,4},{6,5},{7,6},{4,7},{9,8},{10,9},{11,1... | collective-permute-start | bytes 589832 | tf_op jit(solution)/shard_map/ppermute | solution.py:274
  94.3 2.1 %shard_map.94 = (bf16[4,64,256]{2,1,0:T(8,128)(2,1)S(1)}, bf16[4,64,256]{2,1,0:T(8,128)(2,1)}, bf16[4,64,256]{2,1,0:T(8,128)(2,1)}, bf16[4,64,256]{2,1,0:T(8,128)(2,1)}) custom-call(bf16[8,96,256]{2,1,0:T(8,128)(2,1)S(1)} %all-to-all-done.refs_0_, bf16[8,96,256]{2,1,0:T(8,128)(2,1)S(1)} %collective-permute-done.refs_1_, ...), custom_call_target="tpu_custom_call" | custom-call | flops 400000000 | bytes 3000000 | tf_op jit(solution)/shard_map/pallas_call | solution.py:324
  97.7 2.6 %collective-permute-start.9 = (bf16[4,64,256]{2,1,0:T(8,128)(2,1)}, bf16[4,64,256]{2,1,0:T(8,128)(2,1)}, u32[]{:S(2)}, u32[]{:S(2)}) collective-permute-start(bf16[4,64,256]{2,1,0:T(8,128)(2,1)} %get-tuple-element.31), channel_id=1, source_target_pairs={{4,0},{8,4},{12,8},{0,12},{5,1},{9,5},{13,9},{1,13},{6,2},{10,6},{... | collective-permute-start | bytes 393224 | tf_op jit(solution)/shard_map/ppermute | solution.py:274
  104.5 3.2 %collective-permute-done.10.refs_3_ = bf16[4,64,256]{2,1,0:T(8,128)(2,1)} collective-permute-done((bf16[4,64,256]{2,1,0:T(8,128)(2,1)}, bf16[4,64,256]{2,1,0:T(8,128)(2,1)}, u32[]{:S(2)}, u32[]{:S(2)}) %collective-permute-start.10) | collective-permute-done | bytes 131104 | tf_op jit(solution)/shard_map/ppermute | solution.py:274
  112.9 15.5 %shard_map.99 = (bf16[16,64,256]{2,1,0:T(8,128)(2,1)S(1)}, bf16[80,128]{1,0:T(8,128)(2,1)S(1)}, bf16[4,64,256]{2,1,0:T(8,128)(2,1)S(1)}, bf16[4,64,256]{2,1,0:T(...) custom-call(bf16[4,64,256]{2,1,0:T(8,128)(2,1)S(1)} %copy-done.14, ...), custom_call_target="tpu_custom_call" | custom-call | flops 1600000000 | bytes 10000000 | tf_op jit(solution)/shard_map/pallas_call | solution.py:333
  128.6 3.2 %collective-permute-start.28 = (bf16[4,64,256]{2,1,0:T(8,128)(2,1)S(1)}, bf16[4,64,256]{2,1,0:T(8,128)(2,1)S(1)}, u32[]{:S(2)}, u32[]{:S(2)}) collective-permute-start(bf16[4,64,256]{2,1,0:T(8,128)(2,1)S(1)} %get-tuple-element.37), channel_id=1, source_target_pairs={{4,0},{8,4},{12,8},{0,12},{5,1},{9,5},{13,9},{1,13},{6,2},{10,6},{... | collective-permute-start | bytes 393224 | tf_op jit(solution)/shard_map/ppermute | solution.py:274
  133.9 3.3 %collective-permute-done.33.s3_ref = bf16[80,128]{1,0:T(8,128)(2,1)S(1)} collective-permute-done((bf16[80,128]{1,0:T(8,128)(2,1)S(1)}, bf16[80,128]{1,0:T(8,128)(2,1)S(1)}, u32[]{:S(2)}, u32[]{:S(2)}) %collective-permute-start.33) | collective-permute-done | bytes 20512 | tf_op jit(solution)/shard_map/ppermute | solution.py:274
  138.3 2.7 %collective-permute-done.31.s1_ref = bf16[80,128]{1,0:T(8,128)(2,1)S(1)} collective-permute-done((bf16[80,128]{1,0:T(8,128)(2,1)S(1)}, bf16[80,128]{1,0:T(8,128)(2,1)S(1)}, u32[]{:S(2)}, u32[]{:S(2)}) %collective-permute-start.31) | collective-permute-done | bytes 20512 | tf_op jit(solution)/shard_map/ppermute | solution.py:274
  141.0 2.0 %shard_map.100 = bf16[8,4,48,128]{3,2,1,0:T(8,128)(2,1)S(1)} custom-call(bf16[8,96,256]{2,1,0:T(8,128)(2,1)S(1)} %all-to-all-done.refs_0_, bf16[8,96,256]{2,1,0:T(8,128)(2,1)S(1)} %collective-permute-done.refs_1_, bf16[8,96,256]{2,1,0:T(8,128)(2,1)S(1)} %collective-permute-done.1.refs_2_, bf16[4,96,256]{2,1,0:T(8,128)(2,1)S(1)} %collective-permute-done.2.refs_3_, ...), custom_call_target="tpu_custom_call" | custom-call | flops 400000000 | bytes 3000000 | tf_op jit(solution)/shard_map/pallas_call | solution.py:352
  143.1 17.1 %all_to_all.20.part_ref = bf16[32,48,128]{2,1,0:T(8,128)(2,1)S(1)} all-to-all(bf16[32,48,128]{2,1,0:T(8,128)(2,1)S(1)} %bitcast.24), channel_id=1, replica_groups=mesh['y'=4,'c'=2,'x'=4,'z'=4] {'y','c','x'}, dimensions={0} | all-to-all | bytes 786432 | tf_op jit(solution)/shard_map/all_to_all | solution.py:359
  160.3 21.2 %all_to_all.21.in_ref = bf16[16,256,128]{2,1,0:T(8,128)(2,1)S(1)} all-to-all(bf16[16,256,128]{2,1,0:T(8,128)(2,1)S(1)} %shard_map.101), channel_id=1, replica_groups=mesh['y'=4,'c'=2,'x'=4,'z'=4] {'x','z'}, dimensions={0} | all-to-all | bytes 2097152 | tf_op jit(solution)/shard_map/all_to_all | solution.py:361
  181.5 1.4 shard_map.102
  (115 shorter events, 30.6 us)
Async XLA Ops:
  2.8 11.2 %collective-permute-start.12 = (bf16[192,768]{1,0:T(8,128)(2,1)S(1)}, bf16[192,768]{1,0:T(8,128)(2,1)S(1)}, u32[]{:S(2)}, u32[]{:S(2)}) collective-permute-start(bf16[192,768]{1,0:T(8,128)(2,1)S(1)} %get-tuple-element.33.refs_0_), channel_id=1, source_target_pairs={{3,0},{0,1},{1,2},{2,3},{7,4},{4,5},{5,6},{6,7},{11,8},{8,9},{9,10... | collective-permute-start | bytes 884744 | tf_op jit(solution)/shard_map/ppermute | solution.py:274
  4.8 9.2 %collective-permute-start.11 = (bf16[192,768]{1,0:T(8,128)(2,1)S(1)}, bf16[192,768]{1,0:T(8,128)(2,1)S(1)}, u32[]{:S(2)}, u32[]{:S(2)}) collective-permute-start(bf16[192,768]{1,0:T(8,128)(2,1)S(1)} %get-tuple-element.33.refs_0_), channel_id=1, source_target_pairs={{1,0},{2,1},{3,2},{0,3},{5,4},{6,5},{7,6},{4,7},{9,8},{10,9},{11,1... | collective-permute-start | bytes 884744 | tf_op jit(solution)/shard_map/ppermute | solution.py:274
  8.0 13.4 %all-to-all-start = ((bf16[8,96,256]{2,1,0:T(8,128)(2,1)}), bf16[8,96,256]{2,1,0:T(8,128)(2,1)S(1)}, u32[]{:S(2)}, u32[]{:S(2)}) async-start(bf16[8,96,256]{2,1,0:T(8,128)(2,1)} %bitcast.23), calls=%async_computation | async-start | bytes 786432 | tf_op jit(solution)/shard_map/all_to_all | solution.py:292
  14.0 23.2 %collective-permute-start.14 = (bf16[96,768]{1,0:T(8,128)(2,1)S(1)}, bf16[96,768]{1,0:T(8,128)(2,1)S(1)}, u32[]{:S(2)}, u32[]{:S(2)}) collective-permute-start(bf16[96,768]{1,0:T(8,128)(2,1)S(1)} %slice.43), channel_id=1, source_target_pairs={{3,0},{0,1},{1,2},{2,3},{7,4},{4,5},{5,6},{6,7},{11,8},{8,9},{9,10... | collective-permute-start | bytes 442376 | tf_op jit(solution)/shard_map/ppermute | solution.py:274
  14.1 23.1 %collective-permute-start.13 = (bf16[96,768]{1,0:T(8,128)(2,1)S(1)}, bf16[96,768]{1,0:T(8,128)(2,1)S(1)}, u32[]{:S(2)}, u32[]{:S(2)}) collective-permute-start(bf16[96,768]{1,0:T(8,128)(2,1)S(1)} %slice.42), channel_id=1, source_target_pairs={{1,0},{2,1},{3,2},{0,3},{5,4},{6,5},{7,6},{4,7},{9,8},{10,9},{11,1... | collective-permute-start | bytes 442376 | tf_op jit(solution)/shard_map/ppermute | solution.py:274
  22.0 13.4 %all-to-all-start.1 = ((s32[16,4,128]{2,1,0:T(4,128)}), s32[16,4,128]{2,1,0:T(4,128)S(1)}, u32[]{:S(2)}, u32[]{:S(2)}) async-start(s32[16,4,128]{2,1,0:T(4,128)} %broadcast_in_dim.10), calls=%async_computation.1 | async-start | bytes 65536 | tf_op jit(solution)/shard_map/all_to_all | solution.py:304
  37.9 39.2 %collective-permute-start.16 = (bf16[1024,384]{1,0:T(8,128)(2,1)S(1)}, bf16[1024,384]{1,0:T(8,128)(2,1)S(1)}, u32[]{:S(2)}, u32[]{:S(2)}) collective-permute-start(bf16[1024,384]{1,0:T(8,128)(2,1)S(1)} %shard_map.97.refs_8_), channel_id=1, source_target_pairs={{12,0},{0,4},{4,8},{8,12},{13,1},{1,5},{5,9},{9,13},{14,2},{2,6},{... | collective-permute-start | bytes 2359304 | tf_op jit(solution)/shard_map/ppermute | solution.py:274
  38.6 38.7 %collective-permute-start.15 = (bf16[1024,384]{1,0:T(8,128)(2,1)S(1)}, bf16[1024,384]{1,0:T(8,128)(2,1)S(1)}, u32[]{:S(2)}, u32[]{:S(2)}) collective-permute-start(bf16[1024,384]{1,0:T(8,128)(2,1)S(1)} %shard_map.97.refs_8_), channel_id=1, source_target_pairs={{4,0},{8,4},{12,8},{0,12},{5,1},{9,5},{13,9},{1,13},{6,2},{10,6},{... | collective-permute-start | bytes 2359304 | tf_op jit(solution)/shard_map/ppermute | solution.py:274
  41.4 19.7 %collective-permute-start.20 = (bf16[128,768]{1,0:T(8,128)(2,1)S(1)}, bf16[128,768]{1,0:T(8,128)(2,1)S(1)}, u32[]{:S(2)}, u32[]{:S(2)}) collective-permute-start(bf16[128,768]{1,0:T(8,128)(2,1)S(1)} %get-tuple-element.34.refs_0_), channel_id=1, source_target_pairs={{12,0},{0,4},{4,8},{8,12},{13,1},{1,5},{5,9},{9,13},{14,2},{2,6},{... | collective-permute-start | bytes 589832 | tf_op jit(solution)/shard_map/ppermute | solution.py:274
  41.4 20.3 %collective-permute-start.19 = (bf16[128,768]{1,0:T(8,128)(2,1)S(1)}, bf16[128,768]{1,0:T(8,128)(2,1)S(1)}, u32[]{:S(2)}, u32[]{:S(2)}) collective-permute-start(bf16[128,768]{1,0:T(8,128)(2,1)S(1)} %get-tuple-element.34.refs_0_), channel_id=1, source_target_pairs={{4,0},{8,4},{12,8},{0,12},{5,1},{9,5},{13,9},{1,13},{6,2},{10,6},{... | collective-permute-start | bytes 589832 | tf_op jit(solution)/shard_map/ppermute | solution.py:274
  44.7 30.0 %collective-permute-start.1 = (bf16[8,96,256]{2,1,0:T(8,128)(2,1)S(1)}, bf16[8,96,256]{2,1,0:T(8,128)(2,1)S(1)}, u32[]{:S(2)}, u32[]{:S(2)}) collective-permute-start(bf16[8,96,256]{2,1,0:T(8,128)(2,1)S(1)} %all-to-all-done.refs_0_), channel_id=1, source_target_pairs={{3,0},{0,1},{1,2},{2,3},{7,4},{4,5},{5,6},{6,7},{11,8},{8,9},{9,10... | collective-permute-start | bytes 1179656 | tf_op jit(solution)/shard_map/ppermute | solution.py:274
  61.1 6.1 %collective-permute-start.7 = (bf16[2,96,256]{2,1,0:T(8,128)(2,1)S(1)}, bf16[2,96,256]{2,1,0:T(8,128)(2,1)S(1)}, u32[]{:S(2)}, u32[]{:S(2)}) collective-permute-start(bf16[2,96,256]{2,1,0:T(8,128)(2,1)S(1)} %pad_maximum_fusion.refs_5_), channel_id=1, source_target_pairs={{64,0},{96,32},{0,64},{32,96},{65,1},{97,33},{1,65},{33,97},{66,2}... | collective-permute-start | bytes 294920 | tf_op jit(solution)/shard_map/ppermute | solution.py:274
  61.8 5.9 %collective-permute-start.22 = (bf16[64,768]{1,0:T(8,128)(2,1)S(1)}, bf16[64,768]{1,0:T(8,128)(2,1)S(1)}, u32[]{:S(2)}, u32[]{:S(2)}) collective-permute-start(bf16[64,768]{1,0:T(8,128)(2,1)S(1)} %slice.47), channel_id=1, source_target_pairs={{12,0},{0,4},{4,8},{8,12},{13,1},{1,5},{5,9},{9,13},{14,2},{2,6},{... | collective-permute-start | bytes 294920 | tf_op jit(solution)/shard_map/ppermute | solution.py:274
  67.7 6.1 %collective-permute-start.6 = (bf16[2,96,256]{2,1,0:T(8,128)(2,1)S(1)}, bf16[2,96,256]{2,1,0:T(8,128)(2,1)S(1)}, u32[]{:S(2)}, u32[]{:S(2)}) collective-permute-start(bf16[2,96,256]{2,1,0:T(8,128)(2,1)S(1)} %pad_maximum_fusion.refs_5_), channel_id=1, source_target_pairs={{96,0},{0,32},{32,64},{64,96},{97,1},{1,33},{33,65},{65,97},{98,2}... | collective-permute-start | bytes 294920 | tf_op jit(solution)/shard_map/ppermute | solution.py:274
  71.8 12.1 %collective-permute-start = (bf16[8,96,256]{2,1,0:T(8,128)(2,1)S(1)}, bf16[8,96,256]{2,1,0:T(8,128)(2,1)S(1)}, u32[]{:S(2)}, u32[]{:S(2)}) collective-permute-start(bf16[8,96,256]{2,1,0:T(8,128)(2,1)S(1)} %all-to-all-done.refs_0_), channel_id=1, source_target_pairs={{1,0},{2,1},{3,2},{0,3},{5,4},{6,5},{7,6},{4,7},{9,8},{10,9},{11,1... | collective-permute-start | bytes 1179656 | tf_op jit(solution)/shard_map/ppermute | solution.py:274
  73.8 11.4 %collective-permute-start.24 = (bf16[512,384]{1,0:T(8,128)(2,1)S(1)}, bf16[512,384]{1,0:T(8,128)(2,1)S(1)}, u32[]{:S(2)}, u32[]{:S(2)}) collective-permute-start(bf16[512,384]{1,0:T(8,128)(2,1)S(1)} %shard_map.98.refs_13_), channel_id=1, source_target_pairs={{3,0},{0,1},{1,2},{2,3},{7,4},{4,5},{5,6},{6,7},{11,8},{8,9},{9,10... | collective-permute-start | bytes 1179656 | tf_op jit(solution)/shard_map/ppermute | solution.py:274
  74.7 16.1 %collective-permute-start.23 = (bf16[512,384]{1,0:T(8,128)(2,1)S(1)}, bf16[512,384]{1,0:T(8,128)(2,1)S(1)}, u32[]{:S(2)}, u32[]{:S(2)}) collective-permute-start(bf16[512,384]{1,0:T(8,128)(2,1)S(1)} %shard_map.98.refs_13_), channel_id=1, source_target_pairs={{1,0},{2,1},{3,2},{0,3},{5,4},{6,5},{7,6},{4,7},{9,8},{10,9},{11,1... | collective-permute-start | bytes 1179656 | tf_op jit(solution)/shard_map/ppermute | solution.py:274
  77.1 14.2 %collective-permute-start.3 = (bf16[4,96,256]{2,1,0:T(8,128)(2,1)S(1)}, bf16[4,96,256]{2,1,0:T(8,128)(2,1)S(1)}, u32[]{:S(2)}, u32[]{:S(2)}) collective-permute-start(bf16[4,96,256]{2,1,0:T(8,128)(2,1)S(1)} %slice.41), channel_id=1, source_target_pairs={{3,0},{0,1},{1,2},{2,3},{7,4},{4,5},{5,6},{6,7},{11,8},{8,9},{9,10... | collective-permute-start | bytes 589832 | tf_op jit(solution)/shard_map/ppermute | solution.py:274
  77.2 4.7 %collective-permute-start.5 = (bf16[2,96,256]{2,1,0:T(8,128)(2,1)S(1)}, bf16[2,96,256]{2,1,0:T(8,128)(2,1)S(1)}, u32[]{:S(2)}, u32[]{:S(2)}) collective-permute-start(bf16[2,96,256]{2,1,0:T(8,128)(2,1)S(1)} %pad_maximum_fusion.refs_5_), channel_id=1, source_target_pairs={{32,0},{64,32},{96,64},{0,96},{33,1},{65,33},{97,65},{1,97},{34,2}... | collective-permute-start | bytes 294920 | tf_op jit(solution)/shard_map/ppermute | solution.py:274
  81.9 25.8 %collective-permute-start.18 = (bf16[512,384]{1,0:T(8,128)(2,1)}, bf16[512,384]{1,0:T(8,128)(2,1)}, u32[]{:S(2)}, u32[]{:S(2)}) collective-permute-start(bf16[512,384]{1,0:T(8,128)(2,1)} %slice.45), channel_id=1, source_target_pairs={{12,0},{0,4},{4,8},{8,12},{13,1},{1,5},{5,9},{9,13},{14,2},{2,6},{... | collective-permute-start | bytes 1179656 | tf_op jit(solution)/shard_map/ppermute | solution.py:274
  83.9 23.8 %collective-permute-start.17 = (bf16[512,384]{1,0:T(8,128)(2,1)}, bf16[512,384]{1,0:T(8,128)(2,1)}, u32[]{:S(2)}, u32[]{:S(2)}) collective-permute-start(bf16[512,384]{1,0:T(8,128)(2,1)} %slice.44), channel_id=1, source_target_pairs={{4,0},{8,4},{12,8},{0,12},{5,1},{9,5},{13,9},{1,13},{6,2},{10,6},{... | collective-permute-start | bytes 1179656 | tf_op jit(solution)/shard_map/ppermute | solution.py:274
  85.2 9.1 %collective-permute-start.2 = (bf16[4,96,256]{2,1,0:T(8,128)(2,1)S(1)}, bf16[4,96,256]{2,1,0:T(8,128)(2,1)S(1)}, u32[]{:S(2)}, u32[]{:S(2)}) collective-permute-start(bf16[4,96,256]{2,1,0:T(8,128)(2,1)S(1)} %slice.40), channel_id=1, source_target_pairs={{1,0},{2,1},{3,2},{0,3},{5,4},{6,5},{7,6},{4,7},{9,8},{10,9},{11,1... | collective-permute-start | bytes 589832 | tf_op jit(solution)/shard_map/ppermute | solution.py:274
  90.8 6.9 %collective-permute-start.26 = (bf16[256,384]{1,0:T(8,128)(2,1)S(1)}, bf16[256,384]{1,0:T(8,128)(2,1)S(1)}, u32[]{:S(2)}, u32[]{:S(2)}) collective-permute-start(bf16[256,384]{1,0:T(8,128)(2,1)S(1)} %slice.49), channel_id=1, source_target_pairs={{3,0},{0,1},{1,2},{2,3},{7,4},{4,5},{5,6},{6,7},{11,8},{8,9},{9,10... | collective-permute-start | bytes 589832 | tf_op jit(solution)/shard_map/ppermute | solution.py:274
  91.4 8.9 %collective-permute-start.25 = (bf16[256,384]{1,0:T(8,128)(2,1)S(1)}, bf16[256,384]{1,0:T(8,128)(2,1)S(1)}, u32[]{:S(2)}, u32[]{:S(2)}) collective-permute-start(bf16[256,384]{1,0:T(8,128)(2,1)S(1)} %slice.48), channel_id=1, source_target_pairs={{1,0},{2,1},{3,2},{0,3},{5,4},{6,5},{7,6},{4,7},{9,8},{10,9},{11,1... | collective-permute-start | bytes 589832 | tf_op jit(solution)/shard_map/ppermute | solution.py:274
  97.0 6.5 %collective-permute-start.8 = (bf16[4,64,256]{2,1,0:T(8,128)(2,1)}, bf16[4,64,256]{2,1,0:T(8,128)(2,1)}, u32[]{:S(2)}, u32[]{:S(2)}) collective-permute-start(bf16[4,64,256]{2,1,0:T(8,128)(2,1)} %get-tuple-element.30), channel_id=1, source_target_pairs={{12,0},{0,4},{4,8},{8,12},{13,1},{1,5},{5,9},{9,13},{14,2},{2,6},{... | collective-permute-start | bytes 393224 | tf_op jit(solution)/shard_map/ppermute | solution.py:274
  97.7 6.8 %collective-permute-start.9 = (bf16[4,64,256]{2,1,0:T(8,128)(2,1)}, bf16[4,64,256]{2,1,0:T(8,128)(2,1)}, u32[]{:S(2)}, u32[]{:S(2)}) collective-permute-start(bf16[4,64,256]{2,1,0:T(8,128)(2,1)} %get-tuple-element.31), channel_id=1, source_target_pairs={{4,0},{8,4},{12,8},{0,12},{5,1},{9,5},{13,9},{1,13},{6,2},{10,6},{... | collective-permute-start | bytes 393224 | tf_op jit(solution)/shard_map/ppermute | solution.py:274
  100.9 6.8 %collective-permute-start.10 = (bf16[4,64,256]{2,1,0:T(8,128)(2,1)}, bf16[4,64,256]{2,1,0:T(8,128)(2,1)}, u32[]{:S(2)}, u32[]{:S(2)}) collective-permute-start(bf16[4,64,256]{2,1,0:T(8,128)(2,1)} %get-tuple-element.32), channel_id=1, source_target_pairs={{8,0},{12,4},{0,8},{4,12},{9,1},{13,5},{1,9},{5,13},{10,2},{14,6},... | collective-permute-start | bytes 393224 | tf_op jit(solution)/shard_map/ppermute | solution.py:274
  128.5 12.5 %collective-permute-start.27 = (bf16[4,64,256]{2,1,0:T(8,128)(2,1)S(1)}, bf16[4,64,256]{2,1,0:T(8,128)(2,1)S(1)}, u32[]{:S(2)}, u32[]{:S(2)}) collective-permute-start(bf16[4,64,256]{2,1,0:T(8,128)(2,1)S(1)} %get-tuple-element.36), channel_id=1, source_target_pairs={{12,0},{0,4},{4,8},{8,12},{13,1},{1,5},{5,9},{9,13},{14,2},{2,6},{... | collective-permute-start | bytes 393224 | tf_op jit(solution)/shard_map/ppermute | solution.py:274
  128.6 12.4 %collective-permute-start.28 = (bf16[4,64,256]{2,1,0:T(8,128)(2,1)S(1)}, bf16[4,64,256]{2,1,0:T(8,128)(2,1)S(1)}, u32[]{:S(2)}, u32[]{:S(2)}) collective-permute-start(bf16[4,64,256]{2,1,0:T(8,128)(2,1)S(1)} %get-tuple-element.37), channel_id=1, source_target_pairs={{4,0},{8,4},{12,8},{0,12},{5,1},{9,5},{13,9},{1,13},{6,2},{10,6},{... | collective-permute-start | bytes 393224 | tf_op jit(solution)/shard_map/ppermute | solution.py:274
  131.8 9.2 %collective-permute-start.29 = (bf16[4,64,256]{2,1,0:T(8,128)(2,1)S(1)}, bf16[4,64,256]{2,1,0:T(8,128)(2,1)S(1)}, u32[]{:S(2)}, u32[]{:S(2)}) collective-permute-start(bf16[4,64,256]{2,1,0:T(8,128)(2,1)S(1)} %get-tuple-element.38), channel_id=1, source_target_pairs={{8,0},{12,4},{0,8},{4,12},{9,1},{13,5},{1,9},{5,13},{10,2},{14,6},... | collective-permute-start | bytes 393224 | tf_op jit(solution)/shard_map/ppermute | solution.py:274
  131.8 5.4 %collective-permute-start.33 = (bf16[80,128]{1,0:T(8,128)(2,1)S(1)}, bf16[80,128]{1,0:T(8,128)(2,1)S(1)}, u32[]{:S(2)}, u32[]{:S(2)}) collective-permute-start(bf16[80,128]{1,0:T(8,128)(2,1)S(1)} %add_convert_fusion.s0_ref), channel_id=1, source_target_pairs={{64,0},{96,32},{0,64},{32,96},{65,1},{97,33},{1,65},{33,97},{66,2}... | collective-permute-start | bytes 61448 | tf_op jit(solution)/shard_map/ppermute | solution.py:274
  132.8 5.6 %collective-permute-start.32 = (bf16[80,128]{1,0:T(8,128)(2,1)S(1)}, bf16[80,128]{1,0:T(8,128)(2,1)S(1)}, u32[]{:S(2)}, u32[]{:S(2)}) collective-permute-start(bf16[80,128]{1,0:T(8,128)(2,1)S(1)} %add_convert_fusion.s0_ref), channel_id=1, source_target_pairs={{96,0},{0,32},{32,64},{64,96},{97,1},{1,33},{33,65},{65,97},{98,2}... | collective-permute-start | bytes 61448 | tf_op jit(solution)/shard_map/ppermute | solution.py:274
  (23 other events, 158.2 us)

commit v5 on v2

v5 whole, which is shorter than its diff:
```python
import jax
import jax.numpy as jnp
from jax import lax
from jax.experimental import pallas as pl
from jax.experimental.pallas import tpu as pltpu
from jax.sharding import Mesh
from jax.sharding import PartitionSpec as P

BF = jnp.bfloat16
F32 = jnp.float32
I32 = jnp.int32
VMEM = pl.BlockSpec(memory_space=pltpu.VMEM)
SMEM = pl.BlockSpec(memory_space=pltpu.SMEM)
MIB = 1024 * 1024
RING = (0, 1, -1, 2)
NT = (((1,), (1,)), ((), ()))


def dot(a, b, dims=(((1,), (0,)), ((), ()))):
    return lax.dot_general(a, b, dims, preferred_element_type=F32)


def columns_of(row):
    return jnp.broadcast_to(row, (128, 128)).T


def halves(a, b):
    low = lax.broadcasted_iota(I32, a.shape, 1) < 64
    return jnp.where(low, a, pltpu.roll(b, 64, 1)), jnp.where(low, pltpu.roll(a, 64, 1), b)


def owner(block):
    return (block % 4) * 4 + block // 4


def mask_kernel(mask_ref, up_ref, a_ref, b_ref):
    for b, out_ref in enumerate((a_ref, b_ref)):
        for k in range(6):
            out_ref[0:128, k * 128 : k * 128 + 128] = mask_ref[b, k].astype(F32).astype(BF)
    a_ref[128:192, 0:256] = up_ref[0:64, :]
    a_ref[128:192, 256:512] = up_ref[64:128, :]
    rest = jnp.concatenate([up_ref[128:153, :].astype(F32), jnp.zeros((39, 256), F32)], axis=0)
    a_ref[128:192, 512:768] = rest.astype(BF)


def pack_kernel(a_ref, b_ref, c_ref, d_ref, low_ref, high_ref):
    half = a_ref.shape[0]
    low_ref[0:half] = a_ref[...]
    low_ref[half:] = b_ref[...]
    high_ref[0:half] = c_ref[...]
    high_ref[half:] = d_ref[...]


def features_at(refs, k, f):
    return refs[k][f] if k < 3 else refs[3 + f // 4][f % 4]


def project_kernel(*refs):
    x_refs, w_refs, small_ref, at_ref = refs[:5], refs[5:9], refs[9], refs[10]
    v_refs, w_ref, t_ref = refs[11:15], refs[15], refs[16]
    for k, shift in enumerate(RING):
        for flip in range(2):
            f = ((at_ref[3] + shift + 4) % 4) * 2 + (at_ref[4] + flip) % 2
            w_ref[f] = w_refs[k][flip]
    w = w_ref[...].reshape(768, 256).astype(F32).T.astype(BF)
    for k, shift in enumerate(RING):
        z = (at_ref[2] + shift + 4) % 4
        degree = small_ref[at_ref[1] * 4 + z].astype(F32)
        inv = lax.rsqrt(jnp.concatenate([degree[0:1], degree[1:2]], axis=1))
        whole = jnp.concatenate([features_at(x_refs, k, f) for f in range(8)], axis=0)
        t_ref[k] = (inv * dot(w, whole)).astype(BF)
        for v_ref, to in zip(v_refs, RING):
            at = pl.multiple_of(((at_ref[1] + to + 4) % 4) * 64, 64)
            v_ref[z] = t_ref[k, pl.ds(at, 64), :]


def mix_kernel(*refs):
    v_refs, small_ref, links_ref, sw_ref, at_ref = refs[:4], refs[4], refs[5], refs[6], refs[7]
    a_refs, b_refs = refs[8:16], refs[16:24]
    hid_ref, second_ref, g_refs = refs[24], refs[25], refs[26:30]
    src_ref, v2_ref, inv_ref = refs[30:]
    places = []
    for i, dx in enumerate(RING):
        for j, dz in enumerate(RING):
            places.append((i, j, ((at_ref[1] + dx + 4) & 3) * 4 + ((at_ref[2] + dz + 4) & 3)))

    for d in range(16):
        degree = small_ref[d].astype(F32)
        for h in range(2):
            inv_ref[2 * d + h] = lax.rsqrt(degree[h : h + 1])
    for i, j, d in places:
        a_ref, base = a_refs[2 * i + j // 2], (j % 2) * 192 + 128
        v_ref = v_refs[(0, 2, 1, 3)[i]]
        to = (at_ref[2] + RING[j] + 4) & 3
        for h in range(2):
            t = d * 2 + h
            inv = inv_ref[t]
            src_ref[t, 0:64] = v_ref[to, :, h * 128 : h * 128 + 128]
            for c in range(3):
                rows = min(64, 160 - 64 * c)
                up = a_ref[base : base + rows, c * 256 + h * 128 : c * 256 + h * 128 + 128]
                src_ref[t, 64 + 64 * c : 64 + 64 * c + rows] = (inv * up.astype(F32)).astype(BF)

    def spread(i, j, d, h, source):
        if h == 0:
            weights = a_refs[2 * i + j // 2][(j % 2) * 192 : (j % 2) * 192 + 128, :]
        else:
            weights = b_refs[2 * j + i // 2][(i % 2) * 128 : (i % 2) * 128 + 128, :]
        named = [source[links_ref[d, 2, h * 6 + k]] for k in range(6)]
        return source[d * 2 + h].astype(F32) + dot(jnp.concatenate(named, axis=1), weights, NT)

    second = jnp.zeros((160, 64), F32)
    for i, j, d in places:
        ones, pulls = [], []
        for h in range(2):
            t = d * 2 + h
            inv = inv_ref[t]
            total = spread(i, j, d, h, src_ref)
            m = inv * total[0:64]
            s = jax.nn.sigmoid(m)
            hid = (m * s).astype(BF)
            hid_ref[d, :, h * 128 : h * 128 + 128] = hid
            ones.append((inv * hid.astype(F32)).astype(BF))
            pull = total[64:224].astype(BF)
            pulls.append(pull)
            slope = s * (1.0 + m * (1.0 - s))
            v2_ref[t] = (inv * inv * dot(sw_ref[...], pull) * slope).astype(BF)
        second = second + dot(jnp.concatenate(pulls, axis=1), jnp.concatenate(ones, axis=1), NT)
    second_ref[...] = jnp.concatenate([second[:80], second[80:]], axis=1).astype(BF)
    for i, j, d in places:
        to = (at_ref[2] + RING[j] + 4) & 3
        for h in range(2):
            g = inv_ref[d * 2 + h] * spread(i, j, d, h, v2_ref)
            g_refs[i][to, :, h * 128 : h * 128 + 128] = g.astype(BF)


def turn_kernel(in_ref, out_ref):
    for d in range(16):
        block = in_ref[d].astype(F32)
        both = jnp.concatenate([block[:, 0:128], block[:, 128:256]], axis=0)
        out_ref[d] = both.T.astype(BF)


def weigh_kernel(*refs):
    x_refs, g_refs, at_ref, out_ref = refs[:5], refs[5:9], refs[9], refs[10]
    rights = []
    for shift in RING:
        z = (at_ref[2] + shift + 4) % 4
        rights.append(jnp.concatenate([g[z] for g in g_refs], axis=0))
    for f in range(8):
        acc = jnp.zeros((96, 256), F32)
        for k, right in enumerate(rights):
            acc = acc + dot(features_at(x_refs, k, f), right, NT)
        for p in range(2):
            g = acc[:, p * 128 : p * 128 + 128]
            for part, shift in zip(halves(g[:48], g[48:]), RING[2 * p : 2 * p + 2]):
                out_ref[f, (at_ref[1] - shift + 4) % 4] = part.astype(BF)


def add_kernel(part_ref, s0_ref, s1_ref, s2_ref, s3_ref, out_ref):
    first = part_ref[0].astype(F32)
    for i in range(1, 32):
        first = first + part_ref[i].astype(F32)
    second = s0_ref[...].astype(F32)
    for ref in (s1_ref, s2_ref, s3_ref):
        second = second + ref[...].astype(F32)
    both = jnp.concatenate([first, second], axis=0).astype(BF)
    for d in range(16):
        out_ref[d] = both


def hidden_kernel(in_ref, out_ref):
    for j in range(8):
        cols = pl.ds(j * 128, 128)
        one, two = halves(in_ref[owner(2 * j)].astype(F32), in_ref[owner(2 * j + 1)].astype(F32))
        out_ref[0:128, cols] = one.astype(BF)
        out_ref[128:256, cols] = two.astype(BF)


def gradient_kernel(in_ref, first_ref, second_ref):
    for j in range(8):
        cols = pl.ds(j * 128, 128)
        one, two = halves(in_ref[owner(2 * j)].astype(F32), in_ref[owner(2 * j + 1)].astype(F32))
        first_ref[0:48, cols] = one[:48]
        first_ref[48:96, cols] = two[:48]
        second_ref[0:80, cols] = one[48:]
        second_ref[80:153, cols] = two[48:121]


def call(kernel, shape, specs, scratch=(), flops=0, moved=0, limit=8):
    return pl.pallas_call(
        kernel,
        out_shape=shape,
        in_specs=specs,
        out_specs=jax.tree.map(lambda _: VMEM, shape),
        scratch_shapes=list(scratch),
        compiler_params=pltpu.CompilerParams(vmem_limit_bytes=limit * MIB),
        cost_estimate=pl.CostEstimate(flops=flops, bytes_accessed=moved, transcendentals=0),
    )


def fetch(value, axis, shift):
    return lax.ppermute(value, axis, [((i + shift) % 4, i) for i in range(4)])


def ring(value, axis):
    return [value] + [fetch(value, axis, shift) for shift in RING[1:]]


def pack(blocks):
    pair = jax.ShapeDtypeStruct((2 * blocks[0].shape[0], 768), BF)
    return call(pack_kernel, (pair, pair), [VMEM] * 4, moved=2_000_000)(*blocks)


def neighbours(low, high, axis):
    after, before = fetch(low, axis, 1), fetch(high, axis, -1)
    return [after, fetch(high, axis, 1), fetch(low, axis, -1), before]


def body(features, first_weight, second_weight, degree, neighbour_block, neighbour_mask, upstream):
    feat, dom = ("y", "c"), ("x", "z")
    shape = jax.ShapeDtypeStruct
    x, z = lax.axis_index("x"), lax.axis_index("z")
    at = jnp.stack([x * 4 + z, x, z, lax.axis_index("y"), lax.axis_index("c")])
    x_own = lax.all_to_all(
        features.reshape(96, 8, 256).transpose(1, 0, 2), feat, 0, 0, tiled=True
    )
    mask_a, mask_b = call(
        mask_kernel, (shape((192, 768), BF), shape((128, 768), BF)), [VMEM] * 2, moved=1_200_000
    )(neighbour_mask[0], upstream[0].T)
    weight = lax.dynamic_slice(first_weight, (0, z * 256), (96, 256))
    other = lax.ppermute(weight, "c", [(0, 1), (1, 0)])
    *blocks, other = lax.optimization_barrier((*ring(mask_a, "z"), *ring(mask_b, "x"), other))
    own_a, own_b = pack(blocks[:4]), pack(blocks[4:])
    weights = ring(jnp.stack([weight, other]), "y")
    links = jnp.pad(jnp.maximum(neighbour_block.reshape(12), 0), (0, 244))
    small = jnp.concatenate([degree.reshape(2, 128), links.reshape(2, 128)], axis=0)
    small = jnp.broadcast_to(small, (16, 4, 128))
    small, x_own = lax.optimization_barrier((small, x_own))
    small = lax.all_to_all(small, dom, 0, 0, tiled=True)
    near_a, near_b = neighbours(*own_a, "x"), neighbours(*own_b, "z")
    x_after, x_before = fetch(x_own, "z", 1), fetch(x_own, "z", -1)
    a0, a3, b0, b3, x_after, x_before, small = lax.optimization_barrier(
        (near_a[0], near_a[3], near_b[0], near_b[3], x_after, x_before, small)
    )
    x_wide = [x_own, x_after, x_before, fetch(x_after[:4], "z", 1), fetch(x_before[4:], "z", -1)]
    masks = [*own_a, a0, *near_a[1:3], a3, fetch(a0, "x", 1), fetch(a3, "x", -1)]
    masks += [*own_b, b0, *near_b[1:3], b3, fetch(b0, "z", 1), fetch(b3, "z", -1)]
    own_second = lax.dynamic_slice(second_weight, ((z * 4 + x) * 64, 0), (64, 153))
    own_second = jnp.pad(own_second, ((0, 0), (0, 7)))
    part = shape((4, 64, 256), BF)
    v = call(
        project_kernel,
        (part,) * 4,
        [VMEM] * 10 + [SMEM],
        [pltpu.VMEM((8, 96, 256), BF), pltpu.VMEM((4, 256, 256), BF)],
        flops=400_000_000,
        moved=3_000_000,
    )(*x_wide, *weights, small, at)
    v = [v[0]] + [fetch(value, "x", -shift) for value, shift in zip(v[1:], RING[1:])]
    hid, second, *g = call(
        mix_kernel,
        (shape((16, 64, 256), BF), shape((80, 128), BF)) + (part,) * 4,
        [VMEM] * 5 + [SMEM, VMEM, SMEM] + [VMEM] * 16,
        [
            pltpu.VMEM((32, 224, 128), BF),
            pltpu.VMEM((32, 64, 128), BF),
            pltpu.VMEM((32, 1, 128), F32),
        ],
        flops=1_600_000_000,
        moved=10_000_000,
        limit=20,
    )(*v, small, small, own_second, at, *masks)
    g = [g[0]] + [fetch(value, "x", -shift) for value, shift in zip(g[1:], RING[1:])]
    other = lax.ppermute(second, "c", [(0, 1), (1, 0)])
    hid, other = lax.optimization_barrier((hid, other))
    tile = shape((16, 128, 128), BF)
    hid = call(turn_kernel, tile, [VMEM], moved=1_000_000)(hid)
    hid = lax.all_to_all(hid, dom, 0, 0, tiled=True)
    second = ring((second.astype(F32) + other.astype(F32)).astype(BF), "y")
    part = call(
        weigh_kernel,
        shape((8, 4, 48, 128), BF),
        [VMEM] * 9 + [SMEM],
        flops=400_000_000,
        moved=3_000_000,
    )(*x_wide, *g, at)
    part, hid, *rest = lax.optimization_barrier((part, hid, *second[1:]))
    part = lax.all_to_all(part.reshape(32, 48, 128), ("y", "c", "x"), 0, 0, tiled=True)
    done = call(add_kernel, tile, [VMEM] * 5, moved=1_000_000)(part, second[0], *rest)
    done = lax.all_to_all(done, dom, 0, 0, tiled=True)
    hidden = call(hidden_kernel, shape((256, 1024), BF), [VMEM], moved=1_000_000)(hid)
    grad_first, grad_second = call(
        gradient_kernel, (shape((96, 1024), F32), shape((153, 1024), F32)), [VMEM], moved=1_500_000
    )(done)
    return (hidden[None], grad_first, grad_second.T)


def solution(mesh):
    wide = Mesh(mesh.devices.reshape(4, 2, 4, 4), ("y", "c", "x", "z"))
    feat, dom = ("y", "c"), ("x", "z")
    placed = (
        P(feat, dom, None),
        P(feat, None),
        P(),
        P(dom, feat),
        P(dom, feat, None),
        P(dom, feat, None, None, None),
        P(dom, feat, None),
    )
    return jax.shard_map(
        body,
        mesh=wide,
        in_specs=placed,
        out_specs=(P(dom, feat, None), P(feat, None), P()),
        check_vma=False,
    )
```

time: 178 us -> 187 us (1.051)
  starting transfers between devices: 23.7 us -> 71 us
  blocking collectives: 59.4 us -> 27.1 us
  between operations: 14.1 us -> 0.97 us
  local copies, waits for them, and re-layouts: 5.92 us -> 15.9 us
  waiting for transfers between devices: 53.1 us -> 48.6 us
  Pallas kernels: 20.5 us -> 22.6 us
    ppermute x12 -> x34, starting transfers between devices: 19.2 us -> 58.1 us  [fetch(): return lax.ppermute(value, axis, [((i + shift) % 4, i) for i in range(4)])]
    all_to_all x2 -> x1, blocking collectives: 42.8 us -> 10.2 us  [body(): small = lax.all_to_all(small, dom, 0, 0, tiled=True)]
    all_to_all x0 -> x2, waiting for transfers between devices: none -> 11 us  [the longest x1 11 us: body(): done = lax.all_to_all(done, dom, 0, 0, tiled=True)]
    unnamed x12 -> x60, local copies, waits for them, and re-layouts: 4.83 us -> 14.7 us
    all_gather x1 -> x0, waiting for transfers between devices: 9.7 us -> none  [body(): masks = lax.all_gather(masks, dom, axis=0)]
    all_to_all x0 -> x2, starting transfers between devices: none -> 8.18 us  [the longest x1 4.61 us: body(): hid = lax.all_to_all(hid, dom, 0, 0, tiled=True)]
    all_to_all x1, waiting for transfers between devices: 6.75 us -> 0.01 us  [body(): lax.all_to_all(features.reshape(96, 8, 256).transpose(1, 0, 2), feat, 0,...]
    pallas_call x6 -> x10, Pallas kernels: 20.5 us -> 22.6 us  [the longest x1 13.4 us: body(): call(mix_kernel, (shape((16, 64, 256), BF), shape((80, 128), BF)) + (part...]
  transfers between devices with their start and end apart: 19 -> 39, of which waited for: 9 -> 11; matrix products, arithmetic and copies ran while one was open for 2% -> 1% of each run, Pallas kernels for 1% -> 3%
where the time goes in v5:
time: 187 us; the launch traced here: 186 us
  starting transfers between devices  71 us (38%)
  waiting for transfers between devices  48.6 us (26%)
  blocking collectives  27.1 us (14%)
  Pallas kernels  22.6 us (12%)
  local copies, waits for them, and re-layouts  15.9 us (9%)
    ppermute x34, starting transfers between devices, fetch(): return lax.ppermute(value, axis, [((i + shift) % 4, i) for i in range(4)])  58.1 us
    ppermute x34, waiting for transfers between devices, fetch(): return lax.ppermute(value, axis, [((i + shift) % 4, i) for i in range(4)])  36.5 us
    all_to_all x1, blocking collectives, body(): lax.all_to_all(part.reshape(32, 48, 128), ('y', 'c', 'x'), 0, 0, tiled=True)  17 us
    unnamed x60, local copies, waits for them, and re-layouts  14.7 us
    pallas_call x1, Pallas kernels, body(): call(mix_kernel, (shape((16, 64, 256), BF), shape((80, 128), BF)) + (part...  13.4 us
    all_to_all x1, waiting for transfers between devices, body(): done = lax.all_to_all(done, dom, 0, 0, tiled=True)  11 us
    all_to_all x1, blocking collectives, body(): small = lax.all_to_all(small, dom, 0, 0, tiled=True)  10.2 us
    all_to_all x1, starting transfers between devices, body(): lax.all_to_all(features.reshape(96, 8, 256).transpose(1, 0, 2), feat, 0,...  4.69 us
  transfers between devices with their start and end apart: 39, of which 11 were waited for; matrix products, arithmetic and copies ran while one was open for 1% of the time, Pallas kernels for 3%

profile of v5, /device:TPU:0, one launch (start us, length us, event | category | flops | bytes accessed | tf_op | source)
XLA Modules:
  0.0 186.2 jit_solution(16284721852032031052)
XLA Ops:
  2.8 3.2 %collective-permute-start.5 = (bf16[128,768]{1,0:T(8,128)(2,1)S(1)}, bf16[128,768]{1,0:T(8,128)(2,1)S(1)}, u32[]{:S(2)}, u32[]{:S(2)}) collective-permute-start(bf16[128,768]{1,0:T(8,128)(2,1)S(1)} %get-tuple-element.55.a_ref), channel_id=1, source_target_pairs={{8,0},{12,4},{0,8},{4,12},{9,1},{13,5},{1,9},{5,13},{10,2},{14,6},... | collective-permute-start | bytes 589832 | tf_op jit(solution)/shard_map/ppermute | solution.py:203
  6.0 3.9 %collective-permute-start.2 = (bf16[192,768]{1,0:T(8,128)(2,1)S(1)}, bf16[192,768]{1,0:T(8,128)(2,1)S(1)}, u32[]{:S(2)}, u32[]{:S(2)}) collective-permute-start(bf16[192,768]{1,0:T(8,128)(2,1)S(1)} %get-tuple-element.49.a_ref), channel_id=1, source_target_pairs={{2,0},{3,1},{0,2},{1,3},{6,4},{7,5},{4,6},{5,7},{10,8},{11,9},{8,1... | collective-permute-start | bytes 884744 | tf_op jit(solution)/shard_map/ppermute | solution.py:203
  10.9 2.2 %collective-permute-start = (bf16[192,768]{1,0:T(8,128)(2,1)S(1)}, bf16[192,768]{1,0:T(8,128)(2,1)S(1)}, u32[]{:S(2)}, u32[]{:S(2)}) collective-permute-start(bf16[192,768]{1,0:T(8,128)(2,1)S(1)} %get-tuple-element.49.a_ref), channel_id=1, source_target_pairs={{1,0},{2,1},{3,2},{0,3},{5,4},{6,5},{7,6},{4,7},{9,8},{10,9},{11,1... | collective-permute-start | bytes 884744 | tf_op jit(solution)/shard_map/ppermute | solution.py:203
  14.1 4.7 %all-to-all-start = ((bf16[8,96,256]{2,1,0:T(8,128)(2,1)}), bf16[8,96,256]{2,1,0:T(8,128)(2,1)S(1)}, u32[]{:S(2)}, u32[]{:S(2)}) async-start(bf16[8,96,256]{2,1,0:T(8,128)(2,1)} %bitcast.24), calls=%async_computation | async-start | bytes 786432 | tf_op jit(solution)/shard_map/all_to_all | solution.py:225
  19.5 2.6 %collective-permute-start.3 = (bf16[128,768]{1,0:T(8,128)(2,1)S(1)}, bf16[128,768]{1,0:T(8,128)(2,1)S(1)}, u32[]{:S(2)}, u32[]{:S(2)}) collective-permute-start(bf16[128,768]{1,0:T(8,128)(2,1)S(1)} %get-tuple-element.55.a_ref), channel_id=1, source_target_pairs={{4,0},{8,4},{12,8},{0,12},{5,1},{9,5},{13,9},{1,13},{6,2},{10,6},{... | collective-permute-start | bytes 589832 | tf_op jit(solution)/shard_map/ppermute | solution.py:203
  22.2 5.1 %collective-permute-done.4.c_ref = bf16[128,768]{1,0:T(8,128)(2,1)S(1)} collective-permute-done((bf16[128,768]{1,0:T(8,128)(2,1)S(1)}, bf16[128,768]{1,0:T(8,128)(2,1)S(1)}, u32[]{:S(2)}, u32[]{:S(2)}) %collective-permute-start.4) | collective-permute-done | bytes 196640 | tf_op jit(solution)/shard_map/ppermute | solution.py:203
  29.8 2.1 %collective-permute-start.10 = (bf16[256,768]{1,0:T(8,128)(2,1)}, bf16[256,768]{1,0:T(8,128)(2,1)}, u32[]{:S(2)}, u32[]{:S(2)}) collective-permute-start(bf16[256,768]{1,0:T(8,128)(2,1)} %get-tuple-element.60.refs_17_), channel_id=1, source_target_pairs={{3,0},{0,1},{1,2},{2,3},{7,4},{4,5},{5,6},{6,7},{11,8},{8,9},{9,10... | collective-permute-start | bytes 1179656 | tf_op jit(solution)/shard_map/ppermute | solution.py:203
  31.9 3.2 %collective-permute-start.17 = (bf16[2,96,256]{2,1,0:T(8,128)(2,1)S(1)}, bf16[2,96,256]{2,1,0:T(8,128)(2,1)S(1)}, u32[]{:S(2)}, u32[]{:S(2)}) collective-permute-start(bf16[2,96,256]{2,1,0:T(8,128)(2,1)S(1)} %pad_maximum_fusion.refs_5_), channel_id=1, source_target_pairs={{64,0},{96,32},{0,64},{32,96},{65,1},{97,33},{1,65},{33,97},{66,2}... | collective-permute-start | bytes 294920 | tf_op jit(solution)/shard_map/ppermute | solution.py:203
  36.1 3.0 %collective-permute-start.7 = (bf16[384,768]{1,0:T(8,128)(2,1)S(1)}, bf16[384,768]{1,0:T(8,128)(2,1)S(1)}, u32[]{:S(2)}, u32[]{:S(2)}) collective-permute-start(bf16[384,768]{1,0:T(8,128)(2,1)S(1)} %get-tuple-element.53.refs_8_), channel_id=1, source_target_pairs={{4,0},{8,4},{12,8},{0,12},{5,1},{9,5},{13,9},{1,13},{6,2},{10,6},{... | collective-permute-start | bytes 1769480 | tf_op jit(solution)/shard_map/ppermute | solution.py:203
  40.7 2.5 %collective-permute-start.11 = (bf16[8,96,256]{2,1,0:T(8,128)(2,1)S(1)}, bf16[8,96,256]{2,1,0:T(8,128)(2,1)S(1)}, u32[]{:S(2)}, u32[]{:S(2)}) collective-permute-start(bf16[8,96,256]{2,1,0:T(8,128)(2,1)S(1)} %all-to-all-done.refs_0_), channel_id=1, source_target_pairs={{1,0},{2,1},{3,2},{0,3},{5,4},{6,5},{7,6},{4,7},{9,8},{10,9},{11,1... | collective-permute-start | bytes 1179656 | tf_op jit(solution)/shard_map/ppermute | solution.py:203
  44.2 9.0 %collective-permute-done.12.refs_2_ = bf16[8,96,256]{2,1,0:T(8,128)(2,1)S(1)} collective-permute-done((bf16[8,96,256]{2,1,0:T(8,128)(2,1)S(1)}, bf16[8,96,256]{2,1,0:T(8,128)(2,1)S(1)}, u32[]{:S(2)}, u32[]{:S(2)}) %collective-permute-start.12) | collective-permute-done | bytes 393248 | tf_op jit(solution)/shard_map/ppermute | solution.py:203
  53.2 3.2 %collective-permute-start.21 = (bf16[384,768]{1,0:T(8,128)(2,1)S(1)}, bf16[384,768]{1,0:T(8,128)(2,1)}, u32[]{:S(2)}, u32[]{:S(2)}) collective-permute-start(bf16[384,768]{1,0:T(8,128)(2,1)S(1)} %get-tuple-element.54.refs_9_), channel_id=1, source_target_pairs={{4,0},{8,4},{12,8},{0,12},{5,1},{9,5},{13,9},{1,13},{6,2},{10,6},{... | collective-permute-start | bytes 1769480 | tf_op jit(solution)/shard_map/ppermute | solution.py:203
  57.0 2.7 %collective-permute-start.15 = (bf16[2,96,256]{2,1,0:T(8,128)(2,1)S(1)}, bf16[2,96,256]{2,1,0:T(8,128)(2,1)S(1)}, u32[]{:S(2)}, u32[]{:S(2)}) collective-permute-start(bf16[2,96,256]{2,1,0:T(8,128)(2,1)S(1)} %pad_maximum_fusion.refs_5_), channel_id=1, source_target_pairs={{32,0},{64,32},{96,64},{0,96},{33,1},{65,33},{97,65},{1,97},{34,2}... | collective-permute-start | bytes 294920 | tf_op jit(solution)/shard_map/ppermute | solution.py:203
  59.7 10.2 %all_to_all.25.refs_9_.refs_4_.refs_5_ = s32[16,4,128]{2,1,0:T(4,128)S(1)} all-to-all(s32[16,4,128]{2,1,0:T(4,128)S(1)} %broadcast_in_dim.6), channel_id=1, replica_groups=mesh['y'=4,'c'=2,'x'=4,'z'=4] {'x','z'}, dimensions={0} | all-to-all | bytes 65536 | tf_op jit(solution)/shard_map/all_to_all | solution.py:240
  73.4 2.4 %collective-permute-start.13 = (bf16[4,96,256]{2,1,0:T(8,128)(2,1)S(1)}, bf16[4,96,256]{2,1,0:T(8,128)(2,1)S(1)}, u32[]{:S(2)}, u32[]{:S(2)}) collective-permute-start(bf16[4,96,256]{2,1,0:T(8,128)(2,1)S(1)} %slice.6), channel_id=1, source_target_pairs={{1,0},{2,1},{3,2},{0,3},{5,4},{6,5},{7,6},{4,7},{9,8},{10,9},{11,1... | collective-permute-start | bytes 589832 | tf_op jit(solution)/shard_map/ppermute | solution.py:203
  75.9 2.9 %collective-permute-done.14.refs_4_ = bf16[4,96,256]{2,1,0:T(8,128)(2,1)S(1)} collective-permute-done((bf16[4,96,256]{2,1,0:T(8,128)(2,1)S(1)}, bf16[4,96,256]{2,1,0:T(8,128)(2,1)S(1)}, u32[]{:S(2)}, u32[]{:S(2)}) %collective-permute-start.14) | collective-permute-done | bytes 196640 | tf_op jit(solution)/shard_map/ppermute | solution.py:203
  83.2 1.9 %shard_map.97 = (bf16[4,64,256]{2,1,0:T(8,128)(2,1)S(1)}, bf16[4,64,256]{2,1,0:T(8,128)(2,1)S(1)}, bf16[4,64,256]{2,1,0:T(8,128)(2,1)S(1)}, bf16[4,64,256]{2,1,0:T(8,128)(2,1)}) custom-call(bf16[8,96,256]{2,1,0:T(8,128)(2,1)S(1)} %all-to-all-done.refs_0_, bf16[8,96,256]{2,1,0:T(8,128)(2,1)S(1)} %collective-permute-done.11.refs_1_, ...), custom_call_target="tpu_custom_call" | custom-call | flops 400000000 | bytes 3000000 | tf_op jit(solution)/shard_map/pallas_call | solution.py:252
  85.7 2.4 %collective-permute-start.27 = (bf16[256,768]{1,0:T(8,128)(2,1)}, bf16[256,768]{1,0:T(8,128)(2,1)}, u32[]{:S(2)}, u32[]{:S(2)}) collective-permute-start(bf16[256,768]{1,0:T(8,128)(2,1)} %collective-permute-done.9.refs_18_), channel_id=1, source_target_pairs={{1,0},{2,1},{3,2},{0,3},{5,4},{6,5},{7,6},{4,7},{9,8},{10,9},{11,1... | collective-permute-start | bytes 1179656 | tf_op jit(solution)/shard_map/ppermute | solution.py:203
  88.1 5.2 %collective-permute-done.18.refs_1_ = bf16[4,64,256]{2,1,0:T(8,128)(2,1)S(1)} collective-permute-done((bf16[4,64,256]{2,1,0:T(8,128)(2,1)S(1)}, bf16[4,64,256]{2,1,0:T(8,128)(2,1)S(1)}, u32[]{:S(2)}, u32[]{:S(2)}) %collective-permute-start.18) | collective-permute-done | bytes 131104 | tf_op jit(solution)/shard_map/ppermute | solution.py:203
  93.3 5.0 %collective-permute-done.19.refs_2_ = bf16[4,64,256]{2,1,0:T(8,128)(2,1)S(1)} collective-permute-done((bf16[4,64,256]{2,1,0:T(8,128)(2,1)S(1)}, bf16[4,64,256]{2,1,0:T(8,128)(2,1)S(1)}, u32[]{:S(2)}, u32[]{:S(2)}) %collective-permute-start.19) | collective-permute-done | bytes 131104 | tf_op jit(solution)/shard_map/ppermute | solution.py:203
  99.7 6.1 %collective-permute-done.20.refs_3_ = bf16[4,64,256]{2,1,0:T(8,128)(2,1)} collective-permute-done((bf16[4,64,256]{2,1,0:T(8,128)(2,1)}, bf16[4,64,256]{2,1,0:T(8,128)(2,1)}, u32[]{:S(2)}, u32[]{:S(2)}) %collective-permute-start.20) | collective-permute-done | bytes 131104 | tf_op jit(solution)/shard_map/ppermute | solution.py:203
  108.7 13.4 %shard_map.98 = (bf16[16,64,256]{2,1,0:T(8,128)(2,1)S(1)}, bf16[80,128]{1,0:T(8,128)(2,1)S(1)}, bf16[4,64,256]{2,1,0:T(8,128)(2,1)S(1)}, bf16[4,64,256]{2,1,0:T(...) custom-call(bf16[4,64,256]{2,1,0:T(8,128)(2,1)S(1)} %get-tuple-element.66.refs_0_, ...), custom_call_target="tpu_custom_call" | custom-call | flops 1600000000 | bytes 10000000 | tf_op jit(solution)/shard_map/pallas_call | solution.py:261
  127.0 4.6 %all-to-all-start.2 = ((bf16[16,128,128]{2,1,0:T(8,128)(2,1)}), bf16[16,128,128]{2,1,0:T(8,128)(2,1)S(1)}, u32[]{:S(2)}, u32[]{:S(2)}) async-start(bf16[16,128,128]{2,1,0:T(8,128)(2,1)} %shard_map.100), calls=%async_computation.2 | async-start | bytes 1048576 | tf_op jit(solution)/shard_map/all_to_all | solution.py:279
  131.6 2.0 %collective-permute-start.29 = (bf16[4,64,256]{2,1,0:T(8,128)(2,1)S(1)}, bf16[4,64,256]{2,1,0:T(8,128)(2,1)S(1)}, u32[]{:S(2)}, u32[]{:S(2)}) collective-permute-start(bf16[4,64,256]{2,1,0:T(8,128)(2,1)S(1)} %copy-done.24), channel_id=1, source_target_pairs={{12,0},{0,4},{4,8},{8,12},{13,1},{1,5},{5,9},{9,13},{14,2},{2,6},{... | collective-permute-start | bytes 393224 | tf_op jit(solution)/shard_map/ppermute | solution.py:203
  134.9 2.2 %collective-permute-start.31 = (bf16[4,64,256]{2,1,0:T(8,128)(2,1)S(1)}, bf16[4,64,256]{2,1,0:T(8,128)(2,1)S(1)}, u32[]{:S(2)}, u32[]{:S(2)}) collective-permute-start(bf16[4,64,256]{2,1,0:T(8,128)(2,1)S(1)} %copy-done.20), channel_id=1, source_target_pairs={{8,0},{12,4},{0,8},{4,12},{9,1},{13,5},{1,9},{5,13},{10,2},{14,6},... | collective-permute-start | bytes 393224 | tf_op jit(solution)/shard_map/ppermute | solution.py:203
  137.2 4.2 %collective-permute-start.35 = (bf16[80,128]{1,0:T(8,128)(2,1)S(1)}, bf16[80,128]{1,0:T(8,128)(2,1)S(1)}, u32[]{:S(2)}, u32[]{:S(2)}) collective-permute-start(bf16[80,128]{1,0:T(8,128)(2,1)S(1)} %add_convert_fusion.s0_ref), channel_id=1, source_target_pairs={{64,0},{96,32},{0,64},{32,96},{65,1},{97,33},{1,65},{33,97},{66,2}... | collective-permute-start | bytes 61448 | tf_op jit(solution)/shard_map/ppermute | solution.py:203
  142.9 1.7 collective-permute-done.29.refs_6_
  144.6 4.8 %collective-permute-start.33 = (bf16[80,128]{1,0:T(8,128)(2,1)S(1)}, bf16[80,128]{1,0:T(8,128)(2,1)S(1)}, u32[]{:S(2)}, u32[]{:S(2)}) collective-permute-start(bf16[80,128]{1,0:T(8,128)(2,1)S(1)} %add_convert_fusion.s0_ref), channel_id=1, source_target_pairs={{32,0},{64,32},{96,64},{0,96},{33,1},{65,33},{97,65},{1,97},{34,2}... | collective-permute-start | bytes 61448 | tf_op jit(solution)/shard_map/ppermute | solution.py:203
  149.5 2.0 %shard_map.99 = bf16[8,4,48,128]{3,2,1,0:T(8,128)(2,1)S(1)} custom-call(bf16[8,96,256]{2,1,0:T(8,128)(2,1)S(1)} %all-to-all-done.refs_0_, bf16[8,96,256]{2,1,0:T(8,128)(2,1)S(1)} %collective-permute-done.11.refs_1_, bf16[8,96,256]{2,1,0:T(8,128)(2,1)S(1)} %collective-permute-done.12.refs_2_, bf16[4,96,256]{2,1,0:T(8,128)(2,1)S(1)} %collective-permute-done.13.refs_3_, ...), custom_call_target="tpu_custom_call" | custom-call | flops 400000000 | bytes 3000000 | tf_op jit(solution)/shard_map/pallas_call | solution.py:281
  151.6 17.0 %all_to_all.26.part_ref = bf16[32,48,128]{2,1,0:T(8,128)(2,1)S(1)} all-to-all(bf16[32,48,128]{2,1,0:T(8,128)(2,1)S(1)} %bitcast.25), channel_id=1, replica_groups=mesh['y'=4,'c'=2,'x'=4,'z'=4] {'y','c','x'}, dimensions={0} | all-to-all | bytes 786432 | tf_op jit(solution)/shard_map/all_to_all | solution.py:289
  169.5 3.6 %all-to-all-start.4 = ((bf16[16,128,128]{2,1,0:T(8,128)(2,1)}), bf16[16,128,128]{2,1,0:T(8,128)(2,1)S(1)}, u32[]{:S(2)}, u32[]{:S(2)}) async-start(bf16[16,128,128]{2,1,0:T(8,128)(2,1)} %shard_map.102), calls=%async_computation.4 | async-start | bytes 1048576 | tf_op jit(solution)/shard_map/all_to_all | solution.py:291
  174.1 11.0 %all-to-all-done.4.in_ref = bf16[16,128,128]{2,1,0:T(8,128)(2,1)S(1)} async-done(((bf16[16,128,128]{2,1,0:T(8,128)(2,1)}), bf16[16,128,128]{2,1,0:T(8,128)(2,1)S(1)}, u32[]{:S(2)}, u32[]{:S(2)}) %all-to-all-start.4) | async-done | bytes 524320 | tf_op jit(solution)/shard_map/all_to_all | solution.py:291
  (133 shorter events, 35.2 us)
Async XLA Ops:
  2.8 16.7 %collective-permute-start.5 = (bf16[128,768]{1,0:T(8,128)(2,1)S(1)}, bf16[128,768]{1,0:T(8,128)(2,1)S(1)}, u32[]{:S(2)}, u32[]{:S(2)}) collective-permute-start(bf16[128,768]{1,0:T(8,128)(2,1)S(1)} %get-tuple-element.55.a_ref), channel_id=1, source_target_pairs={{8,0},{12,4},{0,8},{4,12},{9,1},{13,5},{1,9},{5,13},{10,2},{14,6},... | collective-permute-start | bytes 589832 | tf_op jit(solution)/shard_map/ppermute | solution.py:203
  6.0 21.4 %collective-permute-start.2 = (bf16[192,768]{1,0:T(8,128)(2,1)S(1)}, bf16[192,768]{1,0:T(8,128)(2,1)S(1)}, u32[]{:S(2)}, u32[]{:S(2)}) collective-permute-start(bf16[192,768]{1,0:T(8,128)(2,1)S(1)} %get-tuple-element.49.a_ref), channel_id=1, source_target_pairs={{2,0},{3,1},{0,2},{1,3},{6,4},{7,5},{4,6},{5,7},{10,8},{11,9},{8,1... | collective-permute-start | bytes 884744 | tf_op jit(solution)/shard_map/ppermute | solution.py:203
  9.8 17.5 %collective-permute-start.1 = (bf16[192,768]{1,0:T(8,128)(2,1)S(1)}, bf16[192,768]{1,0:T(8,128)(2,1)S(1)}, u32[]{:S(2)}, u32[]{:S(2)}) collective-permute-start(bf16[192,768]{1,0:T(8,128)(2,1)S(1)} %get-tuple-element.49.a_ref), channel_id=1, source_target_pairs={{3,0},{0,1},{1,2},{2,3},{7,4},{4,5},{5,6},{6,7},{11,8},{8,9},{9,10... | collective-permute-start | bytes 884744 | tf_op jit(solution)/shard_map/ppermute | solution.py:203
  10.9 17.2 %collective-permute-start = (bf16[192,768]{1,0:T(8,128)(2,1)S(1)}, bf16[192,768]{1,0:T(8,128)(2,1)S(1)}, u32[]{:S(2)}, u32[]{:S(2)}) collective-permute-start(bf16[192,768]{1,0:T(8,128)(2,1)S(1)} %get-tuple-element.49.a_ref), channel_id=1, source_target_pairs={{1,0},{2,1},{3,2},{0,3},{5,4},{6,5},{7,6},{4,7},{9,8},{10,9},{11,1... | collective-permute-start | bytes 884744 | tf_op jit(solution)/shard_map/ppermute | solution.py:203
  14.1 25.7 %all-to-all-start = ((bf16[8,96,256]{2,1,0:T(8,128)(2,1)}), bf16[8,96,256]{2,1,0:T(8,128)(2,1)S(1)}, u32[]{:S(2)}, u32[]{:S(2)}) async-start(bf16[8,96,256]{2,1,0:T(8,128)(2,1)} %bitcast.24), calls=%async_computation | async-start | bytes 786432 | tf_op jit(solution)/shard_map/all_to_all | solution.py:225
  18.8 8.5 %collective-permute-start.4 = (bf16[128,768]{1,0:T(8,128)(2,1)S(1)}, bf16[128,768]{1,0:T(8,128)(2,1)S(1)}, u32[]{:S(2)}, u32[]{:S(2)}) collective-permute-start(bf16[128,768]{1,0:T(8,128)(2,1)S(1)} %get-tuple-element.55.a_ref), channel_id=1, source_target_pairs={{12,0},{0,4},{4,8},{8,12},{13,1},{1,5},{5,9},{9,13},{14,2},{2,6},{... | collective-permute-start | bytes 589832 | tf_op jit(solution)/shard_map/ppermute | solution.py:203
  19.5 7.9 %collective-permute-start.3 = (bf16[128,768]{1,0:T(8,128)(2,1)S(1)}, bf16[128,768]{1,0:T(8,128)(2,1)S(1)}, u32[]{:S(2)}, u32[]{:S(2)}) collective-permute-start(bf16[128,768]{1,0:T(8,128)(2,1)S(1)} %get-tuple-element.55.a_ref), channel_id=1, source_target_pairs={{4,0},{8,4},{12,8},{0,12},{5,1},{9,5},{13,9},{1,13},{6,2},{10,6},{... | collective-permute-start | bytes 589832 | tf_op jit(solution)/shard_map/ppermute | solution.py:203
  29.7 11.0 %collective-permute-start.9 = (bf16[256,768]{1,0:T(8,128)(2,1)}, bf16[256,768]{1,0:T(8,128)(2,1)}, u32[]{:S(2)}, u32[]{:S(2)}) collective-permute-start(bf16[256,768]{1,0:T(8,128)(2,1)} %get-tuple-element.59.refs_16_), channel_id=1, source_target_pairs={{1,0},{2,1},{3,2},{0,3},{5,4},{6,5},{7,6},{4,7},{9,8},{10,9},{11,1... | collective-permute-start | bytes 1179656 | tf_op jit(solution)/shard_map/ppermute | solution.py:203
  29.8 13.4 %collective-permute-start.10 = (bf16[256,768]{1,0:T(8,128)(2,1)}, bf16[256,768]{1,0:T(8,128)(2,1)}, u32[]{:S(2)}, u32[]{:S(2)}) collective-permute-start(bf16[256,768]{1,0:T(8,128)(2,1)} %get-tuple-element.60.refs_17_), channel_id=1, source_target_pairs={{3,0},{0,1},{1,2},{2,3},{7,4},{4,5},{5,6},{6,7},{11,8},{8,9},{9,10... | collective-permute-start | bytes 1179656 | tf_op jit(solution)/shard_map/ppermute | solution.py:203
  31.9 8.0 %collective-permute-start.17 = (bf16[2,96,256]{2,1,0:T(8,128)(2,1)S(1)}, bf16[2,96,256]{2,1,0:T(8,128)(2,1)S(1)}, u32[]{:S(2)}, u32[]{:S(2)}) collective-permute-start(bf16[2,96,256]{2,1,0:T(8,128)(2,1)S(1)} %pad_maximum_fusion.refs_5_), channel_id=1, source_target_pairs={{64,0},{96,32},{0,64},{32,96},{65,1},{97,33},{1,65},{33,97},{66,2}... | collective-permute-start | bytes 294920 | tf_op jit(solution)/shard_map/ppermute | solution.py:203
  36.1 20.3 %collective-permute-start.7 = (bf16[384,768]{1,0:T(8,128)(2,1)S(1)}, bf16[384,768]{1,0:T(8,128)(2,1)S(1)}, u32[]{:S(2)}, u32[]{:S(2)}) collective-permute-start(bf16[384,768]{1,0:T(8,128)(2,1)S(1)} %get-tuple-element.53.refs_8_), channel_id=1, source_target_pairs={{4,0},{8,4},{12,8},{0,12},{5,1},{9,5},{13,9},{1,13},{6,2},{10,6},{... | collective-permute-start | bytes 1769480 | tf_op jit(solution)/shard_map/ppermute | solution.py:203
  39.2 17.9 %collective-permute-start.8 = (bf16[384,768]{1,0:T(8,128)(2,1)S(1)}, bf16[384,768]{1,0:T(8,128)(2,1)}, u32[]{:S(2)}, u32[]{:S(2)}) collective-permute-start(bf16[384,768]{1,0:T(8,128)(2,1)S(1)} %get-tuple-element.54.refs_9_), channel_id=1, source_target_pairs={{12,0},{0,4},{4,8},{8,12},{13,1},{1,5},{5,9},{9,13},{14,2},{2,6},{... | collective-permute-start | bytes 1769480 | tf_op jit(solution)/shard_map/ppermute | solution.py:203
  39.9 13.3 %collective-permute-start.12 = (bf16[8,96,256]{2,1,0:T(8,128)(2,1)S(1)}, bf16[8,96,256]{2,1,0:T(8,128)(2,1)S(1)}, u32[]{:S(2)}, u32[]{:S(2)}) collective-permute-start(bf16[8,96,256]{2,1,0:T(8,128)(2,1)S(1)} %all-to-all-done.refs_0_), channel_id=1, source_target_pairs={{3,0},{0,1},{1,2},{2,3},{7,4},{4,5},{5,6},{6,7},{11,8},{8,9},{9,10... | collective-permute-start | bytes 1179656 | tf_op jit(solution)/shard_map/ppermute | solution.py:203
  40.7 12.5 %collective-permute-start.11 = (bf16[8,96,256]{2,1,0:T(8,128)(2,1)S(1)}, bf16[8,96,256]{2,1,0:T(8,128)(2,1)S(1)}, u32[]{:S(2)}, u32[]{:S(2)}) collective-permute-start(bf16[8,96,256]{2,1,0:T(8,128)(2,1)S(1)} %all-to-all-done.refs_0_), channel_id=1, source_target_pairs={{1,0},{2,1},{3,2},{0,3},{5,4},{6,5},{7,6},{4,7},{9,8},{10,9},{11,1... | collective-permute-start | bytes 1179656 | tf_op jit(solution)/shard_map/ppermute | solution.py:203
  43.2 29.5 %collective-permute-start.26 = (bf16[256,768]{1,0:T(8,128)(2,1)}, bf16[256,768]{1,0:T(8,128)(2,1)S(1)}, u32[]{:S(2)}, u32[]{:S(2)}) collective-permute-start(bf16[256,768]{1,0:T(8,128)(2,1)} %get-tuple-element.59.refs_16_), channel_id=1, source_target_pairs={{3,0},{0,1},{1,2},{2,3},{7,4},{4,5},{5,6},{6,7},{11,8},{8,9},{9,10... | collective-permute-start | bytes 1179656 | tf_op jit(solution)/shard_map/ppermute | solution.py:203
  53.2 32.5 %collective-permute-start.22 = (bf16[384,768]{1,0:T(8,128)(2,1)S(1)}, bf16[384,768]{1,0:T(8,128)(2,1)}, u32[]{:S(2)}, u32[]{:S(2)}) collective-permute-start(bf16[384,768]{1,0:T(8,128)(2,1)S(1)} %get-tuple-element.53.refs_8_), channel_id=1, source_target_pairs={{12,0},{0,4},{4,8},{8,12},{13,1},{1,5},{5,9},{9,13},{14,2},{2,6},{... | collective-permute-start | bytes 1769480 | tf_op jit(solution)/shard_map/ppermute | solution.py:203
  53.2 34.9 %collective-permute-start.21 = (bf16[384,768]{1,0:T(8,128)(2,1)S(1)}, bf16[384,768]{1,0:T(8,128)(2,1)}, u32[]{:S(2)}, u32[]{:S(2)}) collective-permute-start(bf16[384,768]{1,0:T(8,128)(2,1)S(1)} %get-tuple-element.54.refs_9_), channel_id=1, source_target_pairs={{4,0},{8,4},{12,8},{0,12},{5,1},{9,5},{13,9},{1,13},{6,2},{10,6},{... | collective-permute-start | bytes 1769480 | tf_op jit(solution)/shard_map/ppermute | solution.py:203
  56.5 13.4 %collective-permute-start.16 = (bf16[2,96,256]{2,1,0:T(8,128)(2,1)S(1)}, bf16[2,96,256]{2,1,0:T(8,128)(2,1)S(1)}, u32[]{:S(2)}, u32[]{:S(2)}) collective-permute-start(bf16[2,96,256]{2,1,0:T(8,128)(2,1)S(1)} %pad_maximum_fusion.refs_5_), channel_id=1, source_target_pairs={{96,0},{0,32},{32,64},{64,96},{97,1},{1,33},{33,65},{65,97},{98,2}... | collective-permute-start | bytes 294920 | tf_op jit(solution)/shard_map/ppermute | solution.py:203
  57.0 14.7 %collective-permute-start.15 = (bf16[2,96,256]{2,1,0:T(8,128)(2,1)S(1)}, bf16[2,96,256]{2,1,0:T(8,128)(2,1)S(1)}, u32[]{:S(2)}, u32[]{:S(2)}) collective-permute-start(bf16[2,96,256]{2,1,0:T(8,128)(2,1)S(1)} %pad_maximum_fusion.refs_5_), channel_id=1, source_target_pairs={{32,0},{64,32},{96,64},{0,96},{33,1},{65,33},{97,65},{1,97},{34,2}... | collective-permute-start | bytes 294920 | tf_op jit(solution)/shard_map/ppermute | solution.py:203
  70.5 14.5 %collective-permute-start.25 = (bf16[256,768]{1,0:T(8,128)(2,1)}, bf16[256,768]{1,0:T(8,128)(2,1)}, u32[]{:S(2)}, u32[]{:S(2)}) collective-permute-start(bf16[256,768]{1,0:T(8,128)(2,1)} %get-tuple-element.60.refs_17_), channel_id=1, source_target_pairs={{1,0},{2,1},{3,2},{0,3},{5,4},{6,5},{7,6},{4,7},{9,8},{10,9},{11,1... | collective-permute-start | bytes 1179656 | tf_op jit(solution)/shard_map/ppermute | solution.py:203
  78.7 27.0 %collective-permute-start.23 = (bf16[384,768]{1,0:T(8,128)(2,1)}, bf16[384,768]{1,0:T(8,128)(2,1)}, u32[]{:S(2)}, u32[]{:S(2)}) collective-permute-start(bf16[384,768]{1,0:T(8,128)(2,1)} %copy-done.2), channel_id=1, source_target_pairs={{4,0},{8,4},{12,8},{0,12},{5,1},{9,5},{13,9},{1,13},{6,2},{10,6},{... | collective-permute-start | bytes 1769480 | tf_op jit(solution)/shard_map/ppermute | solution.py:203
  80.6 25.1 %collective-permute-start.24 = (bf16[384,768]{1,0:T(8,128)(2,1)}, bf16[384,768]{1,0:T(8,128)(2,1)}, u32[]{:S(2)}, u32[]{:S(2)}) collective-permute-start(bf16[384,768]{1,0:T(8,128)(2,1)} %collective-permute-done.8.refs_13_), channel_id=1, source_target_pairs={{12,0},{0,4},{4,8},{8,12},{13,1},{1,5},{5,9},{9,13},{14,2},{2,6},{... | collective-permute-start | bytes 1769480 | tf_op jit(solution)/shard_map/ppermute | solution.py:203
  85.1 8.3 %collective-permute-start.18 = (bf16[4,64,256]{2,1,0:T(8,128)(2,1)S(1)}, bf16[4,64,256]{2,1,0:T(8,128)(2,1)S(1)}, u32[]{:S(2)}, u32[]{:S(2)}) collective-permute-start(bf16[4,64,256]{2,1,0:T(8,128)(2,1)S(1)} %get-tuple-element.67), channel_id=1, source_target_pairs={{12,0},{0,4},{4,8},{8,12},{13,1},{1,5},{5,9},{9,13},{14,2},{2,6},{... | collective-permute-start | bytes 393224 | tf_op jit(solution)/shard_map/ppermute | solution.py:203
  85.7 20.1 %collective-permute-start.27 = (bf16[256,768]{1,0:T(8,128)(2,1)}, bf16[256,768]{1,0:T(8,128)(2,1)}, u32[]{:S(2)}, u32[]{:S(2)}) collective-permute-start(bf16[256,768]{1,0:T(8,128)(2,1)} %collective-permute-done.9.refs_18_), channel_id=1, source_target_pairs={{1,0},{2,1},{3,2},{0,3},{5,4},{6,5},{7,6},{4,7},{9,8},{10,9},{11,1... | collective-permute-start | bytes 1179656 | tf_op jit(solution)/shard_map/ppermute | solution.py:203
  88.1 17.7 %collective-permute-start.28 = (bf16[256,768]{1,0:T(8,128)(2,1)}, bf16[256,768]{1,0:T(8,128)(2,1)}, u32[]{:S(2)}, u32[]{:S(2)}) collective-permute-start(bf16[256,768]{1,0:T(8,128)(2,1)} %collective-permute-done.10.refs_21_), channel_id=1, source_target_pairs={{3,0},{0,1},{1,2},{2,3},{7,4},{4,5},{5,6},{6,7},{11,8},{8,9},{9,10... | collective-permute-start | bytes 1179656 | tf_op jit(solution)/shard_map/ppermute | solution.py:203
  127.0 24.6 %all-to-all-start.2 = ((bf16[16,128,128]{2,1,0:T(8,128)(2,1)}), bf16[16,128,128]{2,1,0:T(8,128)(2,1)S(1)}, u32[]{:S(2)}, u32[]{:S(2)}) async-start(bf16[16,128,128]{2,1,0:T(8,128)(2,1)} %shard_map.100), calls=%async_computation.2 | async-start | bytes 1048576 | tf_op jit(solution)/shard_map/all_to_all | solution.py:279
  131.6 13.0 %collective-permute-start.29 = (bf16[4,64,256]{2,1,0:T(8,128)(2,1)S(1)}, bf16[4,64,256]{2,1,0:T(8,128)(2,1)S(1)}, u32[]{:S(2)}, u32[]{:S(2)}) collective-permute-start(bf16[4,64,256]{2,1,0:T(8,128)(2,1)S(1)} %copy-done.24), channel_id=1, source_target_pairs={{12,0},{0,4},{4,8},{8,12},{13,1},{1,5},{5,9},{9,13},{14,2},{2,6},{... | collective-permute-start | bytes 393224 | tf_op jit(solution)/shard_map/ppermute | solution.py:203
  133.6 15.9 %collective-permute-start.30 = (bf16[4,64,256]{2,1,0:T(8,128)(2,1)S(1)}, bf16[4,64,256]{2,1,0:T(8,128)(2,1)S(1)}, u32[]{:S(2)}, u32[]{:S(2)}) collective-permute-start(bf16[4,64,256]{2,1,0:T(8,128)(2,1)S(1)} %copy-done.22), channel_id=1, source_target_pairs={{4,0},{8,4},{12,8},{0,12},{5,1},{9,5},{13,9},{1,13},{6,2},{10,6},{... | collective-permute-start | bytes 393224 | tf_op jit(solution)/shard_map/ppermute | solution.py:203
  134.9 14.6 %collective-permute-start.31 = (bf16[4,64,256]{2,1,0:T(8,128)(2,1)S(1)}, bf16[4,64,256]{2,1,0:T(8,128)(2,1)S(1)}, u32[]{:S(2)}, u32[]{:S(2)}) collective-permute-start(bf16[4,64,256]{2,1,0:T(8,128)(2,1)S(1)} %copy-done.20), channel_id=1, source_target_pairs={{8,0},{12,4},{0,8},{4,12},{9,1},{13,5},{1,9},{5,13},{10,2},{14,6},... | collective-permute-start | bytes 393224 | tf_op jit(solution)/shard_map/ppermute | solution.py:203
  137.2 14.4 %collective-permute-start.35 = (bf16[80,128]{1,0:T(8,128)(2,1)S(1)}, bf16[80,128]{1,0:T(8,128)(2,1)S(1)}, u32[]{:S(2)}, u32[]{:S(2)}) collective-permute-start(bf16[80,128]{1,0:T(8,128)(2,1)S(1)} %add_convert_fusion.s0_ref), channel_id=1, source_target_pairs={{64,0},{96,32},{0,64},{32,96},{65,1},{97,33},{1,65},{33,97},{66,2}... | collective-permute-start | bytes 61448 | tf_op jit(solution)/shard_map/ppermute | solution.py:203
  141.4 10.2 %collective-permute-start.34 = (bf16[80,128]{1,0:T(8,128)(2,1)S(1)}, bf16[80,128]{1,0:T(8,128)(2,1)S(1)}, u32[]{:S(2)}, u32[]{:S(2)}) collective-permute-start(bf16[80,128]{1,0:T(8,128)(2,1)S(1)} %add_convert_fusion.s0_ref), channel_id=1, source_target_pairs={{96,0},{0,32},{32,64},{64,96},{97,1},{1,33},{33,65},{65,97},{98,2}... | collective-permute-start | bytes 61448 | tf_op jit(solution)/shard_map/ppermute | solution.py:203
  169.5 15.6 %all-to-all-start.4 = ((bf16[16,128,128]{2,1,0:T(8,128)(2,1)}), bf16[16,128,128]{2,1,0:T(8,128)(2,1)S(1)}, u32[]{:S(2)}, u32[]{:S(2)}) async-start(bf16[16,128,128]{2,1,0:T(8,128)(2,1)} %shard_map.102), calls=%async_computation.4 | async-start | bytes 1048576 | tf_op jit(solution)/shard_map/all_to_all | solution.py:291
  (36 other events, 245.2 us)

commit v6 on v5

v6 whole, which is shorter than its diff:
```python
import jax
import jax.numpy as jnp
from jax import lax
from jax.experimental import pallas as pl
from jax.experimental.pallas import tpu as pltpu
from jax.sharding import Mesh
from jax.sharding import PartitionSpec as P

BF = jnp.bfloat16
F32 = jnp.float32
I32 = jnp.int32
VMEM = pl.BlockSpec(memory_space=pltpu.VMEM)
SMEM = pl.BlockSpec(memory_space=pltpu.SMEM)
MIB = 1024 * 1024
RING = (0, 1, -1, 2)
NT = (((1,), (1,)), ((), ()))


def dot(a, b, dims=(((1,), (0,)), ((), ()))):
    return lax.dot_general(a, b, dims, preferred_element_type=F32)


def halves(a, b):
    low = lax.broadcasted_iota(I32, a.shape, 1) < 64
    return jnp.where(low, a, pltpu.roll(b, 64, 1)), jnp.where(low, pltpu.roll(a, 64, 1), b)


def owner(block):
    return (block % 4) * 4 + block // 4


def mask_kernel(mask_ref, up_ref, deg_ref, links_ref, out_ref):
    for b, at in enumerate((0, 192)):
        for k in range(6):
            out_ref[at : at + 128, k * 128 : k * 128 + 128] = mask_ref[b, k].astype(F32).astype(BF)
    out_ref[128:192, 0:256] = up_ref[0:64, :]
    out_ref[128:192, 256:512] = up_ref[64:128, :]
    rest = jnp.concatenate([up_ref[128:153, :].astype(F32), jnp.zeros((39, 256), F32)], axis=0)
    out_ref[128:192, 512:768] = rest.astype(BF)
    info = []
    for b in range(2):
        degree = deg_ref[b : b + 1, :]
        info += [degree >> 5, degree & 31]
    info = jnp.concatenate(info + [links_ref[...], jnp.zeros((11, 128), I32)], axis=0)
    out_ref[320:336, :] = jnp.zeros((16, 768), BF)
    out_ref[320:336, 0:128] = info.astype(F32).astype(BF)


def block_of(m_refs, k, b):
    if k < 3:
        return m_refs[k][b * 192 : b * 192 + 128, :]
    return m_refs[3 + b][0:128, :]


def info_of(m_refs, k):
    rows = m_refs[k][320:336, 0:128] if k < 3 else m_refs[4][128:144, 0:128]
    return rows.astype(F32)


def inverse_of(info, b):
    return lax.rsqrt(info[2 * b : 2 * b + 1] * 32.0 + info[2 * b + 1 : 2 * b + 2])


def upstream_kernel(*refs):
    m_refs, at_ref, out_ref = refs[:5], refs[5], refs[6]
    for k, shift in enumerate(RING):
        info = info_of(m_refs, k)
        inv = jnp.concatenate([inverse_of(info, 0), inverse_of(info, 1)], axis=1)
        z = (at_ref[2] + shift + 4) & 3
        for c in range(3):
            rows = min(64, 160 - 64 * c)
            up = m_refs[k][128 : 128 + rows, c * 256 : c * 256 + 256]
            out_ref[z, c * 64 : c * 64 + rows] = (inv * up.astype(F32)).astype(BF)


def features_at(refs, k, f):
    return refs[k][f] if k < 3 else refs[3 + f // 4][f % 4]


def project_kernel(*refs):
    x_refs, w_refs, m_refs, at_ref = refs[:5], refs[5:9], refs[9:14], refs[14]
    out_ref, w_ref = refs[15:]
    for k, shift in enumerate(RING):
        for flip in range(2):
            f = ((at_ref[3] + shift + 4) & 3) * 2 + ((at_ref[4] + flip) & 1)
            w_ref[f] = w_refs[k][flip]
    w = w_ref[...].reshape(768, 256).astype(F32).T.astype(BF)
    for k, shift in enumerate(RING):
        info = info_of(m_refs, k)
        inv = jnp.concatenate([inverse_of(info, 0), inverse_of(info, 1)], axis=1)
        whole = jnp.concatenate([features_at(x_refs, k, f) for f in range(8)], axis=0)
        out_ref[(at_ref[2] + shift + 4) & 3] = (inv * dot(w, whole)).astype(BF)


def collect(refs, base, src_ref, at_ref):
    rows = refs[0].shape[1]
    for i, ref in enumerate(refs):
        x = (at_ref[1] + RING[min(i, 3)] + 4) & 3
        for j in range(ref.shape[0]):
            d = x * 4 + (j + 2 if i == 4 else j)
            for h in range(2):
                src_ref[2 * d + h, base : base + rows] = ref[j, :, h * 128 : h * 128 + 128]


def scalars(m_refs, stage_ref, links_ref, sem):
    rows = [info_of(m_refs, k)[4:5] for k in range(4)]
    stage_ref[...] = jnp.concatenate(rows + [jnp.zeros((4, 128), F32)], axis=0).astype(I32)
    copy = pltpu.make_async_copy(stage_ref, links_ref, sem)
    copy.start()
    copy.wait()


def spread(src_ref, links_ref, m_refs, k, b, t):
    named = [src_ref[links_ref[k, b * 6 + s]] for s in range(6)]
    total = dot(jnp.concatenate(named, axis=1), block_of(m_refs, k, b), NT)
    return src_ref[t].astype(F32) + total


def first_mix_kernel(*refs):
    s_refs, u_refs, m_refs, sw_ref, at_ref = refs[:5], refs[5:10], refs[10:15], refs[15], refs[16]
    hid_refs, back_ref, second_ref = refs[17:21], refs[21], refs[22]
    src_ref, stage_ref, links_ref, sem = refs[23:]
    scalars(m_refs, stage_ref, links_ref, sem)
    collect(s_refs, 0, src_ref, at_ref)
    collect(u_refs, 256, src_ref, at_ref)
    second = jnp.zeros((160, 256), F32)
    for k, shift in enumerate(RING):
        z = (at_ref[2] + shift + 4) & 3
        info = info_of(m_refs, k)
        for b in range(2):
            inv = inverse_of(info, b)
            lanes = slice(b * 128, b * 128 + 128)
            total = spread(src_ref, links_ref, m_refs, k, b, (at_ref[1] * 4 + z) * 2 + b)
            m = inv * total[0:256]
            s = jax.nn.sigmoid(m)
            hid = (m * s).astype(BF)
            hid_refs[k][:, lanes] = hid
            one = (inv * hid.astype(F32)).astype(BF)
            pull = total[256:416].astype(BF)
            second = second + dot(pull, one, NT)
            slope = s * (1.0 + m * (1.0 - s))
            back_ref[z, :, lanes] = (inv * inv * dot(sw_ref[...], pull) * slope).astype(BF)
    second_ref[...] = second


def second_mix_kernel(*refs):
    b_refs, m_refs, x_refs, second_ref, at_ref = refs[:5], refs[5:10], refs[10:15], refs[15], refs[16]
    out_ref, src_ref, stage_ref, links_ref, sem = refs[17:]
    scalars(m_refs, stage_ref, links_ref, sem)
    collect(b_refs, 0, src_ref, at_ref)
    rights = []
    for k, shift in enumerate(RING):
        z = (at_ref[2] + shift + 4) & 3
        info = info_of(m_refs, k)
        parts = []
        for b in range(2):
            total = spread(src_ref, links_ref, m_refs, k, b, (at_ref[1] * 4 + z) * 2 + b)
            parts.append((inverse_of(info, b) * total).astype(BF))
        rights.append(jnp.concatenate(parts, axis=1))
    seconds = []
    for p in range(2):
        m = second_ref[:, p * 128 : p * 128 + 128]
        seconds += halves(m[:80], m[80:])
    for f in range(8):
        acc = jnp.zeros((96, 256), F32)
        for k, right in enumerate(rights):
            acc = acc + dot(features_at(x_refs, k, f), right, NT)
        for p in range(2):
            g = acc[:, p * 128 : p * 128 + 128]
            for q, part in enumerate(halves(g[:48], g[48:])):
                both = jnp.concatenate([part, seconds[2 * p + q]], axis=0)
                out_ref[f, 2 * p + q] = both.astype(BF)


def add_kernel(part_ref, out_ref):
    total = part_ref[0].astype(F32)
    for i in range(1, 32):
        total = total + part_ref[i].astype(F32)
    total = total.astype(BF)
    for d in range(16):
        out_ref[d] = total


def hidden_kernel(h0_ref, h1_ref, h2_ref, h3_ref, at_ref, out_ref):
    for ref, shift in zip((h0_ref, h1_ref, h2_ref, h3_ref), RING):
        at = pl.multiple_of(((at_ref[2] - shift + 4) & 3) * 256, 256)
        out_ref[:, pl.ds(at, 256)] = ref[...].astype(F32).T.astype(BF)


def gradient_kernel(in_ref, first_ref, second_ref):
    for j in range(8):
        cols = pl.ds(j * 128, 128)
        one, two = halves(in_ref[owner(2 * j)].astype(F32), in_ref[owner(2 * j + 1)].astype(F32))
        first_ref[0:48, cols] = one[:48]
        first_ref[48:96, cols] = two[:48]
        second_ref[0:80, cols] = one[48:]
        second_ref[80:153, cols] = two[48:121]


def call(kernel, shape, specs, scratch=(), flops=0, moved=0, limit=8):
    return pl.pallas_call(
        kernel,
        out_shape=shape,
        in_specs=specs,
        out_specs=jax.tree.map(lambda _: VMEM, shape),
        scratch_shapes=list(scratch),
        compiler_params=pltpu.CompilerParams(vmem_limit_bytes=limit * MIB),
        cost_estimate=pl.CostEstimate(flops=flops, bytes_accessed=moved, transcendentals=0),
    )


def fetch(value, axis, shift):
    return lax.ppermute(value, axis, [((i + shift) % 4, i) for i in range(4)])


def ring(value, axis):
    return [value] + [fetch(value, axis, shift) for shift in RING[1:]]


def near(value, axis):
    return fetch(value, axis, 1), fetch(value, axis, -1)


def rounds(value, axis, half):
    after, before = near(value, axis)
    return [value, after, before, fetch(after[:half], axis, 1), fetch(before[half:], axis, -1)]


def body(features, first_weight, second_weight, degree, neighbour_block, neighbour_mask, upstream):
    feat, dom = ("y", "c"), ("x", "z")
    shape = jax.ShapeDtypeStruct
    x, z = lax.axis_index("x"), lax.axis_index("z")
    at = jnp.stack([x * 4 + z, x, z, lax.axis_index("y"), lax.axis_index("c")])
    x_own = lax.all_to_all(
        features.reshape(96, 8, 256).transpose(1, 0, 2), feat, 0, 0, tiled=True
    )
    links = jnp.pad(jnp.maximum(neighbour_block.reshape(1, 12), 0), ((0, 0), (0, 116)))
    mask = call(mask_kernel, shape((336, 768), BF), [VMEM] * 4, moved=1_200_000)(
        neighbour_mask[0], upstream[0].T, degree.reshape(2, 128), links
    )
    weight = lax.dynamic_slice(first_weight, (0, z * 256), (96, 256))
    other = lax.ppermute(weight, "c", [(0, 1), (1, 0)])
    after, before, other = lax.optimization_barrier((*near(mask, "z"), other))
    weights = ring(jnp.stack([weight, other]), "y")
    far = [fetch(after[:192], "z", 1), fetch(before[192:], "z", -1)]
    x_own, *far = lax.optimization_barrier((x_own, *far))
    masks = [mask, after, before, *far]
    scaled = call(upstream_kernel, shape((4, 160, 256), BF), [VMEM] * 5 + [SMEM], moved=1_000_000)(
        *masks, at
    )
    x_after, x_before, after, before = lax.optimization_barrier((*near(x_own, "z"), *near(scaled, "x")))
    x_far = [fetch(x_after[:4], "z", 1), fetch(x_before[4:], "z", -1)]
    far = [fetch(after[:2], "x", 1), fetch(before[2:], "x", -1)]
    *x_far, far_low, far_high = lax.optimization_barrier((*x_far, *far))
    x_wide = [x_own, x_after, x_before, *x_far]
    scaled = [scaled, after, before, far_low, far_high]
    s = call(
        project_kernel,
        shape((4, 256, 256), BF),
        [VMEM] * 14 + [SMEM],
        [pltpu.VMEM((8, 96, 256), BF)],
        flops=400_000_000,
        moved=3_000_000,
    )(*x_wide, *weights, *masks, at)
    s = rounds(s, "x", 2)
    own_second = lax.dynamic_slice(second_weight, (z * 256, 0), (256, 153))
    own_second = jnp.pad(own_second, ((0, 0), (0, 7)))
    links_scratch = [
        pltpu.VMEM((8, 128), I32), pltpu.SMEM((8, 128), I32), pltpu.SemaphoreType.DMA
    ]
    *hid, back, second = call(
        first_mix_kernel,
        (shape((256, 256), BF),) * 4 + (shape((4, 256, 256), BF), shape((160, 256), F32)),
        [VMEM] * 16 + [SMEM],
        [pltpu.VMEM((32, 416, 128), BF), *links_scratch],
        flops=700_000_000,
        moved=8_000_000,
        limit=20,
    )(*s, *scaled, *masks, own_second, at)
    after, before, *hid = lax.optimization_barrier((*near(back, "x"), *hid))
    hid = [hid[0]] + [fetch(value, "z", -shift) for value, shift in zip(hid[1:], RING[1:])]
    back = [back, after, before, fetch(after[:2], "x", 1), fetch(before[2:], "x", -1)]
    part = call(
        second_mix_kernel,
        shape((8, 4, 128, 128), BF),
        [VMEM] * 16 + [SMEM],
        [pltpu.VMEM((32, 256, 128), BF), *links_scratch],
        flops=900_000_000,
        moved=8_000_000,
        limit=20,
    )(*back, *masks, *x_wide, second, at)
    part = lax.all_to_all(part.reshape(32, 128, 128), ("y", "c", "x"), 0, 0, tiled=True)
    tile = shape((16, 128, 128), BF)
    done = call(add_kernel, tile, [VMEM], moved=1_500_000)(part)
    done = lax.all_to_all(done, dom, 0, 0, tiled=True)
    hidden = call(hidden_kernel, shape((256, 1024), BF), [VMEM] * 4 + [SMEM], moved=1_000_000)(*hid, at)
    grad_first, grad_second = call(
        gradient_kernel, (shape((96, 1024), F32), shape((153, 1024), F32)), [VMEM], moved=1_500_000
    )(done)
    return (hidden[None], grad_first, grad_second.T)


def solution(mesh):
    wide = Mesh(mesh.devices.reshape(4, 2, 4, 4), ("y", "c", "x", "z"))
    feat, dom = ("y", "c"), ("x", "z")
    placed = (
        P(feat, dom, None),
        P(feat, None),
        P(),
        P(dom, feat),
        P(dom, feat, None),
        P(dom, feat, None, None, None),
        P(dom, feat, None),
    )
    return jax.shard_map(
        body,
        mesh=wide,
        in_specs=placed,
        out_specs=(P(dom, feat, None), P(feat, None), P()),
        check_vma=False,
    )
```

time: 187 us -> 172 us (0.920)
  starting transfers between devices: 71 us -> 54.3 us
  Pallas kernels: 22.6 us -> 15.7 us
  local copies, waits for them, and re-layouts: 15.9 us -> 21.4 us
  waiting for transfers between devices: 48.6 us -> 53.1 us
  blocking collectives: 27.1 us -> 24.8 us
    ppermute x34 -> x26, waiting for transfers between devices: 36.5 us -> 52.8 us  [fetch(): return lax.ppermute(value, axis, [((i + shift) % 4, i) for i in range(4)])]
    ppermute x34 -> x26, starting transfers between devices: 58.1 us -> 46.1 us  [fetch(): return lax.ppermute(value, axis, [((i + shift) % 4, i) for i in range(4)])]
    all_to_all x1, waiting for transfers between devices: 11 us -> 0.01 us  [body(): done = lax.all_to_all(done, dom, 0, 0, tiled=True)]
    pallas_call x9 -> x7, Pallas kernels: 21.4 us -> 14.5 us  [the longest x1 5.37 us: body(): call(first_mix_kernel, (shape((256, 256), BF),) * 4 + (shape((4, 256, 256...]
    all_to_all x1 -> x0, starting transfers between devices: 4.61 us -> none  [body(): hid = lax.all_to_all(hid, dom, 0, 0, tiled=True)]
    slice x2 -> x10, local copies, waits for them, and re-layouts: 0.03 us -> 2.56 us  [the longest x2 0.95 us: body(): x_far = [fetch(x_after[:4], 'z', 1), fetch(x_before[4:], 'z', -1)]]
    all_to_all x2 -> x1, blocking collectives: 27.1 us -> 24.8 us  [body(): lax.all_to_all(part.reshape(32, 128, 128), ('y', 'c', 'x'), 0, 0, tiled=T...]
    unnamed x60 -> x68, local copies, waits for them, and re-layouts: 14.7 us -> 14.6 us
  transfers between devices with their start and end apart: 39 -> 29, of which waited for: 11 -> 14; matrix products, arithmetic and copies ran while one was open for 1% -> 5% of each run, Pallas kernels for 3% -> 1%
where the time goes in v6:
time: 172 us; the launch traced here: 171 us
  starting transfers between devices  54.3 us (32%)
  waiting for transfers between devices  53.1 us (31%)
  blocking collectives  24.8 us (14%)
  local copies, waits for them, and re-layouts  21.4 us (12%)
  Pallas kernels  15.7 us (9%)
    ppermute x26, waiting for transfers between devices, fetch(): return lax.ppermute(value, axis, [((i + shift) % 4, i) for i in range(4)])  52.8 us
    ppermute x26, starting transfers between devices, fetch(): return lax.ppermute(value, axis, [((i + shift) % 4, i) for i in range(4)])  46.1 us
    all_to_all x1, blocking collectives, body(): lax.all_to_all(part.reshape(32, 128, 128), ('y', 'c', 'x'), 0, 0, tiled=T...  24.8 us
    unnamed x68, local copies, waits for them, and re-layouts  14.6 us
    pallas_call x1, Pallas kernels, body(): call(first_mix_kernel, (shape((256, 256), BF),) * 4 + (shape((4, 256, 256...  5.37 us
    all_to_all x1, starting transfers between devices, body(): lax.all_to_all(features.reshape(96, 8, 256).transpose(1, 0, 2), feat, 0,...  4.58 us
    pallas_call x1, Pallas kernels, body(): call(second_mix_kernel, shape((8, 4, 128, 128), BF), [VMEM] * 16 + [SMEM]...  4.27 us
    all_to_all x1, starting transfers between devices, body(): done = lax.all_to_all(done, dom, 0, 0, tiled=True)  3.72 us
  transfers between devices with their start and end apart: 29, of which 14 were waited for; matrix products, arithmetic and copies ran while one was open for 5% of the time, Pallas kernels for 1%

profile of v6, /device:TPU:0, one launch (start us, length us, event | category | flops | bytes accessed | tf_op | source)
XLA Modules:
  0.0 171.0 jit_solution(7072032727384733272)
XLA Ops:
  4.2 2.1 %collective-permute-start.1 = (bf16[336,768]{1,0:T(8,128)(2,1)S(1)}, bf16[336,768]{1,0:T(8,128)(2,1)S(1)}, u32[]{:S(2)}, u32[]{:S(2)}) collective-permute-start(bf16[336,768]{1,0:T(8,128)(2,1)S(1)} %shard_map.94.refs_0_.refs_9_.refs_10_.refs_5_), channel_id=1, source_target_pairs={{3,0},{0,1},{1,2},{2,3},{7,4},{4,5},{5,6},{6,7},{11,8},{8,9},{9,10... | collective-permute-start | bytes 1548296 | tf_op jit(solution)/shard_map/ppermute | solution.py:213
  6.3 2.2 %collective-permute-start = (bf16[336,768]{1,0:T(8,128)(2,1)S(1)}, bf16[336,768]{1,0:T(8,128)(2,1)S(1)}, u32[]{:S(2)}, u32[]{:S(2)}) collective-permute-start(bf16[336,768]{1,0:T(8,128)(2,1)S(1)} %shard_map.94.refs_0_.refs_9_.refs_10_.refs_5_), channel_id=1, source_target_pairs={{1,0},{2,1},{3,2},{0,3},{5,4},{6,5},{7,6},{4,7},{9,8},{10,9},{11,1... | collective-permute-start | bytes 1548296 | tf_op jit(solution)/shard_map/ppermute | solution.py:213
  10.2 4.6 %all-to-all-start = ((bf16[8,96,256]{2,1,0:T(8,128)(2,1)}), bf16[8,96,256]{2,1,0:T(8,128)(2,1)S(1)}, u32[]{:S(2)}, u32[]{:S(2)}) async-start(bf16[8,96,256]{2,1,0:T(8,128)(2,1)} %bitcast.22), calls=%async_computation | async-start | bytes 786432 | tf_op jit(solution)/shard_map/all_to_all | solution.py:234
  14.8 5.4 %collective-permute-done.1.refs_2_.refs_11_.refs_12_.refs_7_ = bf16[336,768]{1,0:T(8,128)(2,1)S(1)} collective-permute-done((bf16[336,768]{1,0:T(8,128)(2,1)S(1)}, bf16[336,768]{1,0:T(8,128)(2,1)S(1)}, u32[]{:S(2)}, u32[]{:S(2)}) %collective-permute-start.1) | collective-permute-done | bytes 516128 | tf_op jit(solution)/shard_map/ppermute | solution.py:213
  20.2 3.1 %collective-permute-start.3 = (bf16[192,768]{1,0:T(8,128)(2,1)S(1)}, bf16[192,768]{1,0:T(8,128)(2,1)S(1)}, u32[]{:S(2)}, u32[]{:S(2)}) collective-permute-start(bf16[192,768]{1,0:T(8,128)(2,1)S(1)} %slice.30), channel_id=1, source_target_pairs={{1,0},{2,1},{3,2},{0,3},{5,4},{6,5},{7,6},{4,7},{9,8},{10,9},{11,1... | collective-permute-start | bytes 884744 | tf_op jit(solution)/shard_map/ppermute | solution.py:213
  23.7 6.9 %collective-permute-done.4.refs_4_.refs_13_.refs_14_.refs_9_ = bf16[144,768]{1,0:T(8,128)(2,1)S(1)} collective-permute-done((bf16[144,768]{1,0:T(8,128)(2,1)S(1)}, bf16[144,768]{1,0:T(8,128)(2,1)S(1)}, u32[]{:S(2)}, u32[]{:S(2)}) %collective-permute-start.4) | collective-permute-done | bytes 221216 | tf_op jit(solution)/shard_map/ppermute | solution.py:213
  30.6 3.2 %collective-permute-start.5 = (bf16[8,96,256]{2,1,0:T(8,128)(2,1)S(1)}, bf16[8,96,256]{2,1,0:T(8,128)(2,1)}, u32[]{:S(2)}, u32[]{:S(2)}) collective-permute-start(bf16[8,96,256]{2,1,0:T(8,128)(2,1)S(1)} %all-to-all-done.refs_0_.refs_10_), channel_id=1, source_target_pairs={{1,0},{2,1},{3,2},{0,3},{5,4},{6,5},{7,6},{4,7},{9,8},{10,9},{11,1... | collective-permute-start | bytes 1179656 | tf_op jit(solution)/shard_map/ppermute | solution.py:213
  34.6 1.6 collective-permute-start.8
  36.1 1.7 %collective-permute-start.7 = (bf16[4,160,256]{2,1,0:T(8,128)(2,1)S(1)}, bf16[4,160,256]{2,1,0:T(8,128)(2,1)S(1)}, u32[]{:S(2)}, u32[]{:S(2)}) collective-permute-start(bf16[4,160,256]{2,1,0:T(8,128)(2,1)S(1)} %shard_map.95.refs_5_), channel_id=1, source_target_pairs={{4,0},{8,4},{12,8},{0,12},{5,1},{9,5},{13,9},{1,13},{6,2},{10,6},{... | collective-permute-start | bytes 983048 | tf_op jit(solution)/shard_map/ppermute | solution.py:213
  37.9 5.0 %collective-permute-done.8.refs_7_ = bf16[4,160,256]{2,1,0:T(8,128)(2,1)S(1)} collective-permute-done((bf16[4,160,256]{2,1,0:T(8,128)(2,1)S(1)}, bf16[4,160,256]{2,1,0:T(8,128)(2,1)S(1)}, u32[]{:S(2)}, u32[]{:S(2)}) %collective-permute-start.8) | collective-permute-done | bytes 327712 | tf_op jit(solution)/shard_map/ppermute | solution.py:213
  45.4 1.7 %collective-permute-start.11 = (bf16[2,160,256]{2,1,0:T(8,128)(2,1)S(1)}, bf16[2,160,256]{2,1,0:T(8,128)(2,1)S(1)}, u32[]{:S(2)}, u32[]{:S(2)}) collective-permute-start(bf16[2,160,256]{2,1,0:T(8,128)(2,1)S(1)} %slice.34), channel_id=1, source_target_pairs={{4,0},{8,4},{12,8},{0,12},{5,1},{9,5},{13,9},{1,13},{6,2},{10,6},{... | collective-permute-start | bytes 491528 | tf_op jit(solution)/shard_map/ppermute | solution.py:213
  49.0 3.2 %collective-permute-start.9 = (bf16[4,96,256]{2,1,0:T(8,128)(2,1)S(1)}, bf16[4,96,256]{2,1,0:T(8,128)(2,1)S(1)}, u32[]{:S(2)}, u32[]{:S(2)}) collective-permute-start(bf16[4,96,256]{2,1,0:T(8,128)(2,1)S(1)} %slice.32), channel_id=1, source_target_pairs={{1,0},{2,1},{3,2},{0,3},{5,4},{6,5},{7,6},{4,7},{9,8},{10,9},{11,1... | collective-permute-start | bytes 589832 | tf_op jit(solution)/shard_map/ppermute | solution.py:213
  52.3 3.3 %collective-permute-start.15 = (bf16[2,96,256]{2,1,0:T(8,128)(2,1)S(1)}, bf16[2,96,256]{2,1,0:T(8,128)(2,1)S(1)}, u32[]{:S(2)}, u32[]{:S(2)}) collective-permute-start(bf16[2,96,256]{2,1,0:T(8,128)(2,1)S(1)} %pad_maximum_fusion.refs_5_), channel_id=1, source_target_pairs={{64,0},{96,32},{0,64},{32,96},{65,1},{97,33},{1,65},{33,97},{66,2}... | collective-permute-start | bytes 294920 | tf_op jit(solution)/shard_map/ppermute | solution.py:213
  57.5 2.6 %collective-permute-start.13 = (bf16[2,96,256]{2,1,0:T(8,128)(2,1)S(1)}, bf16[2,96,256]{2,1,0:T(8,128)(2,1)S(1)}, u32[]{:S(2)}, u32[]{:S(2)}) collective-permute-start(bf16[2,96,256]{2,1,0:T(8,128)(2,1)S(1)} %pad_maximum_fusion.refs_5_), channel_id=1, source_target_pairs={{32,0},{64,32},{96,64},{0,96},{33,1},{65,33},{97,65},{1,97},{34,2}... | collective-permute-start | bytes 294920 | tf_op jit(solution)/shard_map/ppermute | solution.py:213
  60.1 1.9 %collective-permute-done.14.refs_7_ = bf16[2,96,256]{2,1,0:T(8,128)(2,1)S(1)} collective-permute-done((bf16[2,96,256]{2,1,0:T(8,128)(2,1)S(1)}, bf16[2,96,256]{2,1,0:T(8,128)(2,1)S(1)}, u32[]{:S(2)}, u32[]{:S(2)}) %collective-permute-start.14) | collective-permute-done | bytes 98336 | tf_op jit(solution)/shard_map/ppermute | solution.py:213
  62.3 1.7 shard_map.96.refs_0_
  65.7 3.0 %collective-permute-start.16 = (bf16[4,256,256]{2,1,0:T(8,128)(2,1)S(1)}, bf16[4,256,256]{2,1,0:T(8,128)(2,1)S(1)}, u32[]{:S(2)}, u32[]{:S(2)}) collective-permute-start(bf16[4,256,256]{2,1,0:T(8,128)(2,1)S(1)} %shard_map.96.refs_0_), channel_id=1, source_target_pairs={{4,0},{8,4},{12,8},{0,12},{5,1},{9,5},{13,9},{1,13},{6,2},{10,6},{... | collective-permute-start | bytes 1572872 | tf_op jit(solution)/shard_map/ppermute | solution.py:213
  68.6 9.8 %collective-permute-done.17.refs_2_ = bf16[4,256,256]{2,1,0:T(8,128)(2,1)S(1)} collective-permute-done((bf16[4,256,256]{2,1,0:T(8,128)(2,1)S(1)}, bf16[4,256,256]{2,1,0:T(8,128)(2,1)S(1)}, u32[]{:S(2)}, u32[]{:S(2)}) %collective-permute-start.17) | collective-permute-done | bytes 524320 | tf_op jit(solution)/shard_map/ppermute | solution.py:213
  80.7 3.2 %collective-permute-start.18 = (bf16[2,256,256]{2,1,0:T(8,128)(2,1)}, bf16[2,256,256]{2,1,0:T(8,128)(2,1)}, u32[]{:S(2)}, u32[]{:S(2)}) collective-permute-start(bf16[2,256,256]{2,1,0:T(8,128)(2,1)} %slice.40), channel_id=1, source_target_pairs={{4,0},{8,4},{12,8},{0,12},{5,1},{9,5},{13,9},{1,13},{6,2},{10,6},{... | collective-permute-start | bytes 786440 | tf_op jit(solution)/shard_map/ppermute | solution.py:213
  84.6 1.6 copy.13
  94.2 5.4 %shard_map.97 = (bf16[256,256]{1,0:T(8,128)(2,1)S(1)}, bf16[256,256]{1,0:T(8,128)(2,1)S(1)}, bf16[256,256]{1,0:T(8,128)(2,1)S(1)}, bf16[256,256]{1,0:T(8,128)(2,...) custom-call(bf16[4,256,256]{2,1,0:T(8,128)(2,1)S(1)} %copy-done.2, bf16[4,256,256]{2,1,0:T(8,128)(2,1)S(1)} %copy-done.6, ...), custom_call_target="tpu_custom_call" | custom-call | flops 700000000 | bytes 8000000 | tf_op jit(solution)/shard_map/pallas_call | solution.py:271
  99.7 3.8 %collective-permute-start.20 = (bf16[4,256,256]{2,1,0:T(8,128)(2,1)S(1)}, bf16[4,256,256]{2,1,0:T(8,128)(2,1)S(1)}, u32[]{:S(2)}, u32[]{:S(2)}) collective-permute-start(bf16[4,256,256]{2,1,0:T(8,128)(2,1)S(1)} %get-tuple-element.45.refs_0_), channel_id=1, source_target_pairs={{4,0},{8,4},{12,8},{0,12},{5,1},{9,5},{13,9},{1,13},{6,2},{10,6},{... | collective-permute-start | bytes 1572872 | tf_op jit(solution)/shard_map/ppermute | solution.py:213
  103.4 8.6 %collective-permute-done.21.refs_2_ = bf16[4,256,256]{2,1,0:T(8,128)(2,1)S(1)} collective-permute-done((bf16[4,256,256]{2,1,0:T(8,128)(2,1)S(1)}, bf16[4,256,256]{2,1,0:T(8,128)(2,1)S(1)}, u32[]{:S(2)}, u32[]{:S(2)}) %collective-permute-start.21) | collective-permute-done | bytes 524320 | tf_op jit(solution)/shard_map/ppermute | solution.py:213
  113.5 1.9 %collective-permute-start.25 = (bf16[2,256,256]{2,1,0:T(8,128)(2,1)S(1)}, bf16[2,256,256]{2,1,0:T(8,128)(2,1)S(1)}, u32[]{:S(2)}, u32[]{:S(2)}) collective-permute-start(bf16[2,256,256]{2,1,0:T(8,128)(2,1)S(1)} %slice.38), channel_id=1, source_target_pairs={{4,0},{8,4},{12,8},{0,12},{5,1},{9,5},{13,9},{1,13},{6,2},{10,6},{... | collective-permute-start | bytes 786440 | tf_op jit(solution)/shard_map/ppermute | solution.py:213
  115.4 4.3 %collective-permute-done.26.refs_4_ = bf16[2,256,256]{2,1,0:T(8,128)(2,1)S(1)} collective-permute-done((bf16[2,256,256]{2,1,0:T(8,128)(2,1)S(1)}, bf16[2,256,256]{2,1,0:T(8,128)(2,1)S(1)}, u32[]{:S(2)}, u32[]{:S(2)}) %collective-permute-start.26) | collective-permute-done | bytes 262176 | tf_op jit(solution)/shard_map/ppermute | solution.py:213
  119.9 4.3 %shard_map.99 = bf16[8,4,128,128]{3,2,1,0:T(8,128)(2,1)S(1)} custom-call(bf16[4,256,256]{2,1,0:T(8,128)(2,1)S(1)} %get-tuple-element.45.refs_0_, bf16[4,256,256]{2,1,0:T(8,128)(2,1)S(1)} %collective-permute-done.20.refs_1_, bf16[4,256,256]{2,1,0:T(8,128)(2,1)S(1)} %collective-permute-done.21.refs_2_, ...), custom_call_target="tpu_custom_call" | custom-call | flops 900000000 | bytes 8000000 | tf_op jit(solution)/shard_map/pallas_call | solution.py:283
  124.1 24.8 %all_to_all.15.part_ref = bf16[32,128,128]{2,1,0:T(8,128)(2,1)S(1)} all-to-all(bf16[32,128,128]{2,1,0:T(8,128)(2,1)S(1)} %bitcast.23), channel_id=1, replica_groups=mesh['y'=4,'c'=2,'x'=4,'z'=4] {'y','c','x'}, dimensions={0} | all-to-all | bytes 2097152 | tf_op jit(solution)/shard_map/all_to_all | solution.py:292
  149.9 3.7 %all-to-all-start.2 = ((bf16[16,128,128]{2,1,0:T(8,128)(2,1)}), bf16[16,128,128]{2,1,0:T(8,128)(2,1)S(1)}, u32[]{:S(2)}, u32[]{:S(2)}) async-start(bf16[16,128,128]{2,1,0:T(8,128)(2,1)} %shard_map.100), calls=%async_computation.2 | async-start | bytes 1048576 | tf_op jit(solution)/shard_map/all_to_all | solution.py:295
  153.6 1.9 %collective-permute-start.22 = (bf16[256,256]{1,0:T(8,128)(2,1)S(1)}, bf16[256,256]{1,0:T(8,128)(2,1)S(1)}, u32[]{:S(2)}, u32[]{:S(2)}) collective-permute-start(bf16[256,256]{1,0:T(8,128)(2,1)S(1)} %copy-done.29), channel_id=1, source_target_pairs={{3,0},{0,1},{1,2},{2,3},{7,4},{4,5},{5,6},{6,7},{11,8},{8,9},{9,10... | collective-permute-start | bytes 393224 | tf_op jit(solution)/shard_map/ppermute | solution.py:213
  156.9 2.1 %collective-permute-start.24 = (bf16[256,256]{1,0:T(8,128)(2,1)S(1)}, bf16[256,256]{1,0:T(8,128)(2,1)S(1)}, u32[]{:S(2)}, u32[]{:S(2)}) collective-permute-start(bf16[256,256]{1,0:T(8,128)(2,1)S(1)} %copy-done.25), channel_id=1, source_target_pairs={{2,0},{3,1},{0,2},{1,3},{6,4},{7,5},{4,6},{5,7},{10,8},{11,9},{8,1... | collective-permute-start | bytes 393224 | tf_op jit(solution)/shard_map/ppermute | solution.py:213
  159.0 7.4 %collective-permute-done.22.h1_ref = bf16[256,256]{1,0:T(8,128)(2,1)S(1)} collective-permute-done((bf16[256,256]{1,0:T(8,128)(2,1)S(1)}, bf16[256,256]{1,0:T(8,128)(2,1)S(1)}, u32[]{:S(2)}, u32[]{:S(2)}) %collective-permute-start.22) | collective-permute-done | bytes 131104 | tf_op jit(solution)/shard_map/ppermute | solution.py:213
  166.4 1.9 %collective-permute-done.24.h3_ref = bf16[256,256]{1,0:T(8,128)(2,1)S(1)} collective-permute-done((bf16[256,256]{1,0:T(8,128)(2,1)S(1)}, bf16[256,256]{1,0:T(8,128)(2,1)S(1)}, u32[]{:S(2)}, u32[]{:S(2)}) %collective-permute-start.24) | collective-permute-done | bytes 131104 | tf_op jit(solution)/shard_map/ppermute | solution.py:213
  (123 shorter events, 32.3 us)
Async XLA Ops:
  0.6 83.3 %copy-start = (bf16[1024,153]{0,1:T(8,128)(2,1)S(1)}, bf16[1024,153]{0,1:T(8,128)(2,1)}, u32[]{:S(2)}) copy-start(bf16[1024,153]{0,1:T(8,128)(2,1)} %param.9) | copy-start | bytes 940036
  4.2 15.9 %collective-permute-start.1 = (bf16[336,768]{1,0:T(8,128)(2,1)S(1)}, bf16[336,768]{1,0:T(8,128)(2,1)S(1)}, u32[]{:S(2)}, u32[]{:S(2)}) collective-permute-start(bf16[336,768]{1,0:T(8,128)(2,1)S(1)} %shard_map.94.refs_0_.refs_9_.refs_10_.refs_5_), channel_id=1, source_target_pairs={{3,0},{0,1},{1,2},{2,3},{7,4},{4,5},{5,6},{6,7},{11,8},{8,9},{9,10... | collective-permute-start | bytes 1548296 | tf_op jit(solution)/shard_map/ppermute | solution.py:213
  6.3 13.9 %collective-permute-start = (bf16[336,768]{1,0:T(8,128)(2,1)S(1)}, bf16[336,768]{1,0:T(8,128)(2,1)S(1)}, u32[]{:S(2)}, u32[]{:S(2)}) collective-permute-start(bf16[336,768]{1,0:T(8,128)(2,1)S(1)} %shard_map.94.refs_0_.refs_9_.refs_10_.refs_5_), channel_id=1, source_target_pairs={{1,0},{2,1},{3,2},{0,3},{5,4},{6,5},{7,6},{4,7},{9,8},{10,9},{11,1... | collective-permute-start | bytes 1548296 | tf_op jit(solution)/shard_map/ppermute | solution.py:213
  9.3 5.5 %collective-permute-start.2 = (bf16[96,256]{1,0:T(8,128)(2,1)S(1)}, bf16[96,256]{1,0:T(8,128)(2,1)S(1)}, u32[]{:S(2)}, u32[]{:S(2)}) collective-permute-start(bf16[96,256]{1,0:T(8,128)(2,1)S(1)} %constant_dynamic-slice_fusion.1), channel_id=1, source_target_pairs={{0,16},{16,0},{1,17},{17,1},{2,18},{18,2},{3,19},{19,3},{4,20},{20... | collective-permute-start | bytes 147464 | tf_op jit(solution)/shard_map/ppermute | solution.py:242
  10.2 13.5 %all-to-all-start = ((bf16[8,96,256]{2,1,0:T(8,128)(2,1)}), bf16[8,96,256]{2,1,0:T(8,128)(2,1)S(1)}, u32[]{:S(2)}, u32[]{:S(2)}) async-start(bf16[8,96,256]{2,1,0:T(8,128)(2,1)} %bitcast.22), calls=%async_computation | async-start | bytes 786432 | tf_op jit(solution)/shard_map/all_to_all | solution.py:234
  20.2 10.4 %collective-permute-start.3 = (bf16[192,768]{1,0:T(8,128)(2,1)S(1)}, bf16[192,768]{1,0:T(8,128)(2,1)S(1)}, u32[]{:S(2)}, u32[]{:S(2)}) collective-permute-start(bf16[192,768]{1,0:T(8,128)(2,1)S(1)} %slice.30), channel_id=1, source_target_pairs={{1,0},{2,1},{3,2},{0,3},{5,4},{6,5},{7,6},{4,7},{9,8},{10,9},{11,1... | collective-permute-start | bytes 884744 | tf_op jit(solution)/shard_map/ppermute | solution.py:213
  23.3 7.3 %collective-permute-start.4 = (bf16[144,768]{1,0:T(8,128)(2,1)S(1)}, bf16[144,768]{1,0:T(8,128)(2,1)S(1)}, u32[]{:S(2)}, u32[]{:S(2)}) collective-permute-start(bf16[144,768]{1,0:T(8,128)(2,1)S(1)} %slice.31), channel_id=1, source_target_pairs={{3,0},{0,1},{1,2},{2,3},{7,4},{4,5},{5,6},{6,7},{11,8},{8,9},{9,10... | collective-permute-start | bytes 663560 | tf_op jit(solution)/shard_map/ppermute | solution.py:213
  30.6 12.6 %collective-permute-start.6 = (bf16[8,96,256]{2,1,0:T(8,128)(2,1)S(1)}, bf16[8,96,256]{2,1,0:T(8,128)(2,1)S(1)}, u32[]{:S(2)}, u32[]{:S(2)}) collective-permute-start(bf16[8,96,256]{2,1,0:T(8,128)(2,1)S(1)} %all-to-all-done.refs_0_.refs_10_), channel_id=1, source_target_pairs={{3,0},{0,1},{1,2},{2,3},{7,4},{4,5},{5,6},{6,7},{11,8},{8,9},{9,10... | collective-permute-start | bytes 1179656 | tf_op jit(solution)/shard_map/ppermute | solution.py:213
  30.6 12.6 %collective-permute-start.5 = (bf16[8,96,256]{2,1,0:T(8,128)(2,1)S(1)}, bf16[8,96,256]{2,1,0:T(8,128)(2,1)}, u32[]{:S(2)}, u32[]{:S(2)}) collective-permute-start(bf16[8,96,256]{2,1,0:T(8,128)(2,1)S(1)} %all-to-all-done.refs_0_.refs_10_), channel_id=1, source_target_pairs={{1,0},{2,1},{3,2},{0,3},{5,4},{6,5},{7,6},{4,7},{9,8},{10,9},{11,1... | collective-permute-start | bytes 1179656 | tf_op jit(solution)/shard_map/ppermute | solution.py:213
  34.6 8.4 %collective-permute-start.8 = (bf16[4,160,256]{2,1,0:T(8,128)(2,1)S(1)}, bf16[4,160,256]{2,1,0:T(8,128)(2,1)S(1)}, u32[]{:S(2)}, u32[]{:S(2)}) collective-permute-start(bf16[4,160,256]{2,1,0:T(8,128)(2,1)S(1)} %shard_map.95.refs_5_), channel_id=1, source_target_pairs={{12,0},{0,4},{4,8},{8,12},{13,1},{1,5},{5,9},{9,13},{14,2},{2,6},{... | collective-permute-start | bytes 983048 | tf_op jit(solution)/shard_map/ppermute | solution.py:213
  36.1 7.1 %collective-permute-start.7 = (bf16[4,160,256]{2,1,0:T(8,128)(2,1)S(1)}, bf16[4,160,256]{2,1,0:T(8,128)(2,1)S(1)}, u32[]{:S(2)}, u32[]{:S(2)}) collective-permute-start(bf16[4,160,256]{2,1,0:T(8,128)(2,1)S(1)} %shard_map.95.refs_5_), channel_id=1, source_target_pairs={{4,0},{8,4},{12,8},{0,12},{5,1},{9,5},{13,9},{1,13},{6,2},{10,6},{... | collective-permute-start | bytes 983048 | tf_op jit(solution)/shard_map/ppermute | solution.py:213
  43.9 11.6 %collective-permute-start.12 = (bf16[2,160,256]{2,1,0:T(8,128)(2,1)S(1)}, bf16[2,160,256]{2,1,0:T(8,128)(2,1)S(1)}, u32[]{:S(2)}, u32[]{:S(2)}) collective-permute-start(bf16[2,160,256]{2,1,0:T(8,128)(2,1)S(1)} %slice.35), channel_id=1, source_target_pairs={{12,0},{0,4},{4,8},{8,12},{13,1},{1,5},{5,9},{9,13},{14,2},{2,6},{... | collective-permute-start | bytes 491528 | tf_op jit(solution)/shard_map/ppermute | solution.py:213
  45.4 11.5 %collective-permute-start.11 = (bf16[2,160,256]{2,1,0:T(8,128)(2,1)S(1)}, bf16[2,160,256]{2,1,0:T(8,128)(2,1)S(1)}, u32[]{:S(2)}, u32[]{:S(2)}) collective-permute-start(bf16[2,160,256]{2,1,0:T(8,128)(2,1)S(1)} %slice.34), channel_id=1, source_target_pairs={{4,0},{8,4},{12,8},{0,12},{5,1},{9,5},{13,9},{1,13},{6,2},{10,6},{... | collective-permute-start | bytes 491528 | tf_op jit(solution)/shard_map/ppermute | solution.py:213
  48.9 11.2 %collective-permute-start.10 = (bf16[4,96,256]{2,1,0:T(8,128)(2,1)S(1)}, bf16[4,96,256]{2,1,0:T(8,128)(2,1)S(1)}, u32[]{:S(2)}, u32[]{:S(2)}) collective-permute-start(bf16[4,96,256]{2,1,0:T(8,128)(2,1)S(1)} %slice.33), channel_id=1, source_target_pairs={{3,0},{0,1},{1,2},{2,3},{7,4},{4,5},{5,6},{6,7},{11,8},{8,9},{9,10... | collective-permute-start | bytes 589832 | tf_op jit(solution)/shard_map/ppermute | solution.py:213
  49.0 11.1 %collective-permute-start.9 = (bf16[4,96,256]{2,1,0:T(8,128)(2,1)S(1)}, bf16[4,96,256]{2,1,0:T(8,128)(2,1)S(1)}, u32[]{:S(2)}, u32[]{:S(2)}) collective-permute-start(bf16[4,96,256]{2,1,0:T(8,128)(2,1)S(1)} %slice.32), channel_id=1, source_target_pairs={{1,0},{2,1},{3,2},{0,3},{5,4},{6,5},{7,6},{4,7},{9,8},{10,9},{11,1... | collective-permute-start | bytes 589832 | tf_op jit(solution)/shard_map/ppermute | solution.py:213
  52.3 7.9 %collective-permute-start.15 = (bf16[2,96,256]{2,1,0:T(8,128)(2,1)S(1)}, bf16[2,96,256]{2,1,0:T(8,128)(2,1)S(1)}, u32[]{:S(2)}, u32[]{:S(2)}) collective-permute-start(bf16[2,96,256]{2,1,0:T(8,128)(2,1)S(1)} %pad_maximum_fusion.refs_5_), channel_id=1, source_target_pairs={{64,0},{96,32},{0,64},{32,96},{65,1},{97,33},{1,65},{33,97},{66,2}... | collective-permute-start | bytes 294920 | tf_op jit(solution)/shard_map/ppermute | solution.py:213
  56.2 5.8 %collective-permute-start.14 = (bf16[2,96,256]{2,1,0:T(8,128)(2,1)S(1)}, bf16[2,96,256]{2,1,0:T(8,128)(2,1)S(1)}, u32[]{:S(2)}, u32[]{:S(2)}) collective-permute-start(bf16[2,96,256]{2,1,0:T(8,128)(2,1)S(1)} %pad_maximum_fusion.refs_5_), channel_id=1, source_target_pairs={{96,0},{0,32},{32,64},{64,96},{97,1},{1,33},{33,65},{65,97},{98,2}... | collective-permute-start | bytes 294920 | tf_op jit(solution)/shard_map/ppermute | solution.py:213
  57.5 4.8 %collective-permute-start.13 = (bf16[2,96,256]{2,1,0:T(8,128)(2,1)S(1)}, bf16[2,96,256]{2,1,0:T(8,128)(2,1)S(1)}, u32[]{:S(2)}, u32[]{:S(2)}) collective-permute-start(bf16[2,96,256]{2,1,0:T(8,128)(2,1)S(1)} %pad_maximum_fusion.refs_5_), channel_id=1, source_target_pairs={{32,0},{64,32},{96,64},{0,96},{33,1},{65,33},{97,65},{1,97},{34,2}... | collective-permute-start | bytes 294920 | tf_op jit(solution)/shard_map/ppermute | solution.py:213
  65.4 14.6 %copy-start.1 = (bf16[4,256,256]{2,1,0:T(8,128)(2,1)}, bf16[4,256,256]{2,1,0:T(8,128)(2,1)S(1)}, u32[]{:S(2)}) copy-start(bf16[4,256,256]{2,1,0:T(8,128)(2,1)S(1)} %shard_map.96.refs_0_) | copy-start | bytes 1572868
  65.4 13.0 %collective-permute-start.17 = (bf16[4,256,256]{2,1,0:T(8,128)(2,1)S(1)}, bf16[4,256,256]{2,1,0:T(8,128)(2,1)S(1)}, u32[]{:S(2)}, u32[]{:S(2)}) collective-permute-start(bf16[4,256,256]{2,1,0:T(8,128)(2,1)S(1)} %shard_map.96.refs_0_), channel_id=1, source_target_pairs={{12,0},{0,4},{4,8},{8,12},{13,1},{1,5},{5,9},{9,13},{14,2},{2,6},{... | collective-permute-start | bytes 1572872 | tf_op jit(solution)/shard_map/ppermute | solution.py:213
  65.7 13.5 %collective-permute-start.16 = (bf16[4,256,256]{2,1,0:T(8,128)(2,1)S(1)}, bf16[4,256,256]{2,1,0:T(8,128)(2,1)S(1)}, u32[]{:S(2)}, u32[]{:S(2)}) collective-permute-start(bf16[4,256,256]{2,1,0:T(8,128)(2,1)S(1)} %shard_map.96.refs_0_), channel_id=1, source_target_pairs={{4,0},{8,4},{12,8},{0,12},{5,1},{9,5},{13,9},{1,13},{6,2},{10,6},{... | collective-permute-start | bytes 1572872 | tf_op jit(solution)/shard_map/ppermute | solution.py:213
  79.2 8.0 %collective-permute-start.19 = (bf16[2,256,256]{2,1,0:T(8,128)(2,1)}, bf16[2,256,256]{2,1,0:T(8,128)(2,1)}, u32[]{:S(2)}, u32[]{:S(2)}) collective-permute-start(bf16[2,256,256]{2,1,0:T(8,128)(2,1)} %slice.41), channel_id=1, source_target_pairs={{12,0},{0,4},{4,8},{8,12},{13,1},{1,5},{5,9},{9,13},{14,2},{2,6},{... | collective-permute-start | bytes 786440 | tf_op jit(solution)/shard_map/ppermute | solution.py:213
  80.7 7.4 %collective-permute-start.18 = (bf16[2,256,256]{2,1,0:T(8,128)(2,1)}, bf16[2,256,256]{2,1,0:T(8,128)(2,1)}, u32[]{:S(2)}, u32[]{:S(2)}) collective-permute-start(bf16[2,256,256]{2,1,0:T(8,128)(2,1)} %slice.40), channel_id=1, source_target_pairs={{4,0},{8,4},{12,8},{0,12},{5,1},{9,5},{13,9},{1,13},{6,2},{10,6},{... | collective-permute-start | bytes 786440 | tf_op jit(solution)/shard_map/ppermute | solution.py:213
  99.6 12.4 %collective-permute-start.21 = (bf16[4,256,256]{2,1,0:T(8,128)(2,1)S(1)}, bf16[4,256,256]{2,1,0:T(8,128)(2,1)S(1)}, u32[]{:S(2)}, u32[]{:S(2)}) collective-permute-start(bf16[4,256,256]{2,1,0:T(8,128)(2,1)S(1)} %get-tuple-element.45.refs_0_), channel_id=1, source_target_pairs={{12,0},{0,4},{4,8},{8,12},{13,1},{1,5},{5,9},{9,13},{14,2},{2,6},{... | collective-permute-start | bytes 1572872 | tf_op jit(solution)/shard_map/ppermute | solution.py:213
  99.7 12.3 %collective-permute-start.20 = (bf16[4,256,256]{2,1,0:T(8,128)(2,1)S(1)}, bf16[4,256,256]{2,1,0:T(8,128)(2,1)S(1)}, u32[]{:S(2)}, u32[]{:S(2)}) collective-permute-start(bf16[4,256,256]{2,1,0:T(8,128)(2,1)S(1)} %get-tuple-element.45.refs_0_), channel_id=1, source_target_pairs={{4,0},{8,4},{12,8},{0,12},{5,1},{9,5},{13,9},{1,13},{6,2},{10,6},{... | collective-permute-start | bytes 1572872 | tf_op jit(solution)/shard_map/ppermute | solution.py:213
  112.1 7.7 %collective-permute-start.26 = (bf16[2,256,256]{2,1,0:T(8,128)(2,1)S(1)}, bf16[2,256,256]{2,1,0:T(8,128)(2,1)S(1)}, u32[]{:S(2)}, u32[]{:S(2)}) collective-permute-start(bf16[2,256,256]{2,1,0:T(8,128)(2,1)S(1)} %slice.39), channel_id=1, source_target_pairs={{12,0},{0,4},{4,8},{8,12},{13,1},{1,5},{5,9},{9,13},{14,2},{2,6},{... | collective-permute-start | bytes 786440 | tf_op jit(solution)/shard_map/ppermute | solution.py:213
  113.5 6.4 %collective-permute-start.25 = (bf16[2,256,256]{2,1,0:T(8,128)(2,1)S(1)}, bf16[2,256,256]{2,1,0:T(8,128)(2,1)S(1)}, u32[]{:S(2)}, u32[]{:S(2)}) collective-permute-start(bf16[2,256,256]{2,1,0:T(8,128)(2,1)S(1)} %slice.38), channel_id=1, source_target_pairs={{4,0},{8,4},{12,8},{0,12},{5,1},{9,5},{13,9},{1,13},{6,2},{10,6},{... | collective-permute-start | bytes 786440 | tf_op jit(solution)/shard_map/ppermute | solution.py:213
  149.9 18.4 %copy-start.21 = (bf16[256,256]{1,0:T(8,128)(2,1)S(1)}, bf16[256,256]{1,0:T(8,128)(2,1)}, u32[]{:S(2)}) copy-start(bf16[256,256]{1,0:T(8,128)(2,1)} %copy-done.20) | copy-start | bytes 393220
  149.9 19.9 %all-to-all-start.2 = ((bf16[16,128,128]{2,1,0:T(8,128)(2,1)}), bf16[16,128,128]{2,1,0:T(8,128)(2,1)S(1)}, u32[]{:S(2)}, u32[]{:S(2)}) async-start(bf16[16,128,128]{2,1,0:T(8,128)(2,1)} %shard_map.100), calls=%async_computation.2 | async-start | bytes 1048576 | tf_op jit(solution)/shard_map/all_to_all | solution.py:295
  153.6 12.8 %collective-permute-start.22 = (bf16[256,256]{1,0:T(8,128)(2,1)S(1)}, bf16[256,256]{1,0:T(8,128)(2,1)S(1)}, u32[]{:S(2)}, u32[]{:S(2)}) collective-permute-start(bf16[256,256]{1,0:T(8,128)(2,1)S(1)} %copy-done.29), channel_id=1, source_target_pairs={{3,0},{0,1},{1,2},{2,3},{7,4},{4,5},{5,6},{6,7},{11,8},{8,9},{9,10... | collective-permute-start | bytes 393224 | tf_op jit(solution)/shard_map/ppermute | solution.py:213
  155.5 10.9 %collective-permute-start.23 = (bf16[256,256]{1,0:T(8,128)(2,1)S(1)}, bf16[256,256]{1,0:T(8,128)(2,1)S(1)}, u32[]{:S(2)}, u32[]{:S(2)}) collective-permute-start(bf16[256,256]{1,0:T(8,128)(2,1)S(1)} %copy-done.27), channel_id=1, source_target_pairs={{1,0},{2,1},{3,2},{0,3},{5,4},{6,5},{7,6},{4,7},{9,8},{10,9},{11,1... | collective-permute-start | bytes 393224 | tf_op jit(solution)/shard_map/ppermute | solution.py:213
  156.9 11.3 %collective-permute-start.24 = (bf16[256,256]{1,0:T(8,128)(2,1)S(1)}, bf16[256,256]{1,0:T(8,128)(2,1)S(1)}, u32[]{:S(2)}, u32[]{:S(2)}) collective-permute-start(bf16[256,256]{1,0:T(8,128)(2,1)S(1)} %copy-done.25), channel_id=1, source_target_pairs={{2,0},{3,1},{0,2},{1,3},{6,4},{7,5},{4,6},{5,7},{10,8},{11,9},{8,1... | collective-permute-start | bytes 393224 | tf_op jit(solution)/shard_map/ppermute | solution.py:213
  (30 other events, 112.9 us)

commit v7 on v6

--- a/solution.py
+++ b/solution.py
@@ -62,24 +62,23 @@
 
 
 def upstream_kernel(*refs):
-    m_refs, at_ref, out_ref = refs[:5], refs[5], refs[6]
+    m_refs, out_refs = refs[:5], refs[5:7]
     for k, shift in enumerate(RING):
         info = info_of(m_refs, k)
         inv = jnp.concatenate([inverse_of(info, 0), inverse_of(info, 1)], axis=1)
-        z = (at_ref[2] + shift + 4) & 3
         for c in range(3):
             rows = min(64, 160 - 64 * c)
             up = m_refs[k][128 : 128 + rows, c * 256 : c * 256 + 256]
-            out_ref[z, c * 64 : c * 64 + rows] = (inv * up.astype(F32)).astype(BF)
+            out_refs[k // 2][k % 2, c * 64 : c * 64 + rows] = (inv * up.astype(F32)).astype(BF)
 
 
 def features_at(refs, k, f):
-    return refs[k][f] if k < 3 else refs[3 + f // 4][f % 4]
+    return refs[2 * k + f // 4][f % 4]
 
 
 def project_kernel(*refs):
-    x_refs, w_refs, m_refs, at_ref = refs[:5], refs[5:9], refs[9:14], refs[14]
-    out_ref, w_ref = refs[15:]
+    x_refs, w_refs, m_refs, at_ref = refs[:8], refs[8:12], refs[12:17], refs[17]
+    out_refs, w_ref = refs[18:20], refs[20]
     for k, shift in enumerate(RING):
         for flip in range(2):
             f = ((at_ref[3] + shift + 4) & 3) * 2 + ((at_ref[4] + flip) & 1)
@@ -89,15 +88,15 @@
         info = info_of(m_refs, k)
         inv = jnp.concatenate([inverse_of(info, 0), inverse_of(info, 1)], axis=1)
         whole = jnp.concatenate([features_at(x_refs, k, f) for f in range(8)], axis=0)
-        out_ref[(at_ref[2] + shift + 4) & 3] = (inv * dot(w, whole)).astype(BF)
+        out_refs[k // 2][k % 2] = (inv * dot(w, whole)).astype(BF)
 
 
 def collect(refs, base, src_ref, at_ref):
     rows = refs[0].shape[1]
     for i, ref in enumerate(refs):
-        x = (at_ref[1] + RING[min(i, 3)] + 4) & 3
-        for j in range(ref.shape[0]):
-            d = x * 4 + (j + 2 if i == 4 else j)
+        x = (at_ref[1] + RING[i // 2] + 4) & 3
+        for j in range(2):
+            d = x * 4 + ((at_ref[2] + RING[(i % 2) * 2 + j] + 4) & 3)
             for h in range(2):
                 src_ref[2 * d + h, base : base + rows] = ref[j, :, h * 128 : h * 128 + 128]
 
@@ -117,9 +116,9 @@
 
 
 def first_mix_kernel(*refs):
-    s_refs, u_refs, m_refs, sw_ref, at_ref = refs[:5], refs[5:10], refs[10:15], refs[15], refs[16]
-    hid_refs, back_ref, second_ref = refs[17:21], refs[21], refs[22]
-    src_ref, stage_ref, links_ref, sem = refs[23:]
+    s_refs, u_refs, m_refs, sw_ref, at_ref = refs[:8], refs[8:16], refs[16:21], refs[21], refs[22]
+    hid_refs, back_refs, second_ref = refs[23:27], refs[27:29], refs[29]
+    src_ref, stage_ref, links_ref, sem = refs[30:]
     scalars(m_refs, stage_ref, links_ref, sem)
     collect(s_refs, 0, src_ref, at_ref)
     collect(u_refs, 256, src_ref, at_ref)
@@ -139,13 +138,14 @@
             pull = total[256:416].astype(BF)
             second = second + dot(pull, one, NT)
             slope = s * (1.0 + m * (1.0 - s))
-            back_ref[z, :, lanes] = (inv * inv * dot(sw_ref[...], pull) * slope).astype(BF)
+            back = inv * inv * dot(sw_ref[...], pull) * slope
+            back_refs[k // 2][k % 2, :, lanes] = back.astype(BF)
     second_ref[...] = second
 
 
 def second_mix_kernel(*refs):
-    b_refs, m_refs, x_refs, second_ref, at_ref = refs[:5], refs[5:10], refs[10:15], refs[15], refs[16]
-    out_ref, src_ref, stage_ref, links_ref, sem = refs[17:]
+    b_refs, m_refs, x_refs, second_ref, at_ref = refs[:8], refs[8:13], refs[13:21], refs[21], refs[22]
+    out_ref, src_ref, stage_ref, links_ref, sem = refs[23:]
     scalars(m_refs, stage_ref, links_ref, sem)
     collect(b_refs, 0, src_ref, at_ref)
     rights = []
@@ -197,7 +197,7 @@
         second_ref[80:153, cols] = two[48:121]
 
 
-def call(kernel, shape, specs, scratch=(), flops=0, moved=0, limit=8):
+def call(kernel, shape, specs, scratch=(), flops=0, moved=0, limit=20):
     return pl.pallas_call(
         kernel,
         out_shape=shape,
@@ -221,9 +221,13 @@
     return fetch(value, axis, 1), fetch(value, axis, -1)
 
 
-def rounds(value, axis, half):
-    after, before = near(value, axis)
-    return [value, after, before, fetch(after[:half], axis, 1), fetch(before[half:], axis, -1)]
+def neighbours(low, high, axis):
+    return fetch(low, axis, 1), fetch(high, axis, -1), fetch(high, axis, 1), fetch(low, axis, -1)
+
+
+def rounds(low, high, found, passed, axis):
+    far = fetch(passed[0], axis, 1), fetch(passed[1], axis, -1)
+    return [low, high, passed[0], found[2], found[3], passed[1], *far]
 
 
 def body(features, first_weight, second_weight, degree, neighbour_block, neighbour_mask, upstream):
@@ -242,53 +246,56 @@
     other = lax.ppermute(weight, "c", [(0, 1), (1, 0)])
     after, before, other = lax.optimization_barrier((*near(mask, "z"), other))
     weights = ring(jnp.stack([weight, other]), "y")
+    x_low, x_high, after, before = lax.optimization_barrier((x_own[:4], x_own[4:], after, before))
+    x_near = neighbours(x_low, x_high, "z")
     far = [fetch(after[:192], "z", 1), fetch(before[192:], "z", -1)]
-    x_own, *far = lax.optimization_barrier((x_own, *far))
-    masks = [mask, after, before, *far]
-    scaled = call(upstream_kernel, shape((4, 160, 256), BF), [VMEM] * 5 + [SMEM], moved=1_000_000)(
-        *masks, at
-    )
-    x_after, x_before, after, before = lax.optimization_barrier((*near(x_own, "z"), *near(scaled, "x")))
-    x_far = [fetch(x_after[:4], "z", 1), fetch(x_before[4:], "z", -1)]
-    far = [fetch(after[:2], "x", 1), fetch(before[2:], "x", -1)]
-    *x_far, far_low, far_high = lax.optimization_barrier((*x_far, *far))
-    x_wide = [x_own, x_after, x_before, *x_far]
-    scaled = [scaled, after, before, far_low, far_high]
+    *passed, far_low, far_high, w1, w2, w3 = lax.optimization_barrier((*x_near[:2], *far, *weights[1:]))
+    masks = [mask, after, before, far_low, far_high]
+    weights = [weights[0], w1, w2, w3]
+    x_wide = rounds(x_low, x_high, x_near, passed, "z")
+    half = shape((2, 160, 256), BF)
+    scaled = call(upstream_kernel, (half, half), [VMEM] * 5, moved=1_000_000)(*masks)
+    u_near = neighbours(*scaled, "x")
+    *x_far, u0, u1 = lax.optimization_barrier((*x_wide[6:], *u_near[:2]))
+    x_wide = [*x_wide[:6], *x_far]
+    scaled = rounds(*scaled, u_near, (u0, u1), "x")
+    half = shape((2, 256, 256), BF)
     s = call(
         project_kernel,
-        shape((4, 256, 256), BF),
-        [VMEM] * 14 + [SMEM],
+        (half, half),
+        [VMEM] * 17 + [SMEM],
         [pltpu.VMEM((8, 96, 256), BF)],
         flops=400_000_000,
         moved=3_000_000,
     )(*x_wide, *weights, *masks, at)
-    s = rounds(s, "x", 2)
+    s_near = neighbours(*s, "x")
+    s = rounds(*s, s_near, s_near[:2], "x")
     own_second = lax.dynamic_slice(second_weight, (z * 256, 0), (256, 153))
     own_second = jnp.pad(own_second, ((0, 0), (0, 7)))
     links_scratch = [
         pltpu.VMEM((8, 128), I32), pltpu.SMEM((8, 128), I32), pltpu.SemaphoreType.DMA
     ]
-    *hid, back, second = call(
+    *hid, low, high, second = call(
         first_mix_kernel,
-        (shape((256, 256), BF),) * 4 + (shape((4, 256, 256), BF), shape((160, 256), F32)),
-        [VMEM] * 16 + [SMEM],
+        (shape((256, 256), BF),) * 4 + (half, half, shape((160, 256), F32)),
+        [VMEM] * 22 + [SMEM],
         [pltpu.VMEM((32, 416, 128), BF), *links_scratch],
         flops=700_000_000,
         moved=8_000_000,
-        limit=20,
     )(*s, *scaled, *masks, own_second, at)
-    after, before, *hid = lax.optimization_barrier((*near(back, "x"), *hid))
-    hid = [hid[0]] + [fetch(value, "z", -shift) for value, shift in zip(hid[1:], RING[1:])]
-    back = [back, after, before, fetch(after[:2], "x", 1), fetch(before[2:], "x", -1)]
+    b_near = neighbours(low, high, "x")
+    *passed, h1, h2, h3 = lax.optimization_barrier((*b_near[:2], *hid[1:]))
+    back = rounds(low, high, b_near, passed, "x")
+    hid = [hid[0]] + [fetch(value, "z", -shift) for value, shift in zip((h1, h2, h3), RING[1:])]
     part = call(
         second_mix_kernel,
         shape((8, 4, 128, 128), BF),
-        [VMEM] * 16 + [SMEM],
+        [VMEM] * 22 + [SMEM],
         [pltpu.VMEM((32, 256, 128), BF), *links_scratch],
         flops=900_000_000,
         moved=8_000_000,
-        limit=20,
     )(*back, *masks, *x_wide, second, at)
+    part, *hid = lax.optimization_barrier((part, *hid))
     part = lax.all_to_all(part.reshape(32, 128, 128), ("y", "c", "x"), 0, 0, tiled=True)
     tile = shape((16, 128, 128), BF)
     done = call(add_kernel, tile, [VMEM], moved=1_500_000)(part)

time: 172 us -> 162 us (0.942)
  local copies, waits for them, and re-layouts: 21.4 us -> 15.6 us
  blocking collectives: 24.8 us -> 21.8 us
  waiting for transfers between devices: 53.1 us -> 51.2 us
    ppermute x26 -> x34, waiting for transfers between devices: 52.8 us -> 37.6 us  [fetch(): return lax.ppermute(value, axis, [((i + shift) % 4, i) for i in range(4)])]
    all_to_all x1, waiting for transfers between devices: 0.01 us -> 10.1 us  [body(): done = lax.all_to_all(done, dom, 0, 0, tiled=True)]
    all_to_all x1, waiting for transfers between devices: 0.34 us -> 3.58 us  [body(): lax.all_to_all(features.reshape(96, 8, 256).transpose(1, 0, 2), feat, 0,...]
    all_to_all x1, blocking collectives: 24.8 us -> 21.8 us  [body(): lax.all_to_all(part.reshape(32, 128, 128), ('y', 'c', 'x'), 0, 0, tiled=T...]
    slice x8 -> x1, local copies, waits for them, and re-layouts: 2.53 us -> 0.03 us  [body(): x_own[4:]]
    unnamed x68 -> x62, local copies, waits for them, and re-layouts: 14.6 us -> 12.9 us
    ppermute x26 -> x34, starting transfers between devices: 46.1 us -> 45 us  [fetch(): return lax.ppermute(value, axis, [((i + shift) % 4, i) for i in range(4)])]
  transfers between devices with their start and end apart: 29 -> 37, of which waited for: 14 -> 14; matrix products, arithmetic and copies ran while one was open for 5% -> 2% of each run, Pallas kernels for 1% -> 4%
where the time goes in v7:
time: 162 us; the launch traced here: 161 us
  starting transfers between devices  54 us (33%)
  waiting for transfers between devices  51.2 us (32%)
  blocking collectives  21.8 us (13%)
  Pallas kernels  17.3 us (11%)
  local copies, waits for them, and re-layouts  15.6 us (10%)
    ppermute x34, starting transfers between devices, fetch(): return lax.ppermute(value, axis, [((i + shift) % 4, i) for i in range(4)])  45 us
    ppermute x34, waiting for transfers between devices, fetch(): return lax.ppermute(value, axis, [((i + shift) % 4, i) for i in range(4)])  37.6 us
    all_to_all x1, blocking collectives, body(): lax.all_to_all(part.reshape(32, 128, 128), ('y', 'c', 'x'), 0, 0, tiled=T...  21.8 us
    unnamed x62, local copies, waits for them, and re-layouts  12.9 us
    all_to_all x1, waiting for transfers between devices, body(): done = lax.all_to_all(done, dom, 0, 0, tiled=True)  10.1 us
    pallas_call x1, Pallas kernels, body(): call(first_mix_kernel, (shape((256, 256), BF),) * 4 + (half, half, shape(...  5.98 us
    all_to_all x1, starting transfers between devices, body(): lax.all_to_all(features.reshape(96, 8, 256).transpose(1, 0, 2), feat, 0,...  4.69 us
    pallas_call x1, Pallas kernels, body(): call(second_mix_kernel, shape((8, 4, 128, 128), BF), [VMEM] * 22 + [SMEM]...  4.39 us
  transfers between devices with their start and end apart: 37, of which 14 were waited for; matrix products, arithmetic and copies ran while one was open for 2% of the time, Pallas kernels for 4%

profile of v7, /device:TPU:0, one launch (start us, length us, event | category | flops | bytes accessed | tf_op | source)
XLA Modules:
  0.0 160.9 jit_solution(7248357284153085639)
XLA Ops:
  2.6 4.7 %all-to-all-start = ((bf16[8,96,256]{2,1,0:T(8,128)(2,1)}), bf16[8,96,256]{2,1,0:T(8,128)(2,1)S(1)}, u32[]{:S(2)}, u32[]{:S(2)}) async-start(bf16[8,96,256]{2,1,0:T(8,128)(2,1)} %bitcast.22), calls=%async_computation | async-start | bytes 786432 | tf_op jit(solution)/shard_map/all_to_all | solution.py:238
  8.1 2.0 %collective-permute-start.1 = (bf16[336,768]{1,0:T(8,128)(2,1)S(1)}, bf16[336,768]{1,0:T(8,128)(2,1)S(1)}, u32[]{:S(2)}, u32[]{:S(2)}) collective-permute-start(bf16[336,768]{1,0:T(8,128)(2,1)S(1)} %shard_map.94.refs_0_.refs_12_.refs_16_.refs_8_), channel_id=1, source_target_pairs={{3,0},{0,1},{1,2},{2,3},{7,4},{4,5},{5,6},{6,7},{11,8},{8,9},{9,10... | collective-permute-start | bytes 1548296 | tf_op jit(solution)/shard_map/ppermute | solution.py:213
  10.1 2.2 %collective-permute-start = (bf16[336,768]{1,0:T(8,128)(2,1)S(1)}, bf16[336,768]{1,0:T(8,128)(2,1)S(1)}, u32[]{:S(2)}, u32[]{:S(2)}) collective-permute-start(bf16[336,768]{1,0:T(8,128)(2,1)S(1)} %shard_map.94.refs_0_.refs_12_.refs_16_.refs_8_), channel_id=1, source_target_pairs={{1,0},{2,1},{3,2},{0,3},{5,4},{6,5},{7,6},{4,7},{9,8},{10,9},{11,1... | collective-permute-start | bytes 1548296 | tf_op jit(solution)/shard_map/ppermute | solution.py:213
  12.7 3.6 %all-to-all-done = bf16[8,96,256]{2,1,0:T(8,128)(2,1)S(1)} async-done(((bf16[8,96,256]{2,1,0:T(8,128)(2,1)}), bf16[8,96,256]{2,1,0:T(8,128)(2,1)S(1)}, u32[]{:S(2)}, u32[]{:S(2)}) %all-to-all-start) | async-done | bytes 393248 | tf_op jit(solution)/shard_map/all_to_all | solution.py:238
  16.3 8.4 %collective-permute-done.1.refs_2_.refs_14_.refs_18_.refs_10_ = bf16[336,768]{1,0:T(8,128)(2,1)S(1)} collective-permute-done((bf16[336,768]{1,0:T(8,128)(2,1)S(1)}, bf16[336,768]{1,0:T(8,128)(2,1)S(1)}, u32[]{:S(2)}, u32[]{:S(2)}) %collective-permute-start.1) | collective-permute-done | bytes 516128 | tf_op jit(solution)/shard_map/ppermute | solution.py:213
  24.7 3.2 %collective-permute-start.9 = (bf16[2,96,256]{2,1,0:T(8,128)(2,1)S(1)}, bf16[2,96,256]{2,1,0:T(8,128)(2,1)S(1)}, u32[]{:S(2)}, u32[]{:S(2)}) collective-permute-start(bf16[2,96,256]{2,1,0:T(8,128)(2,1)S(1)} %pad_maximum_fusion.refs_8_), channel_id=1, source_target_pairs={{64,0},{96,32},{0,64},{32,96},{65,1},{97,33},{1,65},{33,97},{66,2}... | collective-permute-start | bytes 294920 | tf_op jit(solution)/shard_map/ppermute | solution.py:213
  28.0 3.1 %collective-permute-start.5 = (bf16[192,768]{1,0:T(8,128)(2,1)S(1)}, bf16[192,768]{1,0:T(8,128)(2,1)S(1)}, u32[]{:S(2)}, u32[]{:S(2)}) collective-permute-start(bf16[192,768]{1,0:T(8,128)(2,1)S(1)} %slice.14), channel_id=1, source_target_pairs={{1,0},{2,1},{3,2},{0,3},{5,4},{6,5},{7,6},{4,7},{9,8},{10,9},{11,1... | collective-permute-start | bytes 884744 | tf_op jit(solution)/shard_map/ppermute | solution.py:213
  31.8 3.2 %collective-permute-start.3 = (bf16[4,96,256]{2,1,0:T(8,128)(2,1)S(1)}, bf16[4,96,256]{2,1,0:T(8,128)(2,1)S(1)}, u32[]{:S(2)}, u32[]{:S(2)}) collective-permute-start(bf16[4,96,256]{2,1,0:T(8,128)(2,1)S(1)} %get-tuple-element.46.refs_0_.refs_13_), channel_id=1, source_target_pairs={{1,0},{2,1},{3,2},{0,3},{5,4},{6,5},{7,6},{4,7},{9,8},{10,9},{11,1... | collective-permute-start | bytes 589832 | tf_op jit(solution)/shard_map/ppermute | solution.py:213
  38.3 3.3 %collective-permute-done.7.refs_9_ = bf16[2,96,256]{2,1,0:T(8,128)(2,1)S(1)} collective-permute-done((bf16[2,96,256]{2,1,0:T(8,128)(2,1)S(1)}, bf16[2,96,256]{2,1,0:T(8,128)(2,1)S(1)}, u32[]{:S(2)}, u32[]{:S(2)}) %collective-permute-start.7) | collective-permute-done | bytes 98336 | tf_op jit(solution)/shard_map/ppermute | solution.py:213
  43.4 2.8 %collective-permute-start.14 = (bf16[2,160,256]{2,1,0:T(8,128)(2,1)S(1)}, bf16[2,160,256]{2,1,0:T(8,128)(2,1)S(1)}, u32[]{:S(2)}, u32[]{:S(2)}) collective-permute-start(bf16[2,160,256]{2,1,0:T(8,128)(2,1)S(1)} %get-tuple-element.55.refs_8_), channel_id=1, source_target_pairs={{4,0},{8,4},{12,8},{0,12},{5,1},{9,5},{13,9},{1,13},{6,2},{10,6},{... | collective-permute-start | bytes 491528 | tf_op jit(solution)/shard_map/ppermute | solution.py:213
  46.1 2.2 %collective-permute-start.12 = (bf16[4,96,256]{2,1,0:T(8,128)(2,1)S(1)}, bf16[4,96,256]{2,1,0:T(8,128)(2,1)S(1)}, u32[]{:S(2)}, u32[]{:S(2)}) collective-permute-start(bf16[4,96,256]{2,1,0:T(8,128)(2,1)S(1)} %collective-permute-done.3.refs_2_.refs_15_), channel_id=1, source_target_pairs={{1,0},{2,1},{3,2},{0,3},{5,4},{6,5},{7,6},{4,7},{9,8},{10,9},{11,1... | collective-permute-start | bytes 589832 | tf_op jit(solution)/shard_map/ppermute | solution.py:213
  48.3 3.3 %collective-permute-start.10 = (bf16[4,96,256]{2,1,0:T(8,128)(2,1)S(1)}, bf16[4,96,256]{2,1,0:T(8,128)(2,1)}, u32[]{:S(2)}, u32[]{:S(2)}) collective-permute-start(bf16[4,96,256]{2,1,0:T(8,128)(2,1)S(1)} %get-tuple-element.47.refs_1_.refs_14_), channel_id=1, source_target_pairs={{1,0},{2,1},{3,2},{0,3},{5,4},{6,5},{7,6},{4,7},{9,8},{10,9},{11,1... | collective-permute-start | bytes 589832 | tf_op jit(solution)/shard_map/ppermute | solution.py:213
  52.4 6.8 %collective-permute-done.15.refs_13_ = bf16[2,160,256]{2,1,0:T(8,128)(2,1)} collective-permute-done((bf16[2,160,256]{2,1,0:T(8,128)(2,1)}, bf16[2,160,256]{2,1,0:T(8,128)(2,1)}, u32[]{:S(2)}, u32[]{:S(2)}) %collective-permute-start.15) | collective-permute-done | bytes 163872 | tf_op jit(solution)/shard_map/ppermute | solution.py:213
  61.8 2.5 %shard_map.96 = (bf16[2,256,256]{2,1,0:T(8,128)(2,1)}, bf16[2,256,256]{2,1,0:T(8,128)(2,1)}) custom-call(bf16[4,96,256]{2,1,0:T(8,128)(2,1)S(1)} %get-tuple-element.46.refs_0_.refs_13_, bf16[4,96,256]{2,1,0:T(8,128)(2,1)S(1)} %get-tuple-element.47.refs_1_.refs_14_, bf16[4,96,256]{2,1,0:T(8,128)(2,1)S(1)} %collective-permute-done.3.refs_2_.refs_15_, ...), custom_call_target="tpu_custom_call" | custom-call | flops 400000000 | bytes 3000000 | tf_op jit(solution)/shard_map/pallas_call | solution.py:263
  64.3 2.0 %collective-permute-start.19 = (bf16[2,256,256]{2,1,0:T(8,128)(2,1)}, bf16[2,256,256]{2,1,0:T(8,128)(2,1)}, u32[]{:S(2)}, u32[]{:S(2)}) collective-permute-start(bf16[2,256,256]{2,1,0:T(8,128)(2,1)} %get-tuple-element.63.refs_1_), channel_id=1, source_target_pairs={{12,0},{0,4},{4,8},{8,12},{13,1},{1,5},{5,9},{9,13},{14,2},{2,6},{... | collective-permute-start | bytes 786440 | tf_op jit(solution)/shard_map/ppermute | solution.py:213
  66.4 3.2 %collective-permute-start.22 = (bf16[2,160,256]{2,1,0:T(8,128)(2,1)}, bf16[2,160,256]{2,1,0:T(8,128)(2,1)S(1)}, u32[]{:S(2)}, u32[]{:S(2)}) collective-permute-start(bf16[2,160,256]{2,1,0:T(8,128)(2,1)} %get-tuple-element.56.refs_9_), channel_id=1, source_target_pairs={{4,0},{8,4},{12,8},{0,12},{5,1},{9,5},{13,9},{1,13},{6,2},{10,6},{... | collective-permute-start | bytes 491528 | tf_op jit(solution)/shard_map/ppermute | solution.py:213
  69.6 4.9 %collective-permute-done.23.refs_12_ = bf16[2,160,256]{2,1,0:T(8,128)(2,1)S(1)} collective-permute-done((bf16[2,160,256]{2,1,0:T(8,128)(2,1)S(1)}, bf16[2,160,256]{2,1,0:T(8,128)(2,1)S(1)}, u32[]{:S(2)}, u32[]{:S(2)}) %collective-permute-start.23) | collective-permute-done | bytes 163872 | tf_op jit(solution)/shard_map/ppermute | solution.py:213
  75.2 1.9 %collective-permute-start.18 = (bf16[2,256,256]{2,1,0:T(8,128)(2,1)}, bf16[2,256,256]{2,1,0:T(8,128)(2,1)}, u32[]{:S(2)}, u32[]{:S(2)}) collective-permute-start(bf16[2,256,256]{2,1,0:T(8,128)(2,1)} %get-tuple-element.62.refs_0_), channel_id=1, source_target_pairs={{12,0},{0,4},{4,8},{8,12},{13,1},{1,5},{5,9},{9,13},{14,2},{2,6},{... | collective-permute-start | bytes 786440 | tf_op jit(solution)/shard_map/ppermute | solution.py:213
  79.2 2.0 %collective-permute-start.21 = (bf16[2,256,256]{2,1,0:T(8,128)(2,1)}, bf16[2,256,256]{2,1,0:T(8,128)(2,1)}, u32[]{:S(2)}, u32[]{:S(2)}) collective-permute-start(bf16[2,256,256]{2,1,0:T(8,128)(2,1)} %collective-permute-done.19.refs_5_), channel_id=1, source_target_pairs={{12,0},{0,4},{4,8},{8,12},{13,1},{1,5},{5,9},{9,13},{14,2},{2,6},{... | collective-permute-start | bytes 786440 | tf_op jit(solution)/shard_map/ppermute | solution.py:213
  83.2 1.7 %copy.13 = bf16[256,153]{1,0:T(8,128)(2,1)} copy(bf16[256,153]{0,1:T(8,128)(2,1)} %constant_dynamic-slice_fusion) | data formatting | bytes 156672
  85.8 3.0 %collective-permute-done.25.refs_15_ = bf16[2,160,256]{2,1,0:T(8,128)(2,1)} collective-permute-done((bf16[2,160,256]{2,1,0:T(8,128)(2,1)}, bf16[2,160,256]{2,1,0:T(8,128)(2,1)}, u32[]{:S(2)}, u32[]{:S(2)}) %collective-permute-start.25) | collective-permute-done | bytes 163872 | tf_op jit(solution)/shard_map/ppermute | solution.py:213
  91.6 6.0 %shard_map.97 = (bf16[256,256]{1,0:T(8,128)(2,1)S(1)}, bf16[256,256]{1,0:T(8,128)(2,1)S(1)}, bf16[256,256]{1,0:T(8,128)(2,1)S(1)}, bf16[256,256]{1,0:T(8,128)(2,...) custom-call(bf16[2,256,256]{2,1,0:T(8,128)(2,1)} %get-tuple-element.62.refs_0_, ...), custom_call_target="tpu_custom_call" | custom-call | flops 700000000 | bytes 8000000 | tf_op jit(solution)/shard_map/pallas_call | solution.py:278
  101.1 2.5 %collective-permute-start.28 = (bf16[2,256,256]{2,1,0:T(8,128)(2,1)S(1)}, bf16[2,256,256]{2,1,0:T(8,128)(2,1)S(1)}, u32[]{:S(2)}, u32[]{:S(2)}) collective-permute-start(bf16[2,256,256]{2,1,0:T(8,128)(2,1)S(1)} %get-tuple-element.67.refs_1_), channel_id=1, source_target_pairs={{4,0},{8,4},{12,8},{0,12},{5,1},{9,5},{13,9},{1,13},{6,2},{10,6},{... | collective-permute-start | bytes 786440 | tf_op jit(solution)/shard_map/ppermute | solution.py:213
  103.5 3.7 %collective-permute-done.26.refs_2_ = bf16[2,256,256]{2,1,0:T(8,128)(2,1)S(1)} collective-permute-done((bf16[2,256,256]{2,1,0:T(8,128)(2,1)S(1)}, bf16[2,256,256]{2,1,0:T(8,128)(2,1)S(1)}, u32[]{:S(2)}, u32[]{:S(2)}) %collective-permute-start.26) | collective-permute-done | bytes 262176 | tf_op jit(solution)/shard_map/ppermute | solution.py:213
  107.3 1.6 collective-permute-done.27.refs_5_
  109.2 1.7 %collective-permute-start.31 = (bf16[2,256,256]{2,1,0:T(8,128)(2,1)S(1)}, bf16[2,256,256]{2,1,0:T(8,128)(2,1)S(1)}, u32[]{:S(2)}, u32[]{:S(2)}) collective-permute-start(bf16[2,256,256]{2,1,0:T(8,128)(2,1)S(1)} %collective-permute-done.27.refs_5_), channel_id=1, source_target_pairs={{12,0},{0,4},{4,8},{8,12},{13,1},{1,5},{5,9},{9,13},{14,2},{2,6},{... | collective-permute-start | bytes 786440 | tf_op jit(solution)/shard_map/ppermute | solution.py:213
  111.7 2.5 %collective-permute-start.33 = (bf16[256,256]{1,0:T(8,128)(2,1)S(1)}, bf16[256,256]{1,0:T(8,128)(2,1)S(1)}, u32[]{:S(2)}, u32[]{:S(2)}) collective-permute-start(bf16[256,256]{1,0:T(8,128)(2,1)S(1)} %get-tuple-element.76), channel_id=1, source_target_pairs={{1,0},{2,1},{3,2},{0,3},{5,4},{6,5},{7,6},{4,7},{9,8},{10,9},{11,1... | collective-permute-start | bytes 393224 | tf_op jit(solution)/shard_map/ppermute | solution.py:213
  116.7 4.4 %shard_map.98 = bf16[8,4,128,128]{3,2,1,0:T(8,128)(2,1)S(1)} custom-call(bf16[2,256,256]{2,1,0:T(8,128)(2,1)S(1)} %get-tuple-element.66.refs_0_, bf16[2,256,256]{2,1,0:T(8,128)(2,1)S(1)} %get-tuple-element.67.refs_1_, bf16[2,256,256]{2,1,0:T(8,128)(2,1)S(1)} %collective-permute-done.26.refs_2_, bf16[2,256,256]{2,1,0:T(8,128)(2,1)S(1)} %collective-permute-done.28.refs_3_, ...), custom_call_target="tpu_custom_call" | custom-call | flops 900000000 | bytes 8000000 | tf_op jit(solution)/shard_map/pallas_call | solution.py:290
  121.2 21.8 %all_to_all.15.part_ref = bf16[32,128,128]{2,1,0:T(8,128)(2,1)S(1)} all-to-all(bf16[32,128,128]{2,1,0:T(8,128)(2,1)S(1)} %bitcast.23), channel_id=1, replica_groups=mesh['y'=4,'c'=2,'x'=4,'z'=4] {'y','c','x'}, dimensions={0} | all-to-all | bytes 2097152 | tf_op jit(solution)/shard_map/all_to_all | solution.py:299
  144.0 4.0 %all-to-all-start.2 = ((bf16[16,128,128]{2,1,0:T(8,128)(2,1)}), bf16[16,128,128]{2,1,0:T(8,128)(2,1)S(1)}, u32[]{:S(2)}, u32[]{:S(2)}) async-start(bf16[16,128,128]{2,1,0:T(8,128)(2,1)} %shard_map.100), calls=%async_computation.2 | async-start | bytes 1048576 | tf_op jit(solution)/shard_map/all_to_all | solution.py:302
  148.0 1.5 shard_map.99
  149.6 10.1 %all-to-all-done.2.in_ref = bf16[16,128,128]{2,1,0:T(8,128)(2,1)S(1)} async-done(((bf16[16,128,128]{2,1,0:T(8,128)(2,1)}), bf16[16,128,128]{2,1,0:T(8,128)(2,1)S(1)}, u32[]{:S(2)}, u32[]{:S(2)}) %all-to-all-start.2) | async-done | bytes 524320 | tf_op jit(solution)/shard_map/all_to_all | solution.py:302
  (126 shorter events, 30.2 us)
Async XLA Ops:
  2.6 13.6 %all-to-all-start = ((bf16[8,96,256]{2,1,0:T(8,128)(2,1)}), bf16[8,96,256]{2,1,0:T(8,128)(2,1)S(1)}, u32[]{:S(2)}, u32[]{:S(2)}) async-start(bf16[8,96,256]{2,1,0:T(8,128)(2,1)} %bitcast.22), calls=%async_computation | async-start | bytes 786432 | tf_op jit(solution)/shard_map/all_to_all | solution.py:238
  8.1 16.5 %collective-permute-start.1 = (bf16[336,768]{1,0:T(8,128)(2,1)S(1)}, bf16[336,768]{1,0:T(8,128)(2,1)S(1)}, u32[]{:S(2)}, u32[]{:S(2)}) collective-permute-start(bf16[336,768]{1,0:T(8,128)(2,1)S(1)} %shard_map.94.refs_0_.refs_12_.refs_16_.refs_8_), channel_id=1, source_target_pairs={{3,0},{0,1},{1,2},{2,3},{7,4},{4,5},{5,6},{6,7},{11,8},{8,9},{9,10... | collective-permute-start | bytes 1548296 | tf_op jit(solution)/shard_map/ppermute | solution.py:213
  10.1 14.5 %collective-permute-start = (bf16[336,768]{1,0:T(8,128)(2,1)S(1)}, bf16[336,768]{1,0:T(8,128)(2,1)S(1)}, u32[]{:S(2)}, u32[]{:S(2)}) collective-permute-start(bf16[336,768]{1,0:T(8,128)(2,1)S(1)} %shard_map.94.refs_0_.refs_12_.refs_16_.refs_8_), channel_id=1, source_target_pairs={{1,0},{2,1},{3,2},{0,3},{5,4},{6,5},{7,6},{4,7},{9,8},{10,9},{11,1... | collective-permute-start | bytes 1548296 | tf_op jit(solution)/shard_map/ppermute | solution.py:213
  24.7 10.3 %collective-permute-start.9 = (bf16[2,96,256]{2,1,0:T(8,128)(2,1)S(1)}, bf16[2,96,256]{2,1,0:T(8,128)(2,1)S(1)}, u32[]{:S(2)}, u32[]{:S(2)}) collective-permute-start(bf16[2,96,256]{2,1,0:T(8,128)(2,1)S(1)} %pad_maximum_fusion.refs_8_), channel_id=1, source_target_pairs={{64,0},{96,32},{0,64},{32,96},{65,1},{97,33},{1,65},{33,97},{66,2}... | collective-permute-start | bytes 294920 | tf_op jit(solution)/shard_map/ppermute | solution.py:213
  28.0 14.7 %collective-permute-start.5 = (bf16[192,768]{1,0:T(8,128)(2,1)S(1)}, bf16[192,768]{1,0:T(8,128)(2,1)S(1)}, u32[]{:S(2)}, u32[]{:S(2)}) collective-permute-start(bf16[192,768]{1,0:T(8,128)(2,1)S(1)} %slice.14), channel_id=1, source_target_pairs={{1,0},{2,1},{3,2},{0,3},{5,4},{6,5},{7,6},{4,7},{9,8},{10,9},{11,1... | collective-permute-start | bytes 884744 | tf_op jit(solution)/shard_map/ppermute | solution.py:213
  31.1 11.6 %collective-permute-start.6 = (bf16[144,768]{1,0:T(8,128)(2,1)S(1)}, bf16[144,768]{1,0:T(8,128)(2,1)S(1)}, u32[]{:S(2)}, u32[]{:S(2)}) collective-permute-start(bf16[144,768]{1,0:T(8,128)(2,1)S(1)} %slice.15), channel_id=1, source_target_pairs={{3,0},{0,1},{1,2},{2,3},{7,4},{4,5},{5,6},{6,7},{11,8},{8,9},{9,10... | collective-permute-start | bytes 663560 | tf_op jit(solution)/shard_map/ppermute | solution.py:213
  31.8 9.9 %collective-permute-start.3 = (bf16[4,96,256]{2,1,0:T(8,128)(2,1)S(1)}, bf16[4,96,256]{2,1,0:T(8,128)(2,1)S(1)}, u32[]{:S(2)}, u32[]{:S(2)}) collective-permute-start(bf16[4,96,256]{2,1,0:T(8,128)(2,1)S(1)} %get-tuple-element.46.refs_0_.refs_13_), channel_id=1, source_target_pairs={{1,0},{2,1},{3,2},{0,3},{5,4},{6,5},{7,6},{4,7},{9,8},{10,9},{11,1... | collective-permute-start | bytes 589832 | tf_op jit(solution)/shard_map/ppermute | solution.py:213
  35.6 7.1 %collective-permute-start.4 = (bf16[4,96,256]{2,1,0:T(8,128)(2,1)S(1)}, bf16[4,96,256]{2,1,0:T(8,128)(2,1)S(1)}, u32[]{:S(2)}, u32[]{:S(2)}) collective-permute-start(bf16[4,96,256]{2,1,0:T(8,128)(2,1)S(1)} %get-tuple-element.47.refs_1_.refs_14_), channel_id=1, source_target_pairs={{3,0},{0,1},{1,2},{2,3},{7,4},{4,5},{5,6},{6,7},{11,8},{8,9},{9,10... | collective-permute-start | bytes 589832 | tf_op jit(solution)/shard_map/ppermute | solution.py:213
  43.4 8.2 %collective-permute-start.14 = (bf16[2,160,256]{2,1,0:T(8,128)(2,1)S(1)}, bf16[2,160,256]{2,1,0:T(8,128)(2,1)S(1)}, u32[]{:S(2)}, u32[]{:S(2)}) collective-permute-start(bf16[2,160,256]{2,1,0:T(8,128)(2,1)S(1)} %get-tuple-element.55.refs_8_), channel_id=1, source_target_pairs={{4,0},{8,4},{12,8},{0,12},{5,1},{9,5},{13,9},{1,13},{6,2},{10,6},{... | collective-permute-start | bytes 491528 | tf_op jit(solution)/shard_map/ppermute | solution.py:213
  46.1 13.0 %collective-permute-start.12 = (bf16[4,96,256]{2,1,0:T(8,128)(2,1)S(1)}, bf16[4,96,256]{2,1,0:T(8,128)(2,1)S(1)}, u32[]{:S(2)}, u32[]{:S(2)}) collective-permute-start(bf16[4,96,256]{2,1,0:T(8,128)(2,1)S(1)} %collective-permute-done.3.refs_2_.refs_15_), channel_id=1, source_target_pairs={{1,0},{2,1},{3,2},{0,3},{5,4},{6,5},{7,6},{4,7},{9,8},{10,9},{11,1... | collective-permute-start | bytes 589832 | tf_op jit(solution)/shard_map/ppermute | solution.py:213
  48.3 10.8 %collective-permute-start.13 = (bf16[4,96,256]{2,1,0:T(8,128)(2,1)S(1)}, bf16[4,96,256]{2,1,0:T(8,128)(2,1)}, u32[]{:S(2)}, u32[]{:S(2)}) collective-permute-start(bf16[4,96,256]{2,1,0:T(8,128)(2,1)S(1)} %collective-permute-done.4.refs_5_.refs_18_), channel_id=1, source_target_pairs={{3,0},{0,1},{1,2},{2,3},{7,4},{4,5},{5,6},{6,7},{11,8},{8,9},{9,10... | collective-permute-start | bytes 589832 | tf_op jit(solution)/shard_map/ppermute | solution.py:213
  48.3 10.8 %collective-permute-start.11 = (bf16[4,96,256]{2,1,0:T(8,128)(2,1)S(1)}, bf16[4,96,256]{2,1,0:T(8,128)(2,1)}, u32[]{:S(2)}, u32[]{:S(2)}) collective-permute-start(bf16[4,96,256]{2,1,0:T(8,128)(2,1)S(1)} %get-tuple-element.46.refs_0_.refs_13_), channel_id=1, source_target_pairs={{3,0},{0,1},{1,2},{2,3},{7,4},{4,5},{5,6},{6,7},{11,8},{8,9},{9,10... | collective-permute-start | bytes 589832 | tf_op jit(solution)/shard_map/ppermute | solution.py:213
  48.3 10.8 %collective-permute-start.10 = (bf16[4,96,256]{2,1,0:T(8,128)(2,1)S(1)}, bf16[4,96,256]{2,1,0:T(8,128)(2,1)}, u32[]{:S(2)}, u32[]{:S(2)}) collective-permute-start(bf16[4,96,256]{2,1,0:T(8,128)(2,1)S(1)} %get-tuple-element.47.refs_1_.refs_14_), channel_id=1, source_target_pairs={{1,0},{2,1},{3,2},{0,3},{5,4},{6,5},{7,6},{4,7},{9,8},{10,9},{11,1... | collective-permute-start | bytes 589832 | tf_op jit(solution)/shard_map/ppermute | solution.py:213
  64.3 14.8 %collective-permute-start.16 = (bf16[2,256,256]{2,1,0:T(8,128)(2,1)}, bf16[2,256,256]{2,1,0:T(8,128)(2,1)}, u32[]{:S(2)}, u32[]{:S(2)}) collective-permute-start(bf16[2,256,256]{2,1,0:T(8,128)(2,1)} %get-tuple-element.62.refs_0_), channel_id=1, source_target_pairs={{4,0},{8,4},{12,8},{0,12},{5,1},{9,5},{13,9},{1,13},{6,2},{10,6},{... | collective-permute-start | bytes 786440 | tf_op jit(solution)/shard_map/ppermute | solution.py:213
  64.3 14.8 %collective-permute-start.19 = (bf16[2,256,256]{2,1,0:T(8,128)(2,1)}, bf16[2,256,256]{2,1,0:T(8,128)(2,1)}, u32[]{:S(2)}, u32[]{:S(2)}) collective-permute-start(bf16[2,256,256]{2,1,0:T(8,128)(2,1)} %get-tuple-element.63.refs_1_), channel_id=1, source_target_pairs={{12,0},{0,4},{4,8},{8,12},{13,1},{1,5},{5,9},{9,13},{14,2},{2,6},{... | collective-permute-start | bytes 786440 | tf_op jit(solution)/shard_map/ppermute | solution.py:213
  66.4 8.2 %collective-permute-start.23 = (bf16[2,160,256]{2,1,0:T(8,128)(2,1)S(1)}, bf16[2,160,256]{2,1,0:T(8,128)(2,1)S(1)}, u32[]{:S(2)}, u32[]{:S(2)}) collective-permute-start(bf16[2,160,256]{2,1,0:T(8,128)(2,1)S(1)} %copy-done.3), channel_id=1, source_target_pairs={{12,0},{0,4},{4,8},{8,12},{13,1},{1,5},{5,9},{9,13},{14,2},{2,6},{... | collective-permute-start | bytes 491528 | tf_op jit(solution)/shard_map/ppermute | solution.py:213
  66.4 10.7 %collective-permute-start.22 = (bf16[2,160,256]{2,1,0:T(8,128)(2,1)}, bf16[2,160,256]{2,1,0:T(8,128)(2,1)S(1)}, u32[]{:S(2)}, u32[]{:S(2)}) collective-permute-start(bf16[2,160,256]{2,1,0:T(8,128)(2,1)} %get-tuple-element.56.refs_9_), channel_id=1, source_target_pairs={{4,0},{8,4},{12,8},{0,12},{5,1},{9,5},{13,9},{1,13},{6,2},{10,6},{... | collective-permute-start | bytes 491528 | tf_op jit(solution)/shard_map/ppermute | solution.py:213
  69.6 11.5 %collective-permute-start.24 = (bf16[2,160,256]{2,1,0:T(8,128)(2,1)S(1)}, bf16[2,160,256]{2,1,0:T(8,128)(2,1)S(1)}, u32[]{:S(2)}, u32[]{:S(2)}) collective-permute-start(bf16[2,160,256]{2,1,0:T(8,128)(2,1)S(1)} %copy-done.6), channel_id=1, source_target_pairs={{4,0},{8,4},{12,8},{0,12},{5,1},{9,5},{13,9},{1,13},{6,2},{10,6},{... | collective-permute-start | bytes 491528 | tf_op jit(solution)/shard_map/ppermute | solution.py:213
  75.2 13.6 %collective-permute-start.18 = (bf16[2,256,256]{2,1,0:T(8,128)(2,1)}, bf16[2,256,256]{2,1,0:T(8,128)(2,1)}, u32[]{:S(2)}, u32[]{:S(2)}) collective-permute-start(bf16[2,256,256]{2,1,0:T(8,128)(2,1)} %get-tuple-element.62.refs_0_), channel_id=1, source_target_pairs={{12,0},{0,4},{4,8},{8,12},{13,1},{1,5},{5,9},{9,13},{14,2},{2,6},{... | collective-permute-start | bytes 786440 | tf_op jit(solution)/shard_map/ppermute | solution.py:213
  77.8 11.1 %collective-permute-start.17 = (bf16[2,256,256]{2,1,0:T(8,128)(2,1)}, bf16[2,256,256]{2,1,0:T(8,128)(2,1)}, u32[]{:S(2)}, u32[]{:S(2)}) collective-permute-start(bf16[2,256,256]{2,1,0:T(8,128)(2,1)} %get-tuple-element.63.refs_1_), channel_id=1, source_target_pairs={{4,0},{8,4},{12,8},{0,12},{5,1},{9,5},{13,9},{1,13},{6,2},{10,6},{... | collective-permute-start | bytes 786440 | tf_op jit(solution)/shard_map/ppermute | solution.py:213
  79.1 9.7 %collective-permute-start.20 = (bf16[2,256,256]{2,1,0:T(8,128)(2,1)}, bf16[2,256,256]{2,1,0:T(8,128)(2,1)}, u32[]{:S(2)}, u32[]{:S(2)}) collective-permute-start(bf16[2,256,256]{2,1,0:T(8,128)(2,1)} %collective-permute-done.16.refs_2_), channel_id=1, source_target_pairs={{4,0},{8,4},{12,8},{0,12},{5,1},{9,5},{13,9},{1,13},{6,2},{10,6},{... | collective-permute-start | bytes 786440 | tf_op jit(solution)/shard_map/ppermute | solution.py:213
  79.2 9.7 %collective-permute-start.21 = (bf16[2,256,256]{2,1,0:T(8,128)(2,1)}, bf16[2,256,256]{2,1,0:T(8,128)(2,1)}, u32[]{:S(2)}, u32[]{:S(2)}) collective-permute-start(bf16[2,256,256]{2,1,0:T(8,128)(2,1)} %collective-permute-done.19.refs_5_), channel_id=1, source_target_pairs={{12,0},{0,4},{4,8},{8,12},{13,1},{1,5},{5,9},{9,13},{14,2},{2,6},{... | collective-permute-start | bytes 786440 | tf_op jit(solution)/shard_map/ppermute | solution.py:213
  81.8 7.0 %collective-permute-start.25 = (bf16[2,160,256]{2,1,0:T(8,128)(2,1)}, bf16[2,160,256]{2,1,0:T(8,128)(2,1)}, u32[]{:S(2)}, u32[]{:S(2)}) collective-permute-start(bf16[2,160,256]{2,1,0:T(8,128)(2,1)} %collective-permute-done.15.refs_13_), channel_id=1, source_target_pairs={{12,0},{0,4},{4,8},{8,12},{13,1},{1,5},{5,9},{9,13},{14,2},{2,6},{... | collective-permute-start | bytes 491528 | tf_op jit(solution)/shard_map/ppermute | solution.py:213
  98.3 9.0 %collective-permute-start.26 = (bf16[2,256,256]{2,1,0:T(8,128)(2,1)S(1)}, bf16[2,256,256]{2,1,0:T(8,128)(2,1)S(1)}, u32[]{:S(2)}, u32[]{:S(2)}) collective-permute-start(bf16[2,256,256]{2,1,0:T(8,128)(2,1)S(1)} %get-tuple-element.66.refs_0_), channel_id=1, source_target_pairs={{4,0},{8,4},{12,8},{0,12},{5,1},{9,5},{13,9},{1,13},{6,2},{10,6},{... | collective-permute-start | bytes 786440 | tf_op jit(solution)/shard_map/ppermute | solution.py:213
  99.2 9.6 %collective-permute-start.27 = (bf16[2,256,256]{2,1,0:T(8,128)(2,1)S(1)}, bf16[2,256,256]{2,1,0:T(8,128)(2,1)S(1)}, u32[]{:S(2)}, u32[]{:S(2)}) collective-permute-start(bf16[2,256,256]{2,1,0:T(8,128)(2,1)S(1)} %get-tuple-element.67.refs_1_), channel_id=1, source_target_pairs={{12,0},{0,4},{4,8},{8,12},{13,1},{1,5},{5,9},{9,13},{14,2},{2,6},{... | collective-permute-start | bytes 786440 | tf_op jit(solution)/shard_map/ppermute | solution.py:213
  100.3 11.4 %collective-permute-start.29 = (bf16[2,256,256]{2,1,0:T(8,128)(2,1)S(1)}, bf16[2,256,256]{2,1,0:T(8,128)(2,1)S(1)}, u32[]{:S(2)}, u32[]{:S(2)}) collective-permute-start(bf16[2,256,256]{2,1,0:T(8,128)(2,1)S(1)} %get-tuple-element.66.refs_0_), channel_id=1, source_target_pairs={{12,0},{0,4},{4,8},{8,12},{13,1},{1,5},{5,9},{9,13},{14,2},{2,6},{... | collective-permute-start | bytes 786440 | tf_op jit(solution)/shard_map/ppermute | solution.py:213
  101.1 13.1 %collective-permute-start.28 = (bf16[2,256,256]{2,1,0:T(8,128)(2,1)S(1)}, bf16[2,256,256]{2,1,0:T(8,128)(2,1)S(1)}, u32[]{:S(2)}, u32[]{:S(2)}) collective-permute-start(bf16[2,256,256]{2,1,0:T(8,128)(2,1)S(1)} %get-tuple-element.67.refs_1_), channel_id=1, source_target_pairs={{4,0},{8,4},{12,8},{0,12},{5,1},{9,5},{13,9},{1,13},{6,2},{10,6},{... | collective-permute-start | bytes 786440 | tf_op jit(solution)/shard_map/ppermute | solution.py:213
  109.2 7.6 %collective-permute-start.31 = (bf16[2,256,256]{2,1,0:T(8,128)(2,1)S(1)}, bf16[2,256,256]{2,1,0:T(8,128)(2,1)S(1)}, u32[]{:S(2)}, u32[]{:S(2)}) collective-permute-start(bf16[2,256,256]{2,1,0:T(8,128)(2,1)S(1)} %collective-permute-done.27.refs_5_), channel_id=1, source_target_pairs={{12,0},{0,4},{4,8},{8,12},{13,1},{1,5},{5,9},{9,13},{14,2},{2,6},{... | collective-permute-start | bytes 786440 | tf_op jit(solution)/shard_map/ppermute | solution.py:213
  110.9 10.2 %collective-permute-start.32 = (bf16[256,256]{1,0:T(8,128)(2,1)S(1)}, bf16[256,256]{1,0:T(8,128)(2,1)S(1)}, u32[]{:S(2)}, u32[]{:S(2)}) collective-permute-start(bf16[256,256]{1,0:T(8,128)(2,1)S(1)} %get-tuple-element.75), channel_id=1, source_target_pairs={{3,0},{0,1},{1,2},{2,3},{7,4},{4,5},{5,6},{6,7},{11,8},{8,9},{9,10... | collective-permute-start | bytes 393224 | tf_op jit(solution)/shard_map/ppermute | solution.py:213
  111.7 9.5 %collective-permute-start.33 = (bf16[256,256]{1,0:T(8,128)(2,1)S(1)}, bf16[256,256]{1,0:T(8,128)(2,1)S(1)}, u32[]{:S(2)}, u32[]{:S(2)}) collective-permute-start(bf16[256,256]{1,0:T(8,128)(2,1)S(1)} %get-tuple-element.76), channel_id=1, source_target_pairs={{1,0},{2,1},{3,2},{0,3},{5,4},{6,5},{7,6},{4,7},{9,8},{10,9},{11,1... | collective-permute-start | bytes 393224 | tf_op jit(solution)/shard_map/ppermute | solution.py:213
  114.1 7.0 %collective-permute-start.34 = (bf16[256,256]{1,0:T(8,128)(2,1)S(1)}, bf16[256,256]{1,0:T(8,128)(2,1)S(1)}, u32[]{:S(2)}, u32[]{:S(2)}) collective-permute-start(bf16[256,256]{1,0:T(8,128)(2,1)S(1)} %get-tuple-element.77), channel_id=1, source_target_pairs={{2,0},{3,1},{0,2},{1,3},{6,4},{7,5},{4,6},{5,7},{10,8},{11,9},{8,1... | collective-permute-start | bytes 393224 | tf_op jit(solution)/shard_map/ppermute | solution.py:213
  144.0 15.7 %all-to-all-start.2 = ((bf16[16,128,128]{2,1,0:T(8,128)(2,1)}), bf16[16,128,128]{2,1,0:T(8,128)(2,1)S(1)}, u32[]{:S(2)}, u32[]{:S(2)}) async-start(bf16[16,128,128]{2,1,0:T(8,128)(2,1)} %shard_map.100), calls=%async_computation.2 | async-start | bytes 1048576 | tf_op jit(solution)/shard_map/all_to_all | solution.py:302
  (35 other events, 248.8 us)

commit v8 on v7

--- a/solution.py
+++ b/solution.py
@@ -29,63 +29,58 @@
     return (block % 4) * 4 + block // 4
 
 
-def mask_kernel(mask_ref, up_ref, deg_ref, links_ref, out_ref):
-    for b, at in enumerate((0, 192)):
+def mask_kernel(mask_ref, out_ref):
+    for b in range(2):
         for k in range(6):
-            out_ref[at : at + 128, k * 128 : k * 128 + 128] = mask_ref[b, k].astype(F32).astype(BF)
-    out_ref[128:192, 0:256] = up_ref[0:64, :]
-    out_ref[128:192, 256:512] = up_ref[64:128, :]
-    rest = jnp.concatenate([up_ref[128:153, :].astype(F32), jnp.zeros((39, 256), F32)], axis=0)
-    out_ref[128:192, 512:768] = rest.astype(BF)
-    info = []
+            out_ref[b * 128 : b * 128 + 128, k * 128 : k * 128 + 128] = (
+                mask_ref[b, k].astype(F32).astype(BF)
+            )
+
+
+def node_kernel(up_ref, deg_ref, links_ref, out_ref):
+    info, inv = [], []
     for b in range(2):
         degree = deg_ref[b : b + 1, :]
         info += [degree >> 5, degree & 31]
+        inv.append(lax.rsqrt(degree.astype(F32)))
+    scaled = jnp.concatenate(inv, axis=1) * up_ref[...].astype(F32)
+    out_ref[0:160, :] = jnp.concatenate([scaled, jnp.zeros((7, 256), F32)], axis=0).astype(BF)
     info = jnp.concatenate(info + [links_ref[...], jnp.zeros((11, 128), I32)], axis=0)
-    out_ref[320:336, :] = jnp.zeros((16, 768), BF)
-    out_ref[320:336, 0:128] = info.astype(F32).astype(BF)
+    out_ref[160:176, 0:128] = info.astype(F32).astype(BF)
+    out_ref[160:176, 128:256] = jnp.zeros((16, 128), BF)
+
+
+def pack_kernel(*refs):
+    for k in range(4):
+        refs[4 + k // 2][k % 2] = refs[k][0:160, :]
 
 
 def block_of(m_refs, k, b):
-    if k < 3:
-        return m_refs[k][b * 192 : b * 192 + 128, :]
-    return m_refs[3 + b][0:128, :]
-
-
-def info_of(m_refs, k):
-    rows = m_refs[k][320:336, 0:128] if k < 3 else m_refs[4][128:144, 0:128]
-    return rows.astype(F32)
+    return m_refs[k][b * 128 : b * 128 + 128, :] if k < 3 else m_refs[3 + b][...]
+
+
+def info_of(i_refs, k):
+    return i_refs[k][160:176, 0:128].astype(F32)
 
 
 def inverse_of(info, b):
     return lax.rsqrt(info[2 * b : 2 * b + 1] * 32.0 + info[2 * b + 1 : 2 * b + 2])
 
 
-def upstream_kernel(*refs):
-    m_refs, out_refs = refs[:5], refs[5:7]
-    for k, shift in enumerate(RING):
-        info = info_of(m_refs, k)
-        inv = jnp.concatenate([inverse_of(info, 0), inverse_of(info, 1)], axis=1)
-        for c in range(3):
-            rows = min(64, 160 - 64 * c)
-            up = m_refs[k][128 : 128 + rows, c * 256 : c * 256 + 256]
-            out_refs[k // 2][k % 2, c * 64 : c * 64 + rows] = (inv * up.astype(F32)).astype(BF)
-
-
 def features_at(refs, k, f):
     return refs[2 * k + f // 4][f % 4]
 
 
 def project_kernel(*refs):
-    x_refs, w_refs, m_refs, at_ref = refs[:8], refs[8:12], refs[12:17], refs[17]
-    out_refs, w_ref = refs[18:20], refs[20]
+    x_refs, w_refs, i_refs, at_ref = refs[:8], refs[8:12], refs[12:16], refs[16]
+    out_refs, w_ref = refs[17:19], refs[19]
     for k, shift in enumerate(RING):
         for flip in range(2):
             f = ((at_ref[3] + shift + 4) & 3) * 2 + ((at_ref[4] + flip) & 1)
             w_ref[f] = w_refs[k][flip]
     w = w_ref[...].reshape(768, 256).astype(F32).T.astype(BF)
     for k, shift in enumerate(RING):
-        info = info_of(m_refs, k)
+        info = info_of(i_refs, k)
         inv = jnp.concatenate([inverse_of(info, 0), inverse_of(info, 1)], axis=1)
         whole = jnp.concatenate([features_at(x_refs, k, f) for f in range(8)], axis=0)
         out_refs[k // 2][k % 2] = (inv * dot(w, whole)).astype(BF)
@@ -101,8 +96,8 @@
                 src_ref[2 * d + h, base : base + rows] = ref[j, :, h * 128 : h * 128 + 128]
 
 
-def scalars(m_refs, stage_ref, links_ref, sem):
-    rows = [info_of(m_refs, k)[4:5] for k in range(4)]
+def scalars(i_refs, stage_ref, links_ref, sem):
+    rows = [info_of(i_refs, k)[4:5] for k in range(4)]
     stage_ref[...] = jnp.concatenate(rows + [jnp.zeros((4, 128), F32)], axis=0).astype(I32)
     copy = pltpu.make_async_copy(stage_ref, links_ref, sem)
     copy.start()
@@ -117,15 +112,15 @@
 
 def first_mix_kernel(*refs):
     s_refs, u_refs, m_refs, sw_ref, at_ref = refs[:8], refs[8:16], refs[16:21], refs[21], refs[22]
-    hid_refs, back_refs, second_ref = refs[23:27], refs[27:29], refs[29]
-    src_ref, stage_ref, links_ref, sem = refs[30:]
-    scalars(m_refs, stage_ref, links_ref, sem)
+    i_refs, hid_refs, back_refs, second_ref = refs[23:27], refs[27:31], refs[31:33], refs[33]
+    src_ref, stage_ref, links_ref, sem = refs[34:]
+    scalars(i_refs, stage_ref, links_ref, sem)
     collect(s_refs, 0, src_ref, at_ref)
     collect(u_refs, 256, src_ref, at_ref)
     second = jnp.zeros((160, 256), F32)
     for k, shift in enumerate(RING):
         z = (at_ref[2] + shift + 4) & 3
-        info = info_of(m_refs, k)
+        info = info_of(i_refs, k)
         for b in range(2):
             inv = inverse_of(info, b)
             lanes = slice(b * 128, b * 128 + 128)
@@ -145,13 +140,13 @@
 
 def second_mix_kernel(*refs):
     b_refs, m_refs, x_refs, second_ref, at_ref = refs[:8], refs[8:13], refs[13:21], refs[21], refs[22]
-    out_ref, src_ref, stage_ref, links_ref, sem = refs[23:]
-    scalars(m_refs, stage_ref, links_ref, sem)
+    i_refs, out_ref, src_ref, stage_ref, links_ref, sem = refs[23:27], *refs[27:]
+    scalars(i_refs, stage_ref, links_ref, sem)
     collect(b_refs, 0, src_ref, at_ref)
     rights = []
     for k, shift in enumerate(RING):
         z = (at_ref[2] + shift + 4) & 3
-        info = info_of(m_refs, k)
+        info = info_of(i_refs, k)
         parts = []
         for b in range(2):
             total = spread(src_ref, links_ref, m_refs, k, b, (at_ref[1] * 4 + z) * 2 + b)
@@ -239,37 +234,41 @@
         features.reshape(96, 8, 256).transpose(1, 0, 2), feat, 0, 0, tiled=True
     )
     links = jnp.pad(jnp.maximum(neighbour_block.reshape(1, 12), 0), ((0, 0), (0, 116)))
-    mask = call(mask_kernel, shape((336, 768), BF), [VMEM] * 4, moved=1_200_000)(
-        neighbour_mask[0], upstream[0].T, degree.reshape(2, 128), links
-    )
+    nodes = call(node_kernel, shape((176, 256), BF), [VMEM] * 3, moved=200_000)(
+        upstream[0].T, degree.reshape(2, 128), links
+    )
+    nodes = ring(nodes, "z")
+    half = shape((2, 160, 256), BF)
+    scaled = call(pack_kernel, (half, half), [VMEM] * 4, moved=600_000)(*nodes)
     weight = lax.dynamic_slice(first_weight, (0, z * 256), (96, 256))
     other = lax.ppermute(weight, "c", [(0, 1), (1, 0)])
-    after, before, other = lax.optimization_barrier((*near(mask, "z"), other))
+    mask = call(mask_kernel, shape((256, 768), BF), [VMEM], moved=1_200_000)(neighbour_mask[0])
+    x_low, x_high, *scaled, mask, other = lax.optimization_barrier(
+        (x_own[:4], x_own[4:], *scaled, mask, other)
+    )
+    x_near = neighbours(x_low, x_high, "z")
+    u_near = neighbours(*scaled, "x")
+    x0, x1, u0, u1, other = lax.optimization_barrier((*x_near[:2], *u_near[:2], other))
     weights = ring(jnp.stack([weight, other]), "y")
-    x_low, x_high, after, before = lax.optimization_barrier((x_own[:4], x_own[4:], after, before))
-    x_near = neighbours(x_low, x_high, "z")
-    far = [fetch(after[:192], "z", 1), fetch(before[192:], "z", -1)]
-    *passed, far_low, far_high, w1, w2, w3 = lax.optimization_barrier((*x_near[:2], *far, *weights[1:]))
-    masks = [mask, after, before, far_low, far_high]
-    weights = [weights[0], w1, w2, w3]
-    x_wide = rounds(x_low, x_high, x_near, passed, "z")
-    half = shape((2, 160, 256), BF)
-    scaled = call(upstream_kernel, (half, half), [VMEM] * 5, moved=1_000_000)(*masks)
-    u_near = neighbours(*scaled, "x")
-    *x_far, u0, u1 = lax.optimization_barrier((*x_wide[6:], *u_near[:2]))
+    x_wide = rounds(x_low, x_high, x_near, (x0, x1), "z")
+    scaled = rounds(*scaled, u_near, (u0, u1), "x")
+    *x_far, u2, u3, u4, u5 = lax.optimization_barrier((*x_wide[6:], *scaled[3:5], *scaled[6:]))
     x_wide = [*x_wide[:6], *x_far]
-    scaled = rounds(*scaled, u_near, (u0, u1), "x")
+    scaled = [*scaled[:3], u2, u3, scaled[5], u4, u5]
     half = shape((2, 256, 256), BF)
     s = call(
         project_kernel,
         (half, half),
-        [VMEM] * 17 + [SMEM],
+        [VMEM] * 16 + [SMEM],
         [pltpu.VMEM((8, 96, 256), BF)],
         flops=400_000_000,
         moved=3_000_000,
-    )(*x_wide, *weights, *masks, at)
+    )(*x_wide, *weights, *nodes, at)
+    *s, mask = lax.optimization_barrier((*s, mask))
     s_near = neighbours(*s, "x")
+    after, before = near(mask, "z")
     s = rounds(*s, s_near, s_near[:2], "x")
+    masks = [mask, after, before, fetch(after[:128], "z", 1), fetch(before[128:], "z", -1)]
     own_second = lax.dynamic_slice(second_weight, (z * 256, 0), (256, 153))
     own_second = jnp.pad(own_second, ((0, 0), (0, 7)))
     links_scratch = [
@@ -278,11 +277,11 @@
     *hid, low, high, second = call(
         first_mix_kernel,
         (shape((256, 256), BF),) * 4 + (half, half, shape((160, 256), F32)),
-        [VMEM] * 22 + [SMEM],
+        [VMEM] * 22 + [SMEM] + [VMEM] * 4,
         [pltpu.VMEM((32, 416, 128), BF), *links_scratch],
         flops=700_000_000,
         moved=8_000_000,
-    )(*s, *scaled, *masks, own_second, at)
+    )(*s, *scaled, *masks, own_second, at, *nodes)
     b_near = neighbours(low, high, "x")
     *passed, h1, h2, h3 = lax.optimization_barrier((*b_near[:2], *hid[1:]))
     back = rounds(low, high, b_near, passed, "x")
@@ -290,11 +289,11 @@
     part = call(
         second_mix_kernel,
         shape((8, 4, 128, 128), BF),
-        [VMEM] * 22 + [SMEM],
+        [VMEM] * 22 + [SMEM] + [VMEM] * 4,
         [pltpu.VMEM((32, 256, 128), BF), *links_scratch],
         flops=900_000_000,
         moved=8_000_000,
-    )(*back, *masks, *x_wide, second, at)
+    )(*back, *masks, *x_wide, second, at, *nodes)
     part, *hid = lax.optimization_barrier((part, *hid))
     part = lax.all_to_all(part.reshape(32, 128, 128), ("y", "c", "x"), 0, 0, tiled=True)
     tile = shape((16, 128, 128), BF)

time: 162 us -> 157 us (0.969)
  waiting for transfers between devices: 51.2 us -> 33.6 us
  starting transfers between devices: 54 us -> 66.4 us
  local copies, waits for them, and re-layouts: 15.6 us -> 18.3 us
  Pallas kernels: 17.3 us -> 15.2 us
    ppermute x34 -> x37, waiting for transfers between devices: 37.6 us -> 23.5 us  [fetch(): return lax.ppermute(value, axis, [((i + shift) % 4, i) for i in range(4)])]
    ppermute x34 -> x37, starting transfers between devices: 45 us -> 56.6 us  [fetch(): return lax.ppermute(value, axis, [((i + shift) % 4, i) for i in range(4)])]
    all_to_all x1, waiting for transfers between devices: 3.58 us -> 0.01 us  [body(): lax.all_to_all(features.reshape(96, 8, 256).transpose(1, 0, 2), feat, 0,...]
    unnamed x62 -> x78, local copies, waits for them, and re-layouts: 12.9 us -> 14.9 us
    pallas_call x3 -> x4, Pallas kernels: 3.28 us -> 2.02 us  [the longest x1 1.92 us: body(): call(project_kernel, (half, half), [VMEM] * 16 + [SMEM], [pltpu.VMEM((8,...]
  transfers between devices with their start and end apart: 37 -> 40, of which waited for: 14 -> 14; matrix products, arithmetic and copies ran while one was open for 2% -> 2% of each run, Pallas kernels for 4% -> 3%
where the time goes in v8:
time: 157 us; the launch traced here: 156 us
  starting transfers between devices  66.4 us (42%)
  waiting for transfers between devices  33.6 us (21%)
  blocking collectives  21.7 us (14%)
  local copies, waits for them, and re-layouts  18.3 us (12%)
  Pallas kernels  15.2 us (10%)
    ppermute x37, starting transfers between devices, fetch(): return lax.ppermute(value, axis, [((i + shift) % 4, i) for i in range(4)])  56.6 us
    ppermute x37, waiting for transfers between devices, fetch(): return lax.ppermute(value, axis, [((i + shift) % 4, i) for i in range(4)])  23.5 us
    all_to_all x1, blocking collectives, body(): lax.all_to_all(part.reshape(32, 128, 128), ('y', 'c', 'x'), 0, 0, tiled=T...  21.7 us
    unnamed x78, local copies, waits for them, and re-layouts  14.9 us
    all_to_all x1, waiting for transfers between devices, body(): done = lax.all_to_all(done, dom, 0, 0, tiled=True)  10.1 us
    pallas_call x1, Pallas kernels, body(): call(first_mix_kernel, (shape((256, 256), BF),) * 4 + (half, half, shape(...  5.68 us
    all_to_all x1, starting transfers between devices, body(): done = lax.all_to_all(done, dom, 0, 0, tiled=True)  4.98 us
    all_to_all x1, starting transfers between devices, body(): lax.all_to_all(features.reshape(96, 8, 256).transpose(1, 0, 2), feat, 0,...  4.69 us
  transfers between devices with their start and end apart: 40, of which 14 were waited for; matrix products, arithmetic and copies ran while one was open for 2% of the time, Pallas kernels for 3%

profile of v8, /device:TPU:0, one launch (start us, length us, event | category | flops | bytes accessed | tf_op | source)
XLA Modules:
  0.0 156.3 jit_solution(2424846897252485787)
XLA Ops:
  2.6 4.7 %all-to-all-start = ((bf16[8,96,256]{2,1,0:T(8,128)(2,1)}), bf16[8,96,256]{2,1,0:T(8,128)(2,1)S(1)}, u32[]{:S(2)}, u32[]{:S(2)}) async-start(bf16[8,96,256]{2,1,0:T(8,128)(2,1)} %bitcast.22), calls=%async_computation | async-start | bytes 786432 | tf_op jit(solution)/shard_map/all_to_all | solution.py:233
  8.1 4.0 %collective-permute-start.2 = (bf16[176,256]{1,0:T(8,128)(2,1)S(1)}, bf16[176,256]{1,0:T(8,128)(2,1)S(1)}, u32[]{:S(2)}, u32[]{:S(2)}) collective-permute-start(bf16[176,256]{1,0:T(8,128)(2,1)S(1)} %shard_map.94.refs_0_.refs_12_.refs_23_), channel_id=1, source_target_pairs={{2,0},{3,1},{0,2},{1,3},{6,4},{7,5},{4,6},{5,7},{10,8},{11,9},{8,1... | collective-permute-start | bytes 270344 | tf_op jit(solution)/shard_map/ppermute | solution.py:208
  13.1 2.2 %collective-permute-start = (bf16[176,256]{1,0:T(8,128)(2,1)S(1)}, bf16[176,256]{1,0:T(8,128)(2,1)S(1)}, u32[]{:S(2)}, u32[]{:S(2)}) collective-permute-start(bf16[176,256]{1,0:T(8,128)(2,1)S(1)} %shard_map.94.refs_0_.refs_12_.refs_23_), channel_id=1, source_target_pairs={{1,0},{2,1},{3,2},{0,3},{5,4},{6,5},{7,6},{4,7},{9,8},{10,9},{11,1... | collective-permute-start | bytes 270344 | tf_op jit(solution)/shard_map/ppermute | solution.py:208
  15.5 2.5 %collective-permute-done.1.refs_2_.refs_14_.refs_25_ = bf16[176,256]{1,0:T(8,128)(2,1)S(1)} collective-permute-done((bf16[176,256]{1,0:T(8,128)(2,1)S(1)}, bf16[176,256]{1,0:T(8,128)(2,1)S(1)}, u32[]{:S(2)}, u32[]{:S(2)}) %collective-permute-start.1) | collective-permute-done | bytes 90144 | tf_op jit(solution)/shard_map/ppermute | solution.py:208
  18.1 3.1 %collective-permute-start.4 = (bf16[4,96,256]{2,1,0:T(8,128)(2,1)S(1)}, bf16[4,96,256]{2,1,0:T(8,128)(2,1)S(1)}, u32[]{:S(2)}, u32[]{:S(2)}) collective-permute-start(bf16[4,96,256]{2,1,0:T(8,128)(2,1)S(1)} %get-tuple-element.48.refs_0_.refs_13_), channel_id=1, source_target_pairs={{1,0},{2,1},{3,2},{0,3},{5,4},{6,5},{7,6},{4,7},{9,8},{10,9},{11,1... | collective-permute-start | bytes 589832 | tf_op jit(solution)/shard_map/ppermute | solution.py:208
  21.2 2.8 %collective-permute-start.6 = (bf16[2,160,256]{2,1,0:T(8,128)(2,1)S(1)}, bf16[2,160,256]{2,1,0:T(8,128)(2,1)S(1)}, u32[]{:S(2)}, u32[]{:S(2)}) collective-permute-start(bf16[2,160,256]{2,1,0:T(8,128)(2,1)S(1)} %get-tuple-element.50.refs_8_), channel_id=1, source_target_pairs={{4,0},{8,4},{12,8},{0,12},{5,1},{9,5},{13,9},{1,13},{6,2},{10,6},{... | collective-permute-start | bytes 491528 | tf_op jit(solution)/shard_map/ppermute | solution.py:208
  24.7 2.1 %collective-permute-done.6.refs_10_ = bf16[2,160,256]{2,1,0:T(8,128)(2,1)S(1)} collective-permute-done((bf16[2,160,256]{2,1,0:T(8,128)(2,1)S(1)}, bf16[2,160,256]{2,1,0:T(8,128)(2,1)S(1)}, u32[]{:S(2)}, u32[]{:S(2)}) %collective-permute-start.6) | collective-permute-done | bytes 163872 | tf_op jit(solution)/shard_map/ppermute | solution.py:208
  26.8 3.7 %collective-permute-start.12 = (bf16[2,160,256]{2,1,0:T(8,128)(2,1)S(1)}, bf16[2,160,256]{2,1,0:T(8,128)(2,1)S(1)}, u32[]{:S(2)}, u32[]{:S(2)}) collective-permute-start(bf16[2,160,256]{2,1,0:T(8,128)(2,1)S(1)} %get-tuple-element.51.refs_9_), channel_id=1, source_target_pairs={{4,0},{8,4},{12,8},{0,12},{5,1},{9,5},{13,9},{1,13},{6,2},{10,6},{... | collective-permute-start | bytes 491528 | tf_op jit(solution)/shard_map/ppermute | solution.py:208
  32.3 2.0 %collective-permute-start.15 = (bf16[2,160,256]{2,1,0:T(8,128)(2,1)S(1)}, bf16[2,160,256]{2,1,0:T(8,128)(2,1)S(1)}, u32[]{:S(2)}, u32[]{:S(2)}) collective-permute-start(bf16[2,160,256]{2,1,0:T(8,128)(2,1)S(1)} %collective-permute-done.7.refs_13_), channel_id=1, source_target_pairs={{12,0},{0,4},{4,8},{8,12},{13,1},{1,5},{5,9},{9,13},{14,2},{2,6},{... | collective-permute-start | bytes 491528 | tf_op jit(solution)/shard_map/ppermute | solution.py:208
  35.0 3.0 %collective-permute-start.10 = (bf16[4,96,256]{2,1,0:T(8,128)(2,1)S(1)}, bf16[4,96,256]{2,1,0:T(8,128)(2,1)S(1)}, u32[]{:S(2)}, u32[]{:S(2)}) collective-permute-start(bf16[4,96,256]{2,1,0:T(8,128)(2,1)S(1)} %collective-permute-done.4.refs_2_.refs_15_), channel_id=1, source_target_pairs={{1,0},{2,1},{3,2},{0,3},{5,4},{6,5},{7,6},{4,7},{9,8},{10,9},{11,1... | collective-permute-start | bytes 589832 | tf_op jit(solution)/shard_map/ppermute | solution.py:208
  38.8 3.2 %collective-permute-start.8 = (bf16[4,96,256]{2,1,0:T(8,128)(2,1)S(1)}, bf16[4,96,256]{2,1,0:T(8,128)(2,1)S(1)}, u32[]{:S(2)}, u32[]{:S(2)}) collective-permute-start(bf16[4,96,256]{2,1,0:T(8,128)(2,1)S(1)} %get-tuple-element.49.refs_1_.refs_14_), channel_id=1, source_target_pairs={{1,0},{2,1},{3,2},{0,3},{5,4},{6,5},{7,6},{4,7},{9,8},{10,9},{11,1... | collective-permute-start | bytes 589832 | tf_op jit(solution)/shard_map/ppermute | solution.py:208
  42.7 2.9 %collective-permute-start.18 = (bf16[2,96,256]{2,1,0:T(8,128)(2,1)S(1)}, bf16[2,96,256]{2,1,0:T(8,128)(2,1)S(1)}, u32[]{:S(2)}, u32[]{:S(2)}) collective-permute-start(bf16[2,96,256]{2,1,0:T(8,128)(2,1)S(1)} %pad_maximum_fusion.refs_8_), channel_id=1, source_target_pairs={{64,0},{96,32},{0,64},{32,96},{65,1},{97,33},{1,65},{33,97},{66,2}... | collective-permute-start | bytes 294920 | tf_op jit(solution)/shard_map/ppermute | solution.py:208
  46.2 2.7 %collective-permute-start.16 = (bf16[2,96,256]{2,1,0:T(8,128)(2,1)S(1)}, bf16[2,96,256]{2,1,0:T(8,128)(2,1)S(1)}, u32[]{:S(2)}, u32[]{:S(2)}) collective-permute-start(bf16[2,96,256]{2,1,0:T(8,128)(2,1)S(1)} %pad_maximum_fusion.refs_8_), channel_id=1, source_target_pairs={{32,0},{64,32},{96,64},{0,96},{33,1},{65,33},{97,65},{1,97},{34,2}... | collective-permute-start | bytes 294920 | tf_op jit(solution)/shard_map/ppermute | solution.py:208
  49.0 2.5 %collective-permute-done.17.refs_10_ = bf16[2,96,256]{2,1,0:T(8,128)(2,1)S(1)} collective-permute-done((bf16[2,96,256]{2,1,0:T(8,128)(2,1)S(1)}, bf16[2,96,256]{2,1,0:T(8,128)(2,1)S(1)}, u32[]{:S(2)}, u32[]{:S(2)}) %collective-permute-start.17) | collective-permute-done | bytes 98336 | tf_op jit(solution)/shard_map/ppermute | solution.py:208
  51.5 1.9 %shard_map.97 = (bf16[2,256,256]{2,1,0:T(8,128)(2,1)S(1)}, bf16[2,256,256]{2,1,0:T(8,128)(2,1)}) custom-call(bf16[4,96,256]{2,1,0:T(8,128)(2,1)S(1)} %get-tuple-element.48.refs_0_.refs_13_, bf16[4,96,256]{2,1,0:T(8,128)(2,1)S(1)} %get-tuple-element.49.refs_1_.refs_14_, bf16[4,96,256]{2,1,0:T(8,128)(2,1)S(1)} %collective-permute-done.4.refs_2_.refs_15_, ...), custom_call_target="tpu_custom_call" | custom-call | flops 400000000 | bytes 3000000 | tf_op jit(solution)/shard_map/pallas_call | solution.py:259
  53.5 3.2 %collective-permute-start.25 = (bf16[256,768]{1,0:T(8,128)(2,1)S(1)}, bf16[256,768]{1,0:T(8,128)(2,1)S(1)}, u32[]{:S(2)}, u32[]{:S(2)}) collective-permute-start(bf16[256,768]{1,0:T(8,128)(2,1)S(1)} %shard_map.96.refs_16_.refs_8_), channel_id=1, source_target_pairs={{1,0},{2,1},{3,2},{0,3},{5,4},{6,5},{7,6},{4,7},{9,8},{10,9},{11,1... | collective-permute-start | bytes 1179656 | tf_op jit(solution)/shard_map/ppermute | solution.py:208
  56.7 1.3 collective-permute-start.19
  58.8 7.3 %collective-permute-done.19.refs_2_ = bf16[2,256,256]{2,1,0:T(8,128)(2,1)} collective-permute-done((bf16[2,256,256]{2,1,0:T(8,128)(2,1)S(1)}, bf16[2,256,256]{2,1,0:T(8,128)(2,1)}, u32[]{:S(2)}, u32[]{:S(2)}) %collective-permute-start.19) | collective-permute-done | bytes 262176 | tf_op jit(solution)/shard_map/ppermute | solution.py:208
  66.1 2.5 %collective-permute-start.20 = (bf16[2,256,256]{2,1,0:T(8,128)(2,1)}, bf16[2,256,256]{2,1,0:T(8,128)(2,1)}, u32[]{:S(2)}, u32[]{:S(2)}) collective-permute-start(bf16[2,256,256]{2,1,0:T(8,128)(2,1)} %get-tuple-element.64.refs_1_), channel_id=1, source_target_pairs={{4,0},{8,4},{12,8},{0,12},{5,1},{9,5},{13,9},{1,13},{6,2},{10,6},{... | collective-permute-start | bytes 786440 | tf_op jit(solution)/shard_map/ppermute | solution.py:208
  68.5 2.0 %collective-permute-start.24 = (bf16[2,256,256]{2,1,0:T(8,128)(2,1)}, bf16[2,256,256]{2,1,0:T(8,128)(2,1)}, u32[]{:S(2)}, u32[]{:S(2)}) collective-permute-start(bf16[2,256,256]{2,1,0:T(8,128)(2,1)} %collective-permute-done.22.refs_5_), channel_id=1, source_target_pairs={{12,0},{0,4},{4,8},{8,12},{13,1},{1,5},{5,9},{9,13},{14,2},{2,6},{... | collective-permute-start | bytes 786440 | tf_op jit(solution)/shard_map/ppermute | solution.py:208
  72.6 3.2 %collective-permute-start.27 = (bf16[128,768]{1,0:T(8,128)(2,1)}, bf16[128,768]{1,0:T(8,128)(2,1)S(1)}, u32[]{:S(2)}, u32[]{:S(2)}) collective-permute-start(bf16[128,768]{1,0:T(8,128)(2,1)} %slice.18), channel_id=1, source_target_pairs={{1,0},{2,1},{3,2},{0,3},{5,4},{6,5},{7,6},{4,7},{9,8},{10,9},{11,1... | collective-permute-start | bytes 589832 | tf_op jit(solution)/shard_map/ppermute | solution.py:208
  87.7 5.7 %shard_map.98 = (bf16[256,256]{1,0:T(8,128)(2,1)S(1)}, bf16[256,256]{1,0:T(8,128)(2,1)S(1)}, bf16[256,256]{1,0:T(8,128)(2,1)S(1)}, bf16[256,256]{1,0:T(8,128)(2,...) custom-call(bf16[2,256,256]{2,1,0:T(8,128)(2,1)S(1)} %copy-done.7, ...), custom_call_target="tpu_custom_call" | custom-call | flops 700000000 | bytes 8000000 | tf_op jit(solution)/shard_map/pallas_call | solution.py:277
  96.1 3.2 %collective-permute-start.31 = (bf16[2,256,256]{2,1,0:T(8,128)(2,1)S(1)}, bf16[2,256,256]{2,1,0:T(8,128)(2,1)S(1)}, u32[]{:S(2)}, u32[]{:S(2)}) collective-permute-start(bf16[2,256,256]{2,1,0:T(8,128)(2,1)S(1)} %get-tuple-element.71.refs_1_), channel_id=1, source_target_pairs={{4,0},{8,4},{12,8},{0,12},{5,1},{9,5},{13,9},{1,13},{6,2},{10,6},{... | collective-permute-start | bytes 786440 | tf_op jit(solution)/shard_map/ppermute | solution.py:208
  100.4 2.5 %collective-permute-done.30.refs_5_ = bf16[2,256,256]{2,1,0:T(8,128)(2,1)S(1)} collective-permute-done((bf16[2,256,256]{2,1,0:T(8,128)(2,1)S(1)}, bf16[2,256,256]{2,1,0:T(8,128)(2,1)S(1)}, u32[]{:S(2)}, u32[]{:S(2)}) %collective-permute-start.30) | collective-permute-done | bytes 262176 | tf_op jit(solution)/shard_map/ppermute | solution.py:208
  102.9 2.0 %collective-permute-start.34 = (bf16[2,256,256]{2,1,0:T(8,128)(2,1)S(1)}, bf16[2,256,256]{2,1,0:T(8,128)(2,1)S(1)}, u32[]{:S(2)}, u32[]{:S(2)}) collective-permute-start(bf16[2,256,256]{2,1,0:T(8,128)(2,1)S(1)} %collective-permute-done.30.refs_5_), channel_id=1, source_target_pairs={{12,0},{0,4},{4,8},{8,12},{13,1},{1,5},{5,9},{9,13},{14,2},{2,6},{... | collective-permute-start | bytes 786440 | tf_op jit(solution)/shard_map/ppermute | solution.py:208
  105.7 3.6 %collective-permute-start.36 = (bf16[256,256]{1,0:T(8,128)(2,1)S(1)}, bf16[256,256]{1,0:T(8,128)(2,1)S(1)}, u32[]{:S(2)}, u32[]{:S(2)}) collective-permute-start(bf16[256,256]{1,0:T(8,128)(2,1)S(1)} %get-tuple-element.80), channel_id=1, source_target_pairs={{1,0},{2,1},{3,2},{0,3},{5,4},{6,5},{7,6},{4,7},{9,8},{10,9},{11,1... | collective-permute-start | bytes 393224 | tf_op jit(solution)/shard_map/ppermute | solution.py:208
  110.5 3.8 %shard_map.99 = bf16[8,4,128,128]{3,2,1,0:T(8,128)(2,1)S(1)} custom-call(bf16[2,256,256]{2,1,0:T(8,128)(2,1)S(1)} %get-tuple-element.70.refs_0_, bf16[2,256,256]{2,1,0:T(8,128)(2,1)S(1)} %get-tuple-element.71.refs_1_, bf16[2,256,256]{2,1,0:T(8,128)(2,1)S(1)} %collective-permute-done.29.refs_2_, bf16[2,256,256]{2,1,0:T(8,128)(2,1)S(1)} %collective-permute-done.31.refs_3_, ...), custom_call_target="tpu_custom_call" | custom-call | flops 900000000 | bytes 8000000 | tf_op jit(solution)/shard_map/pallas_call | solution.py:289
  114.3 1.4 collective-permute-done.37.h3_ref
  115.8 21.7 %all_to_all.15.part_ref = bf16[32,128,128]{2,1,0:T(8,128)(2,1)S(1)} all-to-all(bf16[32,128,128]{2,1,0:T(8,128)(2,1)S(1)} %bitcast.23), channel_id=1, replica_groups=mesh['y'=4,'c'=2,'x'=4,'z'=4] {'y','c','x'}, dimensions={0} | all-to-all | bytes 2097152 | tf_op jit(solution)/shard_map/all_to_all | solution.py:298
  138.4 5.0 %all-to-all-start.2 = ((bf16[16,128,128]{2,1,0:T(8,128)(2,1)}), bf16[16,128,128]{2,1,0:T(8,128)(2,1)S(1)}, u32[]{:S(2)}, u32[]{:S(2)}) async-start(bf16[16,128,128]{2,1,0:T(8,128)(2,1)} %shard_map.101), calls=%async_computation.2 | async-start | bytes 1048576 | tf_op jit(solution)/shard_map/all_to_all | solution.py:301
  143.4 1.5 shard_map.100
  145.0 10.1 %all-to-all-done.2.in_ref = bf16[16,128,128]{2,1,0:T(8,128)(2,1)S(1)} async-done(((bf16[16,128,128]{2,1,0:T(8,128)(2,1)}), bf16[16,128,128]{2,1,0:T(8,128)(2,1)S(1)}, u32[]{:S(2)}, u32[]{:S(2)}) %all-to-all-start.2) | async-done | bytes 524320 | tf_op jit(solution)/shard_map/all_to_all | solution.py:301
  (149 shorter events, 32.1 us)
Async XLA Ops:
  2.6 15.5 %all-to-all-start = ((bf16[8,96,256]{2,1,0:T(8,128)(2,1)}), bf16[8,96,256]{2,1,0:T(8,128)(2,1)S(1)}, u32[]{:S(2)}, u32[]{:S(2)}) async-start(bf16[8,96,256]{2,1,0:T(8,128)(2,1)} %bitcast.22), calls=%async_computation | async-start | bytes 786432 | tf_op jit(solution)/shard_map/all_to_all | solution.py:233
  8.1 7.4 %collective-permute-start.2 = (bf16[176,256]{1,0:T(8,128)(2,1)S(1)}, bf16[176,256]{1,0:T(8,128)(2,1)S(1)}, u32[]{:S(2)}, u32[]{:S(2)}) collective-permute-start(bf16[176,256]{1,0:T(8,128)(2,1)S(1)} %shard_map.94.refs_0_.refs_12_.refs_23_), channel_id=1, source_target_pairs={{2,0},{3,1},{0,2},{1,3},{6,4},{7,5},{4,6},{5,7},{10,8},{11,9},{8,1... | collective-permute-start | bytes 270344 | tf_op jit(solution)/shard_map/ppermute | solution.py:208
  18.1 13.5 %collective-permute-start.4 = (bf16[4,96,256]{2,1,0:T(8,128)(2,1)S(1)}, bf16[4,96,256]{2,1,0:T(8,128)(2,1)S(1)}, u32[]{:S(2)}, u32[]{:S(2)}) collective-permute-start(bf16[4,96,256]{2,1,0:T(8,128)(2,1)S(1)} %get-tuple-element.48.refs_0_.refs_13_), channel_id=1, source_target_pairs={{1,0},{2,1},{3,2},{0,3},{5,4},{6,5},{7,6},{4,7},{9,8},{10,9},{11,1... | collective-permute-start | bytes 589832 | tf_op jit(solution)/shard_map/ppermute | solution.py:208
  21.2 10.4 %collective-permute-start.5 = (bf16[4,96,256]{2,1,0:T(8,128)(2,1)S(1)}, bf16[4,96,256]{2,1,0:T(8,128)(2,1)S(1)}, u32[]{:S(2)}, u32[]{:S(2)}) collective-permute-start(bf16[4,96,256]{2,1,0:T(8,128)(2,1)S(1)} %get-tuple-element.49.refs_1_.refs_14_), channel_id=1, source_target_pairs={{3,0},{0,1},{1,2},{2,3},{7,4},{4,5},{5,6},{6,7},{11,8},{8,9},{9,10... | collective-permute-start | bytes 589832 | tf_op jit(solution)/shard_map/ppermute | solution.py:208
  24.0 7.6 %collective-permute-start.7 = (bf16[2,160,256]{2,1,0:T(8,128)(2,1)S(1)}, bf16[2,160,256]{2,1,0:T(8,128)(2,1)S(1)}, u32[]{:S(2)}, u32[]{:S(2)}) collective-permute-start(bf16[2,160,256]{2,1,0:T(8,128)(2,1)S(1)} %get-tuple-element.51.refs_9_), channel_id=1, source_target_pairs={{12,0},{0,4},{4,8},{8,12},{13,1},{1,5},{5,9},{9,13},{14,2},{2,6},{... | collective-permute-start | bytes 491528 | tf_op jit(solution)/shard_map/ppermute | solution.py:208
  24.0 14.0 %collective-permute-start.13 = (bf16[2,160,256]{2,1,0:T(8,128)(2,1)S(1)}, bf16[2,160,256]{2,1,0:T(8,128)(2,1)S(1)}, u32[]{:S(2)}, u32[]{:S(2)}) collective-permute-start(bf16[2,160,256]{2,1,0:T(8,128)(2,1)S(1)} %get-tuple-element.50.refs_8_), channel_id=1, source_target_pairs={{12,0},{0,4},{4,8},{8,12},{13,1},{1,5},{5,9},{9,13},{14,2},{2,6},{... | collective-permute-start | bytes 491528 | tf_op jit(solution)/shard_map/ppermute | solution.py:208
  26.8 11.2 %collective-permute-start.12 = (bf16[2,160,256]{2,1,0:T(8,128)(2,1)S(1)}, bf16[2,160,256]{2,1,0:T(8,128)(2,1)S(1)}, u32[]{:S(2)}, u32[]{:S(2)}) collective-permute-start(bf16[2,160,256]{2,1,0:T(8,128)(2,1)S(1)} %get-tuple-element.51.refs_9_), channel_id=1, source_target_pairs={{4,0},{8,4},{12,8},{0,12},{5,1},{9,5},{13,9},{1,13},{6,2},{10,6},{... | collective-permute-start | bytes 491528 | tf_op jit(solution)/shard_map/ppermute | solution.py:208
  31.6 6.5 %collective-permute-start.14 = (bf16[2,160,256]{2,1,0:T(8,128)(2,1)S(1)}, bf16[2,160,256]{2,1,0:T(8,128)(2,1)S(1)}, u32[]{:S(2)}, u32[]{:S(2)}) collective-permute-start(bf16[2,160,256]{2,1,0:T(8,128)(2,1)S(1)} %collective-permute-done.6.refs_10_), channel_id=1, source_target_pairs={{4,0},{8,4},{12,8},{0,12},{5,1},{9,5},{13,9},{1,13},{6,2},{10,6},{... | collective-permute-start | bytes 491528 | tf_op jit(solution)/shard_map/ppermute | solution.py:208
  32.3 9.7 %collective-permute-start.15 = (bf16[2,160,256]{2,1,0:T(8,128)(2,1)S(1)}, bf16[2,160,256]{2,1,0:T(8,128)(2,1)S(1)}, u32[]{:S(2)}, u32[]{:S(2)}) collective-permute-start(bf16[2,160,256]{2,1,0:T(8,128)(2,1)S(1)} %collective-permute-done.7.refs_13_), channel_id=1, source_target_pairs={{12,0},{0,4},{4,8},{8,12},{13,1},{1,5},{5,9},{9,13},{14,2},{2,6},{... | collective-permute-start | bytes 491528 | tf_op jit(solution)/shard_map/ppermute | solution.py:208
  35.0 10.6 %collective-permute-start.10 = (bf16[4,96,256]{2,1,0:T(8,128)(2,1)S(1)}, bf16[4,96,256]{2,1,0:T(8,128)(2,1)S(1)}, u32[]{:S(2)}, u32[]{:S(2)}) collective-permute-start(bf16[4,96,256]{2,1,0:T(8,128)(2,1)S(1)} %collective-permute-done.4.refs_2_.refs_15_), channel_id=1, source_target_pairs={{1,0},{2,1},{3,2},{0,3},{5,4},{6,5},{7,6},{4,7},{9,8},{10,9},{11,1... | collective-permute-start | bytes 589832 | tf_op jit(solution)/shard_map/ppermute | solution.py:208
  37.9 8.2 %collective-permute-start.11 = (bf16[4,96,256]{2,1,0:T(8,128)(2,1)S(1)}, bf16[4,96,256]{2,1,0:T(8,128)(2,1)S(1)}, u32[]{:S(2)}, u32[]{:S(2)}) collective-permute-start(bf16[4,96,256]{2,1,0:T(8,128)(2,1)S(1)} %collective-permute-done.5.refs_5_.refs_18_), channel_id=1, source_target_pairs={{3,0},{0,1},{1,2},{2,3},{7,4},{4,5},{5,6},{6,7},{11,8},{8,9},{9,10... | collective-permute-start | bytes 589832 | tf_op jit(solution)/shard_map/ppermute | solution.py:208
  38.0 11.0 %collective-permute-start.9 = (bf16[4,96,256]{2,1,0:T(8,128)(2,1)S(1)}, bf16[4,96,256]{2,1,0:T(8,128)(2,1)S(1)}, u32[]{:S(2)}, u32[]{:S(2)}) collective-permute-start(bf16[4,96,256]{2,1,0:T(8,128)(2,1)S(1)} %get-tuple-element.48.refs_0_.refs_13_), channel_id=1, source_target_pairs={{3,0},{0,1},{1,2},{2,3},{7,4},{4,5},{5,6},{6,7},{11,8},{8,9},{9,10... | collective-permute-start | bytes 589832 | tf_op jit(solution)/shard_map/ppermute | solution.py:208
  38.8 10.2 %collective-permute-start.8 = (bf16[4,96,256]{2,1,0:T(8,128)(2,1)S(1)}, bf16[4,96,256]{2,1,0:T(8,128)(2,1)S(1)}, u32[]{:S(2)}, u32[]{:S(2)}) collective-permute-start(bf16[4,96,256]{2,1,0:T(8,128)(2,1)S(1)} %get-tuple-element.49.refs_1_.refs_14_), channel_id=1, source_target_pairs={{1,0},{2,1},{3,2},{0,3},{5,4},{6,5},{7,6},{4,7},{9,8},{10,9},{11,1... | collective-permute-start | bytes 589832 | tf_op jit(solution)/shard_map/ppermute | solution.py:208
  53.4 15.1 %collective-permute-start.26 = (bf16[256,768]{1,0:T(8,128)(2,1)S(1)}, bf16[256,768]{1,0:T(8,128)(2,1)S(1)}, u32[]{:S(2)}, u32[]{:S(2)}) collective-permute-start(bf16[256,768]{1,0:T(8,128)(2,1)S(1)} %shard_map.96.refs_16_.refs_8_), channel_id=1, source_target_pairs={{3,0},{0,1},{1,2},{2,3},{7,4},{4,5},{5,6},{6,7},{11,8},{8,9},{9,10... | collective-permute-start | bytes 1179656 | tf_op jit(solution)/shard_map/ppermute | solution.py:208
  53.5 17.8 %collective-permute-start.25 = (bf16[256,768]{1,0:T(8,128)(2,1)S(1)}, bf16[256,768]{1,0:T(8,128)(2,1)S(1)}, u32[]{:S(2)}, u32[]{:S(2)}) collective-permute-start(bf16[256,768]{1,0:T(8,128)(2,1)S(1)} %shard_map.96.refs_16_.refs_8_), channel_id=1, source_target_pairs={{1,0},{2,1},{3,2},{0,3},{5,4},{6,5},{7,6},{4,7},{9,8},{10,9},{11,1... | collective-permute-start | bytes 1179656 | tf_op jit(solution)/shard_map/ppermute | solution.py:208
  56.7 9.4 %collective-permute-start.19 = (bf16[2,256,256]{2,1,0:T(8,128)(2,1)S(1)}, bf16[2,256,256]{2,1,0:T(8,128)(2,1)}, u32[]{:S(2)}, u32[]{:S(2)}) collective-permute-start(bf16[2,256,256]{2,1,0:T(8,128)(2,1)S(1)} %get-tuple-element.63.refs_0_), channel_id=1, source_target_pairs={{4,0},{8,4},{12,8},{0,12},{5,1},{9,5},{13,9},{1,13},{6,2},{10,6},{... | collective-permute-start | bytes 786440 | tf_op jit(solution)/shard_map/ppermute | solution.py:208
  58.0 10.5 %collective-permute-start.22 = (bf16[2,256,256]{2,1,0:T(8,128)(2,1)}, bf16[2,256,256]{2,1,0:T(8,128)(2,1)}, u32[]{:S(2)}, u32[]{:S(2)}) collective-permute-start(bf16[2,256,256]{2,1,0:T(8,128)(2,1)} %get-tuple-element.64.refs_1_), channel_id=1, source_target_pairs={{12,0},{0,4},{4,8},{8,12},{13,1},{1,5},{5,9},{9,13},{14,2},{2,6},{... | collective-permute-start | bytes 786440 | tf_op jit(solution)/shard_map/ppermute | solution.py:208
  58.7 13.2 %collective-permute-start.21 = (bf16[2,256,256]{2,1,0:T(8,128)(2,1)S(1)}, bf16[2,256,256]{2,1,0:T(8,128)(2,1)S(1)}, u32[]{:S(2)}, u32[]{:S(2)}) collective-permute-start(bf16[2,256,256]{2,1,0:T(8,128)(2,1)S(1)} %get-tuple-element.63.refs_0_), channel_id=1, source_target_pairs={{12,0},{0,4},{4,8},{8,12},{13,1},{1,5},{5,9},{9,13},{14,2},{2,6},{... | collective-permute-start | bytes 786440 | tf_op jit(solution)/shard_map/ppermute | solution.py:208
  66.1 11.6 %collective-permute-start.20 = (bf16[2,256,256]{2,1,0:T(8,128)(2,1)}, bf16[2,256,256]{2,1,0:T(8,128)(2,1)}, u32[]{:S(2)}, u32[]{:S(2)}) collective-permute-start(bf16[2,256,256]{2,1,0:T(8,128)(2,1)} %get-tuple-element.64.refs_1_), channel_id=1, source_target_pairs={{4,0},{8,4},{12,8},{0,12},{5,1},{9,5},{13,9},{1,13},{6,2},{10,6},{... | collective-permute-start | bytes 786440 | tf_op jit(solution)/shard_map/ppermute | solution.py:208
  68.5 9.1 %collective-permute-start.23 = (bf16[2,256,256]{2,1,0:T(8,128)(2,1)}, bf16[2,256,256]{2,1,0:T(8,128)(2,1)}, u32[]{:S(2)}, u32[]{:S(2)}) collective-permute-start(bf16[2,256,256]{2,1,0:T(8,128)(2,1)} %collective-permute-done.19.refs_2_), channel_id=1, source_target_pairs={{4,0},{8,4},{12,8},{0,12},{5,1},{9,5},{13,9},{1,13},{6,2},{10,6},{... | collective-permute-start | bytes 786440 | tf_op jit(solution)/shard_map/ppermute | solution.py:208
  68.5 9.1 %collective-permute-start.24 = (bf16[2,256,256]{2,1,0:T(8,128)(2,1)}, bf16[2,256,256]{2,1,0:T(8,128)(2,1)}, u32[]{:S(2)}, u32[]{:S(2)}) collective-permute-start(bf16[2,256,256]{2,1,0:T(8,128)(2,1)} %collective-permute-done.22.refs_5_), channel_id=1, source_target_pairs={{12,0},{0,4},{4,8},{8,12},{13,1},{1,5},{5,9},{9,13},{14,2},{2,6},{... | collective-permute-start | bytes 786440 | tf_op jit(solution)/shard_map/ppermute | solution.py:208
  71.2 7.1 %collective-permute-start.28 = (bf16[128,768]{1,0:T(8,128)(2,1)}, bf16[128,768]{1,0:T(8,128)(2,1)S(1)}, u32[]{:S(2)}, u32[]{:S(2)}) collective-permute-start(bf16[128,768]{1,0:T(8,128)(2,1)} %slice.19), channel_id=1, source_target_pairs={{3,0},{0,1},{1,2},{2,3},{7,4},{4,5},{5,6},{6,7},{11,8},{8,9},{9,10... | collective-permute-start | bytes 589832 | tf_op jit(solution)/shard_map/ppermute | solution.py:208
  72.6 6.7 %collective-permute-start.27 = (bf16[128,768]{1,0:T(8,128)(2,1)}, bf16[128,768]{1,0:T(8,128)(2,1)S(1)}, u32[]{:S(2)}, u32[]{:S(2)}) collective-permute-start(bf16[128,768]{1,0:T(8,128)(2,1)} %slice.18), channel_id=1, source_target_pairs={{1,0},{2,1},{3,2},{0,3},{5,4},{6,5},{7,6},{4,7},{9,8},{10,9},{11,1... | collective-permute-start | bytes 589832 | tf_op jit(solution)/shard_map/ppermute | solution.py:208
  95.3 7.6 %collective-permute-start.30 = (bf16[2,256,256]{2,1,0:T(8,128)(2,1)S(1)}, bf16[2,256,256]{2,1,0:T(8,128)(2,1)S(1)}, u32[]{:S(2)}, u32[]{:S(2)}) collective-permute-start(bf16[2,256,256]{2,1,0:T(8,128)(2,1)S(1)} %get-tuple-element.71.refs_1_), channel_id=1, source_target_pairs={{12,0},{0,4},{4,8},{8,12},{13,1},{1,5},{5,9},{9,13},{14,2},{2,6},{... | collective-permute-start | bytes 786440 | tf_op jit(solution)/shard_map/ppermute | solution.py:208
  96.0 9.6 %collective-permute-start.32 = (bf16[2,256,256]{2,1,0:T(8,128)(2,1)S(1)}, bf16[2,256,256]{2,1,0:T(8,128)(2,1)S(1)}, u32[]{:S(2)}, u32[]{:S(2)}) collective-permute-start(bf16[2,256,256]{2,1,0:T(8,128)(2,1)S(1)} %get-tuple-element.70.refs_0_), channel_id=1, source_target_pairs={{12,0},{0,4},{4,8},{8,12},{13,1},{1,5},{5,9},{9,13},{14,2},{2,6},{... | collective-permute-start | bytes 786440 | tf_op jit(solution)/shard_map/ppermute | solution.py:208
  96.1 13.2 %collective-permute-start.31 = (bf16[2,256,256]{2,1,0:T(8,128)(2,1)S(1)}, bf16[2,256,256]{2,1,0:T(8,128)(2,1)S(1)}, u32[]{:S(2)}, u32[]{:S(2)}) collective-permute-start(bf16[2,256,256]{2,1,0:T(8,128)(2,1)S(1)} %get-tuple-element.71.refs_1_), channel_id=1, source_target_pairs={{4,0},{8,4},{12,8},{0,12},{5,1},{9,5},{13,9},{1,13},{6,2},{10,6},{... | collective-permute-start | bytes 786440 | tf_op jit(solution)/shard_map/ppermute | solution.py:208
  102.9 7.2 %collective-permute-start.33 = (bf16[2,256,256]{2,1,0:T(8,128)(2,1)S(1)}, bf16[2,256,256]{2,1,0:T(8,128)(2,1)S(1)}, u32[]{:S(2)}, u32[]{:S(2)}) collective-permute-start(bf16[2,256,256]{2,1,0:T(8,128)(2,1)S(1)} %collective-permute-done.29.refs_2_), channel_id=1, source_target_pairs={{4,0},{8,4},{12,8},{0,12},{5,1},{9,5},{13,9},{1,13},{6,2},{10,6},{... | collective-permute-start | bytes 786440 | tf_op jit(solution)/shard_map/ppermute | solution.py:208
  102.9 7.6 %collective-permute-start.34 = (bf16[2,256,256]{2,1,0:T(8,128)(2,1)S(1)}, bf16[2,256,256]{2,1,0:T(8,128)(2,1)S(1)}, u32[]{:S(2)}, u32[]{:S(2)}) collective-permute-start(bf16[2,256,256]{2,1,0:T(8,128)(2,1)S(1)} %collective-permute-done.30.refs_5_), channel_id=1, source_target_pairs={{12,0},{0,4},{4,8},{8,12},{13,1},{1,5},{5,9},{9,13},{14,2},{2,6},{... | collective-permute-start | bytes 786440 | tf_op jit(solution)/shard_map/ppermute | solution.py:208
  104.9 9.4 %collective-permute-start.35 = (bf16[256,256]{1,0:T(8,128)(2,1)S(1)}, bf16[256,256]{1,0:T(8,128)(2,1)S(1)}, u32[]{:S(2)}, u32[]{:S(2)}) collective-permute-start(bf16[256,256]{1,0:T(8,128)(2,1)S(1)} %get-tuple-element.79), channel_id=1, source_target_pairs={{3,0},{0,1},{1,2},{2,3},{7,4},{4,5},{5,6},{6,7},{11,8},{8,9},{9,10... | collective-permute-start | bytes 393224 | tf_op jit(solution)/shard_map/ppermute | solution.py:208
  105.7 8.6 %collective-permute-start.36 = (bf16[256,256]{1,0:T(8,128)(2,1)S(1)}, bf16[256,256]{1,0:T(8,128)(2,1)S(1)}, u32[]{:S(2)}, u32[]{:S(2)}) collective-permute-start(bf16[256,256]{1,0:T(8,128)(2,1)S(1)} %get-tuple-element.80), channel_id=1, source_target_pairs={{1,0},{2,1},{3,2},{0,3},{5,4},{6,5},{7,6},{4,7},{9,8},{10,9},{11,1... | collective-permute-start | bytes 393224 | tf_op jit(solution)/shard_map/ppermute | solution.py:208
  109.3 6.5 %collective-permute-start.37 = (bf16[256,256]{1,0:T(8,128)(2,1)S(1)}, bf16[256,256]{1,0:T(8,128)(2,1)S(1)}, u32[]{:S(2)}, u32[]{:S(2)}) collective-permute-start(bf16[256,256]{1,0:T(8,128)(2,1)S(1)} %get-tuple-element.81), channel_id=1, source_target_pairs={{2,0},{3,1},{0,2},{1,3},{6,4},{7,5},{4,6},{5,7},{10,8},{11,9},{8,1... | collective-permute-start | bytes 393224 | tf_op jit(solution)/shard_map/ppermute | solution.py:208
  138.4 16.7 %all-to-all-start.2 = ((bf16[16,128,128]{2,1,0:T(8,128)(2,1)}), bf16[16,128,128]{2,1,0:T(8,128)(2,1)S(1)}, u32[]{:S(2)}, u32[]{:S(2)}) async-start(bf16[16,128,128]{2,1,0:T(8,128)(2,1)} %shard_map.101), calls=%async_computation.2 | async-start | bytes 1048576 | tf_op jit(solution)/shard_map/all_to_all | solution.py:301
  (46 other events, 392.0 us)

commit v9 on v8

--- a/solution.py
+++ b/solution.py
@@ -96,6 +96,10 @@
                 src_ref[2 * d + h, base : base + rows] = ref[j, :, h * 128 : h * 128 + 128]
 
 
+def collect_kernel(*refs):
+    collect(refs[:8], 0, refs[9], refs[8])
+
+
 def scalars(i_refs, stage_ref, links_ref, sem):
     rows = [info_of(i_refs, k)[4:5] for k in range(4)]
     stage_ref[...] = jnp.concatenate(rows + [jnp.zeros((4, 128), F32)], axis=0).astype(I32)
@@ -104,19 +108,22 @@
     copy.wait()
 
 
-def spread(src_ref, links_ref, m_refs, k, b, t):
-    named = [src_ref[links_ref[k, b * 6 + s]] for s in range(6)]
+def spread(sources, links_ref, m_refs, k, b, t):
+    def field(c):
+        parts = [source[c] for source in sources]
+        return parts[0] if len(parts) == 1 else jnp.concatenate(parts, axis=0)
+
+    named = [field(links_ref[k, b * 6 + s]) for s in range(6)]
     total = dot(jnp.concatenate(named, axis=1), block_of(m_refs, k, b), NT)
-    return src_ref[t].astype(F32) + total
+    return field(t).astype(F32) + total
 
 
 def first_mix_kernel(*refs):
-    s_refs, u_refs, m_refs, sw_ref, at_ref = refs[:8], refs[8:16], refs[16:21], refs[21], refs[22]
-    i_refs, hid_refs, back_refs, second_ref = refs[23:27], refs[27:31], refs[31:33], refs[33]
-    src_ref, stage_ref, links_ref, sem = refs[34:]
+    s_refs, u_ref, m_refs, sw_ref, at_ref = refs[:8], refs[8], refs[9:14], refs[14], refs[15]
+    i_refs, hid_refs, back_refs, second_ref = refs[16:20], refs[20:24], refs[24:26], refs[26]
+    src_ref, stage_ref, links_ref, sem = refs[27:]
     scalars(i_refs, stage_ref, links_ref, sem)
     collect(s_refs, 0, src_ref, at_ref)
-    collect(u_refs, 256, src_ref, at_ref)
     second = jnp.zeros((160, 256), F32)
     for k, shift in enumerate(RING):
         z = (at_ref[2] + shift + 4) & 3
@@ -124,7 +131,7 @@
         for b in range(2):
             inv = inverse_of(info, b)
             lanes = slice(b * 128, b * 128 + 128)
-            total = spread(src_ref, links_ref, m_refs, k, b, (at_ref[1] * 4 + z) * 2 + b)
+            total = spread((src_ref, u_ref), links_ref, m_refs, k, b, (at_ref[1] * 4 + z) * 2 + b)
             m = inv * total[0:256]
             s = jax.nn.sigmoid(m)
             hid = (m * s).astype(BF)
@@ -149,7 +156,7 @@
         info = info_of(i_refs, k)
         parts = []
         for b in range(2):
-            total = spread(src_ref, links_ref, m_refs, k, b, (at_ref[1] * 4 + z) * 2 + b)
+            total = spread((src_ref,), links_ref, m_refs, k, b, (at_ref[1] * 4 + z) * 2 + b)
             parts.append((inverse_of(info, b) * total).astype(BF))
         rights.append(jnp.concatenate(parts, axis=1))
     seconds = []
@@ -243,18 +250,21 @@
     weight = lax.dynamic_slice(first_weight, (0, z * 256), (96, 256))
     other = lax.ppermute(weight, "c", [(0, 1), (1, 0)])
     mask = call(mask_kernel, shape((256, 768), BF), [VMEM], moved=1_200_000)(neighbour_mask[0])
-    x_low, x_high, *scaled, mask, other = lax.optimization_barrier(
-        (x_own[:4], x_own[4:], *scaled, mask, other)
-    )
+    own_second = lax.dynamic_slice(second_weight, (z * 256, 0), (256, 153))
+    own_second = jnp.pad(own_second, ((0, 0), (0, 7)))
+    weights = ring(jnp.stack([weight, other]), "y")
+    x_low, x_high, mask, own_second, *weights, n1, n2, n3 = lax.optimization_barrier(
+        (x_own[:4], x_own[4:], mask, own_second, *weights, *nodes[1:])
+    )
+    nodes = [nodes[0], n1, n2, n3]
     x_near = neighbours(x_low, x_high, "z")
+    x0, x1, *scaled = lax.optimization_barrier((*x_near[:2], *scaled))
+    x_wide = rounds(x_low, x_high, x_near, (x0, x1), "z")
     u_near = neighbours(*scaled, "x")
-    x0, x1, u0, u1, other = lax.optimization_barrier((*x_near[:2], *u_near[:2], other))
-    weights = ring(jnp.stack([weight, other]), "y")
-    x_wide = rounds(x_low, x_high, x_near, (x0, x1), "z")
-    scaled = rounds(*scaled, u_near, (u0, u1), "x")
-    *x_far, u2, u3, u4, u5 = lax.optimization_barrier((*x_wide[6:], *scaled[3:5], *scaled[6:]))
-    x_wide = [*x_wide[:6], *x_far]
-    scaled = [*scaled[:3], u2, u3, scaled[5], u4, u5]
+    scaled = rounds(*scaled, u_near, u_near[:2], "x")
+    scaled = call(collect_kernel, shape((32, 160, 128), BF), [VMEM] * 8 + [SMEM], moved=2_600_000)(
+        *scaled, at
+    )
     half = shape((2, 256, 256), BF)
     s = call(
         project_kernel,
@@ -267,21 +277,20 @@
     *s, mask = lax.optimization_barrier((*s, mask))
     s_near = neighbours(*s, "x")
     after, before = near(mask, "z")
-    s = rounds(*s, s_near, s_near[:2], "x")
+    s0, s1, scaled = lax.optimization_barrier((*s_near[:2], scaled))
+    s = rounds(*s, s_near, (s0, s1), "x")
     masks = [mask, after, before, fetch(after[:128], "z", 1), fetch(before[128:], "z", -1)]
-    own_second = lax.dynamic_slice(second_weight, (z * 256, 0), (256, 153))
-    own_second = jnp.pad(own_second, ((0, 0), (0, 7)))
     links_scratch = [
         pltpu.VMEM((8, 128), I32), pltpu.SMEM((8, 128), I32), pltpu.SemaphoreType.DMA
     ]
     *hid, low, high, second = call(
         first_mix_kernel,
         (shape((256, 256), BF),) * 4 + (half, half, shape((160, 256), F32)),
-        [VMEM] * 22 + [SMEM] + [VMEM] * 4,
-        [pltpu.VMEM((32, 416, 128), BF), *links_scratch],
+        [VMEM] * 15 + [SMEM] + [VMEM] * 4,
+        [pltpu.VMEM((32, 256, 128), BF), *links_scratch],
         flops=700_000_000,
         moved=8_000_000,
-    )(*s, *scaled, *masks, own_second, at, *nodes)
+    )(*s, scaled, *masks, own_second, at, *nodes)
     b_near = neighbours(low, high, "x")
     *passed, h1, h2, h3 = lax.optimization_barrier((*b_near[:2], *hid[1:]))
     back = rounds(low, high, b_near, passed, "x")

time: 157 us -> 147 us (0.936)
  local copies, waits for them, and re-layouts: 18.3 us -> 8.54 us
  waiting for transfers between devices: 33.6 us -> 40.9 us
  starting transfers between devices: 66.4 us -> 60.7 us
  blocking collectives: 21.7 us -> 20.1 us
    unnamed x78 -> x24, local copies, waits for them, and re-layouts: 14.9 us -> 7.42 us
    ppermute x37, waiting for transfers between devices: 23.5 us -> 28.8 us  [fetch(): return lax.ppermute(value, axis, [((i + shift) % 4, i) for i in range(4)])]
    ppermute x37, starting transfers between devices: 56.6 us -> 52 us  [fetch(): return lax.ppermute(value, axis, [((i + shift) % 4, i) for i in range(4)])]
    all_to_all x1, blocking collectives: 21.7 us -> 20.1 us  [body(): lax.all_to_all(part.reshape(32, 128, 128), ('y', 'c', 'x'), 0, 0, tiled=T...]
  transfers between devices with their start and end apart: 40 -> 40, of which waited for: 14 -> 21; matrix products, arithmetic and copies ran while one was open for 2% -> 2% of each run, Pallas kernels for 3% -> 5%
where the time goes in v9:
time: 147 us; the launch traced here: 146 us
  starting transfers between devices  60.7 us (41%)
  waiting for transfers between devices  40.9 us (28%)
  blocking collectives  20.1 us (14%)
  Pallas kernels  14.6 us (10%)
  local copies, waits for them, and re-layouts  8.54 us (6%)
    ppermute x37, starting transfers between devices, fetch(): return lax.ppermute(value, axis, [((i + shift) % 4, i) for i in range(4)])  52 us
    ppermute x37, waiting for transfers between devices, fetch(): return lax.ppermute(value, axis, [((i + shift) % 4, i) for i in range(4)])  28.8 us
    all_to_all x1, blocking collectives, body(): lax.all_to_all(part.reshape(32, 128, 128), ('y', 'c', 'x'), 0, 0, tiled=T...  20.1 us
    all_to_all x1, waiting for transfers between devices, body(): done = lax.all_to_all(done, dom, 0, 0, tiled=True)  10.1 us
    unnamed x24, local copies, waits for them, and re-layouts  7.42 us
    pallas_call x1, Pallas kernels, body(): call(first_mix_kernel, (shape((256, 256), BF),) * 4 + (half, half, shape(...  4.64 us
    all_to_all x1, starting transfers between devices, body(): lax.all_to_all(features.reshape(96, 8, 256).transpose(1, 0, 2), feat, 0,...  4.47 us
    pallas_call x1, Pallas kernels, body(): call(second_mix_kernel, shape((8, 4, 128, 128), BF), [VMEM] * 22 + [SMEM]...  3.81 us
  transfers between devices with their start and end apart: 40, of which 21 were waited for; matrix products, arithmetic and copies ran while one was open for 2% of the time, Pallas kernels for 5%

profile of v9, /device:TPU:0, one launch (start us, length us, event | category | flops | bytes accessed | tf_op | source)
XLA Modules:
  0.0 146.5 jit_solution(13918926831768849886)
XLA Ops:
  3.1 4.0 %collective-permute-start.6 = (bf16[176,256]{1,0:T(8,128)(2,1)S(1)}, bf16[176,256]{1,0:T(8,128)(2,1)S(1)}, u32[]{:S(2)}, u32[]{:S(2)}) collective-permute-start(bf16[176,256]{1,0:T(8,128)(2,1)S(1)} %shard_map.95.refs_0_.refs_12_.refs_16_.refs_23_), channel_id=1, source_target_pairs={{2,0},{3,1},{0,2},{1,3},{6,4},{7,5},{4,6},{5,7},{10,8},{11,9},{8,1... | collective-permute-start | bytes 270344 | tf_op jit(solution)/shard_map/ppermute | solution.py:215
  8.1 2.2 %collective-permute-start.4 = (bf16[176,256]{1,0:T(8,128)(2,1)S(1)}, bf16[176,256]{1,0:T(8,128)(2,1)S(1)}, u32[]{:S(2)}, u32[]{:S(2)}) collective-permute-start(bf16[176,256]{1,0:T(8,128)(2,1)S(1)} %shard_map.95.refs_0_.refs_12_.refs_16_.refs_23_), channel_id=1, source_target_pairs={{1,0},{2,1},{3,2},{0,3},{5,4},{6,5},{7,6},{4,7},{9,8},{10,9},{11,1... | collective-permute-start | bytes 270344 | tf_op jit(solution)/shard_map/ppermute | solution.py:215
  12.3 4.5 %all-to-all-start = ((bf16[8,96,256]{2,1,0:T(8,128)(2,1)}), bf16[8,96,256]{2,1,0:T(8,128)(2,1)S(1)}, u32[]{:S(2)}, u32[]{:S(2)}) async-start(bf16[8,96,256]{2,1,0:T(8,128)(2,1)} %bitcast.22), calls=%async_computation | async-start | bytes 786432 | tf_op jit(solution)/shard_map/all_to_all | solution.py:240
  18.3 3.5 %collective-permute-start.3 = (bf16[2,96,256]{2,1,0:T(8,128)(2,1)S(1)}, bf16[2,96,256]{2,1,0:T(8,128)(2,1)S(1)}, u32[]{:S(2)}, u32[]{:S(2)}) collective-permute-start(bf16[2,96,256]{2,1,0:T(8,128)(2,1)S(1)} %pad_maximum_fusion.refs_8_), channel_id=1, source_target_pairs={{64,0},{96,32},{0,64},{32,96},{65,1},{97,33},{1,65},{33,97},{66,2}... | collective-permute-start | bytes 294920 | tf_op jit(solution)/shard_map/ppermute | solution.py:215
  22.3 2.7 %collective-permute-start.1 = (bf16[2,96,256]{2,1,0:T(8,128)(2,1)S(1)}, bf16[2,96,256]{2,1,0:T(8,128)(2,1)S(1)}, u32[]{:S(2)}, u32[]{:S(2)}) collective-permute-start(bf16[2,96,256]{2,1,0:T(8,128)(2,1)S(1)} %pad_maximum_fusion.refs_8_), channel_id=1, source_target_pairs={{32,0},{64,32},{96,64},{0,96},{33,1},{65,33},{97,65},{1,97},{34,2}... | collective-permute-start | bytes 294920 | tf_op jit(solution)/shard_map/ppermute | solution.py:215
  26.3 2.0 %collective-permute-done.3.refs_11_ = bf16[2,96,256]{2,1,0:T(8,128)(2,1)S(1)} collective-permute-done((bf16[2,96,256]{2,1,0:T(8,128)(2,1)S(1)}, bf16[2,96,256]{2,1,0:T(8,128)(2,1)S(1)}, u32[]{:S(2)}, u32[]{:S(2)}) %collective-permute-start.3) | collective-permute-done | bytes 98336 | tf_op jit(solution)/shard_map/ppermute | solution.py:215
  31.2 2.0 %collective-permute-start.8 = (bf16[4,96,256]{2,1,0:T(8,128)(2,1)S(1)}, bf16[4,96,256]{2,1,0:T(8,128)(2,1)S(1)}, u32[]{:S(2)}, u32[]{:S(2)}) collective-permute-start(bf16[4,96,256]{2,1,0:T(8,128)(2,1)S(1)} %get-tuple-element.48.refs_1_.refs_14_), channel_id=1, source_target_pairs={{3,0},{0,1},{1,2},{2,3},{7,4},{4,5},{5,6},{6,7},{11,8},{8,9},{9,10... | collective-permute-start | bytes 589832 | tf_op jit(solution)/shard_map/ppermute | solution.py:215
  33.3 3.2 %collective-permute-start.9 = (bf16[4,96,256]{2,1,0:T(8,128)(2,1)S(1)}, bf16[4,96,256]{2,1,0:T(8,128)(2,1)S(1)}, u32[]{:S(2)}, u32[]{:S(2)}) collective-permute-start(bf16[4,96,256]{2,1,0:T(8,128)(2,1)S(1)} %get-tuple-element.48.refs_1_.refs_14_), channel_id=1, source_target_pairs={{1,0},{2,1},{3,2},{0,3},{5,4},{6,5},{7,6},{4,7},{9,8},{10,9},{11,1... | collective-permute-start | bytes 589832 | tf_op jit(solution)/shard_map/ppermute | solution.py:215
  36.5 2.5 %collective-permute-done.7.refs_2_.refs_15_ = bf16[4,96,256]{2,1,0:T(8,128)(2,1)S(1)} collective-permute-done((bf16[4,96,256]{2,1,0:T(8,128)(2,1)S(1)}, bf16[4,96,256]{2,1,0:T(8,128)(2,1)S(1)}, u32[]{:S(2)}, u32[]{:S(2)}) %collective-permute-start.7) | collective-permute-done | bytes 196640 | tf_op jit(solution)/shard_map/ppermute | solution.py:215
  40.2 2.0 %collective-permute-start.12 = (bf16[4,96,256]{2,1,0:T(8,128)(2,1)S(1)}, bf16[4,96,256]{2,1,0:T(8,128)(2,1)S(1)}, u32[]{:S(2)}, u32[]{:S(2)}) collective-permute-start(bf16[4,96,256]{2,1,0:T(8,128)(2,1)S(1)} %collective-permute-done.8.refs_5_.refs_18_), channel_id=1, source_target_pairs={{3,0},{0,1},{1,2},{2,3},{7,4},{4,5},{5,6},{6,7},{11,8},{8,9},{9,10... | collective-permute-start | bytes 589832 | tf_op jit(solution)/shard_map/ppermute | solution.py:215
  42.2 2.8 %collective-permute-start.15 = (bf16[2,160,256]{2,1,0:T(8,128)(2,1)S(1)}, bf16[2,160,256]{2,1,0:T(8,128)(2,1)S(1)}, u32[]{:S(2)}, u32[]{:S(2)}) collective-permute-start(bf16[2,160,256]{2,1,0:T(8,128)(2,1)S(1)} %get-tuple-element.65.refs_0_), channel_id=1, source_target_pairs={{4,0},{8,4},{12,8},{0,12},{5,1},{9,5},{13,9},{1,13},{6,2},{10,6},{... | collective-permute-start | bytes 491528 | tf_op jit(solution)/shard_map/ppermute | solution.py:215
  45.8 1.5 %collective-permute-start.17 = (bf16[2,160,256]{2,1,0:T(8,128)(2,1)S(1)}, bf16[2,160,256]{2,1,0:T(8,128)(2,1)}, u32[]{:S(2)}, u32[]{:S(2)}) collective-permute-start(bf16[2,160,256]{2,1,0:T(8,128)(2,1)S(1)} %get-tuple-element.65.refs_0_), channel_id=1, source_target_pairs={{12,0},{0,4},{4,8},{8,12},{13,1},{1,5},{5,9},{9,13},{14,2},{2,6},{... | collective-permute-start | bytes 491528 | tf_op jit(solution)/shard_map/ppermute | solution.py:215
  47.8 3.7 %collective-permute-start.16 = (bf16[2,160,256]{2,1,0:T(8,128)(2,1)S(1)}, bf16[2,160,256]{2,1,0:T(8,128)(2,1)S(1)}, u32[]{:S(2)}, u32[]{:S(2)}) collective-permute-start(bf16[2,160,256]{2,1,0:T(8,128)(2,1)S(1)} %get-tuple-element.66.refs_1_), channel_id=1, source_target_pairs={{4,0},{8,4},{12,8},{0,12},{5,1},{9,5},{13,9},{1,13},{6,2},{10,6},{... | collective-permute-start | bytes 491528 | tf_op jit(solution)/shard_map/ppermute | solution.py:215
  56.8 1.8 %collective-permute-start.20 = (bf16[2,160,256]{2,1,0:T(8,128)(2,1)S(1)}, bf16[2,160,256]{2,1,0:T(8,128)(2,1)S(1)}, u32[]{:S(2)}, u32[]{:S(2)}) collective-permute-start(bf16[2,160,256]{2,1,0:T(8,128)(2,1)S(1)} %collective-permute-done.18.refs_5_), channel_id=1, source_target_pairs={{12,0},{0,4},{4,8},{8,12},{13,1},{1,5},{5,9},{9,13},{14,2},{2,6},{... | collective-permute-start | bytes 491528 | tf_op jit(solution)/shard_map/ppermute | solution.py:215
  58.6 2.2 %collective-permute-start.25 = (bf16[256,768]{1,0:T(8,128)(2,1)S(1)}, bf16[256,768]{1,0:T(8,128)(2,1)S(1)}, u32[]{:S(2)}, u32[]{:S(2)}) collective-permute-start(bf16[256,768]{1,0:T(8,128)(2,1)S(1)} %shard_map.94.refs_9_.refs_8_), channel_id=1, source_target_pairs={{1,0},{2,1},{3,2},{0,3},{5,4},{6,5},{7,6},{4,7},{9,8},{10,9},{11,1... | collective-permute-start | bytes 1179656 | tf_op jit(solution)/shard_map/ppermute | solution.py:215
  62.8 2.2 %collective-permute-done.20.refs_7_ = bf16[2,160,256]{2,1,0:T(8,128)(2,1)S(1)} collective-permute-done((bf16[2,160,256]{2,1,0:T(8,128)(2,1)S(1)}, bf16[2,160,256]{2,1,0:T(8,128)(2,1)S(1)}, u32[]{:S(2)}, u32[]{:S(2)}) %collective-permute-start.20) | collective-permute-done | bytes 163872 | tf_op jit(solution)/shard_map/ppermute | solution.py:215
  66.9 3.1 %collective-permute-done.13.refs_2_ = bf16[2,256,256]{2,1,0:T(8,128)(2,1)S(1)} collective-permute-done((bf16[2,256,256]{2,1,0:T(8,128)(2,1)S(1)}, bf16[2,256,256]{2,1,0:T(8,128)(2,1)S(1)}, u32[]{:S(2)}, u32[]{:S(2)}) %collective-permute-start.13) | collective-permute-done | bytes 262176 | tf_op jit(solution)/shard_map/ppermute | solution.py:215
  70.9 1.6 %collective-permute-done.14.refs_5_ = bf16[2,256,256]{2,1,0:T(8,128)(2,1)S(1)} collective-permute-done((bf16[2,256,256]{2,1,0:T(8,128)(2,1)S(1)}, bf16[2,256,256]{2,1,0:T(8,128)(2,1)S(1)}, u32[]{:S(2)}, u32[]{:S(2)}) %collective-permute-start.14) | collective-permute-done | bytes 262176 | tf_op jit(solution)/shard_map/ppermute | solution.py:215
  72.5 2.0 %collective-permute-start.24 = (bf16[2,256,256]{2,1,0:T(8,128)(2,1)S(1)}, bf16[2,256,256]{2,1,0:T(8,128)(2,1)S(1)}, u32[]{:S(2)}, u32[]{:S(2)}) collective-permute-start(bf16[2,256,256]{2,1,0:T(8,128)(2,1)S(1)} %collective-permute-done.14.refs_5_), channel_id=1, source_target_pairs={{12,0},{0,4},{4,8},{8,12},{13,1},{1,5},{5,9},{9,13},{14,2},{2,6},{... | collective-permute-start | bytes 786440 | tf_op jit(solution)/shard_map/ppermute | solution.py:215
  74.6 2.4 %collective-permute-done.22.refs_4_ = bf16[2,256,256]{2,1,0:T(8,128)(2,1)S(1)} collective-permute-done((bf16[2,256,256]{2,1,0:T(8,128)(2,1)S(1)}, bf16[2,256,256]{2,1,0:T(8,128)(2,1)S(1)}, u32[]{:S(2)}, u32[]{:S(2)}) %collective-permute-start.22) | collective-permute-done | bytes 262176 | tf_op jit(solution)/shard_map/ppermute | solution.py:215
  80.1 1.4 collective-permute-done.28.refs_13_.refs_12_
  82.7 4.6 %shard_map.99 = (bf16[256,256]{1,0:T(8,128)(2,1)S(1)}, bf16[256,256]{1,0:T(8,128)(2,1)S(1)}, bf16[256,256]{1,0:T(8,128)(2,1)S(1)}, bf16[256,256]{1,0:T(8,128)(2,...) custom-call(bf16[2,256,256]{2,1,0:T(8,128)(2,1)S(1)} %get-tuple-element.63.refs_0, ...), custom_call_target="tpu_custom_call" | custom-call | flops 700000000 | bytes 8000000 | tf_op jit(solution)/shard_map/pallas_call | solution.py:286
  87.4 2.0 %collective-permute-start.30 = (bf16[2,256,256]{2,1,0:T(8,128)(2,1)S(1)}, bf16[2,256,256]{2,1,0:T(8,128)(2,1)S(1)}, u32[]{:S(2)}, u32[]{:S(2)}) collective-permute-start(bf16[2,256,256]{2,1,0:T(8,128)(2,1)S(1)} %get-tuple-element.73.refs_1_), channel_id=1, source_target_pairs={{12,0},{0,4},{4,8},{8,12},{13,1},{1,5},{5,9},{9,13},{14,2},{2,6},{... | collective-permute-start | bytes 786440 | tf_op jit(solution)/shard_map/ppermute | solution.py:215
  89.5 3.2 %collective-permute-start.31 = (bf16[2,256,256]{2,1,0:T(8,128)(2,1)S(1)}, bf16[2,256,256]{2,1,0:T(8,128)(2,1)S(1)}, u32[]{:S(2)}, u32[]{:S(2)}) collective-permute-start(bf16[2,256,256]{2,1,0:T(8,128)(2,1)S(1)} %get-tuple-element.73.refs_1_), channel_id=1, source_target_pairs={{4,0},{8,4},{12,8},{0,12},{5,1},{9,5},{13,9},{1,13},{6,2},{10,6},{... | collective-permute-start | bytes 786440 | tf_op jit(solution)/shard_map/ppermute | solution.py:215
  92.7 2.9 %collective-permute-done.29.refs_2_ = bf16[2,256,256]{2,1,0:T(8,128)(2,1)S(1)} collective-permute-done((bf16[2,256,256]{2,1,0:T(8,128)(2,1)S(1)}, bf16[2,256,256]{2,1,0:T(8,128)(2,1)S(1)}, u32[]{:S(2)}, u32[]{:S(2)}) %collective-permute-start.29) | collective-permute-done | bytes 262176 | tf_op jit(solution)/shard_map/ppermute | solution.py:215
  99.6 2.5 %collective-permute-start.36 = (bf16[256,256]{1,0:T(8,128)(2,1)S(1)}, bf16[256,256]{1,0:T(8,128)(2,1)S(1)}, u32[]{:S(2)}, u32[]{:S(2)}) collective-permute-start(bf16[256,256]{1,0:T(8,128)(2,1)S(1)} %get-tuple-element.82), channel_id=1, source_target_pairs={{1,0},{2,1},{3,2},{0,3},{5,4},{6,5},{7,6},{4,7},{9,8},{10,9},{11,1... | collective-permute-start | bytes 393224 | tf_op jit(solution)/shard_map/ppermute | solution.py:215
  103.1 1.9 %collective-permute-done.34.refs_7_ = bf16[2,256,256]{2,1,0:T(8,128)(2,1)S(1)} collective-permute-done((bf16[2,256,256]{2,1,0:T(8,128)(2,1)S(1)}, bf16[2,256,256]{2,1,0:T(8,128)(2,1)S(1)}, u32[]{:S(2)}, u32[]{:S(2)}) %collective-permute-start.34) | collective-permute-done | bytes 262176 | tf_op jit(solution)/shard_map/ppermute | solution.py:215
  105.1 3.8 %shard_map.100 = bf16[8,4,128,128]{3,2,1,0:T(8,128)(2,1)S(1)} custom-call(bf16[2,256,256]{2,1,0:T(8,128)(2,1)S(1)} %get-tuple-element.72.refs_0_, bf16[2,256,256]{2,1,0:T(8,128)(2,1)S(1)} %get-tuple-element.73.refs_1_, bf16[2,256,256]{2,1,0:T(8,128)(2,1)S(1)} %collective-permute-done.29.refs_2_, bf16[2,256,256]{2,1,0:T(8,128)(2,1)S(1)} %collective-permute-done.31.refs_3_, ...), custom_call_target="tpu_custom_call" | custom-call | flops 900000000 | bytes 8000000 | tf_op jit(solution)/shard_map/pallas_call | solution.py:298
  108.9 20.1 %all_to_all.15.part_ref = bf16[32,128,128]{2,1,0:T(8,128)(2,1)S(1)} all-to-all(bf16[32,128,128]{2,1,0:T(8,128)(2,1)S(1)} %bitcast.23), channel_id=1, replica_groups=mesh['y'=4,'c'=2,'x'=4,'z'=4] {'y','c','x'}, dimensions={0} | all-to-all | bytes 2097152 | tf_op jit(solution)/shard_map/all_to_all | solution.py:307
  129.9 3.7 %all-to-all-start.2 = ((bf16[16,128,128]{2,1,0:T(8,128)(2,1)}), bf16[16,128,128]{2,1,0:T(8,128)(2,1)S(1)}, u32[]{:S(2)}, u32[]{:S(2)}) async-start(bf16[16,128,128]{2,1,0:T(8,128)(2,1)} %shard_map.102), calls=%async_computation.2 | async-start | bytes 1048576 | tf_op jit(solution)/shard_map/all_to_all | solution.py:310
  133.6 1.5 %shard_map.101 = bf16[256,1024]{1,0:T(8,128)(2,1)} custom-call(bf16[256,256]{1,0:T(8,128)(2,1)S(1)} %get-tuple-element.84.h0_ref, bf16[256,256]{1,0:T(8,128)(2,1)S(1)} %collective-permute-done.35.h1_ref, bf16[256,256]{1,0:T(8,128)(2,1)S(1)} %collective-permute-done.36.h2_ref, bf16[256,256]{1,0:T(8,128)(2,1)S(1)} %collective-permute-done.37.h3_ref, ...), custom_call_target="tpu_custom_call" | custom-call | bytes 1000000 | tf_op jit(solution)/shard_map/pallas_call | solution.py:311
  135.2 10.1 %all-to-all-done.2.in_ref = bf16[16,128,128]{2,1,0:T(8,128)(2,1)S(1)} async-done(((bf16[16,128,128]{2,1,0:T(8,128)(2,1)}), bf16[16,128,128]{2,1,0:T(8,128)(2,1)S(1)}, u32[]{:S(2)}, u32[]{:S(2)}) %all-to-all-start.2) | async-done | bytes 524320 | tf_op jit(solution)/shard_map/all_to_all | solution.py:310
  (96 shorter events, 36.0 us)
Async XLA Ops:
  3.1 19.2 %collective-permute-start.6 = (bf16[176,256]{1,0:T(8,128)(2,1)S(1)}, bf16[176,256]{1,0:T(8,128)(2,1)S(1)}, u32[]{:S(2)}, u32[]{:S(2)}) collective-permute-start(bf16[176,256]{1,0:T(8,128)(2,1)S(1)} %shard_map.95.refs_0_.refs_12_.refs_16_.refs_23_), channel_id=1, source_target_pairs={{2,0},{3,1},{0,2},{1,3},{6,4},{7,5},{4,6},{5,7},{10,8},{11,9},{8,1... | collective-permute-start | bytes 270344 | tf_op jit(solution)/shard_map/ppermute | solution.py:215
  7.1 19.2 %collective-permute-start.5 = (bf16[176,256]{1,0:T(8,128)(2,1)S(1)}, bf16[176,256]{1,0:T(8,128)(2,1)S(1)}, u32[]{:S(2)}, u32[]{:S(2)}) collective-permute-start(bf16[176,256]{1,0:T(8,128)(2,1)S(1)} %shard_map.95.refs_0_.refs_12_.refs_16_.refs_23_), channel_id=1, source_target_pairs={{3,0},{0,1},{1,2},{2,3},{7,4},{4,5},{5,6},{6,7},{11,8},{8,9},{9,10... | collective-permute-start | bytes 270344 | tf_op jit(solution)/shard_map/ppermute | solution.py:215
  8.1 18.2 %collective-permute-start.4 = (bf16[176,256]{1,0:T(8,128)(2,1)S(1)}, bf16[176,256]{1,0:T(8,128)(2,1)S(1)}, u32[]{:S(2)}, u32[]{:S(2)}) collective-permute-start(bf16[176,256]{1,0:T(8,128)(2,1)S(1)} %shard_map.95.refs_0_.refs_12_.refs_16_.refs_23_), channel_id=1, source_target_pairs={{1,0},{2,1},{3,2},{0,3},{5,4},{6,5},{7,6},{4,7},{9,8},{10,9},{11,1... | collective-permute-start | bytes 270344 | tf_op jit(solution)/shard_map/ppermute | solution.py:215
  12.3 14.0 %all-to-all-start = ((bf16[8,96,256]{2,1,0:T(8,128)(2,1)}), bf16[8,96,256]{2,1,0:T(8,128)(2,1)S(1)}, u32[]{:S(2)}, u32[]{:S(2)}) async-start(bf16[8,96,256]{2,1,0:T(8,128)(2,1)} %bitcast.22), calls=%async_computation | async-start | bytes 786432 | tf_op jit(solution)/shard_map/all_to_all | solution.py:240
  18.3 10.1 %collective-permute-start.3 = (bf16[2,96,256]{2,1,0:T(8,128)(2,1)S(1)}, bf16[2,96,256]{2,1,0:T(8,128)(2,1)S(1)}, u32[]{:S(2)}, u32[]{:S(2)}) collective-permute-start(bf16[2,96,256]{2,1,0:T(8,128)(2,1)S(1)} %pad_maximum_fusion.refs_8_), channel_id=1, source_target_pairs={{64,0},{96,32},{0,64},{32,96},{65,1},{97,33},{1,65},{33,97},{66,2}... | collective-permute-start | bytes 294920 | tf_op jit(solution)/shard_map/ppermute | solution.py:215
  21.7 8.2 %collective-permute-start.2 = (bf16[2,96,256]{2,1,0:T(8,128)(2,1)S(1)}, bf16[2,96,256]{2,1,0:T(8,128)(2,1)S(1)}, u32[]{:S(2)}, u32[]{:S(2)}) collective-permute-start(bf16[2,96,256]{2,1,0:T(8,128)(2,1)S(1)} %pad_maximum_fusion.refs_8_), channel_id=1, source_target_pairs={{96,0},{0,32},{32,64},{64,96},{97,1},{1,33},{33,65},{65,97},{98,2}... | collective-permute-start | bytes 294920 | tf_op jit(solution)/shard_map/ppermute | solution.py:215
  22.3 8.3 %collective-permute-start.1 = (bf16[2,96,256]{2,1,0:T(8,128)(2,1)S(1)}, bf16[2,96,256]{2,1,0:T(8,128)(2,1)S(1)}, u32[]{:S(2)}, u32[]{:S(2)}) collective-permute-start(bf16[2,96,256]{2,1,0:T(8,128)(2,1)S(1)} %pad_maximum_fusion.refs_8_), channel_id=1, source_target_pairs={{32,0},{64,32},{96,64},{0,96},{33,1},{65,33},{97,65},{1,97},{34,2}... | collective-permute-start | bytes 294920 | tf_op jit(solution)/shard_map/ppermute | solution.py:215
  31.2 7.8 %collective-permute-start.7 = (bf16[4,96,256]{2,1,0:T(8,128)(2,1)S(1)}, bf16[4,96,256]{2,1,0:T(8,128)(2,1)S(1)}, u32[]{:S(2)}, u32[]{:S(2)}) collective-permute-start(bf16[4,96,256]{2,1,0:T(8,128)(2,1)S(1)} %get-tuple-element.47.refs_0_.refs_13_), channel_id=1, source_target_pairs={{1,0},{2,1},{3,2},{0,3},{5,4},{6,5},{7,6},{4,7},{9,8},{10,9},{11,1... | collective-permute-start | bytes 589832 | tf_op jit(solution)/shard_map/ppermute | solution.py:215
  31.2 9.0 %collective-permute-start.8 = (bf16[4,96,256]{2,1,0:T(8,128)(2,1)S(1)}, bf16[4,96,256]{2,1,0:T(8,128)(2,1)S(1)}, u32[]{:S(2)}, u32[]{:S(2)}) collective-permute-start(bf16[4,96,256]{2,1,0:T(8,128)(2,1)S(1)} %get-tuple-element.48.refs_1_.refs_14_), channel_id=1, source_target_pairs={{3,0},{0,1},{1,2},{2,3},{7,4},{4,5},{5,6},{6,7},{11,8},{8,9},{9,10... | collective-permute-start | bytes 589832 | tf_op jit(solution)/shard_map/ppermute | solution.py:215
  33.3 11.7 %collective-permute-start.10 = (bf16[4,96,256]{2,1,0:T(8,128)(2,1)S(1)}, bf16[4,96,256]{2,1,0:T(8,128)(2,1)S(1)}, u32[]{:S(2)}, u32[]{:S(2)}) collective-permute-start(bf16[4,96,256]{2,1,0:T(8,128)(2,1)S(1)} %get-tuple-element.47.refs_0_.refs_13_), channel_id=1, source_target_pairs={{3,0},{0,1},{1,2},{2,3},{7,4},{4,5},{5,6},{6,7},{11,8},{8,9},{9,10... | collective-permute-start | bytes 589832 | tf_op jit(solution)/shard_map/ppermute | solution.py:215
  33.3 12.5 %collective-permute-start.9 = (bf16[4,96,256]{2,1,0:T(8,128)(2,1)S(1)}, bf16[4,96,256]{2,1,0:T(8,128)(2,1)S(1)}, u32[]{:S(2)}, u32[]{:S(2)}) collective-permute-start(bf16[4,96,256]{2,1,0:T(8,128)(2,1)S(1)} %get-tuple-element.48.refs_1_.refs_14_), channel_id=1, source_target_pairs={{1,0},{2,1},{3,2},{0,3},{5,4},{6,5},{7,6},{4,7},{9,8},{10,9},{11,1... | collective-permute-start | bytes 589832 | tf_op jit(solution)/shard_map/ppermute | solution.py:215
  40.2 11.3 %collective-permute-start.11 = (bf16[4,96,256]{2,1,0:T(8,128)(2,1)S(1)}, bf16[4,96,256]{2,1,0:T(8,128)(2,1)S(1)}, u32[]{:S(2)}, u32[]{:S(2)}) collective-permute-start(bf16[4,96,256]{2,1,0:T(8,128)(2,1)S(1)} %collective-permute-done.7.refs_2_.refs_15_), channel_id=1, source_target_pairs={{1,0},{2,1},{3,2},{0,3},{5,4},{6,5},{7,6},{4,7},{9,8},{10,9},{11,1... | collective-permute-start | bytes 589832 | tf_op jit(solution)/shard_map/ppermute | solution.py:215
  40.2 11.3 %collective-permute-start.12 = (bf16[4,96,256]{2,1,0:T(8,128)(2,1)S(1)}, bf16[4,96,256]{2,1,0:T(8,128)(2,1)S(1)}, u32[]{:S(2)}, u32[]{:S(2)}) collective-permute-start(bf16[4,96,256]{2,1,0:T(8,128)(2,1)S(1)} %collective-permute-done.8.refs_5_.refs_18_), channel_id=1, source_target_pairs={{3,0},{0,1},{1,2},{2,3},{7,4},{4,5},{5,6},{6,7},{11,8},{8,9},{9,10... | collective-permute-start | bytes 589832 | tf_op jit(solution)/shard_map/ppermute | solution.py:215
  45.0 11.8 %collective-permute-start.18 = (bf16[2,160,256]{2,1,0:T(8,128)(2,1)S(1)}, bf16[2,160,256]{2,1,0:T(8,128)(2,1)S(1)}, u32[]{:S(2)}, u32[]{:S(2)}) collective-permute-start(bf16[2,160,256]{2,1,0:T(8,128)(2,1)S(1)} %get-tuple-element.66.refs_1_), channel_id=1, source_target_pairs={{12,0},{0,4},{4,8},{8,12},{13,1},{1,5},{5,9},{9,13},{14,2},{2,6},{... | collective-permute-start | bytes 491528 | tf_op jit(solution)/shard_map/ppermute | solution.py:215
  45.8 12.7 %collective-permute-start.17 = (bf16[2,160,256]{2,1,0:T(8,128)(2,1)S(1)}, bf16[2,160,256]{2,1,0:T(8,128)(2,1)}, u32[]{:S(2)}, u32[]{:S(2)}) collective-permute-start(bf16[2,160,256]{2,1,0:T(8,128)(2,1)S(1)} %get-tuple-element.65.refs_0_), channel_id=1, source_target_pairs={{12,0},{0,4},{4,8},{8,12},{13,1},{1,5},{5,9},{9,13},{14,2},{2,6},{... | collective-permute-start | bytes 491528 | tf_op jit(solution)/shard_map/ppermute | solution.py:215
  47.8 12.9 %collective-permute-start.16 = (bf16[2,160,256]{2,1,0:T(8,128)(2,1)S(1)}, bf16[2,160,256]{2,1,0:T(8,128)(2,1)S(1)}, u32[]{:S(2)}, u32[]{:S(2)}) collective-permute-start(bf16[2,160,256]{2,1,0:T(8,128)(2,1)S(1)} %get-tuple-element.66.refs_1_), channel_id=1, source_target_pairs={{4,0},{8,4},{12,8},{0,12},{5,1},{9,5},{13,9},{1,13},{6,2},{10,6},{... | collective-permute-start | bytes 491528 | tf_op jit(solution)/shard_map/ppermute | solution.py:215
  51.5 10.5 %collective-permute-start.19 = (bf16[2,160,256]{2,1,0:T(8,128)(2,1)S(1)}, bf16[2,160,256]{2,1,0:T(8,128)(2,1)S(1)}, u32[]{:S(2)}, u32[]{:S(2)}) collective-permute-start(bf16[2,160,256]{2,1,0:T(8,128)(2,1)S(1)} %collective-permute-done.15.refs_2_), channel_id=1, source_target_pairs={{4,0},{8,4},{12,8},{0,12},{5,1},{9,5},{13,9},{1,13},{6,2},{10,6},{... | collective-permute-start | bytes 491528 | tf_op jit(solution)/shard_map/ppermute | solution.py:215
  55.5 17.0 %collective-permute-start.26 = (bf16[256,768]{1,0:T(8,128)(2,1)S(1)}, bf16[256,768]{1,0:T(8,128)(2,1)S(1)}, u32[]{:S(2)}, u32[]{:S(2)}) collective-permute-start(bf16[256,768]{1,0:T(8,128)(2,1)S(1)} %shard_map.94.refs_9_.refs_8_), channel_id=1, source_target_pairs={{3,0},{0,1},{1,2},{2,3},{7,4},{4,5},{5,6},{6,7},{11,8},{8,9},{9,10... | collective-permute-start | bytes 1179656 | tf_op jit(solution)/shard_map/ppermute | solution.py:215
  56.8 8.3 %collective-permute-start.20 = (bf16[2,160,256]{2,1,0:T(8,128)(2,1)S(1)}, bf16[2,160,256]{2,1,0:T(8,128)(2,1)S(1)}, u32[]{:S(2)}, u32[]{:S(2)}) collective-permute-start(bf16[2,160,256]{2,1,0:T(8,128)(2,1)S(1)} %collective-permute-done.18.refs_5_), channel_id=1, source_target_pairs={{12,0},{0,4},{4,8},{8,12},{13,1},{1,5},{5,9},{9,13},{14,2},{2,6},{... | collective-permute-start | bytes 491528 | tf_op jit(solution)/shard_map/ppermute | solution.py:215
  58.6 16.0 %collective-permute-start.25 = (bf16[256,768]{1,0:T(8,128)(2,1)S(1)}, bf16[256,768]{1,0:T(8,128)(2,1)S(1)}, u32[]{:S(2)}, u32[]{:S(2)}) collective-permute-start(bf16[256,768]{1,0:T(8,128)(2,1)S(1)} %shard_map.94.refs_9_.refs_8_), channel_id=1, source_target_pairs={{1,0},{2,1},{3,2},{0,3},{5,4},{6,5},{7,6},{4,7},{9,8},{10,9},{11,1... | collective-permute-start | bytes 1179656 | tf_op jit(solution)/shard_map/ppermute | solution.py:215
  60.8 9.2 %collective-permute-start.13 = (bf16[2,256,256]{2,1,0:T(8,128)(2,1)S(1)}, bf16[2,256,256]{2,1,0:T(8,128)(2,1)S(1)}, u32[]{:S(2)}, u32[]{:S(2)}) collective-permute-start(bf16[2,256,256]{2,1,0:T(8,128)(2,1)S(1)} %get-tuple-element.63.refs_0_), channel_id=1, source_target_pairs={{4,0},{8,4},{12,8},{0,12},{5,1},{9,5},{13,9},{1,13},{6,2},{10,6},{... | collective-permute-start | bytes 786440 | tf_op jit(solution)/shard_map/ppermute | solution.py:215
  62.0 10.5 %collective-permute-start.14 = (bf16[2,256,256]{2,1,0:T(8,128)(2,1)S(1)}, bf16[2,256,256]{2,1,0:T(8,128)(2,1)S(1)}, u32[]{:S(2)}, u32[]{:S(2)}) collective-permute-start(bf16[2,256,256]{2,1,0:T(8,128)(2,1)S(1)} %get-tuple-element.64.refs_1_), channel_id=1, source_target_pairs={{12,0},{0,4},{4,8},{8,12},{13,1},{1,5},{5,9},{9,13},{14,2},{2,6},{... | collective-permute-start | bytes 786440 | tf_op jit(solution)/shard_map/ppermute | solution.py:215
  65.1 12.0 %collective-permute-start.22 = (bf16[2,256,256]{2,1,0:T(8,128)(2,1)S(1)}, bf16[2,256,256]{2,1,0:T(8,128)(2,1)S(1)}, u32[]{:S(2)}, u32[]{:S(2)}) collective-permute-start(bf16[2,256,256]{2,1,0:T(8,128)(2,1)S(1)} %get-tuple-element.63.refs_0_), channel_id=1, source_target_pairs={{12,0},{0,4},{4,8},{8,12},{13,1},{1,5},{5,9},{9,13},{14,2},{2,6},{... | collective-permute-start | bytes 786440 | tf_op jit(solution)/shard_map/ppermute | solution.py:215
  70.0 8.2 %collective-permute-start.21 = (bf16[2,256,256]{2,1,0:T(8,128)(2,1)S(1)}, bf16[2,256,256]{2,1,0:T(8,128)(2,1)S(1)}, u32[]{:S(2)}, u32[]{:S(2)}) collective-permute-start(bf16[2,256,256]{2,1,0:T(8,128)(2,1)S(1)} %get-tuple-element.64.refs_1_), channel_id=1, source_target_pairs={{4,0},{8,4},{12,8},{0,12},{5,1},{9,5},{13,9},{1,13},{6,2},{10,6},{... | collective-permute-start | bytes 786440 | tf_op jit(solution)/shard_map/ppermute | solution.py:215
  72.5 7.6 %collective-permute-start.24 = (bf16[2,256,256]{2,1,0:T(8,128)(2,1)S(1)}, bf16[2,256,256]{2,1,0:T(8,128)(2,1)S(1)}, u32[]{:S(2)}, u32[]{:S(2)}) collective-permute-start(bf16[2,256,256]{2,1,0:T(8,128)(2,1)S(1)} %collective-permute-done.14.refs_5_), channel_id=1, source_target_pairs={{12,0},{0,4},{4,8},{8,12},{13,1},{1,5},{5,9},{9,13},{14,2},{2,6},{... | collective-permute-start | bytes 786440 | tf_op jit(solution)/shard_map/ppermute | solution.py:215
  87.4 8.2 %collective-permute-start.29 = (bf16[2,256,256]{2,1,0:T(8,128)(2,1)S(1)}, bf16[2,256,256]{2,1,0:T(8,128)(2,1)S(1)}, u32[]{:S(2)}, u32[]{:S(2)}) collective-permute-start(bf16[2,256,256]{2,1,0:T(8,128)(2,1)S(1)} %get-tuple-element.72.refs_0_), channel_id=1, source_target_pairs={{4,0},{8,4},{12,8},{0,12},{5,1},{9,5},{13,9},{1,13},{6,2},{10,6},{... | collective-permute-start | bytes 786440 | tf_op jit(solution)/shard_map/ppermute | solution.py:215
  87.4 9.3 %collective-permute-start.30 = (bf16[2,256,256]{2,1,0:T(8,128)(2,1)S(1)}, bf16[2,256,256]{2,1,0:T(8,128)(2,1)S(1)}, u32[]{:S(2)}, u32[]{:S(2)}) collective-permute-start(bf16[2,256,256]{2,1,0:T(8,128)(2,1)S(1)} %get-tuple-element.73.refs_1_), channel_id=1, source_target_pairs={{12,0},{0,4},{4,8},{8,12},{13,1},{1,5},{5,9},{9,13},{14,2},{2,6},{... | collective-permute-start | bytes 786440 | tf_op jit(solution)/shard_map/ppermute | solution.py:215
  89.5 10.1 %collective-permute-start.32 = (bf16[2,256,256]{2,1,0:T(8,128)(2,1)S(1)}, bf16[2,256,256]{2,1,0:T(8,128)(2,1)S(1)}, u32[]{:S(2)}, u32[]{:S(2)}) collective-permute-start(bf16[2,256,256]{2,1,0:T(8,128)(2,1)S(1)} %get-tuple-element.72.refs_0_), channel_id=1, source_target_pairs={{12,0},{0,4},{4,8},{8,12},{13,1},{1,5},{5,9},{9,13},{14,2},{2,6},{... | collective-permute-start | bytes 786440 | tf_op jit(solution)/shard_map/ppermute | solution.py:215
  89.5 12.5 %collective-permute-start.31 = (bf16[2,256,256]{2,1,0:T(8,128)(2,1)S(1)}, bf16[2,256,256]{2,1,0:T(8,128)(2,1)S(1)}, u32[]{:S(2)}, u32[]{:S(2)}) collective-permute-start(bf16[2,256,256]{2,1,0:T(8,128)(2,1)S(1)} %get-tuple-element.73.refs_1_), channel_id=1, source_target_pairs={{4,0},{8,4},{12,8},{0,12},{5,1},{9,5},{13,9},{1,13},{6,2},{10,6},{... | collective-permute-start | bytes 786440 | tf_op jit(solution)/shard_map/ppermute | solution.py:215
  98.8 10.1 %collective-permute-start.35 = (bf16[256,256]{1,0:T(8,128)(2,1)S(1)}, bf16[256,256]{1,0:T(8,128)(2,1)S(1)}, u32[]{:S(2)}, u32[]{:S(2)}) collective-permute-start(bf16[256,256]{1,0:T(8,128)(2,1)S(1)} %get-tuple-element.81), channel_id=1, source_target_pairs={{3,0},{0,1},{1,2},{2,3},{7,4},{4,5},{5,6},{6,7},{11,8},{8,9},{9,10... | collective-permute-start | bytes 393224 | tf_op jit(solution)/shard_map/ppermute | solution.py:215
  99.6 9.3 %collective-permute-start.36 = (bf16[256,256]{1,0:T(8,128)(2,1)S(1)}, bf16[256,256]{1,0:T(8,128)(2,1)S(1)}, u32[]{:S(2)}, u32[]{:S(2)}) collective-permute-start(bf16[256,256]{1,0:T(8,128)(2,1)S(1)} %get-tuple-element.82), channel_id=1, source_target_pairs={{1,0},{2,1},{3,2},{0,3},{5,4},{6,5},{7,6},{4,7},{9,8},{10,9},{11,1... | collective-permute-start | bytes 393224 | tf_op jit(solution)/shard_map/ppermute | solution.py:215
  129.9 15.4 %all-to-all-start.2 = ((bf16[16,128,128]{2,1,0:T(8,128)(2,1)}), bf16[16,128,128]{2,1,0:T(8,128)(2,1)S(1)}, u32[]{:S(2)}, u32[]{:S(2)}) async-start(bf16[16,128,128]{2,1,0:T(8,128)(2,1)} %shard_map.102), calls=%async_computation.2 | async-start | bytes 1048576 | tf_op jit(solution)/shard_map/all_to_all | solution.py:310
  (19 other events, 91.0 us)

commit v10 on v9

--- a/solution.py
+++ b/solution.py
@@ -71,19 +71,22 @@
     return refs[2 * k + f // 4][f % 4]
 
 
-def project_kernel(*refs):
-    x_refs, w_refs, i_refs, at_ref = refs[:8], refs[8:12], refs[12:16], refs[16]
-    out_refs, w_ref = refs[17:19], refs[19]
+def weight_kernel(*refs):
+    w_refs, at_ref, out_ref, w_ref = refs[:4], refs[4], refs[5], refs[6]
     for k, shift in enumerate(RING):
         for flip in range(2):
             f = ((at_ref[3] + shift + 4) & 3) * 2 + ((at_ref[4] + flip) & 1)
             w_ref[f] = w_refs[k][flip]
-    w = w_ref[...].reshape(768, 256).astype(F32).T.astype(BF)
-    for k, shift in enumerate(RING):
+    out_ref[...] = w_ref[...].reshape(768, 256).astype(F32).T.astype(BF)
+
+
+def project_kernel(*refs):
+    x_refs, w_ref, i_refs, out_refs = refs[:8], refs[8], refs[9:13], refs[13:15]
+    for k in range(4):
         info = info_of(i_refs, k)
         inv = jnp.concatenate([inverse_of(info, 0), inverse_of(info, 1)], axis=1)
         whole = jnp.concatenate([features_at(x_refs, k, f) for f in range(8)], axis=0)
-        out_refs[k // 2][k % 2] = (inv * dot(w, whole)).astype(BF)
+        out_refs[k // 2][k % 2] = (inv * dot(w_ref[...], whole)).astype(BF)
 
 
 def collect(refs, base, src_ref, at_ref):
@@ -240,6 +243,9 @@
     x_own = lax.all_to_all(
         features.reshape(96, 8, 256).transpose(1, 0, 2), feat, 0, 0, tiled=True
     )
+    weight = lax.dynamic_slice(first_weight, (0, z * 256), (96, 256))
+    other = lax.ppermute(weight, "c", [(0, 1), (1, 0)])
+    other, degree = lax.optimization_barrier((other, degree))
     links = jnp.pad(jnp.maximum(neighbour_block.reshape(1, 12), 0), ((0, 0), (0, 116)))
     nodes = call(node_kernel, shape((176, 256), BF), [VMEM] * 3, moved=200_000)(
         upstream[0].T, degree.reshape(2, 128), links
@@ -247,14 +253,15 @@
     nodes = ring(nodes, "z")
     half = shape((2, 160, 256), BF)
     scaled = call(pack_kernel, (half, half), [VMEM] * 4, moved=600_000)(*nodes)
-    weight = lax.dynamic_slice(first_weight, (0, z * 256), (96, 256))
-    other = lax.ppermute(weight, "c", [(0, 1), (1, 0)])
     mask = call(mask_kernel, shape((256, 768), BF), [VMEM], moved=1_200_000)(neighbour_mask[0])
     own_second = lax.dynamic_slice(second_weight, (z * 256, 0), (256, 153))
     own_second = jnp.pad(own_second, ((0, 0), (0, 7)))
-    weights = ring(jnp.stack([weight, other]), "y")
-    x_low, x_high, mask, own_second, *weights, n1, n2, n3 = lax.optimization_barrier(
-        (x_own[:4], x_own[4:], mask, own_second, *weights, *nodes[1:])
+    weights = call(
+        weight_kernel, shape((256, 768), BF), [VMEM] * 4 + [SMEM], [pltpu.VMEM((8, 96, 256), BF)],
+        moved=800_000,
+    )(*ring(jnp.stack([weight, other]), "y"), at)
+    x_low, x_high, mask, own_second, weights, n1, n2, n3 = lax.optimization_barrier(
+        (x_own[:4], x_own[4:], mask, own_second, weights, *nodes[1:])
     )
     nodes = [nodes[0], n1, n2, n3]
     x_near = neighbours(x_low, x_high, "z")
@@ -269,11 +276,10 @@
     s = call(
         project_kernel,
         (half, half),
-        [VMEM] * 16 + [SMEM],
-        [pltpu.VMEM((8, 96, 256), BF)],
+        [VMEM] * 13,
         flops=400_000_000,
         moved=3_000_000,
-    )(*x_wide, *weights, *nodes, at)
+    )(*x_wide, weights, *nodes)
     *s, mask = lax.optimization_barrier((*s, mask))
     s_near = neighbours(*s, "x")
     after, before = near(mask, "z")

time: 147 us -> 143 us (0.973)
  starting transfers between devices: 60.7 us -> 66.6 us
  local copies, waits for them, and re-layouts: 8.54 us -> 3.94 us
  waiting for transfers between devices: 40.9 us -> 36.9 us
    unnamed x24 -> x12, local copies, waits for them, and re-layouts: 7.42 us -> 1.2 us
    ppermute x37, starting transfers between devices: 52 us -> 57.9 us  [fetch(): return lax.ppermute(value, axis, [((i + shift) % 4, i) for i in range(4)])]
    ppermute x37, waiting for transfers between devices: 28.8 us -> 26.8 us  [fetch(): return lax.ppermute(value, axis, [((i + shift) % 4, i) for i in range(4)])]
  transfers between devices with their start and end apart: 40 -> 40, of which waited for: 21 -> 16; matrix products, arithmetic and copies ran while one was open for 2% -> 2% of each run, Pallas kernels for 5% -> 5%
where the time goes in v10:
time: 143 us
  starting transfers between devices  66.6 us (47%)
  waiting for transfers between devices  36.9 us (26%)
  blocking collectives  20 us (14%)
  Pallas kernels  14.4 us (10%)
  local copies, waits for them, and re-layouts  3.94 us (3%)
    ppermute x37, starting transfers between devices, fetch(): return lax.ppermute(value, axis, [((i + shift) % 4, i) for i in range(4)])  57.9 us
    ppermute x37, waiting for transfers between devices, fetch(): return lax.ppermute(value, axis, [((i + shift) % 4, i) for i in range(4)])  26.8 us
    all_to_all x1, blocking collectives, body(): lax.all_to_all(part.reshape(32, 128, 128), ('y', 'c', 'x'), 0, 0, tiled=T...  20 us
    all_to_all x1, waiting for transfers between devices, body(): done = lax.all_to_all(done, dom, 0, 0, tiled=True)  10.1 us
    all_to_all x1, starting transfers between devices, body(): lax.all_to_all(features.reshape(96, 8, 256).transpose(1, 0, 2), feat, 0,...  4.8 us
    pallas_call x1, Pallas kernels, body(): call(first_mix_kernel, (shape((256, 256), BF),) * 4 + (half, half, shape(...  4.64 us
    all_to_all x1, starting transfers between devices, body(): done = lax.all_to_all(done, dom, 0, 0, tiled=True)  3.9 us
    pallas_call x1, Pallas kernels, body(): call(second_mix_kernel, shape((8, 4, 128, 128), BF), [VMEM] * 22 + [SMEM]...  3.82 us
  transfers between devices with their start and end apart: 40, of which 16 were waited for; matrix products, arithmetic and copies ran while one was open for 2% of the time, Pallas kernels for 5%

profile of v10, /device:TPU:0, one launch (start us, length us, event | category | flops | bytes accessed | tf_op | source)
XLA Modules:
  0.0 142.7 jit_solution(12699799151787607426)
XLA Ops:
  3.4 4.8 %all-to-all-start = ((bf16[8,96,256]{2,1,0:T(8,128)(2,1)}), bf16[8,96,256]{2,1,0:T(8,128)(2,1)S(1)}, u32[]{:S(2)}, u32[]{:S(2)}) async-start(bf16[8,96,256]{2,1,0:T(8,128)(2,1)} %bitcast.22), calls=%async_computation | async-start | bytes 786432 | tf_op jit(solution)/shard_map/all_to_all | solution.py:243
  9.2 3.6 %collective-permute-start.3 = (bf16[2,96,256]{2,1,0:T(8,128)(2,1)S(1)}, bf16[2,96,256]{2,1,0:T(8,128)(2,1)S(1)}, u32[]{:S(2)}, u32[]{:S(2)}) collective-permute-start(bf16[2,96,256]{2,1,0:T(8,128)(2,1)S(1)} %pad_maximum_fusion.refs_0_), channel_id=1, source_target_pairs={{64,0},{96,32},{0,64},{32,96},{65,1},{97,33},{1,65},{33,97},{66,2}... | collective-permute-start | bytes 294920 | tf_op jit(solution)/shard_map/ppermute | solution.py:218
  13.3 2.7 %collective-permute-start.1 = (bf16[2,96,256]{2,1,0:T(8,128)(2,1)S(1)}, bf16[2,96,256]{2,1,0:T(8,128)(2,1)S(1)}, u32[]{:S(2)}, u32[]{:S(2)}) collective-permute-start(bf16[2,96,256]{2,1,0:T(8,128)(2,1)S(1)} %pad_maximum_fusion.refs_0_), channel_id=1, source_target_pairs={{32,0},{64,32},{96,64},{0,96},{33,1},{65,33},{97,65},{1,97},{34,2}... | collective-permute-start | bytes 294920 | tf_op jit(solution)/shard_map/ppermute | solution.py:218
  16.3 4.0 %collective-permute-start.6 = (bf16[176,256]{1,0:T(8,128)(2,1)S(1)}, bf16[176,256]{1,0:T(8,128)(2,1)S(1)}, u32[]{:S(2)}, u32[]{:S(2)}) collective-permute-start(bf16[176,256]{1,0:T(8,128)(2,1)S(1)} %shard_map.96.refs_0_.refs_9_.refs_16_.refs_23_), channel_id=1, source_target_pairs={{2,0},{3,1},{0,2},{1,3},{6,4},{7,5},{4,6},{5,7},{10,8},{11,9},{8,1... | collective-permute-start | bytes 270344 | tf_op jit(solution)/shard_map/ppermute | solution.py:218
  21.3 2.5 %collective-permute-start.4 = (bf16[176,256]{1,0:T(8,128)(2,1)S(1)}, bf16[176,256]{1,0:T(8,128)(2,1)S(1)}, u32[]{:S(2)}, u32[]{:S(2)}) collective-permute-start(bf16[176,256]{1,0:T(8,128)(2,1)S(1)} %shard_map.96.refs_0_.refs_9_.refs_16_.refs_23_), channel_id=1, source_target_pairs={{1,0},{2,1},{3,2},{0,3},{5,4},{6,5},{7,6},{4,7},{9,8},{10,9},{11,1... | collective-permute-start | bytes 270344 | tf_op jit(solution)/shard_map/ppermute | solution.py:218
  26.0 3.5 %collective-permute-start.7 = (bf16[4,96,256]{2,1,0:T(8,128)(2,1)S(1)}, bf16[4,96,256]{2,1,0:T(8,128)(2,1)S(1)}, u32[]{:S(2)}, u32[]{:S(2)}) collective-permute-start(bf16[4,96,256]{2,1,0:T(8,128)(2,1)S(1)} %get-tuple-element.48.refs_0_.refs_13_), channel_id=1, source_target_pairs={{1,0},{2,1},{3,2},{0,3},{5,4},{6,5},{7,6},{4,7},{9,8},{10,9},{11,1... | collective-permute-start | bytes 589832 | tf_op jit(solution)/shard_map/ppermute | solution.py:218
  29.6 3.3 %collective-permute-start.9 = (bf16[4,96,256]{2,1,0:T(8,128)(2,1)S(1)}, bf16[4,96,256]{2,1,0:T(8,128)(2,1)S(1)}, u32[]{:S(2)}, u32[]{:S(2)}) collective-permute-start(bf16[4,96,256]{2,1,0:T(8,128)(2,1)S(1)} %get-tuple-element.49.refs_1_.refs_14_), channel_id=1, source_target_pairs={{1,0},{2,1},{3,2},{0,3},{5,4},{6,5},{7,6},{4,7},{9,8},{10,9},{11,1... | collective-permute-start | bytes 589832 | tf_op jit(solution)/shard_map/ppermute | solution.py:218
  32.9 1.9 %collective-permute-done.7.refs_2_.refs_15_ = bf16[4,96,256]{2,1,0:T(8,128)(2,1)S(1)} collective-permute-done((bf16[4,96,256]{2,1,0:T(8,128)(2,1)S(1)}, bf16[4,96,256]{2,1,0:T(8,128)(2,1)S(1)}, u32[]{:S(2)}, u32[]{:S(2)}) %collective-permute-start.7) | collective-permute-done | bytes 196640 | tf_op jit(solution)/shard_map/ppermute | solution.py:218
  34.8 3.5 %collective-permute-done.8.refs_5_.refs_18_ = bf16[4,96,256]{2,1,0:T(8,128)(2,1)S(1)} collective-permute-done((bf16[4,96,256]{2,1,0:T(8,128)(2,1)S(1)}, bf16[4,96,256]{2,1,0:T(8,128)(2,1)S(1)}, u32[]{:S(2)}, u32[]{:S(2)}) %collective-permute-start.8) | collective-permute-done | bytes 196640 | tf_op jit(solution)/shard_map/ppermute | solution.py:218
  38.5 1.8 %collective-permute-start.12 = (bf16[4,96,256]{2,1,0:T(8,128)(2,1)S(1)}, bf16[4,96,256]{2,1,0:T(8,128)(2,1)S(1)}, u32[]{:S(2)}, u32[]{:S(2)}) collective-permute-start(bf16[4,96,256]{2,1,0:T(8,128)(2,1)S(1)} %collective-permute-done.8.refs_5_.refs_18_), channel_id=1, source_target_pairs={{3,0},{0,1},{1,2},{2,3},{7,4},{4,5},{5,6},{6,7},{11,8},{8,9},{9,10... | collective-permute-start | bytes 589832 | tf_op jit(solution)/shard_map/ppermute | solution.py:218
  40.3 2.8 %collective-permute-start.15 = (bf16[2,160,256]{2,1,0:T(8,128)(2,1)S(1)}, bf16[2,160,256]{2,1,0:T(8,128)(2,1)S(1)}, u32[]{:S(2)}, u32[]{:S(2)}) collective-permute-start(bf16[2,160,256]{2,1,0:T(8,128)(2,1)S(1)} %get-tuple-element.63.refs_0_), channel_id=1, source_target_pairs={{4,0},{8,4},{12,8},{0,12},{5,1},{9,5},{13,9},{1,13},{6,2},{10,6},{... | collective-permute-start | bytes 491528 | tf_op jit(solution)/shard_map/ppermute | solution.py:218
  43.5 1.5 %collective-permute-start.17 = (bf16[2,160,256]{2,1,0:T(8,128)(2,1)S(1)}, bf16[2,160,256]{2,1,0:T(8,128)(2,1)S(1)}, u32[]{:S(2)}, u32[]{:S(2)}) collective-permute-start(bf16[2,160,256]{2,1,0:T(8,128)(2,1)S(1)} %get-tuple-element.63.refs_0_), channel_id=1, source_target_pairs={{12,0},{0,4},{4,8},{8,12},{13,1},{1,5},{5,9},{9,13},{14,2},{2,6},{... | collective-permute-start | bytes 491528 | tf_op jit(solution)/shard_map/ppermute | solution.py:218
  45.0 2.7 %collective-permute-done.15.refs_2_ = bf16[2,160,256]{2,1,0:T(8,128)(2,1)S(1)} collective-permute-done((bf16[2,160,256]{2,1,0:T(8,128)(2,1)S(1)}, bf16[2,160,256]{2,1,0:T(8,128)(2,1)S(1)}, u32[]{:S(2)}, u32[]{:S(2)}) %collective-permute-start.15) | collective-permute-done | bytes 163872 | tf_op jit(solution)/shard_map/ppermute | solution.py:218
  47.6 3.7 %collective-permute-start.16 = (bf16[2,160,256]{2,1,0:T(8,128)(2,1)S(1)}, bf16[2,160,256]{2,1,0:T(8,128)(2,1)S(1)}, u32[]{:S(2)}, u32[]{:S(2)}) collective-permute-start(bf16[2,160,256]{2,1,0:T(8,128)(2,1)S(1)} %get-tuple-element.64.refs_1_), channel_id=1, source_target_pairs={{4,0},{8,4},{12,8},{0,12},{5,1},{9,5},{13,9},{1,13},{6,2},{10,6},{... | collective-permute-start | bytes 491528 | tf_op jit(solution)/shard_map/ppermute | solution.py:218
  52.0 2.1 %collective-permute-start.20 = (bf16[2,160,256]{2,1,0:T(8,128)(2,1)S(1)}, bf16[2,160,256]{2,1,0:T(8,128)(2,1)S(1)}, u32[]{:S(2)}, u32[]{:S(2)}) collective-permute-start(bf16[2,160,256]{2,1,0:T(8,128)(2,1)S(1)} %collective-permute-done.18.refs_5_), channel_id=1, source_target_pairs={{12,0},{0,4},{4,8},{8,12},{13,1},{1,5},{5,9},{9,13},{14,2},{2,6},{... | collective-permute-start | bytes 491528 | tf_op jit(solution)/shard_map/ppermute | solution.py:218
  54.1 3.1 %collective-permute-start.25 = (bf16[256,768]{1,0:T(8,128)(2,1)S(1)}, bf16[256,768]{1,0:T(8,128)(2,1)S(1)}, u32[]{:S(2)}, u32[]{:S(2)}) collective-permute-start(bf16[256,768]{1,0:T(8,128)(2,1)S(1)} %shard_map.94.refs_9_.refs_8_), channel_id=1, source_target_pairs={{1,0},{2,1},{3,2},{0,3},{5,4},{6,5},{7,6},{4,7},{9,8},{10,9},{11,1... | collective-permute-start | bytes 1179656 | tf_op jit(solution)/shard_map/ppermute | solution.py:218
  61.2 4.9 %collective-permute-done.13.refs_2_ = bf16[2,256,256]{2,1,0:T(8,128)(2,1)S(1)} collective-permute-done((bf16[2,256,256]{2,1,0:T(8,128)(2,1)S(1)}, bf16[2,256,256]{2,1,0:T(8,128)(2,1)S(1)}, u32[]{:S(2)}, u32[]{:S(2)}) %collective-permute-start.13) | collective-permute-done | bytes 262176 | tf_op jit(solution)/shard_map/ppermute | solution.py:218
  66.1 2.8 %collective-permute-start.21 = (bf16[2,256,256]{2,1,0:T(8,128)(2,1)S(1)}, bf16[2,256,256]{2,1,0:T(8,128)(2,1)S(1)}, u32[]{:S(2)}, u32[]{:S(2)}) collective-permute-start(bf16[2,256,256]{2,1,0:T(8,128)(2,1)S(1)} %get-tuple-element.62.refs_1_), channel_id=1, source_target_pairs={{4,0},{8,4},{12,8},{0,12},{5,1},{9,5},{13,9},{1,13},{6,2},{10,6},{... | collective-permute-start | bytes 786440 | tf_op jit(solution)/shard_map/ppermute | solution.py:218
  69.0 2.0 %collective-permute-start.24 = (bf16[2,256,256]{2,1,0:T(8,128)(2,1)S(1)}, bf16[2,256,256]{2,1,0:T(8,128)(2,1)S(1)}, u32[]{:S(2)}, u32[]{:S(2)}) collective-permute-start(bf16[2,256,256]{2,1,0:T(8,128)(2,1)S(1)} %collective-permute-done.14.refs_5_), channel_id=1, source_target_pairs={{12,0},{0,4},{4,8},{8,12},{13,1},{1,5},{5,9},{9,13},{14,2},{2,6},{... | collective-permute-start | bytes 786440 | tf_op jit(solution)/shard_map/ppermute | solution.py:218
  71.4 3.2 %collective-permute-start.27 = (bf16[128,768]{1,0:T(8,128)(2,1)S(1)}, bf16[128,768]{1,0:T(8,128)(2,1)S(1)}, u32[]{:S(2)}, u32[]{:S(2)}) collective-permute-start(bf16[128,768]{1,0:T(8,128)(2,1)S(1)} %slice.18), channel_id=1, source_target_pairs={{1,0},{2,1},{3,2},{0,3},{5,4},{6,5},{7,6},{4,7},{9,8},{10,9},{11,1... | collective-permute-start | bytes 589832 | tf_op jit(solution)/shard_map/ppermute | solution.py:218
  74.6 2.6 %collective-permute-done.23.refs_6_ = bf16[2,256,256]{2,1,0:T(8,128)(2,1)S(1)} collective-permute-done((bf16[2,256,256]{2,1,0:T(8,128)(2,1)S(1)}, bf16[2,256,256]{2,1,0:T(8,128)(2,1)S(1)}, u32[]{:S(2)}, u32[]{:S(2)}) %collective-permute-start.23) | collective-permute-done | bytes 262176 | tf_op jit(solution)/shard_map/ppermute | solution.py:218
  78.0 4.6 %shard_map.100 = (bf16[256,256]{1,0:T(8,128)(2,1)S(1)}, bf16[256,256]{1,0:T(8,128)(2,1)S(1)}, bf16[256,256]{1,0:T(8,128)(2,1)S(1)}, bf16[256,256]{1,0:T(8,128)(2...) custom-call(bf16[2,256,256]{2,1,0:T(8,128)(2,1)S(1)} %get-tuple-element.61.refs_, ...), custom_call_target="tpu_custom_call" | custom-call | flops 700000000 | bytes 8000000 | tf_op jit(solution)/shard_map/pallas_call | solution.py:292
  82.6 3.0 %collective-permute-start.29 = (bf16[2,256,256]{2,1,0:T(8,128)(2,1)S(1)}, bf16[2,256,256]{2,1,0:T(8,128)(2,1)S(1)}, u32[]{:S(2)}, u32[]{:S(2)}) collective-permute-start(bf16[2,256,256]{2,1,0:T(8,128)(2,1)S(1)} %get-tuple-element.70.refs_0_), channel_id=1, source_target_pairs={{4,0},{8,4},{12,8},{0,12},{5,1},{9,5},{13,9},{1,13},{6,2},{10,6},{... | collective-permute-start | bytes 786440 | tf_op jit(solution)/shard_map/ppermute | solution.py:218
  85.6 3.3 %collective-permute-start.31 = (bf16[2,256,256]{2,1,0:T(8,128)(2,1)S(1)}, bf16[2,256,256]{2,1,0:T(8,128)(2,1)S(1)}, u32[]{:S(2)}, u32[]{:S(2)}) collective-permute-start(bf16[2,256,256]{2,1,0:T(8,128)(2,1)S(1)} %get-tuple-element.71.refs_1_), channel_id=1, source_target_pairs={{4,0},{8,4},{12,8},{0,12},{5,1},{9,5},{13,9},{1,13},{6,2},{10,6},{... | collective-permute-start | bytes 786440 | tf_op jit(solution)/shard_map/ppermute | solution.py:218
  89.5 3.7 %collective-permute-done.30.refs_5_ = bf16[2,256,256]{2,1,0:T(8,128)(2,1)S(1)} collective-permute-done((bf16[2,256,256]{2,1,0:T(8,128)(2,1)S(1)}, bf16[2,256,256]{2,1,0:T(8,128)(2,1)S(1)}, u32[]{:S(2)}, u32[]{:S(2)}) %collective-permute-start.30) | collective-permute-done | bytes 262176 | tf_op jit(solution)/shard_map/ppermute | solution.py:218
  93.2 2.0 %collective-permute-start.34 = (bf16[2,256,256]{2,1,0:T(8,128)(2,1)S(1)}, bf16[2,256,256]{2,1,0:T(8,128)(2,1)S(1)}, u32[]{:S(2)}, u32[]{:S(2)}) collective-permute-start(bf16[2,256,256]{2,1,0:T(8,128)(2,1)S(1)} %collective-permute-done.30.refs_5_), channel_id=1, source_target_pairs={{12,0},{0,4},{4,8},{8,12},{13,1},{1,5},{5,9},{9,13},{14,2},{2,6},{... | collective-permute-start | bytes 786440 | tf_op jit(solution)/shard_map/ppermute | solution.py:218
  96.0 2.5 %collective-permute-start.36 = (bf16[256,256]{1,0:T(8,128)(2,1)S(1)}, bf16[256,256]{1,0:T(8,128)(2,1)S(1)}, u32[]{:S(2)}, u32[]{:S(2)}) collective-permute-start(bf16[256,256]{1,0:T(8,128)(2,1)S(1)} %get-tuple-element.80), channel_id=1, source_target_pairs={{1,0},{2,1},{3,2},{0,3},{5,4},{6,5},{7,6},{4,7},{9,8},{10,9},{11,1... | collective-permute-start | bytes 393224 | tf_op jit(solution)/shard_map/ppermute | solution.py:218
  100.8 3.8 %shard_map.101 = bf16[8,4,128,128]{3,2,1,0:T(8,128)(2,1)S(1)} custom-call(bf16[2,256,256]{2,1,0:T(8,128)(2,1)S(1)} %get-tuple-element.70.refs_0_, bf16[2,256,256]{2,1,0:T(8,128)(2,1)S(1)} %get-tuple-element.71.refs_1_, bf16[2,256,256]{2,1,0:T(8,128)(2,1)S(1)} %collective-permute-done.29.refs_2_, bf16[2,256,256]{2,1,0:T(8,128)(2,1)S(1)} %collective-permute-done.31.refs_3_, ...), custom_call_target="tpu_custom_call" | custom-call | flops 900000000 | bytes 8000000 | tf_op jit(solution)/shard_map/pallas_call | solution.py:304
  105.0 20.0 %all_to_all.15.part_ref = bf16[32,128,128]{2,1,0:T(8,128)(2,1)S(1)} all-to-all(bf16[32,128,128]{2,1,0:T(8,128)(2,1)S(1)} %bitcast.23), channel_id=1, replica_groups=mesh['y'=4,'c'=2,'x'=4,'z'=4] {'y','c','x'}, dimensions={0} | all-to-all | bytes 2097152 | tf_op jit(solution)/shard_map/all_to_all | solution.py:313
  126.0 3.9 %all-to-all-start.2 = ((bf16[16,128,128]{2,1,0:T(8,128)(2,1)}), bf16[16,128,128]{2,1,0:T(8,128)(2,1)S(1)}, u32[]{:S(2)}, u32[]{:S(2)}) async-start(bf16[16,128,128]{2,1,0:T(8,128)(2,1)} %shard_map.103), calls=%async_computation.2 | async-start | bytes 1048576 | tf_op jit(solution)/shard_map/all_to_all | solution.py:316
  129.9 1.5 %shard_map.102 = bf16[256,1024]{1,0:T(8,128)(2,1)} custom-call(bf16[256,256]{1,0:T(8,128)(2,1)S(1)} %get-tuple-element.82.h0_ref, bf16[256,256]{1,0:T(8,128)(2,1)S(1)} %collective-permute-done.35.h1_ref, bf16[256,256]{1,0:T(8,128)(2,1)S(1)} %collective-permute-done.36.h2_ref, bf16[256,256]{1,0:T(8,128)(2,1)S(1)} %collective-permute-done.37.h3_ref, ...), custom_call_target="tpu_custom_call" | custom-call | bytes 1000000 | tf_op jit(solution)/shard_map/pallas_call | solution.py:317
  131.4 10.1 %all-to-all-done.2.in_ref = bf16[16,128,128]{2,1,0:T(8,128)(2,1)S(1)} async-done(((bf16[16,128,128]{2,1,0:T(8,128)(2,1)}), bf16[16,128,128]{2,1,0:T(8,128)(2,1)S(1)}, u32[]{:S(2)}, u32[]{:S(2)}) %all-to-all-start.2) | async-done | bytes 524320 | tf_op jit(solution)/shard_map/all_to_all | solution.py:316
  (85 shorter events, 20.4 us)
Async XLA Ops:
  1.5 7.6 %collective-permute-start = (bf16[96,256]{1,0:T(8,128)(2,1)S(1)}, bf16[96,256]{1,0:T(8,128)(2,1)S(1)}, u32[]{:S(2)}, u32[]{:S(2)}) collective-permute-start(bf16[96,256]{1,0:T(8,128)(2,1)S(1)} %constant_dynamic-slice_fusion), channel_id=1, source_target_pairs={{0,16},{16,0},{1,17},{17,1},{2,18},{18,2},{3,19},{19,3},{4,20},{20... | collective-permute-start | bytes 147464 | tf_op jit(solution)/shard_map/ppermute | solution.py:247
  3.4 21.2 %all-to-all-start = ((bf16[8,96,256]{2,1,0:T(8,128)(2,1)}), bf16[8,96,256]{2,1,0:T(8,128)(2,1)S(1)}, u32[]{:S(2)}, u32[]{:S(2)}) async-start(bf16[8,96,256]{2,1,0:T(8,128)(2,1)} %bitcast.22), calls=%async_computation | async-start | bytes 786432 | tf_op jit(solution)/shard_map/all_to_all | solution.py:243
  9.2 12.2 %collective-permute-start.3 = (bf16[2,96,256]{2,1,0:T(8,128)(2,1)S(1)}, bf16[2,96,256]{2,1,0:T(8,128)(2,1)S(1)}, u32[]{:S(2)}, u32[]{:S(2)}) collective-permute-start(bf16[2,96,256]{2,1,0:T(8,128)(2,1)S(1)} %pad_maximum_fusion.refs_0_), channel_id=1, source_target_pairs={{64,0},{96,32},{0,64},{32,96},{65,1},{97,33},{1,65},{33,97},{66,2}... | collective-permute-start | bytes 294920 | tf_op jit(solution)/shard_map/ppermute | solution.py:218
  12.8 11.1 %collective-permute-start.2 = (bf16[2,96,256]{2,1,0:T(8,128)(2,1)S(1)}, bf16[2,96,256]{2,1,0:T(8,128)(2,1)S(1)}, u32[]{:S(2)}, u32[]{:S(2)}) collective-permute-start(bf16[2,96,256]{2,1,0:T(8,128)(2,1)S(1)} %pad_maximum_fusion.refs_0_), channel_id=1, source_target_pairs={{96,0},{0,32},{32,64},{64,96},{97,1},{1,33},{33,65},{65,97},{98,2}... | collective-permute-start | bytes 294920 | tf_op jit(solution)/shard_map/ppermute | solution.py:218
  13.3 10.5 %collective-permute-start.1 = (bf16[2,96,256]{2,1,0:T(8,128)(2,1)S(1)}, bf16[2,96,256]{2,1,0:T(8,128)(2,1)S(1)}, u32[]{:S(2)}, u32[]{:S(2)}) collective-permute-start(bf16[2,96,256]{2,1,0:T(8,128)(2,1)S(1)} %pad_maximum_fusion.refs_0_), channel_id=1, source_target_pairs={{32,0},{64,32},{96,64},{0,96},{33,1},{65,33},{97,65},{1,97},{34,2}... | collective-permute-start | bytes 294920 | tf_op jit(solution)/shard_map/ppermute | solution.py:218
  16.3 8.3 %collective-permute-start.6 = (bf16[176,256]{1,0:T(8,128)(2,1)S(1)}, bf16[176,256]{1,0:T(8,128)(2,1)S(1)}, u32[]{:S(2)}, u32[]{:S(2)}) collective-permute-start(bf16[176,256]{1,0:T(8,128)(2,1)S(1)} %shard_map.96.refs_0_.refs_9_.refs_16_.refs_23_), channel_id=1, source_target_pairs={{2,0},{3,1},{0,2},{1,3},{6,4},{7,5},{4,6},{5,7},{10,8},{11,9},{8,1... | collective-permute-start | bytes 270344 | tf_op jit(solution)/shard_map/ppermute | solution.py:218
  26.0 8.7 %collective-permute-start.7 = (bf16[4,96,256]{2,1,0:T(8,128)(2,1)S(1)}, bf16[4,96,256]{2,1,0:T(8,128)(2,1)S(1)}, u32[]{:S(2)}, u32[]{:S(2)}) collective-permute-start(bf16[4,96,256]{2,1,0:T(8,128)(2,1)S(1)} %get-tuple-element.48.refs_0_.refs_13_), channel_id=1, source_target_pairs={{1,0},{2,1},{3,2},{0,3},{5,4},{6,5},{7,6},{4,7},{9,8},{10,9},{11,1... | collective-permute-start | bytes 589832 | tf_op jit(solution)/shard_map/ppermute | solution.py:218
  29.6 8.7 %collective-permute-start.8 = (bf16[4,96,256]{2,1,0:T(8,128)(2,1)S(1)}, bf16[4,96,256]{2,1,0:T(8,128)(2,1)S(1)}, u32[]{:S(2)}, u32[]{:S(2)}) collective-permute-start(bf16[4,96,256]{2,1,0:T(8,128)(2,1)S(1)} %get-tuple-element.49.refs_1_.refs_14_), channel_id=1, source_target_pairs={{3,0},{0,1},{1,2},{2,3},{7,4},{4,5},{5,6},{6,7},{11,8},{8,9},{9,10... | collective-permute-start | bytes 589832 | tf_op jit(solution)/shard_map/ppermute | solution.py:218
  29.6 13.5 %collective-permute-start.10 = (bf16[4,96,256]{2,1,0:T(8,128)(2,1)S(1)}, bf16[4,96,256]{2,1,0:T(8,128)(2,1)S(1)}, u32[]{:S(2)}, u32[]{:S(2)}) collective-permute-start(bf16[4,96,256]{2,1,0:T(8,128)(2,1)S(1)} %get-tuple-element.48.refs_0_.refs_13_), channel_id=1, source_target_pairs={{3,0},{0,1},{1,2},{2,3},{7,4},{4,5},{5,6},{6,7},{11,8},{8,9},{9,10... | collective-permute-start | bytes 589832 | tf_op jit(solution)/shard_map/ppermute | solution.py:218
  29.6 13.9 %collective-permute-start.9 = (bf16[4,96,256]{2,1,0:T(8,128)(2,1)S(1)}, bf16[4,96,256]{2,1,0:T(8,128)(2,1)S(1)}, u32[]{:S(2)}, u32[]{:S(2)}) collective-permute-start(bf16[4,96,256]{2,1,0:T(8,128)(2,1)S(1)} %get-tuple-element.49.refs_1_.refs_14_), channel_id=1, source_target_pairs={{1,0},{2,1},{3,2},{0,3},{5,4},{6,5},{7,6},{4,7},{9,8},{10,9},{11,1... | collective-permute-start | bytes 589832 | tf_op jit(solution)/shard_map/ppermute | solution.py:218
  38.3 13.0 %collective-permute-start.11 = (bf16[4,96,256]{2,1,0:T(8,128)(2,1)S(1)}, bf16[4,96,256]{2,1,0:T(8,128)(2,1)S(1)}, u32[]{:S(2)}, u32[]{:S(2)}) collective-permute-start(bf16[4,96,256]{2,1,0:T(8,128)(2,1)S(1)} %collective-permute-done.7.refs_2_.refs_15_), channel_id=1, source_target_pairs={{1,0},{2,1},{3,2},{0,3},{5,4},{6,5},{7,6},{4,7},{9,8},{10,9},{11,1... | collective-permute-start | bytes 589832 | tf_op jit(solution)/shard_map/ppermute | solution.py:218
  38.5 12.9 %collective-permute-start.12 = (bf16[4,96,256]{2,1,0:T(8,128)(2,1)S(1)}, bf16[4,96,256]{2,1,0:T(8,128)(2,1)S(1)}, u32[]{:S(2)}, u32[]{:S(2)}) collective-permute-start(bf16[4,96,256]{2,1,0:T(8,128)(2,1)S(1)} %collective-permute-done.8.refs_5_.refs_18_), channel_id=1, source_target_pairs={{3,0},{0,1},{1,2},{2,3},{7,4},{4,5},{5,6},{6,7},{11,8},{8,9},{9,10... | collective-permute-start | bytes 589832 | tf_op jit(solution)/shard_map/ppermute | solution.py:218
  40.3 7.3 %collective-permute-start.15 = (bf16[2,160,256]{2,1,0:T(8,128)(2,1)S(1)}, bf16[2,160,256]{2,1,0:T(8,128)(2,1)S(1)}, u32[]{:S(2)}, u32[]{:S(2)}) collective-permute-start(bf16[2,160,256]{2,1,0:T(8,128)(2,1)S(1)} %get-tuple-element.63.refs_0_), channel_id=1, source_target_pairs={{4,0},{8,4},{12,8},{0,12},{5,1},{9,5},{13,9},{1,13},{6,2},{10,6},{... | collective-permute-start | bytes 491528 | tf_op jit(solution)/shard_map/ppermute | solution.py:218
  43.1 9.0 %collective-permute-start.18 = (bf16[2,160,256]{2,1,0:T(8,128)(2,1)S(1)}, bf16[2,160,256]{2,1,0:T(8,128)(2,1)S(1)}, u32[]{:S(2)}, u32[]{:S(2)}) collective-permute-start(bf16[2,160,256]{2,1,0:T(8,128)(2,1)S(1)} %get-tuple-element.64.refs_1_), channel_id=1, source_target_pairs={{12,0},{0,4},{4,8},{8,12},{13,1},{1,5},{5,9},{9,13},{14,2},{2,6},{... | collective-permute-start | bytes 491528 | tf_op jit(solution)/shard_map/ppermute | solution.py:218
  43.5 10.6 %collective-permute-start.17 = (bf16[2,160,256]{2,1,0:T(8,128)(2,1)S(1)}, bf16[2,160,256]{2,1,0:T(8,128)(2,1)S(1)}, u32[]{:S(2)}, u32[]{:S(2)}) collective-permute-start(bf16[2,160,256]{2,1,0:T(8,128)(2,1)S(1)} %get-tuple-element.63.refs_0_), channel_id=1, source_target_pairs={{12,0},{0,4},{4,8},{8,12},{13,1},{1,5},{5,9},{9,13},{14,2},{2,6},{... | collective-permute-start | bytes 491528 | tf_op jit(solution)/shard_map/ppermute | solution.py:218
  47.6 9.6 %collective-permute-start.16 = (bf16[2,160,256]{2,1,0:T(8,128)(2,1)S(1)}, bf16[2,160,256]{2,1,0:T(8,128)(2,1)S(1)}, u32[]{:S(2)}, u32[]{:S(2)}) collective-permute-start(bf16[2,160,256]{2,1,0:T(8,128)(2,1)S(1)} %get-tuple-element.64.refs_1_), channel_id=1, source_target_pairs={{4,0},{8,4},{12,8},{0,12},{5,1},{9,5},{13,9},{1,13},{6,2},{10,6},{... | collective-permute-start | bytes 491528 | tf_op jit(solution)/shard_map/ppermute | solution.py:218
  51.9 17.0 %collective-permute-start.26 = (bf16[256,768]{1,0:T(8,128)(2,1)S(1)}, bf16[256,768]{1,0:T(8,128)(2,1)S(1)}, u32[]{:S(2)}, u32[]{:S(2)}) collective-permute-start(bf16[256,768]{1,0:T(8,128)(2,1)S(1)} %shard_map.94.refs_9_.refs_8_), channel_id=1, source_target_pairs={{3,0},{0,1},{1,2},{2,3},{7,4},{4,5},{5,6},{6,7},{11,8},{8,9},{9,10... | collective-permute-start | bytes 1179656 | tf_op jit(solution)/shard_map/ppermute | solution.py:218
  52.0 8.4 %collective-permute-start.20 = (bf16[2,160,256]{2,1,0:T(8,128)(2,1)S(1)}, bf16[2,160,256]{2,1,0:T(8,128)(2,1)S(1)}, u32[]{:S(2)}, u32[]{:S(2)}) collective-permute-start(bf16[2,160,256]{2,1,0:T(8,128)(2,1)S(1)} %collective-permute-done.18.refs_5_), channel_id=1, source_target_pairs={{12,0},{0,4},{4,8},{8,12},{13,1},{1,5},{5,9},{9,13},{14,2},{2,6},{... | collective-permute-start | bytes 491528 | tf_op jit(solution)/shard_map/ppermute | solution.py:218
  54.1 16.9 %collective-permute-start.25 = (bf16[256,768]{1,0:T(8,128)(2,1)S(1)}, bf16[256,768]{1,0:T(8,128)(2,1)S(1)}, u32[]{:S(2)}, u32[]{:S(2)}) collective-permute-start(bf16[256,768]{1,0:T(8,128)(2,1)S(1)} %shard_map.94.refs_9_.refs_8_), channel_id=1, source_target_pairs={{1,0},{2,1},{3,2},{0,3},{5,4},{6,5},{7,6},{4,7},{9,8},{10,9},{11,1... | collective-permute-start | bytes 1179656 | tf_op jit(solution)/shard_map/ppermute | solution.py:218
  57.2 8.9 %collective-permute-start.13 = (bf16[2,256,256]{2,1,0:T(8,128)(2,1)S(1)}, bf16[2,256,256]{2,1,0:T(8,128)(2,1)S(1)}, u32[]{:S(2)}, u32[]{:S(2)}) collective-permute-start(bf16[2,256,256]{2,1,0:T(8,128)(2,1)S(1)} %get-tuple-element.61.refs_0_), channel_id=1, source_target_pairs={{4,0},{8,4},{12,8},{0,12},{5,1},{9,5},{13,9},{1,13},{6,2},{10,6},{... | collective-permute-start | bytes 786440 | tf_op jit(solution)/shard_map/ppermute | solution.py:218
  58.5 10.5 %collective-permute-start.14 = (bf16[2,256,256]{2,1,0:T(8,128)(2,1)S(1)}, bf16[2,256,256]{2,1,0:T(8,128)(2,1)S(1)}, u32[]{:S(2)}, u32[]{:S(2)}) collective-permute-start(bf16[2,256,256]{2,1,0:T(8,128)(2,1)S(1)} %get-tuple-element.62.refs_1_), channel_id=1, source_target_pairs={{12,0},{0,4},{4,8},{8,12},{13,1},{1,5},{5,9},{9,13},{14,2},{2,6},{... | collective-permute-start | bytes 786440 | tf_op jit(solution)/shard_map/ppermute | solution.py:218
  60.4 10.9 %collective-permute-start.22 = (bf16[2,256,256]{2,1,0:T(8,128)(2,1)S(1)}, bf16[2,256,256]{2,1,0:T(8,128)(2,1)S(1)}, u32[]{:S(2)}, u32[]{:S(2)}) collective-permute-start(bf16[2,256,256]{2,1,0:T(8,128)(2,1)S(1)} %get-tuple-element.61.refs_0_), channel_id=1, source_target_pairs={{12,0},{0,4},{4,8},{8,12},{13,1},{1,5},{5,9},{9,13},{14,2},{2,6},{... | collective-permute-start | bytes 786440 | tf_op jit(solution)/shard_map/ppermute | solution.py:218
  66.1 8.5 %collective-permute-start.21 = (bf16[2,256,256]{2,1,0:T(8,128)(2,1)S(1)}, bf16[2,256,256]{2,1,0:T(8,128)(2,1)S(1)}, u32[]{:S(2)}, u32[]{:S(2)}) collective-permute-start(bf16[2,256,256]{2,1,0:T(8,128)(2,1)S(1)} %get-tuple-element.62.refs_1_), channel_id=1, source_target_pairs={{4,0},{8,4},{12,8},{0,12},{5,1},{9,5},{13,9},{1,13},{6,2},{10,6},{... | collective-permute-start | bytes 786440 | tf_op jit(solution)/shard_map/ppermute | solution.py:218
  68.9 8.2 %collective-permute-start.23 = (bf16[2,256,256]{2,1,0:T(8,128)(2,1)S(1)}, bf16[2,256,256]{2,1,0:T(8,128)(2,1)S(1)}, u32[]{:S(2)}, u32[]{:S(2)}) collective-permute-start(bf16[2,256,256]{2,1,0:T(8,128)(2,1)S(1)} %collective-permute-done.13.refs_2_), channel_id=1, source_target_pairs={{4,0},{8,4},{12,8},{0,12},{5,1},{9,5},{13,9},{1,13},{6,2},{10,6},{... | collective-permute-start | bytes 786440 | tf_op jit(solution)/shard_map/ppermute | solution.py:218
  69.0 8.2 %collective-permute-start.24 = (bf16[2,256,256]{2,1,0:T(8,128)(2,1)S(1)}, bf16[2,256,256]{2,1,0:T(8,128)(2,1)S(1)}, u32[]{:S(2)}, u32[]{:S(2)}) collective-permute-start(bf16[2,256,256]{2,1,0:T(8,128)(2,1)S(1)} %collective-permute-done.14.refs_5_), channel_id=1, source_target_pairs={{12,0},{0,4},{4,8},{8,12},{13,1},{1,5},{5,9},{9,13},{14,2},{2,6},{... | collective-permute-start | bytes 786440 | tf_op jit(solution)/shard_map/ppermute | solution.py:218
  85.6 7.6 %collective-permute-start.30 = (bf16[2,256,256]{2,1,0:T(8,128)(2,1)S(1)}, bf16[2,256,256]{2,1,0:T(8,128)(2,1)S(1)}, u32[]{:S(2)}, u32[]{:S(2)}) collective-permute-start(bf16[2,256,256]{2,1,0:T(8,128)(2,1)S(1)} %get-tuple-element.71.refs_1_), channel_id=1, source_target_pairs={{12,0},{0,4},{4,8},{8,12},{13,1},{1,5},{5,9},{9,13},{14,2},{2,6},{... | collective-permute-start | bytes 786440 | tf_op jit(solution)/shard_map/ppermute | solution.py:218
  85.6 10.4 %collective-permute-start.32 = (bf16[2,256,256]{2,1,0:T(8,128)(2,1)S(1)}, bf16[2,256,256]{2,1,0:T(8,128)(2,1)S(1)}, u32[]{:S(2)}, u32[]{:S(2)}) collective-permute-start(bf16[2,256,256]{2,1,0:T(8,128)(2,1)S(1)} %get-tuple-element.70.refs_0_), channel_id=1, source_target_pairs={{12,0},{0,4},{4,8},{8,12},{13,1},{1,5},{5,9},{9,13},{14,2},{2,6},{... | collective-permute-start | bytes 786440 | tf_op jit(solution)/shard_map/ppermute | solution.py:218
  85.6 12.8 %collective-permute-start.31 = (bf16[2,256,256]{2,1,0:T(8,128)(2,1)S(1)}, bf16[2,256,256]{2,1,0:T(8,128)(2,1)S(1)}, u32[]{:S(2)}, u32[]{:S(2)}) collective-permute-start(bf16[2,256,256]{2,1,0:T(8,128)(2,1)S(1)} %get-tuple-element.71.refs_1_), channel_id=1, source_target_pairs={{4,0},{8,4},{12,8},{0,12},{5,1},{9,5},{13,9},{1,13},{6,2},{10,6},{... | collective-permute-start | bytes 786440 | tf_op jit(solution)/shard_map/ppermute | solution.py:218
  93.2 7.6 %collective-permute-start.34 = (bf16[2,256,256]{2,1,0:T(8,128)(2,1)S(1)}, bf16[2,256,256]{2,1,0:T(8,128)(2,1)S(1)}, u32[]{:S(2)}, u32[]{:S(2)}) collective-permute-start(bf16[2,256,256]{2,1,0:T(8,128)(2,1)S(1)} %collective-permute-done.30.refs_5_), channel_id=1, source_target_pairs={{12,0},{0,4},{4,8},{8,12},{13,1},{1,5},{5,9},{9,13},{14,2},{2,6},{... | collective-permute-start | bytes 786440 | tf_op jit(solution)/shard_map/ppermute | solution.py:218
  95.2 9.4 %collective-permute-start.35 = (bf16[256,256]{1,0:T(8,128)(2,1)S(1)}, bf16[256,256]{1,0:T(8,128)(2,1)S(1)}, u32[]{:S(2)}, u32[]{:S(2)}) collective-permute-start(bf16[256,256]{1,0:T(8,128)(2,1)S(1)} %get-tuple-element.79), channel_id=1, source_target_pairs={{3,0},{0,1},{1,2},{2,3},{7,4},{4,5},{5,6},{6,7},{11,8},{8,9},{9,10... | collective-permute-start | bytes 393224 | tf_op jit(solution)/shard_map/ppermute | solution.py:218
  96.0 8.6 %collective-permute-start.36 = (bf16[256,256]{1,0:T(8,128)(2,1)S(1)}, bf16[256,256]{1,0:T(8,128)(2,1)S(1)}, u32[]{:S(2)}, u32[]{:S(2)}) collective-permute-start(bf16[256,256]{1,0:T(8,128)(2,1)S(1)} %get-tuple-element.80), channel_id=1, source_target_pairs={{1,0},{2,1},{3,2},{0,3},{5,4},{6,5},{7,6},{4,7},{9,8},{10,9},{11,1... | collective-permute-start | bytes 393224 | tf_op jit(solution)/shard_map/ppermute | solution.py:218
  126.0 15.6 %all-to-all-start.2 = ((bf16[16,128,128]{2,1,0:T(8,128)(2,1)}), bf16[16,128,128]{2,1,0:T(8,128)(2,1)S(1)}, u32[]{:S(2)}, u32[]{:S(2)}) async-start(bf16[16,128,128]{2,1,0:T(8,128)(2,1)} %shard_map.103), calls=%async_computation.2 | async-start | bytes 1048576 | tf_op jit(solution)/shard_map/all_to_all | solution.py:316
  (13 other events, 113.2 us)

commit v11 on v10

--- a/solution.py
+++ b/solution.py
@@ -250,9 +250,6 @@
     nodes = call(node_kernel, shape((176, 256), BF), [VMEM] * 3, moved=200_000)(
         upstream[0].T, degree.reshape(2, 128), links
     )
-    nodes = ring(nodes, "z")
-    half = shape((2, 160, 256), BF)
-    scaled = call(pack_kernel, (half, half), [VMEM] * 4, moved=600_000)(*nodes)
     mask = call(mask_kernel, shape((256, 768), BF), [VMEM], moved=1_200_000)(neighbour_mask[0])
     own_second = lax.dynamic_slice(second_weight, (z * 256, 0), (256, 153))
     own_second = jnp.pad(own_second, ((0, 0), (0, 7)))
@@ -260,11 +257,13 @@
         weight_kernel, shape((256, 768), BF), [VMEM] * 4 + [SMEM], [pltpu.VMEM((8, 96, 256), BF)],
         moved=800_000,
     )(*ring(jnp.stack([weight, other]), "y"), at)
-    x_low, x_high, mask, own_second, weights, n1, n2, n3 = lax.optimization_barrier(
-        (x_own[:4], x_own[4:], mask, own_second, weights, *nodes[1:])
-    )
-    nodes = [nodes[0], n1, n2, n3]
+    x_low, x_high, mask, own_second, weights, nodes = lax.optimization_barrier(
+        (x_own[:4], x_own[4:], mask, own_second, weights, nodes)
+    )
     x_near = neighbours(x_low, x_high, "z")
+    nodes = ring(nodes, "z")
+    half = shape((2, 160, 256), BF)
+    scaled = call(pack_kernel, (half, half), [VMEM] * 4, moved=600_000)(*nodes)
     x0, x1, *scaled = lax.optimization_barrier((*x_near[:2], *scaled))
     x_wide = rounds(x_low, x_high, x_near, (x0, x1), "z")
     u_near = neighbours(*scaled, "x")

time: 143 us -> 147 us (1.028)
  waiting for transfers between devices: 36.9 us -> 45.9 us
  starting transfers between devices: 66.6 us -> 61.6 us
    ppermute x37, waiting for transfers between devices: 26.8 us -> 35.8 us  [fetch(): return lax.ppermute(value, axis, [((i + shift) % 4, i) for i in range(4)])]
    ppermute x37, starting transfers between devices: 57.9 us -> 52.1 us  [fetch(): return lax.ppermute(value, axis, [((i + shift) % 4, i) for i in range(4)])]
  transfers between devices with their start and end apart: 40 -> 40, of which waited for: 16 -> 21; matrix products, arithmetic and copies ran while one was open for 2% -> 2% of each run, Pallas kernels for 5% -> 5%
where the time goes in v11:
time: 147 us
  starting transfers between devices  61.6 us (42%)
  waiting for transfers between devices  45.9 us (31%)
  blocking collectives  20 us (14%)
  Pallas kernels  14.3 us (10%)
  local copies, waits for them, and re-layouts  3.94 us (3%)
    ppermute x37, starting transfers between devices, fetch(): return lax.ppermute(value, axis, [((i + shift) % 4, i) for i in range(4)])  52.1 us
    ppermute x37, waiting for transfers between devices, fetch(): return lax.ppermute(value, axis, [((i + shift) % 4, i) for i in range(4)])  35.8 us
    all_to_all x1, blocking collectives, body(): lax.all_to_all(part.reshape(32, 128, 128), ('y', 'c', 'x'), 0, 0, tiled=T...  20 us
    all_to_all x1, waiting for transfers between devices, body(): done = lax.all_to_all(done, dom, 0, 0, tiled=True)  10.1 us
    all_to_all x1, starting transfers between devices, body(): lax.all_to_all(features.reshape(96, 8, 256).transpose(1, 0, 2), feat, 0,...  4.8 us
    all_to_all x1, starting transfers between devices, body(): done = lax.all_to_all(done, dom, 0, 0, tiled=True)  4.69 us
    pallas_call x1, Pallas kernels, body(): call(first_mix_kernel, (shape((256, 256), BF),) * 4 + (half, half, shape(...  4.63 us
    pallas_call x1, Pallas kernels, body(): call(second_mix_kernel, shape((8, 4, 128, 128), BF), [VMEM] * 22 + [SMEM]...  3.82 us
  transfers between devices with their start and end apart: 40, of which 21 were waited for; matrix products, arithmetic and copies ran while one was open for 2% of the time, Pallas kernels for 5%

profile of v11, /device:TPU:0, one launch (start us, length us, event | category | flops | bytes accessed | tf_op | source)
XLA Modules:
  0.0 146.7 jit_solution(15036627805524989318)
XLA Ops:
  3.4 4.8 %all-to-all-start = ((bf16[8,96,256]{2,1,0:T(8,128)(2,1)}), bf16[8,96,256]{2,1,0:T(8,128)(2,1)S(1)}, u32[]{:S(2)}, u32[]{:S(2)}) async-start(bf16[8,96,256]{2,1,0:T(8,128)(2,1)} %bitcast.22), calls=%async_computation | async-start | bytes 786432 | tf_op jit(solution)/shard_map/all_to_all | solution.py:243
  9.2 3.6 %collective-permute-start.3 = (bf16[2,96,256]{2,1,0:T(8,128)(2,1)S(1)}, bf16[2,96,256]{2,1,0:T(8,128)(2,1)S(1)}, u32[]{:S(2)}, u32[]{:S(2)}) collective-permute-start(bf16[2,96,256]{2,1,0:T(8,128)(2,1)S(1)} %pad_maximum_fusion.refs_0_), channel_id=1, source_target_pairs={{64,0},{96,32},{0,64},{32,96},{65,1},{97,33},{1,65},{33,97},{66,2}... | collective-permute-start | bytes 294920 | tf_op jit(solution)/shard_map/ppermute | solution.py:218
  13.3 2.7 %collective-permute-start.1 = (bf16[2,96,256]{2,1,0:T(8,128)(2,1)S(1)}, bf16[2,96,256]{2,1,0:T(8,128)(2,1)S(1)}, u32[]{:S(2)}, u32[]{:S(2)}) collective-permute-start(bf16[2,96,256]{2,1,0:T(8,128)(2,1)S(1)} %pad_maximum_fusion.refs_0_), channel_id=1, source_target_pairs={{32,0},{64,32},{96,64},{0,96},{33,1},{65,33},{97,65},{1,97},{34,2}... | collective-permute-start | bytes 294920 | tf_op jit(solution)/shard_map/ppermute | solution.py:218
  16.3 3.4 %collective-permute-done.3.refs_3_ = bf16[2,96,256]{2,1,0:T(8,128)(2,1)S(1)} collective-permute-done((bf16[2,96,256]{2,1,0:T(8,128)(2,1)S(1)}, bf16[2,96,256]{2,1,0:T(8,128)(2,1)S(1)}, u32[]{:S(2)}, u32[]{:S(2)}) %collective-permute-start.3) | collective-permute-done | bytes 98336 | tf_op jit(solution)/shard_map/ppermute | solution.py:218
  19.8 1.6 %collective-permute-done.2.refs_2_ = bf16[2,96,256]{2,1,0:T(8,128)(2,1)S(1)} collective-permute-done((bf16[2,96,256]{2,1,0:T(8,128)(2,1)S(1)}, bf16[2,96,256]{2,1,0:T(8,128)(2,1)S(1)}, u32[]{:S(2)}, u32[]{:S(2)}) %collective-permute-start.2) | collective-permute-done | bytes 98336 | tf_op jit(solution)/shard_map/ppermute | solution.py:218
  22.2 4.1 %collective-permute-start.4 = (bf16[4,96,256]{2,1,0:T(8,128)(2,1)S(1)}, bf16[4,96,256]{2,1,0:T(8,128)(2,1)S(1)}, u32[]{:S(2)}, u32[]{:S(2)}) collective-permute-start(bf16[4,96,256]{2,1,0:T(8,128)(2,1)S(1)} %get-tuple-element.46.refs_0_.refs_13_), channel_id=1, source_target_pairs={{1,0},{2,1},{3,2},{0,3},{5,4},{6,5},{7,6},{4,7},{9,8},{10,9},{11,1... | collective-permute-start | bytes 589832 | tf_op jit(solution)/shard_map/ppermute | solution.py:218
  26.3 1.9 %collective-permute-start.8 = (bf16[176,256]{1,0:T(8,128)(2,1)S(1)}, bf16[176,256]{1,0:T(8,128)(2,1)S(1)}, u32[]{:S(2)}, u32[]{:S(2)}) collective-permute-start(bf16[176,256]{1,0:T(8,128)(2,1)S(1)} %shard_map.96.refs_0_.refs_9_.refs_16_.refs_23_), channel_id=1, source_target_pairs={{2,0},{3,1},{0,2},{1,3},{6,4},{7,5},{4,6},{5,7},{10,8},{11,9},{8,1... | collective-permute-start | bytes 270344 | tf_op jit(solution)/shard_map/ppermute | solution.py:218
  28.2 2.2 %collective-permute-start.7 = (bf16[176,256]{1,0:T(8,128)(2,1)S(1)}, bf16[176,256]{1,0:T(8,128)(2,1)S(1)}, u32[]{:S(2)}, u32[]{:S(2)}) collective-permute-start(bf16[176,256]{1,0:T(8,128)(2,1)S(1)} %shard_map.96.refs_0_.refs_9_.refs_16_.refs_23_), channel_id=1, source_target_pairs={{3,0},{0,1},{1,2},{2,3},{7,4},{4,5},{5,6},{6,7},{11,8},{8,9},{9,10... | collective-permute-start | bytes 270344 | tf_op jit(solution)/shard_map/ppermute | solution.py:218
  30.4 5.5 %collective-permute-done.8.refs_3_.refs_12_.refs_19_.refs_26_ = bf16[176,256]{1,0:T(8,128)(2,1)S(1)} collective-permute-done((bf16[176,256]{1,0:T(8,128)(2,1)S(1)}, bf16[176,256]{1,0:T(8,128)(2,1)S(1)}, u32[]{:S(2)}, u32[]{:S(2)}) %collective-permute-start.8) | collective-permute-done | bytes 90144 | tf_op jit(solution)/shard_map/ppermute | solution.py:218
  35.9 3.3 %collective-permute-done.7.refs_2_.refs_11_.refs_18_.refs_25_ = bf16[176,256]{1,0:T(8,128)(2,1)S(1)} collective-permute-done((bf16[176,256]{1,0:T(8,128)(2,1)S(1)}, bf16[176,256]{1,0:T(8,128)(2,1)S(1)}, u32[]{:S(2)}, u32[]{:S(2)}) %collective-permute-start.7) | collective-permute-done | bytes 90144 | tf_op jit(solution)/shard_map/ppermute | solution.py:218
  39.2 2.2 %collective-permute-done.6.refs_1_.refs_10_.refs_17_.refs_24_ = bf16[176,256]{1,0:T(8,128)(2,1)S(1)} collective-permute-done((bf16[176,256]{1,0:T(8,128)(2,1)S(1)}, bf16[176,256]{1,0:T(8,128)(2,1)S(1)}, u32[]{:S(2)}, u32[]{:S(2)}) %collective-permute-start.6) | collective-permute-done | bytes 90144 | tf_op jit(solution)/shard_map/ppermute | solution.py:218
  43.5 2.8 %collective-permute-start.15 = (bf16[2,160,256]{2,1,0:T(8,128)(2,1)S(1)}, bf16[2,160,256]{2,1,0:T(8,128)(2,1)S(1)}, u32[]{:S(2)}, u32[]{:S(2)}) collective-permute-start(bf16[2,160,256]{2,1,0:T(8,128)(2,1)S(1)} %get-tuple-element.59.refs_0_), channel_id=1, source_target_pairs={{4,0},{8,4},{12,8},{0,12},{5,1},{9,5},{13,9},{1,13},{6,2},{10,6},{... | collective-permute-start | bytes 491528 | tf_op jit(solution)/shard_map/ppermute | solution.py:218
  48.1 2.7 %collective-permute-done.15.refs_2_ = bf16[2,160,256]{2,1,0:T(8,128)(2,1)S(1)} collective-permute-done((bf16[2,160,256]{2,1,0:T(8,128)(2,1)S(1)}, bf16[2,160,256]{2,1,0:T(8,128)(2,1)S(1)}, u32[]{:S(2)}, u32[]{:S(2)}) %collective-permute-start.15) | collective-permute-done | bytes 163872 | tf_op jit(solution)/shard_map/ppermute | solution.py:218
  50.8 3.7 %collective-permute-start.16 = (bf16[2,160,256]{2,1,0:T(8,128)(2,1)S(1)}, bf16[2,160,256]{2,1,0:T(8,128)(2,1)S(1)}, u32[]{:S(2)}, u32[]{:S(2)}) collective-permute-start(bf16[2,160,256]{2,1,0:T(8,128)(2,1)S(1)} %get-tuple-element.60.refs_1_), channel_id=1, source_target_pairs={{4,0},{8,4},{12,8},{0,12},{5,1},{9,5},{13,9},{1,13},{6,2},{10,6},{... | collective-permute-start | bytes 491528 | tf_op jit(solution)/shard_map/ppermute | solution.py:218
  55.2 2.1 %collective-permute-start.20 = (bf16[2,160,256]{2,1,0:T(8,128)(2,1)S(1)}, bf16[2,160,256]{2,1,0:T(8,128)(2,1)S(1)}, u32[]{:S(2)}, u32[]{:S(2)}) collective-permute-start(bf16[2,160,256]{2,1,0:T(8,128)(2,1)S(1)} %collective-permute-done.18.refs_5_), channel_id=1, source_target_pairs={{12,0},{0,4},{4,8},{8,12},{13,1},{1,5},{5,9},{9,13},{14,2},{2,6},{... | collective-permute-start | bytes 491528 | tf_op jit(solution)/shard_map/ppermute | solution.py:218
  57.3 3.1 %collective-permute-start.25 = (bf16[256,768]{1,0:T(8,128)(2,1)S(1)}, bf16[256,768]{1,0:T(8,128)(2,1)S(1)}, u32[]{:S(2)}, u32[]{:S(2)}) collective-permute-start(bf16[256,768]{1,0:T(8,128)(2,1)S(1)} %shard_map.94.refs_9_.refs_8_), channel_id=1, source_target_pairs={{1,0},{2,1},{3,2},{0,3},{5,4},{6,5},{7,6},{4,7},{9,8},{10,9},{11,1... | collective-permute-start | bytes 1179656 | tf_op jit(solution)/shard_map/ppermute | solution.py:218
  60.4 2.3 %collective-permute-start.13 = (bf16[2,256,256]{2,1,0:T(8,128)(2,1)S(1)}, bf16[2,256,256]{2,1,0:T(8,128)(2,1)S(1)}, u32[]{:S(2)}, u32[]{:S(2)}) collective-permute-start(bf16[2,256,256]{2,1,0:T(8,128)(2,1)S(1)} %get-tuple-element.57.refs_0_), channel_id=1, source_target_pairs={{4,0},{8,4},{12,8},{0,12},{5,1},{9,5},{13,9},{1,13},{6,2},{10,6},{... | collective-permute-start | bytes 786440 | tf_op jit(solution)/shard_map/ppermute | solution.py:218
  65.2 4.4 %collective-permute-done.13.refs_2_ = bf16[2,256,256]{2,1,0:T(8,128)(2,1)S(1)} collective-permute-done((bf16[2,256,256]{2,1,0:T(8,128)(2,1)S(1)}, bf16[2,256,256]{2,1,0:T(8,128)(2,1)S(1)}, u32[]{:S(2)}, u32[]{:S(2)}) %collective-permute-start.13) | collective-permute-done | bytes 262176 | tf_op jit(solution)/shard_map/ppermute | solution.py:218
  69.6 3.0 %collective-permute-start.21 = (bf16[2,256,256]{2,1,0:T(8,128)(2,1)S(1)}, bf16[2,256,256]{2,1,0:T(8,128)(2,1)S(1)}, u32[]{:S(2)}, u32[]{:S(2)}) collective-permute-start(bf16[2,256,256]{2,1,0:T(8,128)(2,1)S(1)} %get-tuple-element.58.refs_1_), channel_id=1, source_target_pairs={{4,0},{8,4},{12,8},{0,12},{5,1},{9,5},{13,9},{1,13},{6,2},{10,6},{... | collective-permute-start | bytes 786440 | tf_op jit(solution)/shard_map/ppermute | solution.py:218
  72.9 2.0 %collective-permute-start.24 = (bf16[2,256,256]{2,1,0:T(8,128)(2,1)S(1)}, bf16[2,256,256]{2,1,0:T(8,128)(2,1)S(1)}, u32[]{:S(2)}, u32[]{:S(2)}) collective-permute-start(bf16[2,256,256]{2,1,0:T(8,128)(2,1)S(1)} %collective-permute-done.14.refs_5_), channel_id=1, source_target_pairs={{12,0},{0,4},{4,8},{8,12},{13,1},{1,5},{5,9},{9,13},{14,2},{2,6},{... | collective-permute-start | bytes 786440 | tf_op jit(solution)/shard_map/ppermute | solution.py:218
  76.0 2.5 %collective-permute-start.27 = (bf16[128,768]{1,0:T(8,128)(2,1)S(1)}, bf16[128,768]{1,0:T(8,128)(2,1)S(1)}, u32[]{:S(2)}, u32[]{:S(2)}) collective-permute-start(bf16[128,768]{1,0:T(8,128)(2,1)S(1)} %slice.18), channel_id=1, source_target_pairs={{1,0},{2,1},{3,2},{0,3},{5,4},{6,5},{7,6},{4,7},{9,8},{10,9},{11,1... | collective-permute-start | bytes 589832 | tf_op jit(solution)/shard_map/ppermute | solution.py:218
  81.9 4.6 %shard_map.100 = (bf16[256,256]{1,0:T(8,128)(2,1)S(1)}, bf16[256,256]{1,0:T(8,128)(2,1)S(1)}, bf16[256,256]{1,0:T(8,128)(2,1)S(1)}, bf16[256,256]{1,0:T(8,128)(2...) custom-call(bf16[2,256,256]{2,1,0:T(8,128)(2,1)S(1)} %get-tuple-element.57.refs_, ...), custom_call_target="tpu_custom_call" | custom-call | flops 700000000 | bytes 8000000 | tf_op jit(solution)/shard_map/pallas_call | solution.py:291
  88.6 3.2 %collective-permute-start.31 = (bf16[2,256,256]{2,1,0:T(8,128)(2,1)S(1)}, bf16[2,256,256]{2,1,0:T(8,128)(2,1)S(1)}, u32[]{:S(2)}, u32[]{:S(2)}) collective-permute-start(bf16[2,256,256]{2,1,0:T(8,128)(2,1)S(1)} %get-tuple-element.67.refs_1_), channel_id=1, source_target_pairs={{4,0},{8,4},{12,8},{0,12},{5,1},{9,5},{13,9},{1,13},{6,2},{10,6},{... | collective-permute-start | bytes 786440 | tf_op jit(solution)/shard_map/ppermute | solution.py:218
  91.8 3.1 %collective-permute-done.29.refs_2_ = bf16[2,256,256]{2,1,0:T(8,128)(2,1)S(1)} collective-permute-done((bf16[2,256,256]{2,1,0:T(8,128)(2,1)S(1)}, bf16[2,256,256]{2,1,0:T(8,128)(2,1)S(1)}, u32[]{:S(2)}, u32[]{:S(2)}) %collective-permute-start.29) | collective-permute-done | bytes 262176 | tf_op jit(solution)/shard_map/ppermute | solution.py:218
  96.4 1.7 %collective-permute-start.34 = (bf16[2,256,256]{2,1,0:T(8,128)(2,1)S(1)}, bf16[2,256,256]{2,1,0:T(8,128)(2,1)S(1)}, u32[]{:S(2)}, u32[]{:S(2)}) collective-permute-start(bf16[2,256,256]{2,1,0:T(8,128)(2,1)S(1)} %collective-permute-done.30.refs_5_), channel_id=1, source_target_pairs={{12,0},{0,4},{4,8},{8,12},{13,1},{1,5},{5,9},{9,13},{14,2},{2,6},{... | collective-permute-start | bytes 786440 | tf_op jit(solution)/shard_map/ppermute | solution.py:218
  99.0 2.7 %collective-permute-start.36 = (bf16[256,256]{1,0:T(8,128)(2,1)S(1)}, bf16[256,256]{1,0:T(8,128)(2,1)S(1)}, u32[]{:S(2)}, u32[]{:S(2)}) collective-permute-start(bf16[256,256]{1,0:T(8,128)(2,1)S(1)} %get-tuple-element.76), channel_id=1, source_target_pairs={{1,0},{2,1},{3,2},{0,3},{5,4},{6,5},{7,6},{4,7},{9,8},{10,9},{11,1... | collective-permute-start | bytes 393224 | tf_op jit(solution)/shard_map/ppermute | solution.py:218
  102.5 1.5 %collective-permute-done.34.refs_7_ = bf16[2,256,256]{2,1,0:T(8,128)(2,1)S(1)} collective-permute-done((bf16[2,256,256]{2,1,0:T(8,128)(2,1)S(1)}, bf16[2,256,256]{2,1,0:T(8,128)(2,1)S(1)}, u32[]{:S(2)}, u32[]{:S(2)}) %collective-permute-start.34) | collective-permute-done | bytes 262176 | tf_op jit(solution)/shard_map/ppermute | solution.py:218
  104.0 3.8 %shard_map.101 = bf16[8,4,128,128]{3,2,1,0:T(8,128)(2,1)S(1)} custom-call(bf16[2,256,256]{2,1,0:T(8,128)(2,1)S(1)} %get-tuple-element.66.refs_0_, bf16[2,256,256]{2,1,0:T(8,128)(2,1)S(1)} %get-tuple-element.67.refs_1_, bf16[2,256,256]{2,1,0:T(8,128)(2,1)S(1)} %collective-permute-done.29.refs_2_, bf16[2,256,256]{2,1,0:T(8,128)(2,1)S(1)} %collective-permute-done.31.refs_3_, ...), custom_call_target="tpu_custom_call" | custom-call | flops 900000000 | bytes 8000000 | tf_op jit(solution)/shard_map/pallas_call | solution.py:303
  108.2 20.0 %all_to_all.15.part_ref = bf16[32,128,128]{2,1,0:T(8,128)(2,1)S(1)} all-to-all(bf16[32,128,128]{2,1,0:T(8,128)(2,1)S(1)} %bitcast.23), channel_id=1, replica_groups=mesh['y'=4,'c'=2,'x'=4,'z'=4] {'y','c','x'}, dimensions={0} | all-to-all | bytes 2097152 | tf_op jit(solution)/shard_map/all_to_all | solution.py:312
  129.2 4.7 %all-to-all-start.2 = ((bf16[16,128,128]{2,1,0:T(8,128)(2,1)}), bf16[16,128,128]{2,1,0:T(8,128)(2,1)S(1)}, u32[]{:S(2)}, u32[]{:S(2)}) async-start(bf16[16,128,128]{2,1,0:T(8,128)(2,1)} %shard_map.103), calls=%async_computation.2 | async-start | bytes 1048576 | tf_op jit(solution)/shard_map/all_to_all | solution.py:315
  133.9 1.5 %shard_map.102 = bf16[256,1024]{1,0:T(8,128)(2,1)} custom-call(bf16[256,256]{1,0:T(8,128)(2,1)S(1)} %get-tuple-element.78.h0_ref, bf16[256,256]{1,0:T(8,128)(2,1)S(1)} %collective-permute-done.35.h1_ref, bf16[256,256]{1,0:T(8,128)(2,1)S(1)} %collective-permute-done.36.h2_ref, bf16[256,256]{1,0:T(8,128)(2,1)S(1)} %collective-permute-done.37.h3_ref, ...), custom_call_target="tpu_custom_call" | custom-call | bytes 1000000 | tf_op jit(solution)/shard_map/pallas_call | solution.py:316
  135.4 10.1 %all-to-all-done.2.in_ref = bf16[16,128,128]{2,1,0:T(8,128)(2,1)S(1)} async-done(((bf16[16,128,128]{2,1,0:T(8,128)(2,1)}), bf16[16,128,128]{2,1,0:T(8,128)(2,1)S(1)}, u32[]{:S(2)}, u32[]{:S(2)}) %all-to-all-start.2) | async-done | bytes 524320 | tf_op jit(solution)/shard_map/all_to_all | solution.py:315
  (85 shorter events, 24.8 us)
Async XLA Ops:
  1.5 7.6 %collective-permute-start = (bf16[96,256]{1,0:T(8,128)(2,1)S(1)}, bf16[96,256]{1,0:T(8,128)(2,1)S(1)}, u32[]{:S(2)}, u32[]{:S(2)}) collective-permute-start(bf16[96,256]{1,0:T(8,128)(2,1)S(1)} %constant_dynamic-slice_fusion), channel_id=1, source_target_pairs={{0,16},{16,0},{1,17},{17,1},{2,18},{18,2},{3,19},{19,3},{4,20},{20... | collective-permute-start | bytes 147464 | tf_op jit(solution)/shard_map/ppermute | solution.py:247
  3.4 18.7 %all-to-all-start = ((bf16[8,96,256]{2,1,0:T(8,128)(2,1)}), bf16[8,96,256]{2,1,0:T(8,128)(2,1)S(1)}, u32[]{:S(2)}, u32[]{:S(2)}) async-start(bf16[8,96,256]{2,1,0:T(8,128)(2,1)} %bitcast.22), calls=%async_computation | async-start | bytes 786432 | tf_op jit(solution)/shard_map/all_to_all | solution.py:243
  9.2 10.6 %collective-permute-start.3 = (bf16[2,96,256]{2,1,0:T(8,128)(2,1)S(1)}, bf16[2,96,256]{2,1,0:T(8,128)(2,1)S(1)}, u32[]{:S(2)}, u32[]{:S(2)}) collective-permute-start(bf16[2,96,256]{2,1,0:T(8,128)(2,1)S(1)} %pad_maximum_fusion.refs_0_), channel_id=1, source_target_pairs={{64,0},{96,32},{0,64},{32,96},{65,1},{97,33},{1,65},{33,97},{66,2}... | collective-permute-start | bytes 294920 | tf_op jit(solution)/shard_map/ppermute | solution.py:218
  12.8 8.6 %collective-permute-start.2 = (bf16[2,96,256]{2,1,0:T(8,128)(2,1)S(1)}, bf16[2,96,256]{2,1,0:T(8,128)(2,1)S(1)}, u32[]{:S(2)}, u32[]{:S(2)}) collective-permute-start(bf16[2,96,256]{2,1,0:T(8,128)(2,1)S(1)} %pad_maximum_fusion.refs_0_), channel_id=1, source_target_pairs={{96,0},{0,32},{32,64},{64,96},{97,1},{1,33},{33,65},{65,97},{98,2}... | collective-permute-start | bytes 294920 | tf_op jit(solution)/shard_map/ppermute | solution.py:218
  13.3 8.1 %collective-permute-start.1 = (bf16[2,96,256]{2,1,0:T(8,128)(2,1)S(1)}, bf16[2,96,256]{2,1,0:T(8,128)(2,1)S(1)}, u32[]{:S(2)}, u32[]{:S(2)}) collective-permute-start(bf16[2,96,256]{2,1,0:T(8,128)(2,1)S(1)} %pad_maximum_fusion.refs_0_), channel_id=1, source_target_pairs={{32,0},{64,32},{96,64},{0,96},{33,1},{65,33},{97,65},{1,97},{34,2}... | collective-permute-start | bytes 294920 | tf_op jit(solution)/shard_map/ppermute | solution.py:218
  22.2 19.2 %collective-permute-start.4 = (bf16[4,96,256]{2,1,0:T(8,128)(2,1)S(1)}, bf16[4,96,256]{2,1,0:T(8,128)(2,1)S(1)}, u32[]{:S(2)}, u32[]{:S(2)}) collective-permute-start(bf16[4,96,256]{2,1,0:T(8,128)(2,1)S(1)} %get-tuple-element.46.refs_0_.refs_13_), channel_id=1, source_target_pairs={{1,0},{2,1},{3,2},{0,3},{5,4},{6,5},{7,6},{4,7},{9,8},{10,9},{11,1... | collective-permute-start | bytes 589832 | tf_op jit(solution)/shard_map/ppermute | solution.py:218
  26.3 15.1 %collective-permute-start.5 = (bf16[4,96,256]{2,1,0:T(8,128)(2,1)S(1)}, bf16[4,96,256]{2,1,0:T(8,128)(2,1)S(1)}, u32[]{:S(2)}, u32[]{:S(2)}) collective-permute-start(bf16[4,96,256]{2,1,0:T(8,128)(2,1)S(1)} %get-tuple-element.47.refs_1_.refs_14_), channel_id=1, source_target_pairs={{3,0},{0,1},{1,2},{2,3},{7,4},{4,5},{5,6},{6,7},{11,8},{8,9},{9,10... | collective-permute-start | bytes 589832 | tf_op jit(solution)/shard_map/ppermute | solution.py:218
  26.3 9.6 %collective-permute-start.8 = (bf16[176,256]{1,0:T(8,128)(2,1)S(1)}, bf16[176,256]{1,0:T(8,128)(2,1)S(1)}, u32[]{:S(2)}, u32[]{:S(2)}) collective-permute-start(bf16[176,256]{1,0:T(8,128)(2,1)S(1)} %shard_map.96.refs_0_.refs_9_.refs_16_.refs_23_), channel_id=1, source_target_pairs={{2,0},{3,1},{0,2},{1,3},{6,4},{7,5},{4,6},{5,7},{10,8},{11,9},{8,1... | collective-permute-start | bytes 270344 | tf_op jit(solution)/shard_map/ppermute | solution.py:218
  28.2 11.0 %collective-permute-start.7 = (bf16[176,256]{1,0:T(8,128)(2,1)S(1)}, bf16[176,256]{1,0:T(8,128)(2,1)S(1)}, u32[]{:S(2)}, u32[]{:S(2)}) collective-permute-start(bf16[176,256]{1,0:T(8,128)(2,1)S(1)} %shard_map.96.refs_0_.refs_9_.refs_16_.refs_23_), channel_id=1, source_target_pairs={{3,0},{0,1},{1,2},{2,3},{7,4},{4,5},{5,6},{6,7},{11,8},{8,9},{9,10... | collective-permute-start | bytes 270344 | tf_op jit(solution)/shard_map/ppermute | solution.py:218
  30.4 15.9 %collective-permute-start.10 = (bf16[4,96,256]{2,1,0:T(8,128)(2,1)S(1)}, bf16[4,96,256]{2,1,0:T(8,128)(2,1)S(1)}, u32[]{:S(2)}, u32[]{:S(2)}) collective-permute-start(bf16[4,96,256]{2,1,0:T(8,128)(2,1)S(1)} %get-tuple-element.46.refs_0_.refs_13_), channel_id=1, source_target_pairs={{3,0},{0,1},{1,2},{2,3},{7,4},{4,5},{5,6},{6,7},{11,8},{8,9},{9,10... | collective-permute-start | bytes 589832 | tf_op jit(solution)/shard_map/ppermute | solution.py:218
  41.4 13.1 %collective-permute-start.11 = (bf16[4,96,256]{2,1,0:T(8,128)(2,1)S(1)}, bf16[4,96,256]{2,1,0:T(8,128)(2,1)S(1)}, u32[]{:S(2)}, u32[]{:S(2)}) collective-permute-start(bf16[4,96,256]{2,1,0:T(8,128)(2,1)S(1)} %collective-permute-done.4.refs_2_.refs_15_), channel_id=1, source_target_pairs={{1,0},{2,1},{3,2},{0,3},{5,4},{6,5},{7,6},{4,7},{9,8},{10,9},{11,1... | collective-permute-start | bytes 589832 | tf_op jit(solution)/shard_map/ppermute | solution.py:218
  42.5 12.0 %collective-permute-start.12 = (bf16[4,96,256]{2,1,0:T(8,128)(2,1)S(1)}, bf16[4,96,256]{2,1,0:T(8,128)(2,1)S(1)}, u32[]{:S(2)}, u32[]{:S(2)}) collective-permute-start(bf16[4,96,256]{2,1,0:T(8,128)(2,1)S(1)} %collective-permute-done.5.refs_5_.refs_18_), channel_id=1, source_target_pairs={{3,0},{0,1},{1,2},{2,3},{7,4},{4,5},{5,6},{6,7},{11,8},{8,9},{9,10... | collective-permute-start | bytes 589832 | tf_op jit(solution)/shard_map/ppermute | solution.py:218
  46.3 8.9 %collective-permute-start.18 = (bf16[2,160,256]{2,1,0:T(8,128)(2,1)S(1)}, bf16[2,160,256]{2,1,0:T(8,128)(2,1)S(1)}, u32[]{:S(2)}, u32[]{:S(2)}) collective-permute-start(bf16[2,160,256]{2,1,0:T(8,128)(2,1)S(1)} %get-tuple-element.60.refs_1_), channel_id=1, source_target_pairs={{12,0},{0,4},{4,8},{8,12},{13,1},{1,5},{5,9},{9,13},{14,2},{2,6},{... | collective-permute-start | bytes 491528 | tf_op jit(solution)/shard_map/ppermute | solution.py:218
  46.6 10.6 %collective-permute-start.17 = (bf16[2,160,256]{2,1,0:T(8,128)(2,1)S(1)}, bf16[2,160,256]{2,1,0:T(8,128)(2,1)S(1)}, u32[]{:S(2)}, u32[]{:S(2)}) collective-permute-start(bf16[2,160,256]{2,1,0:T(8,128)(2,1)S(1)} %get-tuple-element.59.refs_0_), channel_id=1, source_target_pairs={{12,0},{0,4},{4,8},{8,12},{13,1},{1,5},{5,9},{9,13},{14,2},{2,6},{... | collective-permute-start | bytes 491528 | tf_op jit(solution)/shard_map/ppermute | solution.py:218
  50.8 9.6 %collective-permute-start.16 = (bf16[2,160,256]{2,1,0:T(8,128)(2,1)S(1)}, bf16[2,160,256]{2,1,0:T(8,128)(2,1)S(1)}, u32[]{:S(2)}, u32[]{:S(2)}) collective-permute-start(bf16[2,160,256]{2,1,0:T(8,128)(2,1)S(1)} %get-tuple-element.60.refs_1_), channel_id=1, source_target_pairs={{4,0},{8,4},{12,8},{0,12},{5,1},{9,5},{13,9},{1,13},{6,2},{10,6},{... | collective-permute-start | bytes 491528 | tf_op jit(solution)/shard_map/ppermute | solution.py:218
  54.5 8.3 %collective-permute-start.19 = (bf16[2,160,256]{2,1,0:T(8,128)(2,1)S(1)}, bf16[2,160,256]{2,1,0:T(8,128)(2,1)S(1)}, u32[]{:S(2)}, u32[]{:S(2)}) collective-permute-start(bf16[2,160,256]{2,1,0:T(8,128)(2,1)S(1)} %collective-permute-done.15.refs_2_), channel_id=1, source_target_pairs={{4,0},{8,4},{12,8},{0,12},{5,1},{9,5},{13,9},{1,13},{6,2},{10,6},{... | collective-permute-start | bytes 491528 | tf_op jit(solution)/shard_map/ppermute | solution.py:218
  55.1 17.7 %collective-permute-start.26 = (bf16[256,768]{1,0:T(8,128)(2,1)S(1)}, bf16[256,768]{1,0:T(8,128)(2,1)S(1)}, u32[]{:S(2)}, u32[]{:S(2)}) collective-permute-start(bf16[256,768]{1,0:T(8,128)(2,1)S(1)} %shard_map.94.refs_9_.refs_8_), channel_id=1, source_target_pairs={{3,0},{0,1},{1,2},{2,3},{7,4},{4,5},{5,6},{6,7},{11,8},{8,9},{9,10... | collective-permute-start | bytes 1179656 | tf_op jit(solution)/shard_map/ppermute | solution.py:218
  55.2 8.4 %collective-permute-start.20 = (bf16[2,160,256]{2,1,0:T(8,128)(2,1)S(1)}, bf16[2,160,256]{2,1,0:T(8,128)(2,1)S(1)}, u32[]{:S(2)}, u32[]{:S(2)}) collective-permute-start(bf16[2,160,256]{2,1,0:T(8,128)(2,1)S(1)} %collective-permute-done.18.refs_5_), channel_id=1, source_target_pairs={{12,0},{0,4},{4,8},{8,12},{13,1},{1,5},{5,9},{9,13},{14,2},{2,6},{... | collective-permute-start | bytes 491528 | tf_op jit(solution)/shard_map/ppermute | solution.py:218
  57.3 17.6 %collective-permute-start.25 = (bf16[256,768]{1,0:T(8,128)(2,1)S(1)}, bf16[256,768]{1,0:T(8,128)(2,1)S(1)}, u32[]{:S(2)}, u32[]{:S(2)}) collective-permute-start(bf16[256,768]{1,0:T(8,128)(2,1)S(1)} %shard_map.94.refs_9_.refs_8_), channel_id=1, source_target_pairs={{1,0},{2,1},{3,2},{0,3},{5,4},{6,5},{7,6},{4,7},{9,8},{10,9},{11,1... | collective-permute-start | bytes 1179656 | tf_op jit(solution)/shard_map/ppermute | solution.py:218
  60.4 9.1 %collective-permute-start.13 = (bf16[2,256,256]{2,1,0:T(8,128)(2,1)S(1)}, bf16[2,256,256]{2,1,0:T(8,128)(2,1)S(1)}, u32[]{:S(2)}, u32[]{:S(2)}) collective-permute-start(bf16[2,256,256]{2,1,0:T(8,128)(2,1)S(1)} %get-tuple-element.57.refs_0_), channel_id=1, source_target_pairs={{4,0},{8,4},{12,8},{0,12},{5,1},{9,5},{13,9},{1,13},{6,2},{10,6},{... | collective-permute-start | bytes 786440 | tf_op jit(solution)/shard_map/ppermute | solution.py:218
  62.8 10.1 %collective-permute-start.14 = (bf16[2,256,256]{2,1,0:T(8,128)(2,1)S(1)}, bf16[2,256,256]{2,1,0:T(8,128)(2,1)S(1)}, u32[]{:S(2)}, u32[]{:S(2)}) collective-permute-start(bf16[2,256,256]{2,1,0:T(8,128)(2,1)S(1)} %get-tuple-element.58.refs_1_), channel_id=1, source_target_pairs={{12,0},{0,4},{4,8},{8,12},{13,1},{1,5},{5,9},{9,13},{14,2},{2,6},{... | collective-permute-start | bytes 786440 | tf_op jit(solution)/shard_map/ppermute | solution.py:218
  63.6 12.4 %collective-permute-start.22 = (bf16[2,256,256]{2,1,0:T(8,128)(2,1)S(1)}, bf16[2,256,256]{2,1,0:T(8,128)(2,1)S(1)}, u32[]{:S(2)}, u32[]{:S(2)}) collective-permute-start(bf16[2,256,256]{2,1,0:T(8,128)(2,1)S(1)} %get-tuple-element.57.refs_0_), channel_id=1, source_target_pairs={{12,0},{0,4},{4,8},{8,12},{13,1},{1,5},{5,9},{9,13},{14,2},{2,6},{... | collective-permute-start | bytes 786440 | tf_op jit(solution)/shard_map/ppermute | solution.py:218
  69.6 8.9 %collective-permute-start.21 = (bf16[2,256,256]{2,1,0:T(8,128)(2,1)S(1)}, bf16[2,256,256]{2,1,0:T(8,128)(2,1)S(1)}, u32[]{:S(2)}, u32[]{:S(2)}) collective-permute-start(bf16[2,256,256]{2,1,0:T(8,128)(2,1)S(1)} %get-tuple-element.58.refs_1_), channel_id=1, source_target_pairs={{4,0},{8,4},{12,8},{0,12},{5,1},{9,5},{13,9},{1,13},{6,2},{10,6},{... | collective-permute-start | bytes 786440 | tf_op jit(solution)/shard_map/ppermute | solution.py:218
  72.9 7.6 %collective-permute-start.24 = (bf16[2,256,256]{2,1,0:T(8,128)(2,1)S(1)}, bf16[2,256,256]{2,1,0:T(8,128)(2,1)S(1)}, u32[]{:S(2)}, u32[]{:S(2)}) collective-permute-start(bf16[2,256,256]{2,1,0:T(8,128)(2,1)S(1)} %collective-permute-done.14.refs_5_), channel_id=1, source_target_pairs={{12,0},{0,4},{4,8},{8,12},{13,1},{1,5},{5,9},{9,13},{14,2},{2,6},{... | collective-permute-start | bytes 786440 | tf_op jit(solution)/shard_map/ppermute | solution.py:218
  86.5 8.4 %collective-permute-start.29 = (bf16[2,256,256]{2,1,0:T(8,128)(2,1)S(1)}, bf16[2,256,256]{2,1,0:T(8,128)(2,1)S(1)}, u32[]{:S(2)}, u32[]{:S(2)}) collective-permute-start(bf16[2,256,256]{2,1,0:T(8,128)(2,1)S(1)} %get-tuple-element.66.refs_0_), channel_id=1, source_target_pairs={{4,0},{8,4},{12,8},{0,12},{5,1},{9,5},{13,9},{1,13},{6,2},{10,6},{... | collective-permute-start | bytes 786440 | tf_op jit(solution)/shard_map/ppermute | solution.py:218
  87.8 8.4 %collective-permute-start.30 = (bf16[2,256,256]{2,1,0:T(8,128)(2,1)S(1)}, bf16[2,256,256]{2,1,0:T(8,128)(2,1)S(1)}, u32[]{:S(2)}, u32[]{:S(2)}) collective-permute-start(bf16[2,256,256]{2,1,0:T(8,128)(2,1)S(1)} %get-tuple-element.67.refs_1_), channel_id=1, source_target_pairs={{12,0},{0,4},{4,8},{8,12},{13,1},{1,5},{5,9},{9,13},{14,2},{2,6},{... | collective-permute-start | bytes 786440 | tf_op jit(solution)/shard_map/ppermute | solution.py:218
  88.6 10.4 %collective-permute-start.32 = (bf16[2,256,256]{2,1,0:T(8,128)(2,1)S(1)}, bf16[2,256,256]{2,1,0:T(8,128)(2,1)S(1)}, u32[]{:S(2)}, u32[]{:S(2)}) collective-permute-start(bf16[2,256,256]{2,1,0:T(8,128)(2,1)S(1)} %get-tuple-element.66.refs_0_), channel_id=1, source_target_pairs={{12,0},{0,4},{4,8},{8,12},{13,1},{1,5},{5,9},{9,13},{14,2},{2,6},{... | collective-permute-start | bytes 786440 | tf_op jit(solution)/shard_map/ppermute | solution.py:218
  88.6 13.1 %collective-permute-start.31 = (bf16[2,256,256]{2,1,0:T(8,128)(2,1)S(1)}, bf16[2,256,256]{2,1,0:T(8,128)(2,1)S(1)}, u32[]{:S(2)}, u32[]{:S(2)}) collective-permute-start(bf16[2,256,256]{2,1,0:T(8,128)(2,1)S(1)} %get-tuple-element.67.refs_1_), channel_id=1, source_target_pairs={{4,0},{8,4},{12,8},{0,12},{5,1},{9,5},{13,9},{1,13},{6,2},{10,6},{... | collective-permute-start | bytes 786440 | tf_op jit(solution)/shard_map/ppermute | solution.py:218
  96.4 7.6 %collective-permute-start.34 = (bf16[2,256,256]{2,1,0:T(8,128)(2,1)S(1)}, bf16[2,256,256]{2,1,0:T(8,128)(2,1)S(1)}, u32[]{:S(2)}, u32[]{:S(2)}) collective-permute-start(bf16[2,256,256]{2,1,0:T(8,128)(2,1)S(1)} %collective-permute-done.30.refs_5_), channel_id=1, source_target_pairs={{12,0},{0,4},{4,8},{8,12},{13,1},{1,5},{5,9},{9,13},{14,2},{2,6},{... | collective-permute-start | bytes 786440 | tf_op jit(solution)/shard_map/ppermute | solution.py:218
  98.2 9.7 %collective-permute-start.35 = (bf16[256,256]{1,0:T(8,128)(2,1)S(1)}, bf16[256,256]{1,0:T(8,128)(2,1)S(1)}, u32[]{:S(2)}, u32[]{:S(2)}) collective-permute-start(bf16[256,256]{1,0:T(8,128)(2,1)S(1)} %get-tuple-element.75), channel_id=1, source_target_pairs={{3,0},{0,1},{1,2},{2,3},{7,4},{4,5},{5,6},{6,7},{11,8},{8,9},{9,10... | collective-permute-start | bytes 393224 | tf_op jit(solution)/shard_map/ppermute | solution.py:218
  99.0 8.9 %collective-permute-start.36 = (bf16[256,256]{1,0:T(8,128)(2,1)S(1)}, bf16[256,256]{1,0:T(8,128)(2,1)S(1)}, u32[]{:S(2)}, u32[]{:S(2)}) collective-permute-start(bf16[256,256]{1,0:T(8,128)(2,1)S(1)} %get-tuple-element.76), channel_id=1, source_target_pairs={{1,0},{2,1},{3,2},{0,3},{5,4},{6,5},{7,6},{4,7},{9,8},{10,9},{11,1... | collective-permute-start | bytes 393224 | tf_op jit(solution)/shard_map/ppermute | solution.py:218
  129.2 16.4 %all-to-all-start.2 = ((bf16[16,128,128]{2,1,0:T(8,128)(2,1)}), bf16[16,128,128]{2,1,0:T(8,128)(2,1)S(1)}, u32[]{:S(2)}, u32[]{:S(2)}) async-start(bf16[16,128,128]{2,1,0:T(8,128)(2,1)} %shard_map.103), calls=%async_computation.2 | async-start | bytes 1048576 | tf_op jit(solution)/shard_map/all_to_all | solution.py:315
  (13 other events, 114.6 us)

commit v12 on v10

--- a/solution.py
+++ b/solution.py
@@ -265,7 +265,7 @@
     )
     nodes = [nodes[0], n1, n2, n3]
     x_near = neighbours(x_low, x_high, "z")
-    x0, x1, *scaled = lax.optimization_barrier((*x_near[:2], *scaled))
+    x0, x1 = x_near[:2]
     x_wide = rounds(x_low, x_high, x_near, (x0, x1), "z")
     u_near = neighbours(*scaled, "x")
     scaled = rounds(*scaled, u_near, u_near[:2], "x")

time: 143 us -> 139 us (0.972)
  waiting for transfers between devices: 36.9 us -> 31.8 us
    ppermute x37, waiting for transfers between devices: 26.8 us -> 21.6 us  [fetch(): return lax.ppermute(value, axis, [((i + shift) % 4, i) for i in range(4)])]
  transfers between devices with their start and end apart: 40 -> 40, of which waited for: 16 -> 18; matrix products, arithmetic and copies ran while one was open for 2% -> 2% of each run, Pallas kernels for 5% -> 5%
where the time goes in v12:
time: 139 us
  starting transfers between devices  67.4 us (48%)
  waiting for transfers between devices  31.8 us (23%)
  blocking collectives  20.5 us (15%)
  Pallas kernels  14.3 us (10%)
  local copies, waits for them, and re-layouts  3.94 us (3%)
    ppermute x37, starting transfers between devices, fetch(): return lax.ppermute(value, axis, [((i + shift) % 4, i) for i in range(4)])  57.8 us
    ppermute x37, waiting for transfers between devices, fetch(): return lax.ppermute(value, axis, [((i + shift) % 4, i) for i in range(4)])  21.6 us
    all_to_all x1, blocking collectives, body(): lax.all_to_all(part.reshape(32, 128, 128), ('y', 'c', 'x'), 0, 0, tiled=T...  20.5 us
    all_to_all x1, waiting for transfers between devices, body(): done = lax.all_to_all(done, dom, 0, 0, tiled=True)  10.1 us
    all_to_all x1, starting transfers between devices, body(): done = lax.all_to_all(done, dom, 0, 0, tiled=True)  4.88 us
    all_to_all x1, starting transfers between devices, body(): lax.all_to_all(features.reshape(96, 8, 256).transpose(1, 0, 2), feat, 0,...  4.8 us
    pallas_call x1, Pallas kernels, body(): call(first_mix_kernel, (shape((256, 256), BF),) * 4 + (half, half, shape(...  4.64 us
    pallas_call x1, Pallas kernels, body(): call(second_mix_kernel, shape((8, 4, 128, 128), BF), [VMEM] * 22 + [SMEM]...  3.82 us
  transfers between devices with their start and end apart: 40, of which 18 were waited for; matrix products, arithmetic and copies ran while one was open for 2% of the time, Pallas kernels for 5%

profile of v12, /device:TPU:0, one launch (start us, length us, event | category | flops | bytes accessed | tf_op | source)
XLA Modules:
  0.0 138.9 jit_solution(15810628379997910818)
XLA Ops:
  3.4 4.8 %all-to-all-start = ((bf16[8,96,256]{2,1,0:T(8,128)(2,1)}), bf16[8,96,256]{2,1,0:T(8,128)(2,1)S(1)}, u32[]{:S(2)}, u32[]{:S(2)}) async-start(bf16[8,96,256]{2,1,0:T(8,128)(2,1)} %bitcast.22), calls=%async_computation | async-start | bytes 786432 | tf_op jit(solution)/shard_map/all_to_all | solution.py:243
  9.2 3.6 %collective-permute-start.3 = (bf16[2,96,256]{2,1,0:T(8,128)(2,1)S(1)}, bf16[2,96,256]{2,1,0:T(8,128)(2,1)S(1)}, u32[]{:S(2)}, u32[]{:S(2)}) collective-permute-start(bf16[2,96,256]{2,1,0:T(8,128)(2,1)S(1)} %pad_maximum_fusion.refs_0_), channel_id=1, source_target_pairs={{64,0},{96,32},{0,64},{32,96},{65,1},{97,33},{1,65},{33,97},{66,2}... | collective-permute-start | bytes 294920 | tf_op jit(solution)/shard_map/ppermute | solution.py:218
  13.3 2.7 %collective-permute-start.1 = (bf16[2,96,256]{2,1,0:T(8,128)(2,1)S(1)}, bf16[2,96,256]{2,1,0:T(8,128)(2,1)S(1)}, u32[]{:S(2)}, u32[]{:S(2)}) collective-permute-start(bf16[2,96,256]{2,1,0:T(8,128)(2,1)S(1)} %pad_maximum_fusion.refs_0_), channel_id=1, source_target_pairs={{32,0},{64,32},{96,64},{0,96},{33,1},{65,33},{97,65},{1,97},{34,2}... | collective-permute-start | bytes 294920 | tf_op jit(solution)/shard_map/ppermute | solution.py:218
  16.3 4.0 %collective-permute-start.6 = (bf16[176,256]{1,0:T(8,128)(2,1)S(1)}, bf16[176,256]{1,0:T(8,128)(2,1)S(1)}, u32[]{:S(2)}, u32[]{:S(2)}) collective-permute-start(bf16[176,256]{1,0:T(8,128)(2,1)S(1)} %shard_map.96.refs_9_.refs_0_.refs_16_.refs_23_), channel_id=1, source_target_pairs={{2,0},{3,1},{0,2},{1,3},{6,4},{7,5},{4,6},{5,7},{10,8},{11,9},{8,1... | collective-permute-start | bytes 270344 | tf_op jit(solution)/shard_map/ppermute | solution.py:218
  21.3 2.5 %collective-permute-start.4 = (bf16[176,256]{1,0:T(8,128)(2,1)S(1)}, bf16[176,256]{1,0:T(8,128)(2,1)S(1)}, u32[]{:S(2)}, u32[]{:S(2)}) collective-permute-start(bf16[176,256]{1,0:T(8,128)(2,1)S(1)} %shard_map.96.refs_9_.refs_0_.refs_16_.refs_23_), channel_id=1, source_target_pairs={{1,0},{2,1},{3,2},{0,3},{5,4},{6,5},{7,6},{4,7},{9,8},{10,9},{11,1... | collective-permute-start | bytes 270344 | tf_op jit(solution)/shard_map/ppermute | solution.py:218
  26.0 3.5 %collective-permute-start.7 = (bf16[4,96,256]{2,1,0:T(8,128)(2,1)S(1)}, bf16[4,96,256]{2,1,0:T(8,128)(2,1)S(1)}, u32[]{:S(2)}, u32[]{:S(2)}) collective-permute-start(bf16[4,96,256]{2,1,0:T(8,128)(2,1)S(1)} %get-tuple-element.44.refs_0_.refs_13_), channel_id=1, source_target_pairs={{1,0},{2,1},{3,2},{0,3},{5,4},{6,5},{7,6},{4,7},{9,8},{10,9},{11,1... | collective-permute-start | bytes 589832 | tf_op jit(solution)/shard_map/ppermute | solution.py:218
  29.7 2.8 %collective-permute-start.15 = (bf16[2,160,256]{2,1,0:T(8,128)(2,1)S(1)}, bf16[2,160,256]{2,1,0:T(8,128)(2,1)S(1)}, u32[]{:S(2)}, u32[]{:S(2)}) collective-permute-start(bf16[2,160,256]{2,1,0:T(8,128)(2,1)S(1)} %get-tuple-element.55.refs_0_), channel_id=1, source_target_pairs={{4,0},{8,4},{12,8},{0,12},{5,1},{9,5},{13,9},{1,13},{6,2},{10,6},{... | collective-permute-start | bytes 491528 | tf_op jit(solution)/shard_map/ppermute | solution.py:218
  32.5 3.2 %collective-permute-start.8 = (bf16[4,96,256]{2,1,0:T(8,128)(2,1)S(1)}, bf16[4,96,256]{2,1,0:T(8,128)(2,1)S(1)}, u32[]{:S(2)}, u32[]{:S(2)}) collective-permute-start(bf16[4,96,256]{2,1,0:T(8,128)(2,1)S(1)} %get-tuple-element.45.refs_1_.refs_14_), channel_id=1, source_target_pairs={{1,0},{2,1},{3,2},{0,3},{5,4},{6,5},{7,6},{4,7},{9,8},{10,9},{11,1... | collective-permute-start | bytes 589832 | tf_op jit(solution)/shard_map/ppermute | solution.py:218
  35.7 1.9 %collective-permute-start.11 = (bf16[4,96,256]{2,1,0:T(8,128)(2,1)S(1)}, bf16[4,96,256]{2,1,0:T(8,128)(2,1)S(1)}, u32[]{:S(2)}, u32[]{:S(2)}) collective-permute-start(bf16[4,96,256]{2,1,0:T(8,128)(2,1)S(1)} %collective-permute-done.7.refs_2_.refs_15_), channel_id=1, source_target_pairs={{1,0},{2,1},{3,2},{0,3},{5,4},{6,5},{7,6},{4,7},{9,8},{10,9},{11,1... | collective-permute-start | bytes 589832 | tf_op jit(solution)/shard_map/ppermute | solution.py:218
  37.8 2.0 %collective-permute-start.18 = (bf16[2,160,256]{2,1,0:T(8,128)(2,1)S(1)}, bf16[2,160,256]{2,1,0:T(8,128)(2,1)S(1)}, u32[]{:S(2)}, u32[]{:S(2)}) collective-permute-start(bf16[2,160,256]{2,1,0:T(8,128)(2,1)S(1)} %get-tuple-element.56.refs_1_), channel_id=1, source_target_pairs={{12,0},{0,4},{4,8},{8,12},{13,1},{1,5},{5,9},{9,13},{14,2},{2,6},{... | collective-permute-start | bytes 491528 | tf_op jit(solution)/shard_map/ppermute | solution.py:218
  39.8 1.7 %collective-permute-done.9.refs_4_.refs_17_ = bf16[4,96,256]{2,1,0:T(8,128)(2,1)S(1)} collective-permute-done((bf16[4,96,256]{2,1,0:T(8,128)(2,1)S(1)}, bf16[4,96,256]{2,1,0:T(8,128)(2,1)S(1)}, u32[]{:S(2)}, u32[]{:S(2)}) %collective-permute-start.9) | collective-permute-done | bytes 196640 | tf_op jit(solution)/shard_map/ppermute | solution.py:218
  41.5 2.0 %collective-permute-start.17 = (bf16[2,160,256]{2,1,0:T(8,128)(2,1)S(1)}, bf16[2,160,256]{2,1,0:T(8,128)(2,1)S(1)}, u32[]{:S(2)}, u32[]{:S(2)}) collective-permute-start(bf16[2,160,256]{2,1,0:T(8,128)(2,1)S(1)} %get-tuple-element.55.refs_0_), channel_id=1, source_target_pairs={{12,0},{0,4},{4,8},{8,12},{13,1},{1,5},{5,9},{9,13},{14,2},{2,6},{... | collective-permute-start | bytes 491528 | tf_op jit(solution)/shard_map/ppermute | solution.py:218
  44.7 2.0 %collective-permute-start.19 = (bf16[2,160,256]{2,1,0:T(8,128)(2,1)S(1)}, bf16[2,160,256]{2,1,0:T(8,128)(2,1)S(1)}, u32[]{:S(2)}, u32[]{:S(2)}) collective-permute-start(bf16[2,160,256]{2,1,0:T(8,128)(2,1)S(1)} %collective-permute-done.15.refs_2_), channel_id=1, source_target_pairs={{4,0},{8,4},{12,8},{0,12},{5,1},{9,5},{13,9},{1,13},{6,2},{10,6},{... | collective-permute-start | bytes 491528 | tf_op jit(solution)/shard_map/ppermute | solution.py:218
  47.5 2.2 %collective-permute-done.17.refs_4_ = bf16[2,160,256]{2,1,0:T(8,128)(2,1)S(1)} collective-permute-done((bf16[2,160,256]{2,1,0:T(8,128)(2,1)S(1)}, bf16[2,160,256]{2,1,0:T(8,128)(2,1)S(1)}, u32[]{:S(2)}, u32[]{:S(2)}) %collective-permute-start.17) | collective-permute-done | bytes 163872 | tf_op jit(solution)/shard_map/ppermute | solution.py:218
  50.7 3.2 %collective-permute-start.13 = (bf16[2,256,256]{2,1,0:T(8,128)(2,1)S(1)}, bf16[2,256,256]{2,1,0:T(8,128)(2,1)S(1)}, u32[]{:S(2)}, u32[]{:S(2)}) collective-permute-start(bf16[2,256,256]{2,1,0:T(8,128)(2,1)S(1)} %get-tuple-element.53.refs_0_), channel_id=1, source_target_pairs={{4,0},{8,4},{12,8},{0,12},{5,1},{9,5},{13,9},{1,13},{6,2},{10,6},{... | collective-permute-start | bytes 786440 | tf_op jit(solution)/shard_map/ppermute | solution.py:218
  53.9 1.9 %collective-permute-done.20.refs_7_ = bf16[2,160,256]{2,1,0:T(8,128)(2,1)S(1)} collective-permute-done((bf16[2,160,256]{2,1,0:T(8,128)(2,1)S(1)}, bf16[2,160,256]{2,1,0:T(8,128)(2,1)S(1)}, u32[]{:S(2)}, u32[]{:S(2)}) %collective-permute-start.20) | collective-permute-done | bytes 163872 | tf_op jit(solution)/shard_map/ppermute | solution.py:218
  56.6 2.6 %collective-permute-done.13.refs_2_ = bf16[2,256,256]{2,1,0:T(8,128)(2,1)S(1)} collective-permute-done((bf16[2,256,256]{2,1,0:T(8,128)(2,1)S(1)}, bf16[2,256,256]{2,1,0:T(8,128)(2,1)S(1)}, u32[]{:S(2)}, u32[]{:S(2)}) %collective-permute-start.13) | collective-permute-done | bytes 262176 | tf_op jit(solution)/shard_map/ppermute | solution.py:218
  59.2 3.7 %collective-permute-start.21 = (bf16[2,256,256]{2,1,0:T(8,128)(2,1)S(1)}, bf16[2,256,256]{2,1,0:T(8,128)(2,1)S(1)}, u32[]{:S(2)}, u32[]{:S(2)}) collective-permute-start(bf16[2,256,256]{2,1,0:T(8,128)(2,1)S(1)} %get-tuple-element.54.refs_1_), channel_id=1, source_target_pairs={{4,0},{8,4},{12,8},{0,12},{5,1},{9,5},{13,9},{1,13},{6,2},{10,6},{... | collective-permute-start | bytes 786440 | tf_op jit(solution)/shard_map/ppermute | solution.py:218
  62.9 1.5 %collective-permute-done.14.refs_5_ = bf16[2,256,256]{2,1,0:T(8,128)(2,1)S(1)} collective-permute-done((bf16[2,256,256]{2,1,0:T(8,128)(2,1)S(1)}, bf16[2,256,256]{2,1,0:T(8,128)(2,1)S(1)}, u32[]{:S(2)}, u32[]{:S(2)}) %collective-permute-start.14) | collective-permute-done | bytes 262176 | tf_op jit(solution)/shard_map/ppermute | solution.py:218
  64.4 2.0 %collective-permute-start.24 = (bf16[2,256,256]{2,1,0:T(8,128)(2,1)S(1)}, bf16[2,256,256]{2,1,0:T(8,128)(2,1)S(1)}, u32[]{:S(2)}, u32[]{:S(2)}) collective-permute-start(bf16[2,256,256]{2,1,0:T(8,128)(2,1)S(1)} %collective-permute-done.14.refs_5_), channel_id=1, source_target_pairs={{12,0},{0,4},{4,8},{8,12},{13,1},{1,5},{5,9},{9,13},{14,2},{2,6},{... | collective-permute-start | bytes 786440 | tf_op jit(solution)/shard_map/ppermute | solution.py:218
  66.5 1.5 %collective-permute-done.22.refs_4_ = bf16[2,256,256]{2,1,0:T(8,128)(2,1)S(1)} collective-permute-done((bf16[2,256,256]{2,1,0:T(8,128)(2,1)S(1)}, bf16[2,256,256]{2,1,0:T(8,128)(2,1)S(1)}, u32[]{:S(2)}, u32[]{:S(2)}) %collective-permute-start.22) | collective-permute-done | bytes 262176 | tf_op jit(solution)/shard_map/ppermute | solution.py:218
  68.0 2.0 %collective-permute-start.27 = (bf16[128,768]{1,0:T(8,128)(2,1)S(1)}, bf16[128,768]{1,0:T(8,128)(2,1)S(1)}, u32[]{:S(2)}, u32[]{:S(2)}) collective-permute-start(bf16[128,768]{1,0:T(8,128)(2,1)S(1)} %slice.18), channel_id=1, source_target_pairs={{1,0},{2,1},{3,2},{0,3},{5,4},{6,5},{7,6},{4,7},{9,8},{10,9},{11,1... | collective-permute-start | bytes 589832 | tf_op jit(solution)/shard_map/ppermute | solution.py:218
  73.7 4.6 %shard_map.100 = (bf16[256,256]{1,0:T(8,128)(2,1)S(1)}, bf16[256,256]{1,0:T(8,128)(2,1)S(1)}, bf16[256,256]{1,0:T(8,128)(2,1)S(1)}, bf16[256,256]{1,0:T(8,128)(2...) custom-call(bf16[2,256,256]{2,1,0:T(8,128)(2,1)S(1)} %get-tuple-element.53.refs_, ...), custom_call_target="tpu_custom_call" | custom-call | flops 700000000 | bytes 8000000 | tf_op jit(solution)/shard_map/pallas_call | solution.py:292
  80.5 3.2 %collective-permute-start.31 = (bf16[2,256,256]{2,1,0:T(8,128)(2,1)S(1)}, bf16[2,256,256]{2,1,0:T(8,128)(2,1)S(1)}, u32[]{:S(2)}, u32[]{:S(2)}) collective-permute-start(bf16[2,256,256]{2,1,0:T(8,128)(2,1)S(1)} %get-tuple-element.63.refs_1_), channel_id=1, source_target_pairs={{4,0},{8,4},{12,8},{0,12},{5,1},{9,5},{13,9},{1,13},{6,2},{10,6},{... | collective-permute-start | bytes 786440 | tf_op jit(solution)/shard_map/ppermute | solution.py:218
  83.7 2.4 %collective-permute-done.29.refs_2_ = bf16[2,256,256]{2,1,0:T(8,128)(2,1)S(1)} collective-permute-done((bf16[2,256,256]{2,1,0:T(8,128)(2,1)S(1)}, bf16[2,256,256]{2,1,0:T(8,128)(2,1)S(1)}, u32[]{:S(2)}, u32[]{:S(2)}) %collective-permute-start.29) | collective-permute-done | bytes 262176 | tf_op jit(solution)/shard_map/ppermute | solution.py:218
  87.6 1.7 %collective-permute-start.34 = (bf16[2,256,256]{2,1,0:T(8,128)(2,1)S(1)}, bf16[2,256,256]{2,1,0:T(8,128)(2,1)S(1)}, u32[]{:S(2)}, u32[]{:S(2)}) collective-permute-start(bf16[2,256,256]{2,1,0:T(8,128)(2,1)S(1)} %collective-permute-done.30.refs_5_), channel_id=1, source_target_pairs={{12,0},{0,4},{4,8},{8,12},{13,1},{1,5},{5,9},{9,13},{14,2},{2,6},{... | collective-permute-start | bytes 786440 | tf_op jit(solution)/shard_map/ppermute | solution.py:218
  90.1 3.2 %collective-permute-start.36 = (bf16[256,256]{1,0:T(8,128)(2,1)S(1)}, bf16[256,256]{1,0:T(8,128)(2,1)S(1)}, u32[]{:S(2)}, u32[]{:S(2)}) collective-permute-start(bf16[256,256]{1,0:T(8,128)(2,1)S(1)} %get-tuple-element.72), channel_id=1, source_target_pairs={{1,0},{2,1},{3,2},{0,3},{5,4},{6,5},{7,6},{4,7},{9,8},{10,9},{11,1... | collective-permute-start | bytes 393224 | tf_op jit(solution)/shard_map/ppermute | solution.py:218
  95.1 3.8 %shard_map.101 = bf16[8,4,128,128]{3,2,1,0:T(8,128)(2,1)S(1)} custom-call(bf16[2,256,256]{2,1,0:T(8,128)(2,1)S(1)} %get-tuple-element.62.refs_0_, bf16[2,256,256]{2,1,0:T(8,128)(2,1)S(1)} %get-tuple-element.63.refs_1_, bf16[2,256,256]{2,1,0:T(8,128)(2,1)S(1)} %collective-permute-done.29.refs_2_, bf16[2,256,256]{2,1,0:T(8,128)(2,1)S(1)} %collective-permute-done.31.refs_3_, ...), custom_call_target="tpu_custom_call" | custom-call | flops 900000000 | bytes 8000000 | tf_op jit(solution)/shard_map/pallas_call | solution.py:304
  99.7 20.5 %all_to_all.15.part_ref = bf16[32,128,128]{2,1,0:T(8,128)(2,1)S(1)} all-to-all(bf16[32,128,128]{2,1,0:T(8,128)(2,1)S(1)} %bitcast.23), channel_id=1, replica_groups=mesh['y'=4,'c'=2,'x'=4,'z'=4] {'y','c','x'}, dimensions={0} | all-to-all | bytes 2097152 | tf_op jit(solution)/shard_map/all_to_all | solution.py:313
  121.1 4.9 %all-to-all-start.2 = ((bf16[16,128,128]{2,1,0:T(8,128)(2,1)}), bf16[16,128,128]{2,1,0:T(8,128)(2,1)S(1)}, u32[]{:S(2)}, u32[]{:S(2)}) async-start(bf16[16,128,128]{2,1,0:T(8,128)(2,1)} %shard_map.103), calls=%async_computation.2 | async-start | bytes 1048576 | tf_op jit(solution)/shard_map/all_to_all | solution.py:316
  126.0 1.5 %shard_map.102 = bf16[256,1024]{1,0:T(8,128)(2,1)} custom-call(bf16[256,256]{1,0:T(8,128)(2,1)S(1)} %get-tuple-element.74.h0_ref, bf16[256,256]{1,0:T(8,128)(2,1)S(1)} %collective-permute-done.35.h1_ref, bf16[256,256]{1,0:T(8,128)(2,1)S(1)} %collective-permute-done.36.h2_ref, bf16[256,256]{1,0:T(8,128)(2,1)S(1)} %collective-permute-done.37.h3_ref, ...), custom_call_target="tpu_custom_call" | custom-call | bytes 1000000 | tf_op jit(solution)/shard_map/pallas_call | solution.py:317
  127.6 10.1 %all-to-all-done.2.in_ref = bf16[16,128,128]{2,1,0:T(8,128)(2,1)S(1)} async-done(((bf16[16,128,128]{2,1,0:T(8,128)(2,1)}), bf16[16,128,128]{2,1,0:T(8,128)(2,1)S(1)}, u32[]{:S(2)}, u32[]{:S(2)}) %all-to-all-start.2) | async-done | bytes 524320 | tf_op jit(solution)/shard_map/all_to_all | solution.py:316
  (85 shorter events, 24.8 us)
Async XLA Ops:
  1.5 7.6 %collective-permute-start = (bf16[96,256]{1,0:T(8,128)(2,1)S(1)}, bf16[96,256]{1,0:T(8,128)(2,1)S(1)}, u32[]{:S(2)}, u32[]{:S(2)}) collective-permute-start(bf16[96,256]{1,0:T(8,128)(2,1)S(1)} %constant_dynamic-slice_fusion), channel_id=1, source_target_pairs={{0,16},{16,0},{1,17},{17,1},{2,18},{18,2},{3,19},{19,3},{4,20},{20... | collective-permute-start | bytes 147464 | tf_op jit(solution)/shard_map/ppermute | solution.py:247
  3.4 21.2 %all-to-all-start = ((bf16[8,96,256]{2,1,0:T(8,128)(2,1)}), bf16[8,96,256]{2,1,0:T(8,128)(2,1)S(1)}, u32[]{:S(2)}, u32[]{:S(2)}) async-start(bf16[8,96,256]{2,1,0:T(8,128)(2,1)} %bitcast.22), calls=%async_computation | async-start | bytes 786432 | tf_op jit(solution)/shard_map/all_to_all | solution.py:243
  9.2 12.2 %collective-permute-start.3 = (bf16[2,96,256]{2,1,0:T(8,128)(2,1)S(1)}, bf16[2,96,256]{2,1,0:T(8,128)(2,1)S(1)}, u32[]{:S(2)}, u32[]{:S(2)}) collective-permute-start(bf16[2,96,256]{2,1,0:T(8,128)(2,1)S(1)} %pad_maximum_fusion.refs_0_), channel_id=1, source_target_pairs={{64,0},{96,32},{0,64},{32,96},{65,1},{97,33},{1,65},{33,97},{66,2}... | collective-permute-start | bytes 294920 | tf_op jit(solution)/shard_map/ppermute | solution.py:218
  12.8 11.1 %collective-permute-start.2 = (bf16[2,96,256]{2,1,0:T(8,128)(2,1)S(1)}, bf16[2,96,256]{2,1,0:T(8,128)(2,1)S(1)}, u32[]{:S(2)}, u32[]{:S(2)}) collective-permute-start(bf16[2,96,256]{2,1,0:T(8,128)(2,1)S(1)} %pad_maximum_fusion.refs_0_), channel_id=1, source_target_pairs={{96,0},{0,32},{32,64},{64,96},{97,1},{1,33},{33,65},{65,97},{98,2}... | collective-permute-start | bytes 294920 | tf_op jit(solution)/shard_map/ppermute | solution.py:218
  13.3 10.5 %collective-permute-start.1 = (bf16[2,96,256]{2,1,0:T(8,128)(2,1)S(1)}, bf16[2,96,256]{2,1,0:T(8,128)(2,1)S(1)}, u32[]{:S(2)}, u32[]{:S(2)}) collective-permute-start(bf16[2,96,256]{2,1,0:T(8,128)(2,1)S(1)} %pad_maximum_fusion.refs_0_), channel_id=1, source_target_pairs={{32,0},{64,32},{96,64},{0,96},{33,1},{65,33},{97,65},{1,97},{34,2}... | collective-permute-start | bytes 294920 | tf_op jit(solution)/shard_map/ppermute | solution.py:218
  16.3 8.3 %collective-permute-start.6 = (bf16[176,256]{1,0:T(8,128)(2,1)S(1)}, bf16[176,256]{1,0:T(8,128)(2,1)S(1)}, u32[]{:S(2)}, u32[]{:S(2)}) collective-permute-start(bf16[176,256]{1,0:T(8,128)(2,1)S(1)} %shard_map.96.refs_9_.refs_0_.refs_16_.refs_23_), channel_id=1, source_target_pairs={{2,0},{3,1},{0,2},{1,3},{6,4},{7,5},{4,6},{5,7},{10,8},{11,9},{8,1... | collective-permute-start | bytes 270344 | tf_op jit(solution)/shard_map/ppermute | solution.py:218
  26.0 9.7 %collective-permute-start.7 = (bf16[4,96,256]{2,1,0:T(8,128)(2,1)S(1)}, bf16[4,96,256]{2,1,0:T(8,128)(2,1)S(1)}, u32[]{:S(2)}, u32[]{:S(2)}) collective-permute-start(bf16[4,96,256]{2,1,0:T(8,128)(2,1)S(1)} %get-tuple-element.44.refs_0_.refs_13_), channel_id=1, source_target_pairs={{1,0},{2,1},{3,2},{0,3},{5,4},{6,5},{7,6},{4,7},{9,8},{10,9},{11,1... | collective-permute-start | bytes 589832 | tf_op jit(solution)/shard_map/ppermute | solution.py:218
  29.6 8.2 %collective-permute-start.10 = (bf16[4,96,256]{2,1,0:T(8,128)(2,1)S(1)}, bf16[4,96,256]{2,1,0:T(8,128)(2,1)S(1)}, u32[]{:S(2)}, u32[]{:S(2)}) collective-permute-start(bf16[4,96,256]{2,1,0:T(8,128)(2,1)S(1)} %get-tuple-element.45.refs_1_.refs_14_), channel_id=1, source_target_pairs={{3,0},{0,1},{1,2},{2,3},{7,4},{4,5},{5,6},{6,7},{11,8},{8,9},{9,10... | collective-permute-start | bytes 589832 | tf_op jit(solution)/shard_map/ppermute | solution.py:218
  29.6 11.9 %collective-permute-start.9 = (bf16[4,96,256]{2,1,0:T(8,128)(2,1)S(1)}, bf16[4,96,256]{2,1,0:T(8,128)(2,1)S(1)}, u32[]{:S(2)}, u32[]{:S(2)}) collective-permute-start(bf16[4,96,256]{2,1,0:T(8,128)(2,1)S(1)} %get-tuple-element.44.refs_0_.refs_13_), channel_id=1, source_target_pairs={{3,0},{0,1},{1,2},{2,3},{7,4},{4,5},{5,6},{6,7},{11,8},{8,9},{9,10... | collective-permute-start | bytes 589832 | tf_op jit(solution)/shard_map/ppermute | solution.py:218
  29.7 8.1 %collective-permute-start.15 = (bf16[2,160,256]{2,1,0:T(8,128)(2,1)S(1)}, bf16[2,160,256]{2,1,0:T(8,128)(2,1)S(1)}, u32[]{:S(2)}, u32[]{:S(2)}) collective-permute-start(bf16[2,160,256]{2,1,0:T(8,128)(2,1)S(1)} %get-tuple-element.55.refs_0_), channel_id=1, source_target_pairs={{4,0},{8,4},{12,8},{0,12},{5,1},{9,5},{13,9},{1,13},{6,2},{10,6},{... | collective-permute-start | bytes 491528 | tf_op jit(solution)/shard_map/ppermute | solution.py:218
  32.5 11.0 %collective-permute-start.8 = (bf16[4,96,256]{2,1,0:T(8,128)(2,1)S(1)}, bf16[4,96,256]{2,1,0:T(8,128)(2,1)S(1)}, u32[]{:S(2)}, u32[]{:S(2)}) collective-permute-start(bf16[4,96,256]{2,1,0:T(8,128)(2,1)S(1)} %get-tuple-element.45.refs_1_.refs_14_), channel_id=1, source_target_pairs={{1,0},{2,1},{3,2},{0,3},{5,4},{6,5},{7,6},{4,7},{9,8},{10,9},{11,1... | collective-permute-start | bytes 589832 | tf_op jit(solution)/shard_map/ppermute | solution.py:218
  35.7 9.0 %collective-permute-start.11 = (bf16[4,96,256]{2,1,0:T(8,128)(2,1)S(1)}, bf16[4,96,256]{2,1,0:T(8,128)(2,1)S(1)}, u32[]{:S(2)}, u32[]{:S(2)}) collective-permute-start(bf16[4,96,256]{2,1,0:T(8,128)(2,1)S(1)} %collective-permute-done.7.refs_2_.refs_15_), channel_id=1, source_target_pairs={{1,0},{2,1},{3,2},{0,3},{5,4},{6,5},{7,6},{4,7},{9,8},{10,9},{11,1... | collective-permute-start | bytes 589832 | tf_op jit(solution)/shard_map/ppermute | solution.py:218
  37.8 9.0 %collective-permute-start.12 = (bf16[4,96,256]{2,1,0:T(8,128)(2,1)S(1)}, bf16[4,96,256]{2,1,0:T(8,128)(2,1)S(1)}, u32[]{:S(2)}, u32[]{:S(2)}) collective-permute-start(bf16[4,96,256]{2,1,0:T(8,128)(2,1)S(1)} %collective-permute-done.10.refs_5_.refs_18_), channel_id=1, source_target_pairs={{3,0},{0,1},{1,2},{2,3},{7,4},{4,5},{5,6},{6,7},{11,8},{8,9},{9,10... | collective-permute-start | bytes 589832 | tf_op jit(solution)/shard_map/ppermute | solution.py:218
  37.8 9.7 %collective-permute-start.18 = (bf16[2,160,256]{2,1,0:T(8,128)(2,1)S(1)}, bf16[2,160,256]{2,1,0:T(8,128)(2,1)S(1)}, u32[]{:S(2)}, u32[]{:S(2)}) collective-permute-start(bf16[2,160,256]{2,1,0:T(8,128)(2,1)S(1)} %get-tuple-element.56.refs_1_), channel_id=1, source_target_pairs={{12,0},{0,4},{4,8},{8,12},{13,1},{1,5},{5,9},{9,13},{14,2},{2,6},{... | collective-permute-start | bytes 491528 | tf_op jit(solution)/shard_map/ppermute | solution.py:218
  41.5 8.2 %collective-permute-start.17 = (bf16[2,160,256]{2,1,0:T(8,128)(2,1)S(1)}, bf16[2,160,256]{2,1,0:T(8,128)(2,1)S(1)}, u32[]{:S(2)}, u32[]{:S(2)}) collective-permute-start(bf16[2,160,256]{2,1,0:T(8,128)(2,1)S(1)} %get-tuple-element.55.refs_0_), channel_id=1, source_target_pairs={{12,0},{0,4},{4,8},{8,12},{13,1},{1,5},{5,9},{9,13},{14,2},{2,6},{... | collective-permute-start | bytes 491528 | tf_op jit(solution)/shard_map/ppermute | solution.py:218
  44.7 9.2 %collective-permute-start.19 = (bf16[2,160,256]{2,1,0:T(8,128)(2,1)S(1)}, bf16[2,160,256]{2,1,0:T(8,128)(2,1)S(1)}, u32[]{:S(2)}, u32[]{:S(2)}) collective-permute-start(bf16[2,160,256]{2,1,0:T(8,128)(2,1)S(1)} %collective-permute-done.15.refs_2_), channel_id=1, source_target_pairs={{4,0},{8,4},{12,8},{0,12},{5,1},{9,5},{13,9},{1,13},{6,2},{10,6},{... | collective-permute-start | bytes 491528 | tf_op jit(solution)/shard_map/ppermute | solution.py:218
  47.4 17.0 %collective-permute-start.26 = (bf16[256,768]{1,0:T(8,128)(2,1)S(1)}, bf16[256,768]{1,0:T(8,128)(2,1)S(1)}, u32[]{:S(2)}, u32[]{:S(2)}) collective-permute-start(bf16[256,768]{1,0:T(8,128)(2,1)S(1)} %shard_map.94.refs_9_.refs_8_), channel_id=1, source_target_pairs={{3,0},{0,1},{1,2},{2,3},{7,4},{4,5},{5,6},{6,7},{11,8},{8,9},{9,10... | collective-permute-start | bytes 1179656 | tf_op jit(solution)/shard_map/ppermute | solution.py:218
  47.4 8.4 %collective-permute-start.20 = (bf16[2,160,256]{2,1,0:T(8,128)(2,1)S(1)}, bf16[2,160,256]{2,1,0:T(8,128)(2,1)S(1)}, u32[]{:S(2)}, u32[]{:S(2)}) collective-permute-start(bf16[2,160,256]{2,1,0:T(8,128)(2,1)S(1)} %collective-permute-done.18.refs_5_), channel_id=1, source_target_pairs={{12,0},{0,4},{4,8},{8,12},{13,1},{1,5},{5,9},{9,13},{14,2},{2,6},{... | collective-permute-start | bytes 491528 | tf_op jit(solution)/shard_map/ppermute | solution.py:218
  49.7 16.7 %collective-permute-start.25 = (bf16[256,768]{1,0:T(8,128)(2,1)S(1)}, bf16[256,768]{1,0:T(8,128)(2,1)S(1)}, u32[]{:S(2)}, u32[]{:S(2)}) collective-permute-start(bf16[256,768]{1,0:T(8,128)(2,1)S(1)} %shard_map.94.refs_9_.refs_8_), channel_id=1, source_target_pairs={{1,0},{2,1},{3,2},{0,3},{5,4},{6,5},{7,6},{4,7},{9,8},{10,9},{11,1... | collective-permute-start | bytes 1179656 | tf_op jit(solution)/shard_map/ppermute | solution.py:218
  50.7 8.5 %collective-permute-start.13 = (bf16[2,256,256]{2,1,0:T(8,128)(2,1)S(1)}, bf16[2,256,256]{2,1,0:T(8,128)(2,1)S(1)}, u32[]{:S(2)}, u32[]{:S(2)}) collective-permute-start(bf16[2,256,256]{2,1,0:T(8,128)(2,1)S(1)} %get-tuple-element.53.refs_0_), channel_id=1, source_target_pairs={{4,0},{8,4},{12,8},{0,12},{5,1},{9,5},{13,9},{1,13},{6,2},{10,6},{... | collective-permute-start | bytes 786440 | tf_op jit(solution)/shard_map/ppermute | solution.py:218
  53.9 10.5 %collective-permute-start.14 = (bf16[2,256,256]{2,1,0:T(8,128)(2,1)S(1)}, bf16[2,256,256]{2,1,0:T(8,128)(2,1)S(1)}, u32[]{:S(2)}, u32[]{:S(2)}) collective-permute-start(bf16[2,256,256]{2,1,0:T(8,128)(2,1)S(1)} %get-tuple-element.54.refs_1_), channel_id=1, source_target_pairs={{12,0},{0,4},{4,8},{8,12},{13,1},{1,5},{5,9},{9,13},{14,2},{2,6},{... | collective-permute-start | bytes 786440 | tf_op jit(solution)/shard_map/ppermute | solution.py:218
  55.8 12.2 %collective-permute-start.22 = (bf16[2,256,256]{2,1,0:T(8,128)(2,1)S(1)}, bf16[2,256,256]{2,1,0:T(8,128)(2,1)S(1)}, u32[]{:S(2)}, u32[]{:S(2)}) collective-permute-start(bf16[2,256,256]{2,1,0:T(8,128)(2,1)S(1)} %get-tuple-element.53.refs_0_), channel_id=1, source_target_pairs={{12,0},{0,4},{4,8},{8,12},{13,1},{1,5},{5,9},{9,13},{14,2},{2,6},{... | collective-permute-start | bytes 786440 | tf_op jit(solution)/shard_map/ppermute | solution.py:218
  59.2 10.8 %collective-permute-start.21 = (bf16[2,256,256]{2,1,0:T(8,128)(2,1)S(1)}, bf16[2,256,256]{2,1,0:T(8,128)(2,1)S(1)}, u32[]{:S(2)}, u32[]{:S(2)}) collective-permute-start(bf16[2,256,256]{2,1,0:T(8,128)(2,1)S(1)} %get-tuple-element.54.refs_1_), channel_id=1, source_target_pairs={{4,0},{8,4},{12,8},{0,12},{5,1},{9,5},{13,9},{1,13},{6,2},{10,6},{... | collective-permute-start | bytes 786440 | tf_op jit(solution)/shard_map/ppermute | solution.py:218
  64.4 7.6 %collective-permute-start.24 = (bf16[2,256,256]{2,1,0:T(8,128)(2,1)S(1)}, bf16[2,256,256]{2,1,0:T(8,128)(2,1)S(1)}, u32[]{:S(2)}, u32[]{:S(2)}) collective-permute-start(bf16[2,256,256]{2,1,0:T(8,128)(2,1)S(1)} %collective-permute-done.14.refs_5_), channel_id=1, source_target_pairs={{12,0},{0,4},{4,8},{8,12},{13,1},{1,5},{5,9},{9,13},{14,2},{2,6},{... | collective-permute-start | bytes 786440 | tf_op jit(solution)/shard_map/ppermute | solution.py:218
  78.3 7.7 %collective-permute-start.29 = (bf16[2,256,256]{2,1,0:T(8,128)(2,1)S(1)}, bf16[2,256,256]{2,1,0:T(8,128)(2,1)S(1)}, u32[]{:S(2)}, u32[]{:S(2)}) collective-permute-start(bf16[2,256,256]{2,1,0:T(8,128)(2,1)S(1)} %get-tuple-element.62.refs_0_), channel_id=1, source_target_pairs={{4,0},{8,4},{12,8},{0,12},{5,1},{9,5},{13,9},{1,13},{6,2},{10,6},{... | collective-permute-start | bytes 786440 | tf_op jit(solution)/shard_map/ppermute | solution.py:218
  79.3 7.9 %collective-permute-start.30 = (bf16[2,256,256]{2,1,0:T(8,128)(2,1)S(1)}, bf16[2,256,256]{2,1,0:T(8,128)(2,1)S(1)}, u32[]{:S(2)}, u32[]{:S(2)}) collective-permute-start(bf16[2,256,256]{2,1,0:T(8,128)(2,1)S(1)} %get-tuple-element.63.refs_1_), channel_id=1, source_target_pairs={{12,0},{0,4},{4,8},{8,12},{13,1},{1,5},{5,9},{9,13},{14,2},{2,6},{... | collective-permute-start | bytes 786440 | tf_op jit(solution)/shard_map/ppermute | solution.py:218
  80.4 9.6 %collective-permute-start.32 = (bf16[2,256,256]{2,1,0:T(8,128)(2,1)S(1)}, bf16[2,256,256]{2,1,0:T(8,128)(2,1)S(1)}, u32[]{:S(2)}, u32[]{:S(2)}) collective-permute-start(bf16[2,256,256]{2,1,0:T(8,128)(2,1)S(1)} %get-tuple-element.62.refs_0_), channel_id=1, source_target_pairs={{12,0},{0,4},{4,8},{8,12},{13,1},{1,5},{5,9},{9,13},{14,2},{2,6},{... | collective-permute-start | bytes 786440 | tf_op jit(solution)/shard_map/ppermute | solution.py:218
  80.5 12.8 %collective-permute-start.31 = (bf16[2,256,256]{2,1,0:T(8,128)(2,1)S(1)}, bf16[2,256,256]{2,1,0:T(8,128)(2,1)S(1)}, u32[]{:S(2)}, u32[]{:S(2)}) collective-permute-start(bf16[2,256,256]{2,1,0:T(8,128)(2,1)S(1)} %get-tuple-element.63.refs_1_), channel_id=1, source_target_pairs={{4,0},{8,4},{12,8},{0,12},{5,1},{9,5},{13,9},{1,13},{6,2},{10,6},{... | collective-permute-start | bytes 786440 | tf_op jit(solution)/shard_map/ppermute | solution.py:218
  87.6 7.6 %collective-permute-start.34 = (bf16[2,256,256]{2,1,0:T(8,128)(2,1)S(1)}, bf16[2,256,256]{2,1,0:T(8,128)(2,1)S(1)}, u32[]{:S(2)}, u32[]{:S(2)}) collective-permute-start(bf16[2,256,256]{2,1,0:T(8,128)(2,1)S(1)} %collective-permute-done.30.refs_5_), channel_id=1, source_target_pairs={{12,0},{0,4},{4,8},{8,12},{13,1},{1,5},{5,9},{9,13},{14,2},{2,6},{... | collective-permute-start | bytes 786440 | tf_op jit(solution)/shard_map/ppermute | solution.py:218
  89.3 9.7 %collective-permute-start.35 = (bf16[256,256]{1,0:T(8,128)(2,1)S(1)}, bf16[256,256]{1,0:T(8,128)(2,1)S(1)}, u32[]{:S(2)}, u32[]{:S(2)}) collective-permute-start(bf16[256,256]{1,0:T(8,128)(2,1)S(1)} %get-tuple-element.71), channel_id=1, source_target_pairs={{3,0},{0,1},{1,2},{2,3},{7,4},{4,5},{5,6},{6,7},{11,8},{8,9},{9,10... | collective-permute-start | bytes 393224 | tf_op jit(solution)/shard_map/ppermute | solution.py:218
  90.1 8.9 %collective-permute-start.36 = (bf16[256,256]{1,0:T(8,128)(2,1)S(1)}, bf16[256,256]{1,0:T(8,128)(2,1)S(1)}, u32[]{:S(2)}, u32[]{:S(2)}) collective-permute-start(bf16[256,256]{1,0:T(8,128)(2,1)S(1)} %get-tuple-element.72), channel_id=1, source_target_pairs={{1,0},{2,1},{3,2},{0,3},{5,4},{6,5},{7,6},{4,7},{9,8},{10,9},{11,1... | collective-permute-start | bytes 393224 | tf_op jit(solution)/shard_map/ppermute | solution.py:218
  121.1 16.5 %all-to-all-start.2 = ((bf16[16,128,128]{2,1,0:T(8,128)(2,1)}), bf16[16,128,128]{2,1,0:T(8,128)(2,1)S(1)}, u32[]{:S(2)}, u32[]{:S(2)}) async-start(bf16[16,128,128]{2,1,0:T(8,128)(2,1)} %shard_map.103), calls=%async_computation.2 | async-start | bytes 1048576 | tf_op jit(solution)/shard_map/all_to_all | solution.py:316
  (13 other events, 112.7 us)

commit v13 on v12

--- a/solution.py
+++ b/solution.py
@@ -265,7 +265,7 @@
     )
     nodes = [nodes[0], n1, n2, n3]
     x_near = neighbours(x_low, x_high, "z")
-    x0, x1 = x_near[:2]
+    x0, x1, mask = lax.optimization_barrier((*x_near[:2], mask))
     x_wide = rounds(x_low, x_high, x_near, (x0, x1), "z")
     u_near = neighbours(*scaled, "x")
     scaled = rounds(*scaled, u_near, u_near[:2], "x")
@@ -280,7 +280,6 @@
         flops=400_000_000,
         moved=3_000_000,
     )(*x_wide, weights, *nodes)
-    *s, mask = lax.optimization_barrier((*s, mask))
     s_near = neighbours(*s, "x")
     after, before = near(mask, "z")
     s0, s1, scaled = lax.optimization_barrier((*s_near[:2], scaled))

time: 139 us -> 137 us (0.986)
  starting transfers between devices: 67.4 us -> 60.6 us
  waiting for transfers between devices: 31.8 us -> 36.2 us
    ppermute x37, starting transfers between devices: 57.8 us -> 51.1 us  [fetch(): return lax.ppermute(value, axis, [((i + shift) % 4, i) for i in range(4)])]
    ppermute x37, waiting for transfers between devices: 21.6 us -> 26.1 us  [fetch(): return lax.ppermute(value, axis, [((i + shift) % 4, i) for i in range(4)])]
  transfers between devices with their start and end apart: 40 -> 40, of which waited for: 18 -> 15; matrix products, arithmetic and copies ran while one was open for 2% -> 2% of each run, Pallas kernels for 5% -> 6%
where the time goes in v13:
time: 137 us; the launch traced here: 136 us
  starting transfers between devices  60.6 us (44%)
  waiting for transfers between devices  36.2 us (26%)
  blocking collectives  20 us (15%)
  Pallas kernels  14.4 us (11%)
  local copies, waits for them, and re-layouts  3.94 us (3%)
    ppermute x37, starting transfers between devices, fetch(): return lax.ppermute(value, axis, [((i + shift) % 4, i) for i in range(4)])  51.1 us
    ppermute x37, waiting for transfers between devices, fetch(): return lax.ppermute(value, axis, [((i + shift) % 4, i) for i in range(4)])  26.1 us
    all_to_all x1, blocking collectives, body(): lax.all_to_all(part.reshape(32, 128, 128), ('y', 'c', 'x'), 0, 0, tiled=T...  20 us
    all_to_all x1, waiting for transfers between devices, body(): done = lax.all_to_all(done, dom, 0, 0, tiled=True)  10.1 us
    all_to_all x1, starting transfers between devices, body(): lax.all_to_all(features.reshape(96, 8, 256).transpose(1, 0, 2), feat, 0,...  4.8 us
    all_to_all x1, starting transfers between devices, body(): done = lax.all_to_all(done, dom, 0, 0, tiled=True)  4.66 us
    pallas_call x1, Pallas kernels, body(): call(first_mix_kernel, (shape((256, 256), BF),) * 4 + (half, half, shape(...  4.64 us
    pallas_call x1, Pallas kernels, body(): call(second_mix_kernel, shape((8, 4, 128, 128), BF), [VMEM] * 22 + [SMEM]...  3.82 us
  transfers between devices with their start and end apart: 40, of which 15 were waited for; matrix products, arithmetic and copies ran while one was open for 2% of the time, Pallas kernels for 6%

profile of v13, /device:TPU:0, one launch (start us, length us, event | category | flops | bytes accessed | tf_op | source)
XLA Modules:
  0.0 136.1 jit_solution(4334557972967019944)
XLA Ops:
  3.4 4.8 %all-to-all-start = ((bf16[8,96,256]{2,1,0:T(8,128)(2,1)}), bf16[8,96,256]{2,1,0:T(8,128)(2,1)S(1)}, u32[]{:S(2)}, u32[]{:S(2)}) async-start(bf16[8,96,256]{2,1,0:T(8,128)(2,1)} %bitcast.22), calls=%async_computation | async-start | bytes 786432 | tf_op jit(solution)/shard_map/all_to_all | solution.py:243
  9.2 3.6 %collective-permute-start.3 = (bf16[2,96,256]{2,1,0:T(8,128)(2,1)S(1)}, bf16[2,96,256]{2,1,0:T(8,128)(2,1)S(1)}, u32[]{:S(2)}, u32[]{:S(2)}) collective-permute-start(bf16[2,96,256]{2,1,0:T(8,128)(2,1)S(1)} %pad_maximum_fusion.refs_0_), channel_id=1, source_target_pairs={{64,0},{96,32},{0,64},{32,96},{65,1},{97,33},{1,65},{33,97},{66,2}... | collective-permute-start | bytes 294920 | tf_op jit(solution)/shard_map/ppermute | solution.py:218
  13.3 2.7 %collective-permute-start.1 = (bf16[2,96,256]{2,1,0:T(8,128)(2,1)S(1)}, bf16[2,96,256]{2,1,0:T(8,128)(2,1)S(1)}, u32[]{:S(2)}, u32[]{:S(2)}) collective-permute-start(bf16[2,96,256]{2,1,0:T(8,128)(2,1)S(1)} %pad_maximum_fusion.refs_0_), channel_id=1, source_target_pairs={{32,0},{64,32},{96,64},{0,96},{33,1},{65,33},{97,65},{1,97},{34,2}... | collective-permute-start | bytes 294920 | tf_op jit(solution)/shard_map/ppermute | solution.py:218
  16.3 4.0 %collective-permute-start.6 = (bf16[176,256]{1,0:T(8,128)(2,1)S(1)}, bf16[176,256]{1,0:T(8,128)(2,1)S(1)}, u32[]{:S(2)}, u32[]{:S(2)}) collective-permute-start(bf16[176,256]{1,0:T(8,128)(2,1)S(1)} %shard_map.96.refs_9_.refs_0_.refs_16_.refs_23_), channel_id=1, source_target_pairs={{2,0},{3,1},{0,2},{1,3},{6,4},{7,5},{4,6},{5,7},{10,8},{11,9},{8,1... | collective-permute-start | bytes 270344 | tf_op jit(solution)/shard_map/ppermute | solution.py:218
  21.3 2.5 %collective-permute-start.4 = (bf16[176,256]{1,0:T(8,128)(2,1)S(1)}, bf16[176,256]{1,0:T(8,128)(2,1)S(1)}, u32[]{:S(2)}, u32[]{:S(2)}) collective-permute-start(bf16[176,256]{1,0:T(8,128)(2,1)S(1)} %shard_map.96.refs_9_.refs_0_.refs_16_.refs_23_), channel_id=1, source_target_pairs={{1,0},{2,1},{3,2},{0,3},{5,4},{6,5},{7,6},{4,7},{9,8},{10,9},{11,1... | collective-permute-start | bytes 270344 | tf_op jit(solution)/shard_map/ppermute | solution.py:218
  26.0 3.5 %collective-permute-start.7 = (bf16[4,96,256]{2,1,0:T(8,128)(2,1)S(1)}, bf16[4,96,256]{2,1,0:T(8,128)(2,1)S(1)}, u32[]{:S(2)}, u32[]{:S(2)}) collective-permute-start(bf16[4,96,256]{2,1,0:T(8,128)(2,1)S(1)} %get-tuple-element.44.refs_0_.refs_13_), channel_id=1, source_target_pairs={{1,0},{2,1},{3,2},{0,3},{5,4},{6,5},{7,6},{4,7},{9,8},{10,9},{11,1... | collective-permute-start | bytes 589832 | tf_op jit(solution)/shard_map/ppermute | solution.py:218
  29.6 1.6 %collective-permute-start.17 = (bf16[2,160,256]{2,1,0:T(8,128)(2,1)S(1)}, bf16[2,160,256]{2,1,0:T(8,128)(2,1)S(1)}, u32[]{:S(2)}, u32[]{:S(2)}) collective-permute-start(bf16[2,160,256]{2,1,0:T(8,128)(2,1)S(1)} %get-tuple-element.55.refs_0_), channel_id=1, source_target_pairs={{12,0},{0,4},{4,8},{8,12},{13,1},{1,5},{5,9},{9,13},{14,2},{2,6},{... | collective-permute-start | bytes 491528 | tf_op jit(solution)/shard_map/ppermute | solution.py:218
  31.2 1.7 %collective-permute-start.15 = (bf16[2,160,256]{2,1,0:T(8,128)(2,1)S(1)}, bf16[2,160,256]{2,1,0:T(8,128)(2,1)S(1)}, u32[]{:S(2)}, u32[]{:S(2)}) collective-permute-start(bf16[2,160,256]{2,1,0:T(8,128)(2,1)S(1)} %get-tuple-element.55.refs_0_), channel_id=1, source_target_pairs={{4,0},{8,4},{12,8},{0,12},{5,1},{9,5},{13,9},{1,13},{6,2},{10,6},{... | collective-permute-start | bytes 491528 | tf_op jit(solution)/shard_map/ppermute | solution.py:218
  34.3 4.2 %collective-permute-done.8.refs_5_.refs_18_ = bf16[4,96,256]{2,1,0:T(8,128)(2,1)S(1)} collective-permute-done((bf16[4,96,256]{2,1,0:T(8,128)(2,1)S(1)}, bf16[4,96,256]{2,1,0:T(8,128)(2,1)S(1)}, u32[]{:S(2)}, u32[]{:S(2)}) %collective-permute-start.8) | collective-permute-done | bytes 196640 | tf_op jit(solution)/shard_map/ppermute | solution.py:218
  38.4 2.5 %collective-permute-start.11 = (bf16[4,96,256]{2,1,0:T(8,128)(2,1)S(1)}, bf16[4,96,256]{2,1,0:T(8,128)(2,1)S(1)}, u32[]{:S(2)}, u32[]{:S(2)}) collective-permute-start(bf16[4,96,256]{2,1,0:T(8,128)(2,1)S(1)} %collective-permute-done.7.refs_2_.refs_15_), channel_id=1, source_target_pairs={{1,0},{2,1},{3,2},{0,3},{5,4},{6,5},{7,6},{4,7},{9,8},{10,9},{11,1... | collective-permute-start | bytes 589832 | tf_op jit(solution)/shard_map/ppermute | solution.py:218
  41.0 1.7 %collective-permute-start.16 = (bf16[2,160,256]{2,1,0:T(8,128)(2,1)S(1)}, bf16[2,160,256]{2,1,0:T(8,128)(2,1)S(1)}, u32[]{:S(2)}, u32[]{:S(2)}) collective-permute-start(bf16[2,160,256]{2,1,0:T(8,128)(2,1)S(1)} %get-tuple-element.56.refs_1_), channel_id=1, source_target_pairs={{4,0},{8,4},{12,8},{0,12},{5,1},{9,5},{13,9},{1,13},{6,2},{10,6},{... | collective-permute-start | bytes 491528 | tf_op jit(solution)/shard_map/ppermute | solution.py:218
  45.4 1.9 %collective-permute-done.11.refs_6_.refs_19_ = bf16[4,96,256]{2,1,0:T(8,128)(2,1)S(1)} collective-permute-done((bf16[4,96,256]{2,1,0:T(8,128)(2,1)S(1)}, bf16[4,96,256]{2,1,0:T(8,128)(2,1)S(1)}, u32[]{:S(2)}, u32[]{:S(2)}) %collective-permute-start.11) | collective-permute-done | bytes 196640 | tf_op jit(solution)/shard_map/ppermute | solution.py:218
  48.1 1.7 %collective-permute-done.12.refs_7_.refs_20_ = bf16[4,96,256]{2,1,0:T(8,128)(2,1)S(1)} collective-permute-done((bf16[4,96,256]{2,1,0:T(8,128)(2,1)S(1)}, bf16[4,96,256]{2,1,0:T(8,128)(2,1)S(1)}, u32[]{:S(2)}, u32[]{:S(2)}) %collective-permute-start.12) | collective-permute-done | bytes 196640 | tf_op jit(solution)/shard_map/ppermute | solution.py:218
  52.5 3.1 %collective-permute-done.20.refs_7_ = bf16[2,160,256]{2,1,0:T(8,128)(2,1)S(1)} collective-permute-done((bf16[2,160,256]{2,1,0:T(8,128)(2,1)S(1)}, bf16[2,160,256]{2,1,0:T(8,128)(2,1)S(1)}, u32[]{:S(2)}, u32[]{:S(2)}) %collective-permute-start.20) | collective-permute-done | bytes 163872 | tf_op jit(solution)/shard_map/ppermute | solution.py:218
  56.4 3.2 %collective-permute-done.13.refs_2_ = bf16[2,256,256]{2,1,0:T(8,128)(2,1)S(1)} collective-permute-done((bf16[2,256,256]{2,1,0:T(8,128)(2,1)S(1)}, bf16[2,256,256]{2,1,0:T(8,128)(2,1)S(1)}, u32[]{:S(2)}, u32[]{:S(2)}) %collective-permute-start.13) | collective-permute-done | bytes 262176 | tf_op jit(solution)/shard_map/ppermute | solution.py:218
  62.2 2.0 %collective-permute-start.24 = (bf16[2,256,256]{2,1,0:T(8,128)(2,1)S(1)}, bf16[2,256,256]{2,1,0:T(8,128)(2,1)S(1)}, u32[]{:S(2)}, u32[]{:S(2)}) collective-permute-start(bf16[2,256,256]{2,1,0:T(8,128)(2,1)S(1)} %collective-permute-done.14.refs_5_), channel_id=1, source_target_pairs={{12,0},{0,4},{4,8},{8,12},{13,1},{1,5},{5,9},{9,13},{14,2},{2,6},{... | collective-permute-start | bytes 786440 | tf_op jit(solution)/shard_map/ppermute | solution.py:218
  64.3 1.5 %collective-permute-start.28 = (bf16[128,768]{1,0:T(8,128)(2,1)S(1)}, bf16[128,768]{1,0:T(8,128)(2,1)S(1)}, u32[]{:S(2)}, u32[]{:S(2)}) collective-permute-start(bf16[128,768]{1,0:T(8,128)(2,1)S(1)} %slice.19), channel_id=1, source_target_pairs={{3,0},{0,1},{1,2},{2,3},{7,4},{4,5},{5,6},{6,7},{11,8},{8,9},{9,10... | collective-permute-start | bytes 589832 | tf_op jit(solution)/shard_map/ppermute | solution.py:218
  65.8 2.1 %collective-permute-start.27 = (bf16[128,768]{1,0:T(8,128)(2,1)S(1)}, bf16[128,768]{1,0:T(8,128)(2,1)S(1)}, u32[]{:S(2)}, u32[]{:S(2)}) collective-permute-start(bf16[128,768]{1,0:T(8,128)(2,1)S(1)} %slice.18), channel_id=1, source_target_pairs={{1,0},{2,1},{3,2},{0,3},{5,4},{6,5},{7,6},{4,7},{9,8},{10,9},{11,1... | collective-permute-start | bytes 589832 | tf_op jit(solution)/shard_map/ppermute | solution.py:218
  67.9 3.4 %collective-permute-done.28.refs_13_.refs_12_ = bf16[128,768]{1,0:T(8,128)(2,1)S(1)} collective-permute-done((bf16[128,768]{1,0:T(8,128)(2,1)S(1)}, bf16[128,768]{1,0:T(8,128)(2,1)S(1)}, u32[]{:S(2)}, u32[]{:S(2)}) %collective-permute-start.28) | collective-permute-done | bytes 196640 | tf_op jit(solution)/shard_map/ppermute | solution.py:218
  71.7 4.6 %shard_map.100 = (bf16[256,256]{1,0:T(8,128)(2,1)S(1)}, bf16[256,256]{1,0:T(8,128)(2,1)S(1)}, bf16[256,256]{1,0:T(8,128)(2,1)S(1)}, bf16[256,256]{1,0:T(8,128)(2...) custom-call(bf16[2,256,256]{2,1,0:T(8,128)(2,1)S(1)} %get-tuple-element.53.refs_, ...), custom_call_target="tpu_custom_call" | custom-call | flops 700000000 | bytes 8000000 | tf_op jit(solution)/shard_map/pallas_call | solution.py:291
  76.4 1.6 %collective-permute-start.29 = (bf16[2,256,256]{2,1,0:T(8,128)(2,1)S(1)}, bf16[2,256,256]{2,1,0:T(8,128)(2,1)S(1)}, u32[]{:S(2)}, u32[]{:S(2)}) collective-permute-start(bf16[2,256,256]{2,1,0:T(8,128)(2,1)S(1)} %get-tuple-element.62.refs_0_), channel_id=1, source_target_pairs={{4,0},{8,4},{12,8},{0,12},{5,1},{9,5},{13,9},{1,13},{6,2},{10,6},{... | collective-permute-start | bytes 786440 | tf_op jit(solution)/shard_map/ppermute | solution.py:218
  78.6 3.1 %collective-permute-start.31 = (bf16[2,256,256]{2,1,0:T(8,128)(2,1)S(1)}, bf16[2,256,256]{2,1,0:T(8,128)(2,1)S(1)}, u32[]{:S(2)}, u32[]{:S(2)}) collective-permute-start(bf16[2,256,256]{2,1,0:T(8,128)(2,1)S(1)} %get-tuple-element.63.refs_1_), channel_id=1, source_target_pairs={{4,0},{8,4},{12,8},{0,12},{5,1},{9,5},{13,9},{1,13},{6,2},{10,6},{... | collective-permute-start | bytes 786440 | tf_op jit(solution)/shard_map/ppermute | solution.py:218
  81.7 2.1 %collective-permute-done.29.refs_2_ = bf16[2,256,256]{2,1,0:T(8,128)(2,1)S(1)} collective-permute-done((bf16[2,256,256]{2,1,0:T(8,128)(2,1)S(1)}, bf16[2,256,256]{2,1,0:T(8,128)(2,1)S(1)}, u32[]{:S(2)}, u32[]{:S(2)}) %collective-permute-start.29) | collective-permute-done | bytes 262176 | tf_op jit(solution)/shard_map/ppermute | solution.py:218
  83.9 1.7 %collective-permute-done.30.refs_5_ = bf16[2,256,256]{2,1,0:T(8,128)(2,1)S(1)} collective-permute-done((bf16[2,256,256]{2,1,0:T(8,128)(2,1)S(1)}, bf16[2,256,256]{2,1,0:T(8,128)(2,1)S(1)}, u32[]{:S(2)}, u32[]{:S(2)}) %collective-permute-start.30) | collective-permute-done | bytes 262176 | tf_op jit(solution)/shard_map/ppermute | solution.py:218
  85.6 2.0 %collective-permute-start.34 = (bf16[2,256,256]{2,1,0:T(8,128)(2,1)S(1)}, bf16[2,256,256]{2,1,0:T(8,128)(2,1)S(1)}, u32[]{:S(2)}, u32[]{:S(2)}) collective-permute-start(bf16[2,256,256]{2,1,0:T(8,128)(2,1)S(1)} %collective-permute-done.30.refs_5_), channel_id=1, source_target_pairs={{12,0},{0,4},{4,8},{8,12},{13,1},{1,5},{5,9},{9,13},{14,2},{2,6},{... | collective-permute-start | bytes 786440 | tf_op jit(solution)/shard_map/ppermute | solution.py:218
  87.6 1.5 %collective-permute-start.35 = (bf16[256,256]{1,0:T(8,128)(2,1)S(1)}, bf16[256,256]{1,0:T(8,128)(2,1)S(1)}, u32[]{:S(2)}, u32[]{:S(2)}) collective-permute-start(bf16[256,256]{1,0:T(8,128)(2,1)S(1)} %get-tuple-element.71), channel_id=1, source_target_pairs={{3,0},{0,1},{1,2},{2,3},{7,4},{4,5},{5,6},{6,7},{11,8},{8,9},{9,10... | collective-permute-start | bytes 393224 | tf_op jit(solution)/shard_map/ppermute | solution.py:218
  89.1 2.0 %collective-permute-start.36 = (bf16[256,256]{1,0:T(8,128)(2,1)S(1)}, bf16[256,256]{1,0:T(8,128)(2,1)S(1)}, u32[]{:S(2)}, u32[]{:S(2)}) collective-permute-start(bf16[256,256]{1,0:T(8,128)(2,1)S(1)} %get-tuple-element.72), channel_id=1, source_target_pairs={{1,0},{2,1},{3,2},{0,3},{5,4},{6,5},{7,6},{4,7},{9,8},{10,9},{11,1... | collective-permute-start | bytes 393224 | tf_op jit(solution)/shard_map/ppermute | solution.py:218
  93.2 3.8 %shard_map.101 = bf16[8,4,128,128]{3,2,1,0:T(8,128)(2,1)S(1)} custom-call(bf16[2,256,256]{2,1,0:T(8,128)(2,1)S(1)} %get-tuple-element.62.refs_0_, bf16[2,256,256]{2,1,0:T(8,128)(2,1)S(1)} %get-tuple-element.63.refs_1_, bf16[2,256,256]{2,1,0:T(8,128)(2,1)S(1)} %collective-permute-done.29.refs_2_, bf16[2,256,256]{2,1,0:T(8,128)(2,1)S(1)} %collective-permute-done.31.refs_3_, ...), custom_call_target="tpu_custom_call" | custom-call | flops 900000000 | bytes 8000000 | tf_op jit(solution)/shard_map/pallas_call | solution.py:303
  97.5 20.0 %all_to_all.15.part_ref = bf16[32,128,128]{2,1,0:T(8,128)(2,1)S(1)} all-to-all(bf16[32,128,128]{2,1,0:T(8,128)(2,1)S(1)} %bitcast.23), channel_id=1, replica_groups=mesh['y'=4,'c'=2,'x'=4,'z'=4] {'y','c','x'}, dimensions={0} | all-to-all | bytes 2097152 | tf_op jit(solution)/shard_map/all_to_all | solution.py:312
  118.6 4.7 %all-to-all-start.2 = ((bf16[16,128,128]{2,1,0:T(8,128)(2,1)}), bf16[16,128,128]{2,1,0:T(8,128)(2,1)S(1)}, u32[]{:S(2)}, u32[]{:S(2)}) async-start(bf16[16,128,128]{2,1,0:T(8,128)(2,1)} %shard_map.103), calls=%async_computation.2 | async-start | bytes 1048576 | tf_op jit(solution)/shard_map/all_to_all | solution.py:315
  123.2 1.5 %shard_map.102 = bf16[256,1024]{1,0:T(8,128)(2,1)} custom-call(bf16[256,256]{1,0:T(8,128)(2,1)S(1)} %get-tuple-element.74.h0_ref, bf16[256,256]{1,0:T(8,128)(2,1)S(1)} %collective-permute-done.35.h1_ref, bf16[256,256]{1,0:T(8,128)(2,1)S(1)} %collective-permute-done.36.h2_ref, bf16[256,256]{1,0:T(8,128)(2,1)S(1)} %collective-permute-done.37.h3_ref, ...), custom_call_target="tpu_custom_call" | custom-call | bytes 1000000 | tf_op jit(solution)/shard_map/pallas_call | solution.py:316
  124.8 10.1 %all-to-all-done.2.in_ref = bf16[16,128,128]{2,1,0:T(8,128)(2,1)S(1)} async-done(((bf16[16,128,128]{2,1,0:T(8,128)(2,1)}), bf16[16,128,128]{2,1,0:T(8,128)(2,1)S(1)}, u32[]{:S(2)}, u32[]{:S(2)}) %all-to-all-start.2) | async-done | bytes 524320 | tf_op jit(solution)/shard_map/all_to_all | solution.py:315
  (85 shorter events, 24.7 us)
Async XLA Ops:
  1.5 7.6 %collective-permute-start = (bf16[96,256]{1,0:T(8,128)(2,1)S(1)}, bf16[96,256]{1,0:T(8,128)(2,1)S(1)}, u32[]{:S(2)}, u32[]{:S(2)}) collective-permute-start(bf16[96,256]{1,0:T(8,128)(2,1)S(1)} %constant_dynamic-slice_fusion), channel_id=1, source_target_pairs={{0,16},{16,0},{1,17},{17,1},{2,18},{18,2},{3,19},{19,3},{4,20},{20... | collective-permute-start | bytes 147464 | tf_op jit(solution)/shard_map/ppermute | solution.py:247
  3.4 21.2 %all-to-all-start = ((bf16[8,96,256]{2,1,0:T(8,128)(2,1)}), bf16[8,96,256]{2,1,0:T(8,128)(2,1)S(1)}, u32[]{:S(2)}, u32[]{:S(2)}) async-start(bf16[8,96,256]{2,1,0:T(8,128)(2,1)} %bitcast.22), calls=%async_computation | async-start | bytes 786432 | tf_op jit(solution)/shard_map/all_to_all | solution.py:243
  9.2 12.2 %collective-permute-start.3 = (bf16[2,96,256]{2,1,0:T(8,128)(2,1)S(1)}, bf16[2,96,256]{2,1,0:T(8,128)(2,1)S(1)}, u32[]{:S(2)}, u32[]{:S(2)}) collective-permute-start(bf16[2,96,256]{2,1,0:T(8,128)(2,1)S(1)} %pad_maximum_fusion.refs_0_), channel_id=1, source_target_pairs={{64,0},{96,32},{0,64},{32,96},{65,1},{97,33},{1,65},{33,97},{66,2}... | collective-permute-start | bytes 294920 | tf_op jit(solution)/shard_map/ppermute | solution.py:218
  12.8 11.1 %collective-permute-start.2 = (bf16[2,96,256]{2,1,0:T(8,128)(2,1)S(1)}, bf16[2,96,256]{2,1,0:T(8,128)(2,1)S(1)}, u32[]{:S(2)}, u32[]{:S(2)}) collective-permute-start(bf16[2,96,256]{2,1,0:T(8,128)(2,1)S(1)} %pad_maximum_fusion.refs_0_), channel_id=1, source_target_pairs={{96,0},{0,32},{32,64},{64,96},{97,1},{1,33},{33,65},{65,97},{98,2}... | collective-permute-start | bytes 294920 | tf_op jit(solution)/shard_map/ppermute | solution.py:218
  13.3 10.5 %collective-permute-start.1 = (bf16[2,96,256]{2,1,0:T(8,128)(2,1)S(1)}, bf16[2,96,256]{2,1,0:T(8,128)(2,1)S(1)}, u32[]{:S(2)}, u32[]{:S(2)}) collective-permute-start(bf16[2,96,256]{2,1,0:T(8,128)(2,1)S(1)} %pad_maximum_fusion.refs_0_), channel_id=1, source_target_pairs={{32,0},{64,32},{96,64},{0,96},{33,1},{65,33},{97,65},{1,97},{34,2}... | collective-permute-start | bytes 294920 | tf_op jit(solution)/shard_map/ppermute | solution.py:218
  16.3 8.3 %collective-permute-start.6 = (bf16[176,256]{1,0:T(8,128)(2,1)S(1)}, bf16[176,256]{1,0:T(8,128)(2,1)S(1)}, u32[]{:S(2)}, u32[]{:S(2)}) collective-permute-start(bf16[176,256]{1,0:T(8,128)(2,1)S(1)} %shard_map.96.refs_9_.refs_0_.refs_16_.refs_23_), channel_id=1, source_target_pairs={{2,0},{3,1},{0,2},{1,3},{6,4},{7,5},{4,6},{5,7},{10,8},{11,9},{8,1... | collective-permute-start | bytes 270344 | tf_op jit(solution)/shard_map/ppermute | solution.py:218
  29.6 8.9 %collective-permute-start.8 = (bf16[4,96,256]{2,1,0:T(8,128)(2,1)S(1)}, bf16[4,96,256]{2,1,0:T(8,128)(2,1)S(1)}, u32[]{:S(2)}, u32[]{:S(2)}) collective-permute-start(bf16[4,96,256]{2,1,0:T(8,128)(2,1)S(1)} %get-tuple-element.45.refs_1_.refs_14_), channel_id=1, source_target_pairs={{3,0},{0,1},{1,2},{2,3},{7,4},{4,5},{5,6},{6,7},{11,8},{8,9},{9,10... | collective-permute-start | bytes 589832 | tf_op jit(solution)/shard_map/ppermute | solution.py:218
  29.6 8.8 %collective-permute-start.17 = (bf16[2,160,256]{2,1,0:T(8,128)(2,1)S(1)}, bf16[2,160,256]{2,1,0:T(8,128)(2,1)S(1)}, u32[]{:S(2)}, u32[]{:S(2)}) collective-permute-start(bf16[2,160,256]{2,1,0:T(8,128)(2,1)S(1)} %get-tuple-element.55.refs_0_), channel_id=1, source_target_pairs={{12,0},{0,4},{4,8},{8,12},{13,1},{1,5},{5,9},{9,13},{14,2},{2,6},{... | collective-permute-start | bytes 491528 | tf_op jit(solution)/shard_map/ppermute | solution.py:218
  31.2 9.8 %collective-permute-start.15 = (bf16[2,160,256]{2,1,0:T(8,128)(2,1)S(1)}, bf16[2,160,256]{2,1,0:T(8,128)(2,1)S(1)}, u32[]{:S(2)}, u32[]{:S(2)}) collective-permute-start(bf16[2,160,256]{2,1,0:T(8,128)(2,1)S(1)} %get-tuple-element.55.refs_0_), channel_id=1, source_target_pairs={{4,0},{8,4},{12,8},{0,12},{5,1},{9,5},{13,9},{1,13},{6,2},{10,6},{... | collective-permute-start | bytes 491528 | tf_op jit(solution)/shard_map/ppermute | solution.py:218
  32.9 9.7 %collective-permute-start.10 = (bf16[4,96,256]{2,1,0:T(8,128)(2,1)S(1)}, bf16[4,96,256]{2,1,0:T(8,128)(2,1)S(1)}, u32[]{:S(2)}, u32[]{:S(2)}) collective-permute-start(bf16[4,96,256]{2,1,0:T(8,128)(2,1)S(1)} %get-tuple-element.44.refs_0_.refs_13_), channel_id=1, source_target_pairs={{3,0},{0,1},{1,2},{2,3},{7,4},{4,5},{5,6},{6,7},{11,8},{8,9},{9,10... | collective-permute-start | bytes 589832 | tf_op jit(solution)/shard_map/ppermute | solution.py:218
  32.9 8.1 %collective-permute-start.18 = (bf16[2,160,256]{2,1,0:T(8,128)(2,1)S(1)}, bf16[2,160,256]{2,1,0:T(8,128)(2,1)S(1)}, u32[]{:S(2)}, u32[]{:S(2)}) collective-permute-start(bf16[2,160,256]{2,1,0:T(8,128)(2,1)S(1)} %get-tuple-element.56.refs_1_), channel_id=1, source_target_pairs={{12,0},{0,4},{4,8},{8,12},{13,1},{1,5},{5,9},{9,13},{14,2},{2,6},{... | collective-permute-start | bytes 491528 | tf_op jit(solution)/shard_map/ppermute | solution.py:218
  38.4 8.9 %collective-permute-start.11 = (bf16[4,96,256]{2,1,0:T(8,128)(2,1)S(1)}, bf16[4,96,256]{2,1,0:T(8,128)(2,1)S(1)}, u32[]{:S(2)}, u32[]{:S(2)}) collective-permute-start(bf16[4,96,256]{2,1,0:T(8,128)(2,1)S(1)} %collective-permute-done.7.refs_2_.refs_15_), channel_id=1, source_target_pairs={{1,0},{2,1},{3,2},{0,3},{5,4},{6,5},{7,6},{4,7},{9,8},{10,9},{11,1... | collective-permute-start | bytes 589832 | tf_op jit(solution)/shard_map/ppermute | solution.py:218
  41.0 8.9 %collective-permute-start.12 = (bf16[4,96,256]{2,1,0:T(8,128)(2,1)S(1)}, bf16[4,96,256]{2,1,0:T(8,128)(2,1)S(1)}, u32[]{:S(2)}, u32[]{:S(2)}) collective-permute-start(bf16[4,96,256]{2,1,0:T(8,128)(2,1)S(1)} %collective-permute-done.8.refs_5_.refs_18_), channel_id=1, source_target_pairs={{3,0},{0,1},{1,2},{2,3},{7,4},{4,5},{5,6},{6,7},{11,8},{8,9},{9,10... | collective-permute-start | bytes 589832 | tf_op jit(solution)/shard_map/ppermute | solution.py:218
  41.0 9.5 %collective-permute-start.16 = (bf16[2,160,256]{2,1,0:T(8,128)(2,1)S(1)}, bf16[2,160,256]{2,1,0:T(8,128)(2,1)S(1)}, u32[]{:S(2)}, u32[]{:S(2)}) collective-permute-start(bf16[2,160,256]{2,1,0:T(8,128)(2,1)S(1)} %get-tuple-element.56.refs_1_), channel_id=1, source_target_pairs={{4,0},{8,4},{12,8},{0,12},{5,1},{9,5},{13,9},{1,13},{6,2},{10,6},{... | collective-permute-start | bytes 491528 | tf_op jit(solution)/shard_map/ppermute | solution.py:218
  42.6 9.1 %collective-permute-start.19 = (bf16[2,160,256]{2,1,0:T(8,128)(2,1)S(1)}, bf16[2,160,256]{2,1,0:T(8,128)(2,1)S(1)}, u32[]{:S(2)}, u32[]{:S(2)}) collective-permute-start(bf16[2,160,256]{2,1,0:T(8,128)(2,1)S(1)} %collective-permute-done.15.refs_2_), channel_id=1, source_target_pairs={{4,0},{8,4},{12,8},{0,12},{5,1},{9,5},{13,9},{1,13},{6,2},{10,6},{... | collective-permute-start | bytes 491528 | tf_op jit(solution)/shard_map/ppermute | solution.py:218
  44.1 18.1 %collective-permute-start.26 = (bf16[256,768]{1,0:T(8,128)(2,1)S(1)}, bf16[256,768]{1,0:T(8,128)(2,1)S(1)}, u32[]{:S(2)}, u32[]{:S(2)}) collective-permute-start(bf16[256,768]{1,0:T(8,128)(2,1)S(1)} %shard_map.94.refs_9_.refs_8_), channel_id=1, source_target_pairs={{3,0},{0,1},{1,2},{2,3},{7,4},{4,5},{5,6},{6,7},{11,8},{8,9},{9,10... | collective-permute-start | bytes 1179656 | tf_op jit(solution)/shard_map/ppermute | solution.py:218
  47.3 8.3 %collective-permute-start.20 = (bf16[2,160,256]{2,1,0:T(8,128)(2,1)S(1)}, bf16[2,160,256]{2,1,0:T(8,128)(2,1)S(1)}, u32[]{:S(2)}, u32[]{:S(2)}) collective-permute-start(bf16[2,160,256]{2,1,0:T(8,128)(2,1)S(1)} %collective-permute-done.18.refs_5_), channel_id=1, source_target_pairs={{12,0},{0,4},{4,8},{8,12},{13,1},{1,5},{5,9},{9,13},{14,2},{2,6},{... | collective-permute-start | bytes 491528 | tf_op jit(solution)/shard_map/ppermute | solution.py:218
  49.8 14.4 %collective-permute-start.25 = (bf16[256,768]{1,0:T(8,128)(2,1)S(1)}, bf16[256,768]{1,0:T(8,128)(2,1)S(1)}, u32[]{:S(2)}, u32[]{:S(2)}) collective-permute-start(bf16[256,768]{1,0:T(8,128)(2,1)S(1)} %shard_map.94.refs_9_.refs_8_), channel_id=1, source_target_pairs={{1,0},{2,1},{3,2},{0,3},{5,4},{6,5},{7,6},{4,7},{9,8},{10,9},{11,1... | collective-permute-start | bytes 1179656 | tf_op jit(solution)/shard_map/ppermute | solution.py:218
  50.4 9.2 %collective-permute-start.13 = (bf16[2,256,256]{2,1,0:T(8,128)(2,1)S(1)}, bf16[2,256,256]{2,1,0:T(8,128)(2,1)S(1)}, u32[]{:S(2)}, u32[]{:S(2)}) collective-permute-start(bf16[2,256,256]{2,1,0:T(8,128)(2,1)S(1)} %get-tuple-element.53.refs_0_), channel_id=1, source_target_pairs={{4,0},{8,4},{12,8},{0,12},{5,1},{9,5},{13,9},{1,13},{6,2},{10,6},{... | collective-permute-start | bytes 786440 | tf_op jit(solution)/shard_map/ppermute | solution.py:218
  51.8 10.5 %collective-permute-start.14 = (bf16[2,256,256]{2,1,0:T(8,128)(2,1)S(1)}, bf16[2,256,256]{2,1,0:T(8,128)(2,1)S(1)}, u32[]{:S(2)}, u32[]{:S(2)}) collective-permute-start(bf16[2,256,256]{2,1,0:T(8,128)(2,1)S(1)} %get-tuple-element.54.refs_1_), channel_id=1, source_target_pairs={{12,0},{0,4},{4,8},{8,12},{13,1},{1,5},{5,9},{9,13},{14,2},{2,6},{... | collective-permute-start | bytes 786440 | tf_op jit(solution)/shard_map/ppermute | solution.py:218
  55.6 10.2 %collective-permute-start.22 = (bf16[2,256,256]{2,1,0:T(8,128)(2,1)S(1)}, bf16[2,256,256]{2,1,0:T(8,128)(2,1)S(1)}, u32[]{:S(2)}, u32[]{:S(2)}) collective-permute-start(bf16[2,256,256]{2,1,0:T(8,128)(2,1)S(1)} %get-tuple-element.53.refs_0_), channel_id=1, source_target_pairs={{12,0},{0,4},{4,8},{8,12},{13,1},{1,5},{5,9},{9,13},{14,2},{2,6},{... | collective-permute-start | bytes 786440 | tf_op jit(solution)/shard_map/ppermute | solution.py:218
  59.6 8.2 %collective-permute-start.21 = (bf16[2,256,256]{2,1,0:T(8,128)(2,1)S(1)}, bf16[2,256,256]{2,1,0:T(8,128)(2,1)S(1)}, u32[]{:S(2)}, u32[]{:S(2)}) collective-permute-start(bf16[2,256,256]{2,1,0:T(8,128)(2,1)S(1)} %get-tuple-element.54.refs_1_), channel_id=1, source_target_pairs={{4,0},{8,4},{12,8},{0,12},{5,1},{9,5},{13,9},{1,13},{6,2},{10,6},{... | collective-permute-start | bytes 786440 | tf_op jit(solution)/shard_map/ppermute | solution.py:218
  62.2 9.5 %collective-permute-start.23 = (bf16[2,256,256]{2,1,0:T(8,128)(2,1)S(1)}, bf16[2,256,256]{2,1,0:T(8,128)(2,1)S(1)}, u32[]{:S(2)}, u32[]{:S(2)}) collective-permute-start(bf16[2,256,256]{2,1,0:T(8,128)(2,1)S(1)} %collective-permute-done.13.refs_2_), channel_id=1, source_target_pairs={{4,0},{8,4},{12,8},{0,12},{5,1},{9,5},{13,9},{1,13},{6,2},{10,6},{... | collective-permute-start | bytes 786440 | tf_op jit(solution)/shard_map/ppermute | solution.py:218
  62.2 9.5 %collective-permute-start.24 = (bf16[2,256,256]{2,1,0:T(8,128)(2,1)S(1)}, bf16[2,256,256]{2,1,0:T(8,128)(2,1)S(1)}, u32[]{:S(2)}, u32[]{:S(2)}) collective-permute-start(bf16[2,256,256]{2,1,0:T(8,128)(2,1)S(1)} %collective-permute-done.14.refs_5_), channel_id=1, source_target_pairs={{12,0},{0,4},{4,8},{8,12},{13,1},{1,5},{5,9},{9,13},{14,2},{2,6},{... | collective-permute-start | bytes 786440 | tf_op jit(solution)/shard_map/ppermute | solution.py:218
  76.4 7.5 %collective-permute-start.29 = (bf16[2,256,256]{2,1,0:T(8,128)(2,1)S(1)}, bf16[2,256,256]{2,1,0:T(8,128)(2,1)S(1)}, u32[]{:S(2)}, u32[]{:S(2)}) collective-permute-start(bf16[2,256,256]{2,1,0:T(8,128)(2,1)S(1)} %get-tuple-element.62.refs_0_), channel_id=1, source_target_pairs={{4,0},{8,4},{12,8},{0,12},{5,1},{9,5},{13,9},{1,13},{6,2},{10,6},{... | collective-permute-start | bytes 786440 | tf_op jit(solution)/shard_map/ppermute | solution.py:218
  78.0 7.6 %collective-permute-start.30 = (bf16[2,256,256]{2,1,0:T(8,128)(2,1)S(1)}, bf16[2,256,256]{2,1,0:T(8,128)(2,1)S(1)}, u32[]{:S(2)}, u32[]{:S(2)}) collective-permute-start(bf16[2,256,256]{2,1,0:T(8,128)(2,1)S(1)} %get-tuple-element.63.refs_1_), channel_id=1, source_target_pairs={{12,0},{0,4},{4,8},{8,12},{13,1},{1,5},{5,9},{9,13},{14,2},{2,6},{... | collective-permute-start | bytes 786440 | tf_op jit(solution)/shard_map/ppermute | solution.py:218
  78.5 10.6 %collective-permute-start.32 = (bf16[2,256,256]{2,1,0:T(8,128)(2,1)S(1)}, bf16[2,256,256]{2,1,0:T(8,128)(2,1)S(1)}, u32[]{:S(2)}, u32[]{:S(2)}) collective-permute-start(bf16[2,256,256]{2,1,0:T(8,128)(2,1)S(1)} %get-tuple-element.62.refs_0_), channel_id=1, source_target_pairs={{12,0},{0,4},{4,8},{8,12},{13,1},{1,5},{5,9},{9,13},{14,2},{2,6},{... | collective-permute-start | bytes 786440 | tf_op jit(solution)/shard_map/ppermute | solution.py:218
  78.6 12.5 %collective-permute-start.31 = (bf16[2,256,256]{2,1,0:T(8,128)(2,1)S(1)}, bf16[2,256,256]{2,1,0:T(8,128)(2,1)S(1)}, u32[]{:S(2)}, u32[]{:S(2)}) collective-permute-start(bf16[2,256,256]{2,1,0:T(8,128)(2,1)S(1)} %get-tuple-element.63.refs_1_), channel_id=1, source_target_pairs={{4,0},{8,4},{12,8},{0,12},{5,1},{9,5},{13,9},{1,13},{6,2},{10,6},{... | collective-permute-start | bytes 786440 | tf_op jit(solution)/shard_map/ppermute | solution.py:218
  85.6 7.6 %collective-permute-start.34 = (bf16[2,256,256]{2,1,0:T(8,128)(2,1)S(1)}, bf16[2,256,256]{2,1,0:T(8,128)(2,1)S(1)}, u32[]{:S(2)}, u32[]{:S(2)}) collective-permute-start(bf16[2,256,256]{2,1,0:T(8,128)(2,1)S(1)} %collective-permute-done.30.refs_5_), channel_id=1, source_target_pairs={{12,0},{0,4},{4,8},{8,12},{13,1},{1,5},{5,9},{9,13},{14,2},{2,6},{... | collective-permute-start | bytes 786440 | tf_op jit(solution)/shard_map/ppermute | solution.py:218
  87.6 9.4 %collective-permute-start.35 = (bf16[256,256]{1,0:T(8,128)(2,1)S(1)}, bf16[256,256]{1,0:T(8,128)(2,1)S(1)}, u32[]{:S(2)}, u32[]{:S(2)}) collective-permute-start(bf16[256,256]{1,0:T(8,128)(2,1)S(1)} %get-tuple-element.71), channel_id=1, source_target_pairs={{3,0},{0,1},{1,2},{2,3},{7,4},{4,5},{5,6},{6,7},{11,8},{8,9},{9,10... | collective-permute-start | bytes 393224 | tf_op jit(solution)/shard_map/ppermute | solution.py:218
  89.1 7.9 %collective-permute-start.36 = (bf16[256,256]{1,0:T(8,128)(2,1)S(1)}, bf16[256,256]{1,0:T(8,128)(2,1)S(1)}, u32[]{:S(2)}, u32[]{:S(2)}) collective-permute-start(bf16[256,256]{1,0:T(8,128)(2,1)S(1)} %get-tuple-element.72), channel_id=1, source_target_pairs={{1,0},{2,1},{3,2},{0,3},{5,4},{6,5},{7,6},{4,7},{9,8},{10,9},{11,1... | collective-permute-start | bytes 393224 | tf_op jit(solution)/shard_map/ppermute | solution.py:218
  118.6 16.3 %all-to-all-start.2 = ((bf16[16,128,128]{2,1,0:T(8,128)(2,1)}), bf16[16,128,128]{2,1,0:T(8,128)(2,1)S(1)}, u32[]{:S(2)}, u32[]{:S(2)}) async-start(bf16[16,128,128]{2,1,0:T(8,128)(2,1)} %shard_map.103), calls=%async_computation.2 | async-start | bytes 1048576 | tf_op jit(solution)/shard_map/all_to_all | solution.py:315
  (13 other events, 111.4 us)
